TPU v7x, 128 devices: a whole 4x4x4 slice. The times are simulated.
128 devices in a mesh: row: 32 (over z, y, core), col: 4 (over x).
Axes of the slice: x: 4, y: 4, z: 4, core: 2. Of those that a mesh axis runs over, the one named last changes fastest.
Arguments:
- rhs: bfloat16 [8, 32, 64, 128], P(None, 'row'), may hold values from -6 to 6
- boundary: bfloat16 [512, 64, 128], P('row'), may hold values from -6 to 6
- diag_inv: bfloat16 [8, 32, 128, 128], P(None, 'row'), may hold values from -0.5 to 0.5
- off_blocks: bfloat16 [7, 32, 128, 128, 128], P(None, 'row', 'col'), may hold values from -0.09375 to 0.09375
- coupling: int32 [7, 32, 128], P(None, 'row', 'col'), may hold values from 0 to 735, as said below
- present: int32 [7, 32, 128], P(None, 'row', 'col'), may hold values 0 or 1
Outputs:
- solution: bfloat16 [8, 32, 64, 128], P(None, 'row')
Inputs may be any that keep to these rules, and one draw needn't show every extreme that they name: coupling[l, q, k] is below 512 + (l + 1) * 32: it names a boundary block or a block of an earlier level; the slots of one block row name distinct blocks.
All inputs are finite; a program needn't handle non-finite values. No bound on the sum of `present` on one device may be relied on, other than what follows from the above.
Results may differ from a plain program's by a relative error of at most 0.012.
Values may be sent and summed in bfloat16 or wider, within the bound.
No kernel may reach another device: no remote copies, remote signals or barrier semaphores. Data moves between devices by JAX's collectives and lax.ppermute only.
A program may use at most 128 MiB of HBM per device.

v0:
```python
import functools

import jax
import jax.numpy as jnp
from jax import lax
from jax.experimental import pallas as pl
from jax.experimental.pallas import tpu as pltpu
from jax.sharding import Mesh, PartitionSpec as P

ROWS = ("z", "y", "core")
VMEM_LIMIT = 24 * 1024 * 1024


def xor_pairs(n, k):
    return [(i, i ^ k) for i in range(n)]


def shift_pairs(n, k):
    return [(i, (i + k) % n) for i in range(n)]


def swap_cores(v):
    return lax.ppermute(v, "core", xor_pairs(2, 1))


def direct_gather(v, axis):
    return jnp.concatenate([v] + [lax.ppermute(v, axis, xor_pairs(4, k)) for k in (1, 2, 3)])


def ring_gather(v, axis):
    before = lax.ppermute(v, axis, shift_pairs(4, 1))
    after = lax.ppermute(v, axis, shift_pairs(4, 3))
    half = v.shape[0] // 2
    far_a = lax.ppermute(before[:half], axis, shift_pairs(4, 1))
    far_b = lax.ppermute(after[half:], axis, shift_pairs(4, 3))
    return [v, before, after, far_a, far_b]


def nt_dot(x, a):
    return lax.dot_general(x, a, (((1,), (1,)), ((), ())), preferred_element_type=jnp.float32)


GROUP = 8


def pick(sources, first, which, place, target, sem):
    if len(sources) == 1:
        pltpu.make_async_copy(sources[0].at[place], target, sem).start()
        return
    middle = len(sources) // 2

    @pl.when(which < first + middle)
    def _():
        pick(sources[:middle], first, which, place, target, sem)

    @pl.when(which >= first + middle)
    def _():
        pick(sources[middle:], first + middle, which, place, target, sem)


def old_kernel(level, code_ref, *refs):
    sources, (own_ref, other_ref, out_ref, picked, blocks, sem, block_sems) = refs[:-7], refs[-7:]
    slots = code_ref.shape[0]
    per_row = slots // 2
    loads = [
        pltpu.make_async_copy(a_ref.at[level - 1, 0], blocks.at[pl.ds(r * per_row, per_row)], block_sems.at[r])
        for r, a_ref in enumerate((own_ref, other_ref))
    ]
    for load in loads:
        load.start()

    def fetch(k, carry):
        code = jnp.maximum(code_ref[k], 0)
        pick(sources, 0, code >> 10, code & 1023, picked.at[k], sem)
        return carry

    lax.fori_loop(0, slots, fetch, 0)
    pltpu.make_async_copy(sources[0].at[pl.ds(0, slots)], picked, sem).wait()
    for r in range(2):
        loads[r].wait()
        total = None
        for g in range(r * per_row, (r + 1) * per_row, GROUP):
            xs, group = [], []
            for k in range(g, g + GROUP):
                kept = (code_ref[k] >= 0).astype(jnp.float32)
                xs.append((picked[k].astype(jnp.float32) * kept).astype(jnp.bfloat16))
                group.append(blocks[k])
            part = nt_dot(jnp.concatenate(xs, axis=1), jnp.concatenate(group, axis=1))
            total = part if total is None else total + part
        out_ref[r] = total


def old_sum(level, code, sources, own, other):
    slots, (rhs_cols, block) = code.shape[0], sources[0].shape[1:]
    return pl.pallas_call(
        functools.partial(old_kernel, level),
        out_shape=jax.ShapeDtypeStruct((2, rhs_cols, block), jnp.float32),
        in_specs=[pl.BlockSpec(memory_space=pltpu.SMEM)]
        + [pl.BlockSpec(memory_space=pl.ANY)] * len(sources)
        + [pl.BlockSpec(memory_space=pltpu.HBM)] * 2,
        out_specs=pl.BlockSpec(memory_space=pltpu.VMEM),
        scratch_shapes=[
            pltpu.VMEM((slots, rhs_cols, block), jnp.bfloat16),
            pltpu.VMEM((slots, block, block), jnp.bfloat16),
            pltpu.SemaphoreType.DMA,
            pltpu.SemaphoreType.DMA((2,)),
        ],
        compiler_params=pltpu.CompilerParams(vmem_limit_bytes=VMEM_LIMIT),
        cost_estimate=pl.CostEstimate(
            flops=2 * slots * rhs_cols * block * block,
            bytes_accessed=slots * block * (block + 2 * rhs_cols) * 4,
            transcendentals=0,
        ),
        name="old_sum",
    )(code, *sources, own, other)


def fresh_kernel(level, code_ref, old_ref, x_ref, own_ref, other_ref, out_ref, which, near_x, near_a, x_sems, a_sems):
    slots = code_ref.shape[0]
    per_row = slots // 2

    def fetch(slot, count):
        code = code_ref[slot]

        @pl.when(code >= 0)
        def _():
            which[count] = slot
            pltpu.make_async_copy(x_ref.at[code], near_x.at[count], x_sems.at[count]).start()

            @pl.when(slot < per_row)
            def _():
                pltpu.make_async_copy(own_ref.at[level - 1, 0, slot], near_a.at[count], a_sems.at[count]).start()

            @pl.when(slot >= per_row)
            def _():
                pltpu.make_async_copy(other_ref.at[level - 1, 0, slot - per_row], near_a.at[count], a_sems.at[count]).start()

        return count + (code >= 0).astype(jnp.int32)

    count = lax.fori_loop(0, slots, fetch, jnp.int32(0))
    out_ref[...] = old_ref[...]

    def add(n, carry):
        slot = which[n]
        pltpu.make_async_copy(x_ref.at[0], near_x.at[n], x_sems.at[n]).wait()
        pltpu.make_async_copy(own_ref.at[level - 1, 0, 0], near_a.at[n], a_sems.at[n]).wait()
        out_ref[(slot >= per_row).astype(jnp.int32)] += nt_dot(near_x[n], near_a[n])
        return carry

    lax.fori_loop(0, count, add, 0)


def fresh_sum(level, code, solved, old, own, other):
    slots, (rhs_cols, block) = code.shape[0], solved.shape[1:]
    return pl.pallas_call(
        functools.partial(fresh_kernel, level),
        out_shape=jax.ShapeDtypeStruct(old.shape, jnp.float32),
        in_specs=[
            pl.BlockSpec(memory_space=pltpu.SMEM),
            pl.BlockSpec(memory_space=pltpu.VMEM),
            pl.BlockSpec(memory_space=pl.ANY),
            pl.BlockSpec(memory_space=pltpu.HBM),
            pl.BlockSpec(memory_space=pltpu.HBM),
        ],
        out_specs=pl.BlockSpec(memory_space=pltpu.VMEM),
        scratch_shapes=[
            pltpu.SMEM((slots,), jnp.int32),
            pltpu.VMEM((slots, rhs_cols, block), jnp.bfloat16),
            pltpu.VMEM((slots, block, block), jnp.bfloat16),
            pltpu.SemaphoreType.DMA((slots,)),
            pltpu.SemaphoreType.DMA((slots,)),
        ],
        compiler_params=pltpu.CompilerParams(vmem_limit_bytes=VMEM_LIMIT),
        cost_estimate=pl.CostEstimate(
            flops=2 * 8 * rhs_cols * block * block, bytes_accessed=slots * block * block * 2, transcendentals=0
        ),
        name="fresh_sum",
    )(code, old, solved, own, other)


def solve_kernel(core_ref, p0, p1, p2, p3, rhs_ref, own_d_ref, other_d_ref, out_ref, *refs):
    for r, d_ref in enumerate((own_d_ref, other_d_ref)):
        coupled = (p0[r] + p1[r]) + (p2[r] + p3[r])
        reduced = (rhs_ref[r].astype(jnp.float32) - coupled).astype(jnp.bfloat16)
        solved = nt_dot(reduced, d_ref[...]).astype(jnp.bfloat16)
        out_ref[r] = solved
        if refs:
            refs[1][core_ref[0] ^ r] = solved
    if refs:
        all_ref, both, sems = refs
        sends = [pltpu.make_async_copy(both, all_ref.at[i], sems.at[i]) for i in range(all_ref.shape[0])]
        for send in sends:
            send.start()
        for send in sends:
            send.wait()


def solve_level(level, core, partials, rhs, own_d, other_d, copies):
    _, rhs_cols, block = partials[0].shape
    vmem = pl.BlockSpec(memory_space=pltpu.VMEM)
    out_shape, out_specs, scratch = [jax.ShapeDtypeStruct((2, rhs_cols, block), jnp.bfloat16)], [vmem], []
    if copies:
        out_shape.append(jax.ShapeDtypeStruct((copies, 2, rhs_cols, block), jnp.bfloat16))
        out_specs.append(pl.BlockSpec(memory_space=pltpu.HBM))
        scratch = [pltpu.VMEM((2, rhs_cols, block), jnp.bfloat16), pltpu.SemaphoreType.DMA((copies,))]
    return pl.pallas_call(
        solve_kernel,
        out_shape=out_shape,
        in_specs=[pl.BlockSpec(memory_space=pltpu.SMEM)] + [vmem] * 7,
        out_specs=out_specs,
        scratch_shapes=scratch,
        compiler_params=pltpu.CompilerParams(vmem_limit_bytes=VMEM_LIMIT),
        name="solve_level",
    )(core, *partials, rhs[level], own_d[level, 0], other_d[level, 0])


def on_device(rhs, boundary, diag_inv, off_blocks, coupling, present):
    levels, _, rhs_cols, block = rhs.shape
    outer_each = boundary.shape[0]
    outer = outer_each * 32
    half = rhs_cols // 2
    z, y, core = lax.axis_index("z"), lax.axis_index("y"), lax.axis_index("core")

    def my_half(v, axis):
        return lax.dynamic_slice_in_dim(v, core * half, half, axis)

    def their_half(v, axis):
        return lax.dynamic_slice_in_dim(v, (1 - core) * half, half, axis)

    first = jnp.einsum("rb,ab->ra", rhs[0, 0], diag_inv[0, 0], preferred_element_type=jnp.float32).astype(jnp.bfloat16)
    known = jnp.concatenate([boundary, first[None]])
    known_own = my_half(known, 1)
    known_own, known_other = lax.optimization_barrier((known_own, swap_cores(their_half(known, 1))))
    code_own = (coupling + 1024 * present)[:, 0]
    code_both = jnp.stack([code_own, swap_cores(code_own)], axis=1)
    rhs_both = jnp.concatenate([my_half(rhs, 2), swap_cores(their_half(rhs, 2))], axis=1)
    diag_other = swap_cores(diag_inv)
    off_sent, known_own = lax.optimization_barrier((off_blocks, known_own))
    off_other = swap_cores(off_sent)

    color_a = ring_gather(direct_gather(known_own, "z"), "y")
    color_b = ring_gather(direct_gather(known_other, "y"), "z")

    keep, index = code_both >= 1024, code_both % 1024
    in_outer = index < outer
    row = jnp.where(in_outer, index // outer_each, index - outer)
    member = jnp.where(in_outer, index % outer_each, outer_each)
    src_z, src_y, src_core = row // 8, (row // 2) % 4, row % 2
    each = outer_each + 1
    mine_too = src_core == core
    away = jnp.where(mine_too, src_y - y, src_z - z) % 4
    place = jnp.where(mine_too, src_z ^ z, src_y ^ y) * each + member
    far_half = (away == 2) & (place >= 2 * each)
    piece = jnp.where(away == 3, 1, jnp.where(away == 1, 2, jnp.where(away == 2, 3, 0))) + far_half
    place = jnp.where(far_half, place - 2 * each, place)
    code_known = (piece + jnp.where(mine_too, 0, 5)) * 1024 + place
    level_of = jnp.maximum(index - outer, 0) // 32
    code = jnp.where(level_of == 0, code_known, (9 + level_of) * 1024 + (index - outer) % 32)
    this = jnp.arange(levels - 1)[:, None, None]
    is_fresh = (level_of == this) & (level_of > 0)
    old_code = jnp.where(keep & ~is_fresh, code, -1).reshape(levels - 1, -1)
    fresh_code = jnp.where(keep & is_fresh, code % 1024, -1).reshape(levels - 1, -1)

    core_arr = jnp.reshape(core, (1,)).astype(jnp.int32)
    sources = color_a + color_b
    own_rows, other_rows = [], []
    value = old_sum(1, old_code[0], sources, off_blocks, off_other)
    for level in range(1, levels):
        partials = [value] + [lax.ppermute(value, "x", xor_pairs(4, k)) for k in (1, 2, 3)]
        last = level == levels - 1
        outs = solve_level(level, core_arr, partials, rhs_both, diag_inv, diag_other, 0 if last else 16)
        own_rows.append(outs[0][0])
        other_rows.append(outs[0][1])
        if not last:
            next_code, sent = lax.optimization_barrier((old_code[level], outs[1]))
            solved = lax.all_to_all(sent, ("z", "y"), 0, 0).reshape(32, half, block)
            old = old_sum(level + 1, next_code, sources, off_blocks, off_other)
            value = fresh_sum(level + 1, fresh_code[level], solved, old, off_blocks, off_other)
            sources = sources + [solved]

    mine = jnp.stack(own_rows)
    theirs = swap_cores(jnp.stack(other_rows))
    low = jnp.where(core == 0, mine, theirs)
    high = jnp.where(core == 0, theirs, mine)
    rest = jnp.concatenate([low, high], axis=1)
    return jnp.concatenate([first[None], rest])[:, None]


def solution(mesh):
    split = Mesh(mesh.devices.reshape(4, 4, 2, 4), ("z", "y", "core", "x"))
    in_specs = (
        P(None, ROWS, None, None),
        P(ROWS, None, None),
        P(None, ROWS, None, None),
        P(None, ROWS, "x", None, None),
        P(None, ROWS, "x"),
        P(None, ROWS, "x"),
    )
    return jax.shard_map(
        on_device, mesh=split, in_specs=in_specs, out_specs=P(None, ROWS, None, None), check_vma=False
    )
```

profile of v0, /device:TPU:1, one launch (start us, length us, event | category | flops | bytes accessed | tf_op | source)
XLA Modules:
  0.0 304.5 jit_solution(17614197038004906684)
XLA Ops:
  11.2 3.8 %collective-permute-start.4 = (bf16[17,32,128]{2,1,0:T(8,128)(2,1)S(1)}, bf16[17,32,128]{2,1,0:T(8,128)(2,1)S(1)}, u32[]{:S(2)}, u32[]{:S(2)}) collective-permute-start(bf16[17,32,128]{2,1,0:T(8,128)(2,1)S(1)} %get-tuple-element.34), channel_id=1, source_target_pairs={{0,96},{32,64},{64,32},{96,0},{1,97},{33,65},{65,33},{97,1},{2,98}... | collective-permute-start | bytes 417800 | tf_op jit(solution)/shard_map/ppermute | solution.py:27
  19.4 3.3 %collective-permute-done.11 = bf16[17,32,128]{2,1,0:T(8,128)(2,1)S(1)} collective-permute-done((bf16[17,32,128]{2,1,0:T(8,128)(2,1)S(1)}, bf16[17,32,128]{2,1,0:T(8,128)(2,1)S(1)}, u32[]{:S(2)}, u32[]{:S(2)}) %collective-permute-start.11) | collective-permute-done | bytes 139296 | tf_op jit(solution)/shard_map/ppermute | solution.py:27
  22.8 3.6 %collective-permute-start.3 = (bf16[17,32,128]{2,1,0:T(8,128)(2,1)S(1)}, bf16[17,32,128]{2,1,0:T(8,128)(2,1)S(1)}, u32[]{:S(2)}, u32[]{:S(2)}) collective-permute-start(bf16[17,32,128]{2,1,0:T(8,128)(2,1)S(1)} %get-tuple-element.34), channel_id=1, source_target_pairs={{0,64},{32,96},{64,0},{96,32},{1,65},{33,97},{65,1},{97,33},{2,66}... | collective-permute-start | bytes 417800 | tf_op jit(solution)/shard_map/ppermute | solution.py:27
  32.9 7.7 %collective-permute-done.13.refs_7_ = bf16[68,32,128]{2,1,0:T(8,128)(2,1)S(1)} collective-permute-done((bf16[68,32,128]{2,1,0:T(8,128)(2,1)S(1)}, bf16[68,32,128]{2,1,0:T(8,128)(2,1)S(1)}, u32[]{:S(2)}, u32[]{:S(2)}) %collective-permute-start.13) | collective-permute-done | bytes 557088 | tf_op jit(solution)/shard_map/ppermute | solution.py:32
  40.7 3.5 %collective-permute-start.15 = (bf16[34,32,128]{2,1,0:T(8,128)(2,1)S(1)}, bf16[34,32,128]{2,1,0:T(8,128)(2,1)S(1)}, u32[]{:S(2)}, u32[]{:S(2)}) collective-permute-start(bf16[34,32,128]{2,1,0:T(8,128)(2,1)S(1)} %slice.233), channel_id=1, source_target_pairs={{0,96},{32,0},{64,32},{96,64},{1,97},{33,1},{65,33},{97,65},{2,98}... | collective-permute-start | bytes 835592 | tf_op jit(solution)/shard_map/ppermute | solution.py:35
  54.4 3.6 %collective-permute-done.14.refs_8_ = bf16[34,32,128]{2,1,0:T(8,128)(2,1)} collective-permute-done((bf16[34,32,128]{2,1,0:T(8,128)(2,1)}, bf16[34,32,128]{2,1,0:T(8,128)(2,1)}, u32[]{:S(2)}, u32[]{:S(2)}) %collective-permute-start.14) | collective-permute-done | bytes 278560 | tf_op jit(solution)/shard_map/ppermute | solution.py:34
  63.5 5.3 %old_sum.7.p0 = f32[2,32,128]{2,1,0:T(8,128)S(1)} custom-call(s32[64]{0:T(128)S(1)} %squeeze.114.code_ref, bf16[68,32,128]{2,1,0:T(8,128)(2,1)S(1)} %constant_dynamic-update-slice_fusion.refs_0_, bf16[68,32,128]{2,1,0:T(8,128)(2,1)S(1)} %collective-permute-done.5.refs_1_, bf16[68,32,128]{2,1,0:T(8,128)(2,1)S(1)} %collective-permute-done.6.refs_2_, ...), custom_call_target="tpu_custom_call" | custom-call | flops 67108864 | bytes 6291456 | tf_op jit(solution)/shard_map/old_sum/pallas_call | solution.py:95
  76.4 4.3 %all-to-all-start = ((bf16[16,2,32,128]{3,2,1,0:T(8,128)(2,1)}), bf16[16,2,32,128]{3,2,1,0:T(8,128)(2,1)}, u32[]{:S(2)}, u32[]{:S(2)}) async-start(bf16[16,2,32,128]{3,2,1,0:T(8,128)(2,1)} %copy-done.23), calls=%async_computation | async-start | bytes 524288 | tf_op jit(solution)/shard_map/all_to_all | solution.py:276
  87.3 4.7 %old_sum.8.old_ref = f32[2,32,128]{2,1,0:T(8,128)S(1)} custom-call(s32[64]{0:T(128)S(1)} %copy-done.56, bf16[68,32,128]{2,1,0:T(8,128)(2,1)S(1)} %constant_dynamic-update-slice_fusion.refs_0_, bf16[68,32,128]{2,1,0:T(8,128)(2,1)S(1)} %collective-permute-done.5.refs_1_, bf16[68,32,128]{2,1,0:T(8,128)(2,1)S(1)} %collective-permute-done.6.refs_2_, ...), custom_call_target="tpu_custom_call" | custom-call | flops 67108864 | bytes 6291456 | tf_op jit(solution)/shard_map/old_sum/pallas_call | solution.py:95
  109.9 7.5 %all-to-all-start.1 = ((bf16[16,2,32,128]{3,2,1,0:T(8,128)(2,1)}), bf16[16,2,32,128]{3,2,1,0:T(8,128)(2,1)}, u32[]{:S(2)}, u32[]{:S(2)}) async-start(bf16[16,2,32,128]{3,2,1,0:T(8,128)(2,1)} %copy-done.24), calls=%async_computation.1 | async-start | bytes 524288 | tf_op jit(solution)/shard_map/all_to_all | solution.py:276
  123.2 5.3 %old_sum.9.old_ref = f32[2,32,128]{2,1,0:T(8,128)S(1)} custom-call(s32[64]{0:T(128)S(1)} %copy-done.59, bf16[68,32,128]{2,1,0:T(8,128)(2,1)S(1)} %constant_dynamic-update-slice_fusion.refs_0_, bf16[68,32,128]{2,1,0:T(8,128)(2,1)S(1)} %collective-permute-done.5.refs_1_, bf16[68,32,128]{2,1,0:T(8,128)(2,1)S(1)} %collective-permute-done.6.refs_2_, ...), custom_call_target="tpu_custom_call" | custom-call | flops 67108864 | bytes 6291456 | tf_op jit(solution)/shard_map/old_sum/pallas_call | solution.py:95
  132.1 3.3 %fresh_sum.7.p0 = f32[2,32,128]{2,1,0:T(8,128)S(1)} custom-call(s32[64]{0:T(128)S(1)} %copy-done.63, f32[2,32,128]{2,1,0:T(8,128)S(1)} %old_sum.9.old_ref, bf16[32,32,128]{2,1,0:T(8,128)(2,1)} %bitcast.11.x_ref.refs_11_, bf16[7,1,32,128,128]{4,3,2,1,0:T(8,128)(2,1)S(1)} %copy-done.4, ...), custom_call_target="tpu_custom_call" | custom-call | flops 8388608 | bytes 2097152 | tf_op jit(solution)/shard_map/fresh_sum/pallas_call | solution.py:155
  147.2 6.6 %all-to-all-start.2 = ((bf16[16,2,32,128]{3,2,1,0:T(8,128)(2,1)}), bf16[16,2,32,128]{3,2,1,0:T(8,128)(2,1)}, u32[]{:S(2)}, u32[]{:S(2)}) async-start(bf16[16,2,32,128]{3,2,1,0:T(8,128)(2,1)} %copy-done.25), calls=%async_computation.2 | async-start | bytes 524288 | tf_op jit(solution)/shard_map/all_to_all | solution.py:276
  159.7 5.2 %old_sum.10.old_ref = f32[2,32,128]{2,1,0:T(8,128)S(1)} custom-call(s32[64]{0:T(128)S(1)} %copy-done.60, bf16[68,32,128]{2,1,0:T(8,128)(2,1)S(1)} %constant_dynamic-update-slice_fusion.refs_0_, bf16[68,32,128]{2,1,0:T(8,128)(2,1)S(1)} %collective-permute-done.5.refs_1_, bf16[68,32,128]{2,1,0:T(8,128)(2,1)S(1)} %collective-permute-done.6.refs_2_, ...), custom_call_target="tpu_custom_call" | custom-call | flops 67108864 | bytes 6291456 | tf_op jit(solution)/shard_map/old_sum/pallas_call | solution.py:95
  168.6 3.4 %fresh_sum.8.p0 = f32[2,32,128]{2,1,0:T(8,128)S(1)} custom-call(s32[64]{0:T(128)S(1)} %copy-done.64, f32[2,32,128]{2,1,0:T(8,128)S(1)} %old_sum.10.old_ref, bf16[32,32,128]{2,1,0:T(8,128)(2,1)} %bitcast.15.x_ref.refs_12_, bf16[7,1,32,128,128]{4,3,2,1,0:T(8,128)(2,1)S(1)} %copy-done.6, ...), custom_call_target="tpu_custom_call" | custom-call | flops 8388608 | bytes 2097152 | tf_op jit(solution)/shard_map/fresh_sum/pallas_call | solution.py:155
  183.3 6.8 %all-to-all-start.3 = ((bf16[16,2,32,128]{3,2,1,0:T(8,128)(2,1)}), bf16[16,2,32,128]{3,2,1,0:T(8,128)(2,1)}, u32[]{:S(2)}, u32[]{:S(2)}) async-start(bf16[16,2,32,128]{3,2,1,0:T(8,128)(2,1)} %copy-done.26), calls=%async_computation.3 | async-start | bytes 524288 | tf_op jit(solution)/shard_map/all_to_all | solution.py:276
  196.1 5.2 %old_sum.11.old_ref = f32[2,32,128]{2,1,0:T(8,128)S(1)} custom-call(s32[64]{0:T(128)S(1)} %copy-done.61, bf16[68,32,128]{2,1,0:T(8,128)(2,1)S(1)} %constant_dynamic-update-slice_fusion.refs_0_, bf16[68,32,128]{2,1,0:T(8,128)(2,1)S(1)} %collective-permute-done.5.refs_1_, bf16[68,32,128]{2,1,0:T(8,128)(2,1)S(1)} %collective-permute-done.6.refs_2_, ...), custom_call_target="tpu_custom_call" | custom-call | flops 67108864 | bytes 6291456 | tf_op jit(solution)/shard_map/old_sum/pallas_call | solution.py:95
  205.1 3.4 %fresh_sum.9.p0 = f32[2,32,128]{2,1,0:T(8,128)S(1)} custom-call(s32[64]{0:T(128)S(1)} %copy-done.65, f32[2,32,128]{2,1,0:T(8,128)S(1)} %old_sum.11.old_ref, bf16[32,32,128]{2,1,0:T(8,128)(2,1)} %bitcast.19.x_ref.refs_13_, bf16[7,1,32,128,128]{4,3,2,1,0:T(8,128)(2,1)S(1)} %copy-done.8, ...), custom_call_target="tpu_custom_call" | custom-call | flops 8388608 | bytes 2097152 | tf_op jit(solution)/shard_map/fresh_sum/pallas_call | solution.py:155
  221.7 6.6 %all-to-all-start.4 = ((bf16[16,2,32,128]{3,2,1,0:T(8,128)(2,1)}), bf16[16,2,32,128]{3,2,1,0:T(8,128)(2,1)}, u32[]{:S(2)}, u32[]{:S(2)}) async-start(bf16[16,2,32,128]{3,2,1,0:T(8,128)(2,1)} %copy-done.22), calls=%async_computation.4 | async-start | bytes 524288 | tf_op jit(solution)/shard_map/all_to_all | solution.py:276
  235.5 5.4 %old_sum.12.old_ref = f32[2,32,128]{2,1,0:T(8,128)S(1)} custom-call(s32[64]{0:T(128)S(1)} %copy-done.58, bf16[68,32,128]{2,1,0:T(8,128)(2,1)S(1)} %constant_dynamic-update-slice_fusion.refs_0_, bf16[68,32,128]{2,1,0:T(8,128)(2,1)S(1)} %collective-permute-done.5.refs_1_, bf16[68,32,128]{2,1,0:T(8,128)(2,1)S(1)} %collective-permute-done.6.refs_2_, ...), custom_call_target="tpu_custom_call" | custom-call | flops 67108864 | bytes 6291456 | tf_op jit(solution)/shard_map/old_sum/pallas_call | solution.py:95
  244.0 3.6 %fresh_sum.10.p0 = f32[2,32,128]{2,1,0:T(8,128)S(1)} custom-call(s32[64]{0:T(128)S(1)} %copy-done.57, f32[2,32,128]{2,1,0:T(8,128)S(1)} %old_sum.12.old_ref, bf16[32,32,128]{2,1,0:T(8,128)(2,1)} %bitcast.23.x_ref.refs_14_, bf16[7,1,32,128,128]{4,3,2,1,0:T(8,128)(2,1)S(1)} %copy-done.10, ...), custom_call_target="tpu_custom_call" | custom-call | flops 8388608 | bytes 2097152 | tf_op jit(solution)/shard_map/fresh_sum/pallas_call | solution.py:155
  255.2 6.4 %all-to-all-start.5 = ((bf16[16,2,32,128]{3,2,1,0:T(8,128)(2,1)}), bf16[16,2,32,128]{3,2,1,0:T(8,128)(2,1)}, u32[]{:S(2)}, u32[]{:S(2)}) async-start(bf16[16,2,32,128]{3,2,1,0:T(8,128)(2,1)} %copy-done.21), calls=%async_computation.5 | async-start | bytes 524288 | tf_op jit(solution)/shard_map/all_to_all | solution.py:276
  268.8 5.3 %old_sum.13.old_ref = f32[2,32,128]{2,1,0:T(8,128)S(1)} custom-call(s32[64]{0:T(128)S(1)} %copy-done.55, bf16[68,32,128]{2,1,0:T(8,128)(2,1)S(1)} %constant_dynamic-update-slice_fusion.refs_0_, bf16[68,32,128]{2,1,0:T(8,128)(2,1)S(1)} %collective-permute-done.5.refs_1_, bf16[68,32,128]{2,1,0:T(8,128)(2,1)S(1)} %collective-permute-done.6.refs_2_, ...), custom_call_target="tpu_custom_call" | custom-call | flops 67108864 | bytes 6291456 | tf_op jit(solution)/shard_map/old_sum/pallas_call | solution.py:95
  286.4 15.5 %collective-permute-start.40 = (bf16[7,32,128]{2,1,0:T(8,128)(2,1)}, bf16[7,32,128]{2,1,0:T(8,128)(2,1)S(1)}, u32[]{:S(2)}, u32[]{:S(2)}) collective-permute-start(bf16[7,32,128]{2,1,0:T(8,128)(2,1)} %get-tuple-element.92), channel_id=1, source_target_pairs={{0,4},{4,0},{1,5},{5,1},{2,6},{6,2},{3,7},{7,3},{8,12},{12,8},{9,1... | collective-permute-start | bytes 172040 | tf_op jit(solution)/shard_map/ppermute | solution.py:23
  (275 shorter events, 174.8 us)
Async XLA Ops:
  5.0 54.5 %collective-permute-start.16 = (bf16[7,1,32,128,128]{4,3,2,1,0:T(8,128)(2,1)}, bf16[7,1,32,128,128]{4,3,2,1,0:T(8,128)(2,1)}, u32[]{:S(2)}, u32[]{:S(2)}) collective-permute-start(bf16[7,1,32,128,128]{4,3,2,1,0:T(8,128)(2,1)} %own_ref.11), channel_id=1, source_target_pairs={{0,4},{4,0},{1,5},{5,1},{2,6},{6,2},{3,7},{7,3},{8,12},{12,8},{9,1... | collective-permute-start | bytes 22020104 | tf_op jit(solution)/shard_map/ppermute | solution.py:23
  6.1 24.9 %collective-permute-start = (s32[7,32]{1,0:T(8,128)S(1)}, s32[7,32]{1,0:T(8,128)S(1)}, u32[]{:S(2)}, u32[]{:S(2)}) collective-permute-start(s32[7,32]{1,0:T(8,128)S(1)} %bitcast.64), channel_id=1, source_target_pairs={{0,4},{4,0},{1,5},{5,1},{2,6},{6,2},{3,7},{7,3},{8,12},{12,8},{9,1... | collective-permute-start | bytes 2696 | tf_op jit(solution)/shard_map/ppermute | solution.py:23
  7.8 9.8 %collective-permute-start.10 = (bf16[17,32,128]{2,1,0:T(8,128)(2,1)S(1)}, bf16[17,32,128]{2,1,0:T(8,128)(2,1)S(1)}, u32[]{:S(2)}, u32[]{:S(2)}) collective-permute-start(bf16[17,32,128]{2,1,0:T(8,128)(2,1)S(1)} %collective-permute-done.1), channel_id=1, source_target_pairs={{0,16},{8,24},{16,0},{24,8},{1,17},{9,25},{17,1},{25,9},{2,18},{10... | collective-permute-start | bytes 417800 | tf_op jit(solution)/shard_map/ppermute | solution.py:27
  10.8 6.8 %collective-permute-start.9 = (bf16[17,32,128]{2,1,0:T(8,128)(2,1)S(1)}, bf16[17,32,128]{2,1,0:T(8,128)(2,1)S(1)}, u32[]{:S(2)}, u32[]{:S(2)}) collective-permute-start(bf16[17,32,128]{2,1,0:T(8,128)(2,1)S(1)} %collective-permute-done.1), channel_id=1, source_target_pairs={{0,8},{8,0},{16,24},{24,16},{1,9},{9,1},{17,25},{25,17},{2,10},{10... | collective-permute-start | bytes 417800 | tf_op jit(solution)/shard_map/ppermute | solution.py:27
  11.2 18.6 %collective-permute-start.4 = (bf16[17,32,128]{2,1,0:T(8,128)(2,1)S(1)}, bf16[17,32,128]{2,1,0:T(8,128)(2,1)S(1)}, u32[]{:S(2)}, u32[]{:S(2)}) collective-permute-start(bf16[17,32,128]{2,1,0:T(8,128)(2,1)S(1)} %get-tuple-element.34), channel_id=1, source_target_pairs={{0,96},{32,64},{64,32},{96,0},{1,97},{33,65},{65,33},{97,1},{2,98}... | collective-permute-start | bytes 417800 | tf_op jit(solution)/shard_map/ppermute | solution.py:27
  17.7 8.7 %collective-permute-start.2 = (bf16[17,32,128]{2,1,0:T(8,128)(2,1)S(1)}, bf16[17,32,128]{2,1,0:T(8,128)(2,1)S(1)}, u32[]{:S(2)}, u32[]{:S(2)}) collective-permute-start(bf16[17,32,128]{2,1,0:T(8,128)(2,1)S(1)} %get-tuple-element.34), channel_id=1, source_target_pairs={{0,32},{32,0},{64,96},{96,64},{1,33},{33,1},{65,97},{97,65},{2,34}... | collective-permute-start | bytes 417800 | tf_op jit(solution)/shard_map/ppermute | solution.py:27
  26.4 14.3 %collective-permute-start.13 = (bf16[68,32,128]{2,1,0:T(8,128)(2,1)S(1)}, bf16[68,32,128]{2,1,0:T(8,128)(2,1)S(1)}, u32[]{:S(2)}, u32[]{:S(2)}) collective-permute-start(bf16[68,32,128]{2,1,0:T(8,128)(2,1)S(1)} %constant_dynamic-update-slice_fusion.4.refs_5_), channel_id=1, source_target_pairs={{0,96},{32,0},{64,32},{96,64},{1,97},{33,1},{65,33},{97,65},{2,98}... | collective-permute-start | bytes 1671176 | tf_op jit(solution)/shard_map/ppermute | solution.py:32
  28.8 16.1 %collective-permute-start.12 = (bf16[68,32,128]{2,1,0:T(8,128)(2,1)S(1)}, bf16[68,32,128]{2,1,0:T(8,128)(2,1)S(1)}, u32[]{:S(2)}, u32[]{:S(2)}) collective-permute-start(bf16[68,32,128]{2,1,0:T(8,128)(2,1)S(1)} %constant_dynamic-update-slice_fusion.4.refs_5_), channel_id=1, source_target_pairs={{0,32},{32,64},{64,96},{96,0},{1,33},{33,65},{65,97},{97,1},{2,34}... | collective-permute-start | bytes 1671176 | tf_op jit(solution)/shard_map/ppermute | solution.py:31
  29.9 18.1 %collective-permute-start.6 = (bf16[68,32,128]{2,1,0:T(8,128)(2,1)S(1)}, bf16[68,32,128]{2,1,0:T(8,128)(2,1)S(1)}, u32[]{:S(2)}, u32[]{:S(2)}) collective-permute-start(bf16[68,32,128]{2,1,0:T(8,128)(2,1)S(1)} %constant_dynamic-update-slice_fusion.refs_0_), channel_id=1, source_target_pairs={{0,24},{8,0},{16,8},{24,16},{1,25},{9,1},{17,9},{25,17},{2,26},{10... | collective-permute-start | bytes 1671176 | tf_op jit(solution)/shard_map/ppermute | solution.py:32
  31.0 17.7 %collective-permute-start.5 = (bf16[68,32,128]{2,1,0:T(8,128)(2,1)S(1)}, bf16[68,32,128]{2,1,0:T(8,128)(2,1)S(1)}, u32[]{:S(2)}, u32[]{:S(2)}) collective-permute-start(bf16[68,32,128]{2,1,0:T(8,128)(2,1)S(1)} %constant_dynamic-update-slice_fusion.refs_0_), channel_id=1, source_target_pairs={{0,8},{8,16},{16,24},{24,0},{1,9},{9,17},{17,25},{25,1},{2,10},{10... | collective-permute-start | bytes 1671176 | tf_op jit(solution)/shard_map/ppermute | solution.py:31
  40.7 8.8 %collective-permute-start.15 = (bf16[34,32,128]{2,1,0:T(8,128)(2,1)S(1)}, bf16[34,32,128]{2,1,0:T(8,128)(2,1)S(1)}, u32[]{:S(2)}, u32[]{:S(2)}) collective-permute-start(bf16[34,32,128]{2,1,0:T(8,128)(2,1)S(1)} %slice.233), channel_id=1, source_target_pairs={{0,96},{32,0},{64,32},{96,64},{1,97},{33,1},{65,33},{97,65},{2,98}... | collective-permute-start | bytes 835592 | tf_op jit(solution)/shard_map/ppermute | solution.py:35
  48.0 24.2 %collective-permute-start.21 = (bf16[8,1,128,128]{3,2,1,0:T(8,128)(2,1)}, bf16[8,1,128,128]{3,2,1,0:T(8,128)(2,1)}, u32[]{:S(2)}, u32[]{:S(2)}) collective-permute-start(bf16[8,1,128,128]{3,2,1,0:T(8,128)(2,1)} %param.8), channel_id=1, source_target_pairs={{0,4},{4,0},{1,5},{5,1},{2,6},{6,2},{3,7},{7,3},{8,12},{12,8},{9,1... | collective-permute-start | bytes 786440 | tf_op jit(solution)/shard_map/ppermute | solution.py:23
  48.7 9.2 %collective-permute-start.14 = (bf16[34,32,128]{2,1,0:T(8,128)(2,1)}, bf16[34,32,128]{2,1,0:T(8,128)(2,1)}, u32[]{:S(2)}, u32[]{:S(2)}) collective-permute-start(bf16[34,32,128]{2,1,0:T(8,128)(2,1)} %slice.232), channel_id=1, source_target_pairs={{0,32},{32,64},{64,96},{96,0},{1,33},{33,65},{65,97},{97,1},{2,34}... | collective-permute-start | bytes 835592 | tf_op jit(solution)/shard_map/ppermute | solution.py:34
  49.4 8.5 %collective-permute-start.8 = (bf16[34,32,128]{2,1,0:T(8,128)(2,1)}, bf16[34,32,128]{2,1,0:T(8,128)(2,1)}, u32[]{:S(2)}, u32[]{:S(2)}) collective-permute-start(bf16[34,32,128]{2,1,0:T(8,128)(2,1)} %slice.231), channel_id=1, source_target_pairs={{0,24},{8,0},{16,8},{24,16},{1,25},{9,1},{17,9},{25,17},{2,26},{10... | collective-permute-start | bytes 835592 | tf_op jit(solution)/shard_map/ppermute | solution.py:35
  50.8 8.7 %collective-permute-start.7 = (bf16[34,32,128]{2,1,0:T(8,128)(2,1)}, bf16[34,32,128]{2,1,0:T(8,128)(2,1)}, u32[]{:S(2)}, u32[]{:S(2)}) collective-permute-start(bf16[34,32,128]{2,1,0:T(8,128)(2,1)} %slice.230), channel_id=1, source_target_pairs={{0,8},{8,16},{16,24},{24,0},{1,9},{9,17},{17,25},{25,1},{2,10},{10... | collective-permute-start | bytes 835592 | tf_op jit(solution)/shard_map/ppermute | solution.py:34
  76.4 15.6 %all-to-all-start = ((bf16[16,2,32,128]{3,2,1,0:T(8,128)(2,1)}), bf16[16,2,32,128]{3,2,1,0:T(8,128)(2,1)}, u32[]{:S(2)}, u32[]{:S(2)}) async-start(bf16[16,2,32,128]{3,2,1,0:T(8,128)(2,1)} %copy-done.23), calls=%async_computation | async-start | bytes 524288 | tf_op jit(solution)/shard_map/all_to_all | solution.py:276
  109.9 18.6 %all-to-all-start.1 = ((bf16[16,2,32,128]{3,2,1,0:T(8,128)(2,1)}), bf16[16,2,32,128]{3,2,1,0:T(8,128)(2,1)}, u32[]{:S(2)}, u32[]{:S(2)}) async-start(bf16[16,2,32,128]{3,2,1,0:T(8,128)(2,1)} %copy-done.24), calls=%async_computation.1 | async-start | bytes 524288 | tf_op jit(solution)/shard_map/all_to_all | solution.py:276
  147.2 17.7 %all-to-all-start.2 = ((bf16[16,2,32,128]{3,2,1,0:T(8,128)(2,1)}), bf16[16,2,32,128]{3,2,1,0:T(8,128)(2,1)}, u32[]{:S(2)}, u32[]{:S(2)}) async-start(bf16[16,2,32,128]{3,2,1,0:T(8,128)(2,1)} %copy-done.25), calls=%async_computation.2 | async-start | bytes 524288 | tf_op jit(solution)/shard_map/all_to_all | solution.py:276
  183.3 18.0 %all-to-all-start.3 = ((bf16[16,2,32,128]{3,2,1,0:T(8,128)(2,1)}), bf16[16,2,32,128]{3,2,1,0:T(8,128)(2,1)}, u32[]{:S(2)}, u32[]{:S(2)}) async-start(bf16[16,2,32,128]{3,2,1,0:T(8,128)(2,1)} %copy-done.26), calls=%async_computation.3 | async-start | bytes 524288 | tf_op jit(solution)/shard_map/all_to_all | solution.py:276
  208.4 8.3 %collective-permute-start.33 = (f32[2,32,128]{2,1,0:T(8,128)S(1)}, f32[2,32,128]{2,1,0:T(8,128)S(1)}, u32[]{:S(2)}, u32[]{:S(2)}) collective-permute-start(f32[2,32,128]{2,1,0:T(8,128)S(1)} %fresh_sum.9.p0), channel_id=1, source_target_pairs={{0,3},{1,2},{2,1},{3,0},{4,7},{5,6},{6,5},{7,4},{8,11},{9,10},{10,... | collective-permute-start | bytes 98312 | tf_op jit(solution)/shard_map/ppermute | solution.py:269
  210.5 6.8 %collective-permute-start.32 = (f32[2,32,128]{2,1,0:T(8,128)S(1)}, f32[2,32,128]{2,1,0:T(8,128)}, u32[]{:S(2)}, u32[]{:S(2)}) collective-permute-start(f32[2,32,128]{2,1,0:T(8,128)S(1)} %fresh_sum.9.p0), channel_id=1, source_target_pairs={{0,2},{1,3},{2,0},{3,1},{4,6},{5,7},{6,4},{7,5},{8,10},{9,11},{10,... | collective-permute-start | bytes 98312 | tf_op jit(solution)/shard_map/ppermute | solution.py:269
  221.7 19.2 %all-to-all-start.4 = ((bf16[16,2,32,128]{3,2,1,0:T(8,128)(2,1)}), bf16[16,2,32,128]{3,2,1,0:T(8,128)(2,1)}, u32[]{:S(2)}, u32[]{:S(2)}) async-start(bf16[16,2,32,128]{3,2,1,0:T(8,128)(2,1)} %copy-done.22), calls=%async_computation.4 | async-start | bytes 524288 | tf_op jit(solution)/shard_map/all_to_all | solution.py:276
  255.2 18.9 %all-to-all-start.5 = ((bf16[16,2,32,128]{3,2,1,0:T(8,128)(2,1)}), bf16[16,2,32,128]{3,2,1,0:T(8,128)(2,1)}, u32[]{:S(2)}, u32[]{:S(2)}) async-start(bf16[16,2,32,128]{3,2,1,0:T(8,128)(2,1)} %copy-done.21), calls=%async_computation.5 | async-start | bytes 524288 | tf_op jit(solution)/shard_map/all_to_all | solution.py:276
  286.4 16.6 %collective-permute-start.40 = (bf16[7,32,128]{2,1,0:T(8,128)(2,1)}, bf16[7,32,128]{2,1,0:T(8,128)(2,1)S(1)}, u32[]{:S(2)}, u32[]{:S(2)}) collective-permute-start(bf16[7,32,128]{2,1,0:T(8,128)(2,1)} %get-tuple-element.92), channel_id=1, source_target_pairs={{0,4},{4,0},{1,5},{5,1},{2,6},{6,2},{3,7},{7,3},{8,12},{12,8},{9,1... | collective-permute-start | bytes 172040 | tf_op jit(solution)/shard_map/ppermute | solution.py:23
  (92 other events, 259.9 us)
where the time goes:
time: 308 us; the launch traced here: 304 us
  local copies, waits for them, and re-layouts  104 us (34%)
  starting transfers between devices  101 us (33%)
  Pallas kernels  63.2 us (21%)
  waiting for transfers between devices  29.3 us (10%)
  other arithmetic  5.49 us (2%)
    unnamed x151, local copies, waits for them, and re-layouts  80.9 us
    all_to_all x6, starting transfers between devices, on_device(): solved = lax.all_to_all(sent, ('z', 'y'), 0, 0).reshape(32, half, block)  38.2 us
    pallas_call x7, Pallas kernels, old_sum(): pl.pallas_call(functools.partial(old_kernel, level), out_shape=jax.ShapeD...  36.3 us
    ppermute x21, starting transfers between devices, on_device(): lax.ppermute(value, 'x', xor_pairs(4, k))  23.3 us
    ppermute x6, starting transfers between devices, swap_cores(): return lax.ppermute(v, 'core', xor_pairs(2, 1))  19.8 us
    pallas_call x6, Pallas kernels, fresh_sum(): pl.pallas_call(functools.partial(fresh_kernel, level), out_shape=jax.Shap...  19.8 us
    ppermute x6, starting transfers between devices, direct_gather(): lax.ppermute(v, axis, xor_pairs(4, k))  12.5 us
    ppermute x6, waiting for transfers between devices, direct_gather(): lax.ppermute(v, axis, xor_pairs(4, k))  7.86 us
  transfers between devices with their start and end apart: 47, of which 16 were waited for; matrix products, arithmetic and copies ran while one was open for 10% of the time, Pallas kernels for 12%

commit v1 on v0

v1 whole, which is shorter than its diff:
```python
import functools

import jax
import jax.numpy as jnp
from jax import lax
from jax.experimental import pallas as pl
from jax.experimental.pallas import tpu as pltpu
from jax.sharding import Mesh, PartitionSpec as P

ROWS = ("z", "y", "core")
VMEM_LIMIT = 48 * 1024 * 1024


def xor_pairs(n, k):
    return [(i, i ^ k) for i in range(n)]


def shift_pairs(n, k):
    return [(i, (i + k) % n) for i in range(n)]


def swap_cores(v):
    return lax.ppermute(v, "core", xor_pairs(2, 1))


def direct_gather(v, axis):
    return jnp.concatenate([v] + [lax.ppermute(v, axis, xor_pairs(4, k)) for k in (1, 2, 3)])


def ring_gather(v, axis):
    before = lax.ppermute(v, axis, shift_pairs(4, 1))
    after = lax.ppermute(v, axis, shift_pairs(4, 3))
    half = v.shape[0] // 2
    far_a = lax.ppermute(before[:half], axis, shift_pairs(4, 1))
    far_b = lax.ppermute(after[half:], axis, shift_pairs(4, 3))
    return [v, before, after, far_a, far_b]


def nt_dot(x, a):
    return lax.dot_general(x, a, (((1,), (1,)), ((), ())), preferred_element_type=jnp.float32)


GROUP = 8
NEAR = 16


def pick(sources, first, which, place, target, sem):
    if len(sources) == 1:
        pltpu.make_async_copy(sources[0].at[place], target, sem).start()
        return
    middle = len(sources) // 2

    @pl.when(which < first + middle)
    def _():
        pick(sources[:middle], first, which, place, target, sem)

    @pl.when(which >= first + middle)
    def _():
        pick(sources[middle:], first + middle, which, place, target, sem)


def gather_sum(level, code_ref, sources, own_ref, other_ref, out_ref, picked, blocks, sem, block_sems, between=None):
    slots = code_ref.shape[1]
    per_row = slots // 2
    loads = [
        pltpu.make_async_copy(a_ref.at[level - 1, 0], blocks.at[pl.ds(r * per_row, per_row)], block_sems.at[r])
        for r, a_ref in enumerate((own_ref, other_ref))
    ]
    for load in loads:
        load.start()

    def fetch(k, carry):
        code = jnp.maximum(code_ref[level - 1, k], 0)
        pick(sources, 0, code >> 10, code & 1023, picked.at[k], sem)
        return carry

    lax.fori_loop(0, slots, fetch, 0)
    if between is not None:
        between()
    pltpu.make_async_copy(sources[0].at[pl.ds(0, slots)], picked, sem).wait()
    for r in range(2):
        loads[r].wait()
        total = None
        for g in range(r * per_row, (r + 1) * per_row, GROUP):
            xs, group = [], []
            for k in range(g, g + GROUP):
                kept = (code_ref[level - 1, k] >= 0).astype(jnp.float32)
                xs.append((picked[k].astype(jnp.float32) * kept).astype(jnp.bfloat16))
                group.append(blocks[k])
            part = nt_dot(jnp.concatenate(xs, axis=1), jnp.concatenate(group, axis=1))
            total = part if total is None else total + part
        out_ref[r] = total


def first_kernel(code_ref, *refs):
    sources, refs = refs[:-9], refs[-9:]
    own_ref, other_ref, out_ref, store_ref, picked, blocks, sem, block_sems, pack_sems = refs
    packs, start = [], 0
    for i, source in enumerate(sources):
        packs.append(pltpu.make_async_copy(source, store_ref.at[pl.ds(start, source.shape[0])], pack_sems.at[i]))
        start += source.shape[0]

    def between():
        for pack in packs:
            pack.start()

    gather_sum(1, code_ref, sources, own_ref, other_ref, out_ref, picked, blocks, sem, block_sems, between)
    for pack in packs:
        pack.wait()


def old_kernel(level, code_ref, fresh_ref, *refs):
    sources, refs = refs[:-9], refs[-9:]
    own_ref, other_ref, out_ref, list_ref, near_ref, picked, blocks, sem, block_sems = refs
    gather_sum(level, code_ref, sources, own_ref, other_ref, out_ref, picked, blocks, sem, block_sems)

    def note(slot, count):
        code = fresh_ref[level - 1, slot]

        @pl.when(code >= 0)
        def _():
            list_ref[1 + count] = code * 1024 + slot

        @pl.when((code >= 0) & (count < NEAR))
        def _():
            near_ref[count] = blocks[slot]

        return count + (code >= 0).astype(jnp.int32)

    list_ref[0] = lax.fori_loop(0, fresh_ref.shape[1], note, jnp.int32(0))


def sum_call(kernel, codes, sources, own, other, outs, out_spaces, extra, name):
    slots, (rhs_cols, block) = codes[0].shape[1], sources[0].shape[1:]
    return pl.pallas_call(
        kernel,
        out_shape=[jax.ShapeDtypeStruct((2, rhs_cols, block), jnp.float32)] + outs,
        in_specs=[pl.BlockSpec(memory_space=pltpu.SMEM)] * len(codes)
        + [pl.BlockSpec(memory_space=pl.ANY)] * len(sources)
        + [pl.BlockSpec(memory_space=pltpu.HBM)] * 2,
        out_specs=[pl.BlockSpec(memory_space=space) for space in [pltpu.VMEM] + out_spaces],
        scratch_shapes=[
            pltpu.VMEM((slots, rhs_cols, block), jnp.bfloat16),
            pltpu.VMEM((slots, block, block), jnp.bfloat16),
            pltpu.SemaphoreType.DMA,
            pltpu.SemaphoreType.DMA((2,)),
        ]
        + extra,
        compiler_params=pltpu.CompilerParams(vmem_limit_bytes=VMEM_LIMIT),
        cost_estimate=pl.CostEstimate(
            flops=2 * slots * rhs_cols * block * block,
            bytes_accessed=slots * block * (block + 2 * rhs_cols) * 4,
            transcendentals=0,
        ),
        name=name,
    )(*codes, *sources, own, other)


def first_sum(code, sources, own, other):
    store = jax.ShapeDtypeStruct((sum(s.shape[0] for s in sources),) + sources[0].shape[1:], jnp.bfloat16)
    extra = [pltpu.SemaphoreType.DMA((len(sources),))]
    return sum_call(first_kernel, [code], sources, own, other, [store], [pltpu.HBM], extra, "first_sum")


def old_sum(level, code, fresh, sources, own, other):
    block = sources[0].shape[-1]
    outs = [
        jax.ShapeDtypeStruct((code.shape[1] + 1,), jnp.int32),
        jax.ShapeDtypeStruct((NEAR, block, block), jnp.bfloat16),
    ]
    kernel = functools.partial(old_kernel, level)
    return sum_call(kernel, [code, fresh], sources, own, other, outs, [pltpu.SMEM, pltpu.VMEM], [], "old_sum")


def fresh_kernel(level, list_ref, old_ref, x_ref, near_ref, own_ref, other_ref, out_ref, far, sem):
    per_row = own_ref.shape[2]
    out_ref[...] = old_ref[...]
    count = list_ref[0]

    def add(block, entry):
        row = ((entry & 1023) >= per_row).astype(jnp.int32)
        out_ref[row] += nt_dot(x_ref[entry >> 10], block)

    def add_near(n, carry):
        add(near_ref[n], list_ref[1 + n])
        return carry

    def add_far(n, carry):
        slot = list_ref[1 + n] & 1023

        @pl.when(slot < per_row)
        def _():
            pltpu.make_async_copy(own_ref.at[level - 1, 0, slot], far, sem).start()

        @pl.when(slot >= per_row)
        def _():
            pltpu.make_async_copy(other_ref.at[level - 1, 0, slot - per_row], far, sem).start()

        pltpu.make_async_copy(own_ref.at[level - 1, 0, 0], far, sem).wait()
        add(far[...], list_ref[1 + n])
        return carry

    lax.fori_loop(0, jnp.minimum(count, NEAR), add_near, 0)
    lax.fori_loop(NEAR, count, add_far, 0)


def fresh_sum(level, listed, solved, old, near, own, other):
    block = solved.shape[-1]
    vmem = pl.BlockSpec(memory_space=pltpu.VMEM)
    return pl.pallas_call(
        functools.partial(fresh_kernel, level),
        out_shape=jax.ShapeDtypeStruct(old.shape, jnp.float32),
        in_specs=[pl.BlockSpec(memory_space=pltpu.SMEM), vmem, vmem, vmem] + [pl.BlockSpec(memory_space=pltpu.HBM)] * 2,
        out_specs=vmem,
        scratch_shapes=[pltpu.VMEM((block, block), jnp.bfloat16), pltpu.SemaphoreType.DMA],
        compiler_params=pltpu.CompilerParams(vmem_limit_bytes=VMEM_LIMIT),
        name="fresh_sum",
    )(listed, old, solved, near, own, other)


def solve_kernel(level, p0, p1, p2, p3, rhs_ref, own_d_ref, other_d_ref, out_ref, *refs):
    core = lax.axis_index("core")
    for r, d_ref in enumerate((own_d_ref, other_d_ref)):
        coupled = (p0[r] + p1[r]) + (p2[r] + p3[r])
        reduced = (rhs_ref[level, r].astype(jnp.float32) - coupled).astype(jnp.bfloat16)
        solved = nt_dot(reduced, d_ref[level, 0]).astype(jnp.bfloat16)
        out_ref[r] = solved
        if refs:
            refs[1][core ^ r] = solved
    if refs:
        all_ref, both, sems = refs
        sends = [pltpu.make_async_copy(both, all_ref.at[i], sems.at[i]) for i in range(all_ref.shape[0])]
        for send in sends:
            send.start()
        for send in sends:
            send.wait()


def solve_level(level, partials, rhs, own_d, other_d, copies):
    _, rhs_cols, block = partials[0].shape
    vmem = pl.BlockSpec(memory_space=pltpu.VMEM)
    out_shape, out_specs, scratch = [jax.ShapeDtypeStruct((2, rhs_cols, block), jnp.bfloat16)], [vmem], []
    if copies:
        out_shape.append(jax.ShapeDtypeStruct((copies, 2, rhs_cols, block), jnp.bfloat16))
        out_specs.append(pl.BlockSpec(memory_space=pltpu.HBM))
        scratch = [pltpu.VMEM((2, rhs_cols, block), jnp.bfloat16), pltpu.SemaphoreType.DMA((copies,))]
    return pl.pallas_call(
        functools.partial(solve_kernel, level),
        out_shape=out_shape,
        in_specs=[vmem] * 7,
        out_specs=out_specs,
        scratch_shapes=scratch,
        compiler_params=pltpu.CompilerParams(vmem_limit_bytes=VMEM_LIMIT),
        name="solve_level",
    )(*partials, rhs, own_d, other_d)


def on_device(rhs, boundary, diag_inv, off_blocks, coupling, present):
    levels, _, rhs_cols, block = rhs.shape
    outer_each = boundary.shape[0]
    outer = outer_each * 32
    half = rhs_cols // 2
    z, y, core = lax.axis_index("z"), lax.axis_index("y"), lax.axis_index("core")

    def my_half(v, axis):
        return lax.dynamic_slice_in_dim(v, core * half, half, axis)

    def their_half(v, axis):
        return lax.dynamic_slice_in_dim(v, (1 - core) * half, half, axis)

    first = jnp.einsum("rb,ab->ra", rhs[0, 0], diag_inv[0, 0], preferred_element_type=jnp.float32).astype(jnp.bfloat16)
    known = jnp.concatenate([boundary, first[None]])
    known_own = my_half(known, 1)
    known_own, known_other = lax.optimization_barrier((known_own, swap_cores(their_half(known, 1))))
    code_own = (coupling + 1024 * present)[:, 0]
    code_both = jnp.stack([code_own, swap_cores(code_own)], axis=1)
    rhs_both = jnp.concatenate([my_half(rhs, 2), swap_cores(their_half(rhs, 2))], axis=1)
    diag_other = swap_cores(diag_inv)
    off_sent, known_own = lax.optimization_barrier((off_blocks, known_own))
    off_other = swap_cores(off_sent)

    color_a = ring_gather(direct_gather(known_own, "z"), "y")
    color_b = ring_gather(direct_gather(known_other, "y"), "z")

    keep, index = code_both >= 1024, code_both % 1024
    in_outer = index < outer
    row = jnp.where(in_outer, index // outer_each, index - outer)
    member = jnp.where(in_outer, index % outer_each, outer_each)
    src_z, src_y, src_core = row // 8, (row // 2) % 4, row % 2
    each = outer_each + 1
    mine_too = src_core == core
    away = jnp.where(mine_too, src_y - y, src_z - z) % 4
    place = jnp.where(mine_too, src_z ^ z, src_y ^ y) * each + member
    far_half = (away == 2) & (place >= 2 * each)
    piece = jnp.where(away == 3, 1, jnp.where(away == 1, 2, jnp.where(away == 2, 3, 0))) + far_half
    place = jnp.where(far_half, place - 2 * each, place)
    piece_code = (piece + jnp.where(mine_too, 0, 5)) * 1024 + place
    store_code = jnp.where(mine_too, 0, 16 * each) + piece * (4 * each) - jnp.where(piece == 4, 2 * each, 0) + place
    level_of = jnp.maximum(index - outer, 0) // 32
    this = jnp.arange(levels - 1)[:, None, None]
    is_fresh = (level_of == this) & (level_of > 0)
    place_level = (index - outer) % 32
    old_code = jnp.where(level_of == 0, jnp.where(this == 0, piece_code, store_code), level_of * 1024 + place_level)
    old_code = jnp.where(keep & ~is_fresh, old_code, -1).reshape(levels - 1, -1)
    fresh_code = jnp.where(keep & is_fresh, place_level, -1).reshape(levels - 1, -1)

    own_rows, other_rows = [], []
    value, store = first_sum(old_code, color_a + color_b, off_blocks, off_other)
    sources = [store]
    for level in range(1, levels):
        partials = [value] + [lax.ppermute(value, "x", xor_pairs(4, k)) for k in (1, 2, 3)]
        last = level == levels - 1
        outs = solve_level(level, partials, rhs_both, diag_inv, diag_other, 0 if last else 16)
        own_rows.append(outs[0][0])
        other_rows.append(outs[0][1])
        if not last:
            next_fresh, sent = lax.optimization_barrier((fresh_code, outs[1]))
            solved = lax.all_to_all(sent, ("z", "y"), 0, 0).reshape(32, half, block)
            old, listed, near = old_sum(level + 1, old_code, next_fresh, sources, off_blocks, off_other)
            value = fresh_sum(level + 1, listed, solved, old, near, off_blocks, off_other)
            sources = sources + [solved]

    mine = jnp.stack(own_rows)
    theirs = swap_cores(jnp.stack(other_rows))
    low = jnp.where(core == 0, mine, theirs)
    high = jnp.where(core == 0, theirs, mine)
    rest = jnp.concatenate([low, high], axis=1)
    return jnp.concatenate([first[None], rest])[:, None]


def solution(mesh):
    split = Mesh(mesh.devices.reshape(4, 4, 2, 4), ("z", "y", "core", "x"))
    in_specs = (
        P(None, ROWS, None, None),
        P(ROWS, None, None),
        P(None, ROWS, None, None),
        P(None, ROWS, "x", None, None),
        P(None, ROWS, "x"),
        P(None, ROWS, "x"),
    )
    return jax.shard_map(
        on_device, mesh=split, in_specs=in_specs, out_specs=P(None, ROWS, None, None), check_vma=False
    )
```

time: 308 us -> 248 us (0.81)
  local copies, waits for them, and re-layouts: 104 us -> 16.8 us
  Pallas kernels: 63.2 us -> 75.8 us
  waiting for transfers between devices: 29.3 us -> 39.9 us
  starting transfers between devices: 101 us -> 111 us
    unnamed x151 -> x33, local copies, waits for them, and re-layouts: 80.9 us -> 13.5 us
    pallas_call x14, Pallas kernels: 43.4 us -> 70.8 us  [the longest x7 64.5 us: sum_call(): pl.pallas_call(kernel, out_shape=[jax.ShapeDtypeStruct((2, rhs_cols, bloc...]
    squeeze x15 -> x0, local copies, waits for them, and re-layouts: 16.7 us -> none  [the longest x6 6.92 us: on_device(): fresh_code[level]]
    pallas_call x6, Pallas kernels: 19.8 us -> 5 us  [fresh_sum(): pl.pallas_call(functools.partial(fresh_kernel, level), out_shape=jax.Shap...]
    ppermute x21, waiting for transfers between devices: 6.43 us -> 21 us  [on_device(): lax.ppermute(value, 'x', xor_pairs(4, k))]
    ppermute x2, waiting for transfers between devices: 0.01 us -> 8.02 us  [ring_gather(): before = lax.ppermute(v, axis, shift_pairs(4, 1))]
    ppermute x2, waiting for transfers between devices: 7.72 us -> 0.01 us  [ring_gather(): after = lax.ppermute(v, axis, shift_pairs(4, 3))]
    ppermute x6, waiting for transfers between devices: 7.86 us -> 2.95 us  [direct_gather(): lax.ppermute(v, axis, xor_pairs(4, k))]
  transfers between devices with their start and end apart: 47 -> 47, of which waited for: 16 -> 23; matrix products, arithmetic and copies ran while one was open for 10% -> 2% of each run, Pallas kernels for 12% -> 26%
where the time goes in v1:
time: 248 us; the launch traced here: 247 us
  starting transfers between devices  111 us (45%)
  Pallas kernels  75.8 us (31%)
  waiting for transfers between devices  39.9 us (16%)
  local copies, waits for them, and re-layouts  16.8 us (7%)
  other arithmetic  2.51 us (1%)
    pallas_call x7, Pallas kernels, sum_call(): pl.pallas_call(kernel, out_shape=[jax.ShapeDtypeStruct((2, rhs_cols, bloc...  64.5 us
    all_to_all x6, starting transfers between devices, on_device(): solved = lax.all_to_all(sent, ('z', 'y'), 0, 0).reshape(32, half, block)  36.7 us
    ppermute x21, starting transfers between devices, on_device(): lax.ppermute(value, 'x', xor_pairs(4, k))  28.1 us
    ppermute x6, starting transfers between devices, swap_cores(): return lax.ppermute(v, 'core', xor_pairs(2, 1))  22 us
    ppermute x21, waiting for transfers between devices, on_device(): lax.ppermute(value, 'x', xor_pairs(4, k))  21 us
    unnamed x33, local copies, waits for them, and re-layouts  13.5 us
    ppermute x6, starting transfers between devices, direct_gather(): lax.ppermute(v, axis, xor_pairs(4, k))  12.9 us
    ppermute x2, waiting for transfers between devices, ring_gather(): before = lax.ppermute(v, axis, shift_pairs(4, 1))  8.02 us
  transfers between devices with their start and end apart: 47, of which 23 were waited for; matrix products, arithmetic and copies ran while one was open for 2% of the time, Pallas kernels for 26%

profile of v1, /device:TPU:1, one launch (start us, length us, event | category | flops | bytes accessed | tf_op | source)
XLA Modules:
  0.0 247.0 jit_solution(11454320602935831173)
XLA Ops:
  6.2 2.7 %collective-permute-start.10 = (bf16[17,32,128]{2,1,0:T(8,128)(2,1)S(1)}, bf16[17,32,128]{2,1,0:T(8,128)(2,1)S(1)}, u32[]{:S(2)}, u32[]{:S(2)}) collective-permute-start(bf16[17,32,128]{2,1,0:T(8,128)(2,1)S(1)} %collective-permute-done.1), channel_id=1, source_target_pairs={{0,16},{8,24},{16,0},{24,8},{1,17},{9,25},{17,1},{25,9},{2,18},{10... | collective-permute-start | bytes 417800 | tf_op jit(solution)/shard_map/ppermute | solution.py:27
  10.6 3.3 %collective-permute-start.3 = (bf16[17,32,128]{2,1,0:T(8,128)(2,1)S(1)}, bf16[17,32,128]{2,1,0:T(8,128)(2,1)S(1)}, u32[]{:S(2)}, u32[]{:S(2)}) collective-permute-start(bf16[17,32,128]{2,1,0:T(8,128)(2,1)S(1)} %get-tuple-element.54), channel_id=1, source_target_pairs={{0,64},{32,96},{64,0},{96,32},{1,65},{33,97},{65,1},{97,33},{2,66}... | collective-permute-start | bytes 417800 | tf_op jit(solution)/shard_map/ppermute | solution.py:27
  15.5 3.8 %collective-permute-start.4 = (bf16[17,32,128]{2,1,0:T(8,128)(2,1)S(1)}, bf16[17,32,128]{2,1,0:T(8,128)(2,1)S(1)}, u32[]{:S(2)}, u32[]{:S(2)}) collective-permute-start(bf16[17,32,128]{2,1,0:T(8,128)(2,1)S(1)} %get-tuple-element.54), channel_id=1, source_target_pairs={{0,96},{32,64},{64,32},{96,0},{1,97},{33,65},{65,33},{97,1},{2,98}... | collective-permute-start | bytes 417800 | tf_op jit(solution)/shard_map/ppermute | solution.py:27
  27.0 8.0 %collective-permute-done.12.refs_6_ = bf16[68,32,128]{2,1,0:T(8,128)(2,1)S(1)} collective-permute-done((bf16[68,32,128]{2,1,0:T(8,128)(2,1)S(1)}, bf16[68,32,128]{2,1,0:T(8,128)(2,1)S(1)}, u32[]{:S(2)}, u32[]{:S(2)}) %collective-permute-start.12) | collective-permute-done | bytes 557088 | tf_op jit(solution)/shard_map/ppermute | solution.py:31
  37.3 2.7 %collective-permute-start.15 = (bf16[34,32,128]{2,1,0:T(8,128)(2,1)}, bf16[34,32,128]{2,1,0:T(8,128)(2,1)}, u32[]{:S(2)}, u32[]{:S(2)}) collective-permute-start(bf16[34,32,128]{2,1,0:T(8,128)(2,1)} %slice.83), channel_id=1, source_target_pairs={{0,96},{32,0},{64,32},{96,64},{1,97},{33,1},{65,33},{97,65},{2,98}... | collective-permute-start | bytes 835592 | tf_op jit(solution)/shard_map/ppermute | solution.py:35
  42.4 2.7 %collective-permute-start.8 = (bf16[34,32,128]{2,1,0:T(8,128)(2,1)}, bf16[34,32,128]{2,1,0:T(8,128)(2,1)}, u32[]{:S(2)}, u32[]{:S(2)}) collective-permute-start(bf16[34,32,128]{2,1,0:T(8,128)(2,1)} %slice.81), channel_id=1, source_target_pairs={{0,24},{8,0},{16,8},{24,16},{1,25},{9,1},{17,9},{25,17},{2,26},{10... | collective-permute-start | bytes 835592 | tf_op jit(solution)/shard_map/ppermute | solution.py:35
  47.2 3.6 %collective-permute-done.7.refs_3_ = bf16[34,32,128]{2,1,0:T(8,128)(2,1)} collective-permute-done((bf16[34,32,128]{2,1,0:T(8,128)(2,1)}, bf16[34,32,128]{2,1,0:T(8,128)(2,1)}, u32[]{:S(2)}, u32[]{:S(2)}) %collective-permute-start.7) | collective-permute-done | bytes 278560 | tf_op jit(solution)/shard_map/ppermute | solution.py:34
  52.9 29.8 %first_sum.1 = (f32[2,32,128]{2,1,0:T(8,128)S(1)}, bf16[544,32,128]{2,1,0:T(8,128)(2,1)}) custom-call(s32[7,64]{1,0:T(8,128)S(1)} %get-tuple-element.122.code_ref, bf16[68,32,128]{2,1,0:T(8,128)(2,1)S(1)} %copy-done.7, bf16[68,32,128]{2,1,0:T(8,128)(2,1)S(1)} %collective-permute-done.5.refs_1_, bf16[68,32,128]{2,1,0:T(8,128)(2,1)S(1)} %collective-permute-done.6.refs_2_, ...), custom_call_target="tpu_custom_call" | custom-call | flops 67108864 | bytes 6291456 | tf_op jit(solution)/shard_map/first_sum/pallas_call | solution.py:135
  91.8 4.5 %all-to-all-start = ((bf16[16,2,32,128]{3,2,1,0:T(8,128)(2,1)}), bf16[16,2,32,128]{3,2,1,0:T(8,128)(2,1)S(1)}, u32[]{:S(2)}, u32[]{:S(2)}) async-start(bf16[16,2,32,128]{3,2,1,0:T(8,128)(2,1)} %get-tuple-element.64), calls=%async_computation | async-start | bytes 524288 | tf_op jit(solution)/shard_map/all_to_all | solution.py:318
  98.6 5.1 %old_sum.6 = (f32[2,32,128]{2,1,0:T(8,128)S(1)}, s32[65]{0:T(128)S(1)}, bf16[16,128,128]{2,1,0:T(8,128)(2,1)S(1)}) custom-call(s32[7,64]{1,0:T(8,128)S(1)} %get-tuple-element.122.code_ref, s32[7,64]{1,0:T(8,128)S(1)} %get-tuple-element.96.fresh_ref, bf16[544,32,128]{2,1,0:T(8,128)(2,1)S(1)} %copy-done, bf16[7,1,32,128,128]{4,3,2,1,0:T(8,128)(2,1)} %own_ref.11, ...), custom_call_target="tpu_custom_call" | custom-call | flops 67108864 | bytes 6291456 | tf_op jit(solution)/shard_map/old_sum/pallas_call | solution.py:135
  110.9 6.7 %all-to-all-start.1 = ((bf16[16,2,32,128]{3,2,1,0:T(8,128)(2,1)}), bf16[16,2,32,128]{3,2,1,0:T(8,128)(2,1)S(1)}, u32[]{:S(2)}, u32[]{:S(2)}) async-start(bf16[16,2,32,128]{3,2,1,0:T(8,128)(2,1)} %get-tuple-element.71), calls=%async_computation.1 | async-start | bytes 524288 | tf_op jit(solution)/shard_map/all_to_all | solution.py:318
  119.8 5.6 %old_sum.7 = (f32[2,32,128]{2,1,0:T(8,128)S(1)}, s32[65]{0:T(128)S(1)}, bf16[16,128,128]{2,1,0:T(8,128)(2,1)S(1)}) custom-call(s32[7,64]{1,0:T(8,128)S(1)} %get-tuple-element.122.code_ref, s32[7,64]{1,0:T(8,128)S(1)} %get-tuple-element.96.fresh_ref, bf16[544,32,128]{2,1,0:T(8,128)(2,1)S(1)} %copy-done.1, bf16[32,32,128]{2,1,0:T(8,128)(2,1)S(1)} %bitcast.22, ...), custom_call_target="tpu_custom_call" | custom-call | flops 67108864 | bytes 6291456 | tf_op jit(solution)/shard_map/old_sum/pallas_call | solution.py:135
  126.9 3.7 %collective-permute-start.26 = (f32[2,32,128]{2,1,0:T(8,128)S(1)}, f32[2,32,128]{2,1,0:T(8,128)S(1)}, u32[]{:S(2)}, u32[]{:S(2)}) collective-permute-start(f32[2,32,128]{2,1,0:T(8,128)S(1)} %fresh_sum.7.p0), channel_id=1, source_target_pairs={{0,2},{1,3},{2,0},{3,1},{4,6},{5,7},{6,4},{7,5},{8,10},{9,11},{10,... | collective-permute-start | bytes 98312 | tf_op jit(solution)/shard_map/ppermute | solution.py:311
  135.7 5.9 %all-to-all-start.2 = ((bf16[16,2,32,128]{3,2,1,0:T(8,128)(2,1)}), bf16[16,2,32,128]{3,2,1,0:T(8,128)(2,1)S(1)}, u32[]{:S(2)}, u32[]{:S(2)}) async-start(bf16[16,2,32,128]{3,2,1,0:T(8,128)(2,1)} %get-tuple-element.78), calls=%async_computation.2 | async-start | bytes 524288 | tf_op jit(solution)/shard_map/all_to_all | solution.py:318
  143.9 5.6 %old_sum.8 = (f32[2,32,128]{2,1,0:T(8,128)S(1)}, s32[65]{0:T(128)S(1)}, bf16[16,128,128]{2,1,0:T(8,128)(2,1)S(1)}) custom-call(s32[7,64]{1,0:T(8,128)S(1)} %get-tuple-element.122.code_ref, s32[7,64]{1,0:T(8,128)S(1)} %get-tuple-element.96.fresh_ref, bf16[544,32,128]{2,1,0:T(8,128)(2,1)S(1)} %copy-done.2, bf16[32,32,128]{2,1,0:T(8,128)(2,1)S(1)} %bitcast.23, ...), custom_call_target="tpu_custom_call" | custom-call | flops 67108864 | bytes 6291456 | tf_op jit(solution)/shard_map/old_sum/pallas_call | solution.py:135
  157.7 6.1 %all-to-all-start.3 = ((bf16[16,2,32,128]{3,2,1,0:T(8,128)(2,1)}), bf16[16,2,32,128]{3,2,1,0:T(8,128)(2,1)S(1)}, u32[]{:S(2)}, u32[]{:S(2)}) async-start(bf16[16,2,32,128]{3,2,1,0:T(8,128)(2,1)} %get-tuple-element.85), calls=%async_computation.3 | async-start | bytes 524288 | tf_op jit(solution)/shard_map/all_to_all | solution.py:318
  166.0 6.1 %old_sum.9 = (f32[2,32,128]{2,1,0:T(8,128)S(1)}, s32[65]{0:T(128)S(1)}, bf16[16,128,128]{2,1,0:T(8,128)(2,1)S(1)}) custom-call(s32[7,64]{1,0:T(8,128)S(1)} %get-tuple-element.122.code_ref, s32[7,64]{1,0:T(8,128)S(1)} %get-tuple-element.96.fresh_ref, bf16[544,32,128]{2,1,0:T(8,128)(2,1)S(1)} %copy-done.3, bf16[32,32,128]{2,1,0:T(8,128)(2,1)S(1)} %bitcast.24, ...), custom_call_target="tpu_custom_call" | custom-call | flops 67108864 | bytes 6291456 | tf_op jit(solution)/shard_map/old_sum/pallas_call | solution.py:135
  173.9 3.0 %collective-permute-start.32 = (f32[2,32,128]{2,1,0:T(8,128)S(1)}, f32[2,32,128]{2,1,0:T(8,128)S(1)}, u32[]{:S(2)}, u32[]{:S(2)}) collective-permute-start(f32[2,32,128]{2,1,0:T(8,128)S(1)} %fresh_sum.9.p0), channel_id=1, source_target_pairs={{0,2},{1,3},{2,0},{3,1},{4,6},{5,7},{6,4},{7,5},{8,10},{9,11},{10,... | collective-permute-start | bytes 98312 | tf_op jit(solution)/shard_map/ppermute | solution.py:311
  182.1 6.7 %all-to-all-start.4 = ((bf16[16,2,32,128]{3,2,1,0:T(8,128)(2,1)}), bf16[16,2,32,128]{3,2,1,0:T(8,128)(2,1)S(1)}, u32[]{:S(2)}, u32[]{:S(2)}) async-start(bf16[16,2,32,128]{3,2,1,0:T(8,128)(2,1)} %get-tuple-element.92), calls=%async_computation.4 | async-start | bytes 524288 | tf_op jit(solution)/shard_map/all_to_all | solution.py:318
  191.1 6.1 %old_sum.10 = (f32[2,32,128]{2,1,0:T(8,128)S(1)}, s32[65]{0:T(128)S(1)}, bf16[16,128,128]{2,1,0:T(8,128)(2,1)S(1)}) custom-call(s32[7,64]{1,0:T(8,128)S(1)} %get-tuple-element.122.code_ref, s32[7,64]{1,0:T(8,128)S(1)} %get-tuple-element.96.fresh_ref, bf16[544,32,128]{2,1,0:T(8,128)(2,1)S(1)} %copy-done.4, bf16[32,32,128]{2,1,0:T(8,128)(2,1)S(1)} %bitcast.25, ...), custom_call_target="tpu_custom_call" | custom-call | flops 67108864 | bytes 6291456 | tf_op jit(solution)/shard_map/old_sum/pallas_call | solution.py:135
  204.7 6.8 %all-to-all-start.5 = ((bf16[16,2,32,128]{3,2,1,0:T(8,128)(2,1)}), bf16[16,2,32,128]{3,2,1,0:T(8,128)(2,1)S(1)}, u32[]{:S(2)}, u32[]{:S(2)}) async-start(bf16[16,2,32,128]{3,2,1,0:T(8,128)(2,1)} %get-tuple-element.99), calls=%async_computation.5 | async-start | bytes 524288 | tf_op jit(solution)/shard_map/all_to_all | solution.py:318
  211.5 6.1 %old_sum.11 = (f32[2,32,128]{2,1,0:T(8,128)S(1)}, s32[65]{0:T(128)S(1)}, bf16[16,128,128]{2,1,0:T(8,128)(2,1)S(1)}) custom-call(s32[7,64]{1,0:T(8,128)S(1)} %get-tuple-element.122.code_ref, s32[7,64]{1,0:T(8,128)S(1)} %get-tuple-element.96.fresh_ref, bf16[544,32,128]{2,1,0:T(8,128)(2,1)} %get-tuple-element.61.refs_0_, bf16[32,32,128]{2,1,0:T(8,128)(2,1)S(1)} %bitcast.26, ...), custom_call_target="tpu_custom_call" | custom-call | flops 67108864 | bytes 6291456 | tf_op jit(solution)/shard_map/old_sum/pallas_call | solution.py:135
  220.4 3.2 %collective-permute-start.38 = (f32[2,32,128]{2,1,0:T(8,128)S(1)}, f32[2,32,128]{2,1,0:T(8,128)S(1)}, u32[]{:S(2)}, u32[]{:S(2)}) collective-permute-start(f32[2,32,128]{2,1,0:T(8,128)S(1)} %fresh_sum.11.p0), channel_id=1, source_target_pairs={{0,2},{1,3},{2,0},{3,1},{4,6},{5,7},{6,4},{7,5},{8,10},{9,11},{10,... | collective-permute-start | bytes 98312 | tf_op jit(solution)/shard_map/ppermute | solution.py:311
  227.8 17.7 %collective-permute-start.40 = (bf16[7,32,128]{2,1,0:T(8,128)(2,1)S(1)}, bf16[7,32,128]{2,1,0:T(8,128)(2,1)S(1)}, u32[]{:S(2)}, u32[]{:S(2)}) collective-permute-start(bf16[7,32,128]{2,1,0:T(8,128)(2,1)S(1)} %get-tuple-element.108), channel_id=1, source_target_pairs={{0,4},{4,0},{1,5},{5,1},{2,6},{6,2},{3,7},{7,3},{8,12},{12,8},{9,1... | collective-permute-start | bytes 172040 | tf_op jit(solution)/shard_map/ppermute | solution.py:23
  (142 shorter events, 91.1 us)
Async XLA Ops:
  4.4 46.4 %collective-permute-start.16 = (bf16[7,1,32,128,128]{4,3,2,1,0:T(8,128)(2,1)}, bf16[7,1,32,128,128]{4,3,2,1,0:T(8,128)(2,1)}, u32[]{:S(2)}, u32[]{:S(2)}) collective-permute-start(bf16[7,1,32,128,128]{4,3,2,1,0:T(8,128)(2,1)} %own_ref.11), channel_id=1, source_target_pairs={{0,4},{4,0},{1,5},{5,1},{2,6},{6,2},{3,7},{7,3},{8,12},{12,8},{9,1... | collective-permute-start | bytes 22020104 | tf_op jit(solution)/shard_map/ppermute | solution.py:23
  4.8 5.8 %collective-permute-start.9 = (bf16[17,32,128]{2,1,0:T(8,128)(2,1)S(1)}, bf16[17,32,128]{2,1,0:T(8,128)(2,1)S(1)}, u32[]{:S(2)}, u32[]{:S(2)}) collective-permute-start(bf16[17,32,128]{2,1,0:T(8,128)(2,1)S(1)} %collective-permute-done.1), channel_id=1, source_target_pairs={{0,8},{8,0},{16,24},{24,16},{1,9},{9,1},{17,25},{25,17},{2,10},{10... | collective-permute-start | bytes 417800 | tf_op jit(solution)/shard_map/ppermute | solution.py:27
  6.2 9.3 %collective-permute-start.10 = (bf16[17,32,128]{2,1,0:T(8,128)(2,1)S(1)}, bf16[17,32,128]{2,1,0:T(8,128)(2,1)S(1)}, u32[]{:S(2)}, u32[]{:S(2)}) collective-permute-start(bf16[17,32,128]{2,1,0:T(8,128)(2,1)S(1)} %collective-permute-done.1), channel_id=1, source_target_pairs={{0,16},{8,24},{16,0},{24,8},{1,17},{9,25},{17,1},{25,9},{2,18},{10... | collective-permute-start | bytes 417800 | tf_op jit(solution)/shard_map/ppermute | solution.py:27
  8.9 10.4 %collective-permute-start.11 = (bf16[17,32,128]{2,1,0:T(8,128)(2,1)S(1)}, bf16[17,32,128]{2,1,0:T(8,128)(2,1)S(1)}, u32[]{:S(2)}, u32[]{:S(2)}) collective-permute-start(bf16[17,32,128]{2,1,0:T(8,128)(2,1)S(1)} %collective-permute-done.1), channel_id=1, source_target_pairs={{0,24},{8,16},{16,8},{24,0},{1,25},{9,17},{17,9},{25,1},{2,26},{10... | collective-permute-start | bytes 417800 | tf_op jit(solution)/shard_map/ppermute | solution.py:27
  8.9 10.9 %collective-permute-start.2 = (bf16[17,32,128]{2,1,0:T(8,128)(2,1)S(1)}, bf16[17,32,128]{2,1,0:T(8,128)(2,1)S(1)}, u32[]{:S(2)}, u32[]{:S(2)}) collective-permute-start(bf16[17,32,128]{2,1,0:T(8,128)(2,1)S(1)} %get-tuple-element.54), channel_id=1, source_target_pairs={{0,32},{32,0},{64,96},{96,64},{1,33},{33,1},{65,97},{97,65},{2,34}... | collective-permute-start | bytes 417800 | tf_op jit(solution)/shard_map/ppermute | solution.py:27
  10.6 11.5 %collective-permute-start.3 = (bf16[17,32,128]{2,1,0:T(8,128)(2,1)S(1)}, bf16[17,32,128]{2,1,0:T(8,128)(2,1)S(1)}, u32[]{:S(2)}, u32[]{:S(2)}) collective-permute-start(bf16[17,32,128]{2,1,0:T(8,128)(2,1)S(1)} %get-tuple-element.54), channel_id=1, source_target_pairs={{0,64},{32,96},{64,0},{96,32},{1,65},{33,97},{65,1},{97,33},{2,66}... | collective-permute-start | bytes 417800 | tf_op jit(solution)/shard_map/ppermute | solution.py:27
  15.5 8.0 %collective-permute-start.4 = (bf16[17,32,128]{2,1,0:T(8,128)(2,1)S(1)}, bf16[17,32,128]{2,1,0:T(8,128)(2,1)S(1)}, u32[]{:S(2)}, u32[]{:S(2)}) collective-permute-start(bf16[17,32,128]{2,1,0:T(8,128)(2,1)S(1)} %get-tuple-element.54), channel_id=1, source_target_pairs={{0,96},{32,64},{64,32},{96,0},{1,97},{33,65},{65,33},{97,1},{2,98}... | collective-permute-start | bytes 417800 | tf_op jit(solution)/shard_map/ppermute | solution.py:27
  19.3 15.7 %collective-permute-start.12 = (bf16[68,32,128]{2,1,0:T(8,128)(2,1)S(1)}, bf16[68,32,128]{2,1,0:T(8,128)(2,1)S(1)}, u32[]{:S(2)}, u32[]{:S(2)}) collective-permute-start(bf16[68,32,128]{2,1,0:T(8,128)(2,1)S(1)} %constant_dynamic-update-slice_fusion.4.refs_5_), channel_id=1, source_target_pairs={{0,32},{32,64},{64,96},{96,0},{1,33},{33,65},{65,97},{97,1},{2,34}... | collective-permute-start | bytes 1671176 | tf_op jit(solution)/shard_map/ppermute | solution.py:31
  19.8 16.7 %collective-permute-start.13 = (bf16[68,32,128]{2,1,0:T(8,128)(2,1)S(1)}, bf16[68,32,128]{2,1,0:T(8,128)(2,1)S(1)}, u32[]{:S(2)}, u32[]{:S(2)}) collective-permute-start(bf16[68,32,128]{2,1,0:T(8,128)(2,1)S(1)} %constant_dynamic-update-slice_fusion.4.refs_5_), channel_id=1, source_target_pairs={{0,96},{32,0},{64,32},{96,64},{1,97},{33,1},{65,33},{97,65},{2,98}... | collective-permute-start | bytes 1671176 | tf_op jit(solution)/shard_map/ppermute | solution.py:32
  23.6 17.3 %collective-permute-start.5 = (bf16[68,32,128]{2,1,0:T(8,128)(2,1)S(1)}, bf16[68,32,128]{2,1,0:T(8,128)(2,1)S(1)}, u32[]{:S(2)}, u32[]{:S(2)}) collective-permute-start(bf16[68,32,128]{2,1,0:T(8,128)(2,1)S(1)} %constant_dynamic-update-slice_fusion.refs_0_), channel_id=1, source_target_pairs={{0,8},{8,16},{16,24},{24,0},{1,9},{9,17},{17,25},{25,1},{2,10},{10... | collective-permute-start | bytes 1671176 | tf_op jit(solution)/shard_map/ppermute | solution.py:31
  23.8 17.8 %collective-permute-start.6 = (bf16[68,32,128]{2,1,0:T(8,128)(2,1)S(1)}, bf16[68,32,128]{2,1,0:T(8,128)(2,1)S(1)}, u32[]{:S(2)}, u32[]{:S(2)}) collective-permute-start(bf16[68,32,128]{2,1,0:T(8,128)(2,1)S(1)} %constant_dynamic-update-slice_fusion.refs_0_), channel_id=1, source_target_pairs={{0,24},{8,0},{16,8},{24,16},{1,25},{9,1},{17,9},{25,17},{2,26},{10... | collective-permute-start | bytes 1671176 | tf_op jit(solution)/shard_map/ppermute | solution.py:32
  36.5 9.6 %collective-permute-start.14 = (bf16[34,32,128]{2,1,0:T(8,128)(2,1)S(1)}, bf16[34,32,128]{2,1,0:T(8,128)(2,1)S(1)}, u32[]{:S(2)}, u32[]{:S(2)}) collective-permute-start(bf16[34,32,128]{2,1,0:T(8,128)(2,1)S(1)} %slice.82), channel_id=1, source_target_pairs={{0,32},{32,64},{64,96},{96,0},{1,33},{33,65},{65,97},{97,1},{2,34}... | collective-permute-start | bytes 835592 | tf_op jit(solution)/shard_map/ppermute | solution.py:34
  37.3 9.5 %collective-permute-start.15 = (bf16[34,32,128]{2,1,0:T(8,128)(2,1)}, bf16[34,32,128]{2,1,0:T(8,128)(2,1)}, u32[]{:S(2)}, u32[]{:S(2)}) collective-permute-start(bf16[34,32,128]{2,1,0:T(8,128)(2,1)} %slice.83), channel_id=1, source_target_pairs={{0,96},{32,0},{64,32},{96,64},{1,97},{33,1},{65,33},{97,65},{2,98}... | collective-permute-start | bytes 835592 | tf_op jit(solution)/shard_map/ppermute | solution.py:35
  41.6 9.2 %collective-permute-start.7 = (bf16[34,32,128]{2,1,0:T(8,128)(2,1)}, bf16[34,32,128]{2,1,0:T(8,128)(2,1)}, u32[]{:S(2)}, u32[]{:S(2)}) collective-permute-start(bf16[34,32,128]{2,1,0:T(8,128)(2,1)} %slice.80), channel_id=1, source_target_pairs={{0,8},{8,16},{16,24},{24,0},{1,9},{9,17},{17,25},{25,1},{2,10},{10... | collective-permute-start | bytes 835592 | tf_op jit(solution)/shard_map/ppermute | solution.py:34
  42.4 8.4 %collective-permute-start.8 = (bf16[34,32,128]{2,1,0:T(8,128)(2,1)}, bf16[34,32,128]{2,1,0:T(8,128)(2,1)}, u32[]{:S(2)}, u32[]{:S(2)}) collective-permute-start(bf16[34,32,128]{2,1,0:T(8,128)(2,1)} %slice.81), channel_id=1, source_target_pairs={{0,24},{8,0},{16,8},{24,16},{1,25},{9,1},{17,9},{25,17},{2,26},{10... | collective-permute-start | bytes 835592 | tf_op jit(solution)/shard_map/ppermute | solution.py:35
  46.1 40.6 %collective-permute-start.21 = (bf16[8,1,128,128]{3,2,1,0:T(8,128)(2,1)}, bf16[8,1,128,128]{3,2,1,0:T(8,128)(2,1)S(1)}, u32[]{:S(2)}, u32[]{:S(2)}) collective-permute-start(bf16[8,1,128,128]{3,2,1,0:T(8,128)(2,1)} %own_d_ref.13), channel_id=1, source_target_pairs={{0,4},{4,0},{1,5},{5,1},{2,6},{6,2},{3,7},{7,3},{8,12},{12,8},{9,1... | collective-permute-start | bytes 786440 | tf_op jit(solution)/shard_map/ppermute | solution.py:23
  46.8 39.8 %collective-permute-start.20 = (bf16[8,1,32,128]{3,2,1,0:T(8,128)(2,1)S(1)}, bf16[8,1,32,128]{3,2,1,0:T(8,128)(2,1)S(1)}, u32[]{:S(2)}, u32[]{:S(2)}) collective-permute-start(bf16[8,1,32,128]{3,2,1,0:T(8,128)(2,1)S(1)} %get-tuple-element.104), channel_id=1, source_target_pairs={{0,4},{4,0},{1,5},{5,1},{2,6},{6,2},{3,7},{7,3},{8,12},{12,8},{9,1... | collective-permute-start | bytes 196616 | tf_op jit(solution)/shard_map/ppermute | solution.py:23
  91.8 12.0 %all-to-all-start = ((bf16[16,2,32,128]{3,2,1,0:T(8,128)(2,1)}), bf16[16,2,32,128]{3,2,1,0:T(8,128)(2,1)S(1)}, u32[]{:S(2)}, u32[]{:S(2)}) async-start(bf16[16,2,32,128]{3,2,1,0:T(8,128)(2,1)} %get-tuple-element.64), calls=%async_computation | async-start | bytes 524288 | tf_op jit(solution)/shard_map/all_to_all | solution.py:318
  110.9 14.6 %all-to-all-start.1 = ((bf16[16,2,32,128]{3,2,1,0:T(8,128)(2,1)}), bf16[16,2,32,128]{3,2,1,0:T(8,128)(2,1)S(1)}, u32[]{:S(2)}, u32[]{:S(2)}) async-start(bf16[16,2,32,128]{3,2,1,0:T(8,128)(2,1)} %get-tuple-element.71), calls=%async_computation.1 | async-start | bytes 524288 | tf_op jit(solution)/shard_map/all_to_all | solution.py:318
  135.7 13.9 %all-to-all-start.2 = ((bf16[16,2,32,128]{3,2,1,0:T(8,128)(2,1)}), bf16[16,2,32,128]{3,2,1,0:T(8,128)(2,1)S(1)}, u32[]{:S(2)}, u32[]{:S(2)}) async-start(bf16[16,2,32,128]{3,2,1,0:T(8,128)(2,1)} %get-tuple-element.78), calls=%async_computation.2 | async-start | bytes 524288 | tf_op jit(solution)/shard_map/all_to_all | solution.py:318
  157.7 14.4 %all-to-all-start.3 = ((bf16[16,2,32,128]{3,2,1,0:T(8,128)(2,1)}), bf16[16,2,32,128]{3,2,1,0:T(8,128)(2,1)S(1)}, u32[]{:S(2)}, u32[]{:S(2)}) async-start(bf16[16,2,32,128]{3,2,1,0:T(8,128)(2,1)} %get-tuple-element.85), calls=%async_computation.3 | async-start | bytes 524288 | tf_op jit(solution)/shard_map/all_to_all | solution.py:318
  182.1 15.1 %all-to-all-start.4 = ((bf16[16,2,32,128]{3,2,1,0:T(8,128)(2,1)}), bf16[16,2,32,128]{3,2,1,0:T(8,128)(2,1)S(1)}, u32[]{:S(2)}, u32[]{:S(2)}) async-start(bf16[16,2,32,128]{3,2,1,0:T(8,128)(2,1)} %get-tuple-element.92), calls=%async_computation.4 | async-start | bytes 524288 | tf_op jit(solution)/shard_map/all_to_all | solution.py:318
  204.7 14.4 %all-to-all-start.5 = ((bf16[16,2,32,128]{3,2,1,0:T(8,128)(2,1)}), bf16[16,2,32,128]{3,2,1,0:T(8,128)(2,1)S(1)}, u32[]{:S(2)}, u32[]{:S(2)}) async-start(bf16[16,2,32,128]{3,2,1,0:T(8,128)(2,1)} %get-tuple-element.99), calls=%async_computation.5 | async-start | bytes 524288 | tf_op jit(solution)/shard_map/all_to_all | solution.py:318
  227.8 18.6 %collective-permute-start.40 = (bf16[7,32,128]{2,1,0:T(8,128)(2,1)S(1)}, bf16[7,32,128]{2,1,0:T(8,128)(2,1)S(1)}, u32[]{:S(2)}, u32[]{:S(2)}) collective-permute-start(bf16[7,32,128]{2,1,0:T(8,128)(2,1)S(1)} %get-tuple-element.108), channel_id=1, source_target_pairs={{0,4},{4,0},{1,5},{5,1},{2,6},{6,2},{3,7},{7,3},{8,12},{12,8},{9,1... | collective-permute-start | bytes 172040 | tf_op jit(solution)/shard_map/ppermute | solution.py:23
  (33 other events, 184.2 us)

commit v2 on v1

--- a/solution.py
+++ b/solution.py
@@ -44,23 +44,9 @@
 NEAR = 16
 
 
-def pick(sources, first, which, place, target, sem):
-    if len(sources) == 1:
-        pltpu.make_async_copy(sources[0].at[place], target, sem).start()
-        return
-    middle = len(sources) // 2
-
-    @pl.when(which < first + middle)
-    def _():
-        pick(sources[:middle], first, which, place, target, sem)
-
-    @pl.when(which >= first + middle)
-    def _():
-        pick(sources[middle:], first + middle, which, place, target, sem)
-
-
-def gather_sum(level, code_ref, sources, own_ref, other_ref, out_ref, picked, blocks, sem, block_sems, between=None):
+def gather_sum(level, code_ref, store_ref, solved_ref, own_ref, other_ref, out_ref, blocks, block_sems, between=None):
     slots = code_ref.shape[1]
+    known = store_ref.shape[0]
     per_row = slots // 2
     loads = [
         pltpu.make_async_copy(a_ref.at[level - 1, 0], blocks.at[pl.ds(r * per_row, per_row)], block_sems.at[r])
@@ -68,24 +54,20 @@
     ]
     for load in loads:
         load.start()
-
-    def fetch(k, carry):
-        code = jnp.maximum(code_ref[level - 1, k], 0)
-        pick(sources, 0, code >> 10, code & 1023, picked.at[k], sem)
-        return carry
-
-    lax.fori_loop(0, slots, fetch, 0)
     if between is not None:
         between()
-    pltpu.make_async_copy(sources[0].at[pl.ds(0, slots)], picked, sem).wait()
     for r in range(2):
         loads[r].wait()
         total = None
         for g in range(r * per_row, (r + 1) * per_row, GROUP):
             xs, group = [], []
             for k in range(g, g + GROUP):
-                kept = (code_ref[level - 1, k] >= 0).astype(jnp.float32)
-                xs.append((picked[k].astype(jnp.float32) * kept).astype(jnp.bfloat16))
+                code = code_ref[level - 1, k]
+                kept = (code >= 0).astype(jnp.float32)
+                picked = store_ref[jnp.clip(code, 0, known - 1)]
+                if solved_ref is not None:
+                    picked = jnp.where(code >= known, solved_ref[jnp.maximum(code - known, 0)], picked)
+                xs.append((picked.astype(jnp.float32) * kept).astype(jnp.bfloat16))
                 group.append(blocks[k])
             part = nt_dot(jnp.concatenate(xs, axis=1), jnp.concatenate(group, axis=1))
             total = part if total is None else total + part
@@ -93,8 +75,8 @@
 
 
 def first_kernel(code_ref, *refs):
-    sources, refs = refs[:-9], refs[-9:]
-    own_ref, other_ref, out_ref, store_ref, picked, blocks, sem, block_sems, pack_sems = refs
+    sources, refs = refs[:-7], refs[-7:]
+    own_ref, other_ref, out_ref, store_ref, blocks, block_sems, pack_sems = refs
     packs, start = [], 0
     for i, source in enumerate(sources):
         packs.append(pltpu.make_async_copy(source, store_ref.at[pl.ds(start, source.shape[0])], pack_sems.at[i]))
@@ -103,16 +85,22 @@
     def between():
         for pack in packs:
             pack.start()
-
-    gather_sum(1, code_ref, sources, own_ref, other_ref, out_ref, picked, blocks, sem, block_sems, between)
-    for pack in packs:
-        pack.wait()
-
-
-def old_kernel(level, code_ref, fresh_ref, *refs):
-    sources, refs = refs[:-9], refs[-9:]
-    own_ref, other_ref, out_ref, list_ref, near_ref, picked, blocks, sem, block_sems = refs
-    gather_sum(level, code_ref, sources, own_ref, other_ref, out_ref, picked, blocks, sem, block_sems)
+        for pack in packs:
+            pack.wait()
+
+    gather_sum(1, code_ref, store_ref, None, own_ref, other_ref, out_ref, blocks, block_sems, between)
+
+
+def old_kernel(level, code_ref, fresh_ref, store_ref, *refs):
+    solved, refs = refs[: level - 2], refs[level - 2 :]
+    own_ref, other_ref, out_ref, list_ref, near_ref, blocks, block_sems = refs[:7]
+    solved_ref = refs[7] if solved else None
+
+    def between():
+        for i, one in enumerate(solved):
+            solved_ref[i * one.shape[0] : (i + 1) * one.shape[0]] = one[...]
+
+    gather_sum(level, code_ref, store_ref, solved_ref, own_ref, other_ref, out_ref, blocks, block_sems, between)
 
     def note(slot, count):
         code = fresh_ref[level - 1, slot]
@@ -130,22 +118,16 @@
     list_ref[0] = lax.fori_loop(0, fresh_ref.shape[1], note, jnp.int32(0))
 
 
-def sum_call(kernel, codes, sources, own, other, outs, out_spaces, extra, name):
+def sum_call(kernel, codes, sources, source_space, own, other, outs, out_spaces, extra, name):
     slots, (rhs_cols, block) = codes[0].shape[1], sources[0].shape[1:]
     return pl.pallas_call(
         kernel,
         out_shape=[jax.ShapeDtypeStruct((2, rhs_cols, block), jnp.float32)] + outs,
         in_specs=[pl.BlockSpec(memory_space=pltpu.SMEM)] * len(codes)
-        + [pl.BlockSpec(memory_space=pl.ANY)] * len(sources)
+        + [pl.BlockSpec(memory_space=source_space)] * len(sources)
         + [pl.BlockSpec(memory_space=pltpu.HBM)] * 2,
         out_specs=[pl.BlockSpec(memory_space=space) for space in [pltpu.VMEM] + out_spaces],
-        scratch_shapes=[
-            pltpu.VMEM((slots, rhs_cols, block), jnp.bfloat16),
-            pltpu.VMEM((slots, block, block), jnp.bfloat16),
-            pltpu.SemaphoreType.DMA,
-            pltpu.SemaphoreType.DMA((2,)),
-        ]
-        + extra,
+        scratch_shapes=[pltpu.VMEM((slots, block, block), jnp.bfloat16), pltpu.SemaphoreType.DMA((2,))] + extra,
         compiler_params=pltpu.CompilerParams(vmem_limit_bytes=VMEM_LIMIT),
         cost_estimate=pl.CostEstimate(
             flops=2 * slots * rhs_cols * block * block,
@@ -157,19 +139,21 @@
 
 
 def first_sum(code, sources, own, other):
-    store = jax.ShapeDtypeStruct((sum(s.shape[0] for s in sources),) + sources[0].shape[1:], jnp.bfloat16)
+    store = jax.ShapeDtypeStruct((sum(v.shape[0] for v in sources),) + sources[0].shape[1:], jnp.bfloat16)
     extra = [pltpu.SemaphoreType.DMA((len(sources),))]
-    return sum_call(first_kernel, [code], sources, own, other, [store], [pltpu.HBM], extra, "first_sum")
-
-
-def old_sum(level, code, fresh, sources, own, other):
-    block = sources[0].shape[-1]
+    return sum_call(first_kernel, [code], sources, pl.ANY, own, other, [store], [pltpu.VMEM], extra, "first_sum")
+
+
+def old_sum(level, code, fresh, store, solved, own, other):
+    block = store.shape[-1]
     outs = [
         jax.ShapeDtypeStruct((code.shape[1] + 1,), jnp.int32),
         jax.ShapeDtypeStruct((NEAR, block, block), jnp.bfloat16),
     ]
     kernel = functools.partial(old_kernel, level)
-    return sum_call(kernel, [code, fresh], sources, own, other, outs, [pltpu.SMEM, pltpu.VMEM], [], "old_sum")
+    spaces = [pltpu.SMEM, pltpu.VMEM]
+    extra = [pltpu.VMEM((sum(v.shape[0] for v in solved),) + store.shape[1:], jnp.bfloat16)] if solved else []
+    return sum_call(kernel, [code, fresh], [store] + solved, pltpu.VMEM, own, other, outs, spaces, extra, "old_sum")
 
 
 def fresh_kernel(level, list_ref, old_ref, x_ref, near_ref, own_ref, other_ref, out_ref, far, sem):
@@ -210,7 +194,7 @@
     return pl.pallas_call(
         functools.partial(fresh_kernel, level),
         out_shape=jax.ShapeDtypeStruct(old.shape, jnp.float32),
-        in_specs=[pl.BlockSpec(memory_space=pltpu.SMEM), vmem, vmem, vmem] + [pl.BlockSpec(memory_space=pltpu.HBM)] * 2,
+        in_specs=[pl.BlockSpec(memory_space=pltpu.SMEM)] + [vmem] * 3 + [pl.BlockSpec(memory_space=pltpu.HBM)] * 2,
         out_specs=vmem,
         scratch_shapes=[pltpu.VMEM((block, block), jnp.bfloat16), pltpu.SemaphoreType.DMA],
         compiler_params=pltpu.CompilerParams(vmem_limit_bytes=VMEM_LIMIT),
@@ -294,19 +278,18 @@
     far_half = (away == 2) & (place >= 2 * each)
     piece = jnp.where(away == 3, 1, jnp.where(away == 1, 2, jnp.where(away == 2, 3, 0))) + far_half
     place = jnp.where(far_half, place - 2 * each, place)
-    piece_code = (piece + jnp.where(mine_too, 0, 5)) * 1024 + place
-    store_code = jnp.where(mine_too, 0, 16 * each) + piece * (4 * each) - jnp.where(piece == 4, 2 * each, 0) + place
+    known_place = jnp.where(mine_too, 0, 16 * each) + piece * (4 * each) - jnp.where(piece == 4, 2 * each, 0) + place
     level_of = jnp.maximum(index - outer, 0) // 32
     this = jnp.arange(levels - 1)[:, None, None]
     is_fresh = (level_of == this) & (level_of > 0)
     place_level = (index - outer) % 32
-    old_code = jnp.where(level_of == 0, jnp.where(this == 0, piece_code, store_code), level_of * 1024 + place_level)
+    old_code = jnp.where(level_of == 0, known_place, 32 * each + (level_of - 1) * 32 + place_level)
     old_code = jnp.where(keep & ~is_fresh, old_code, -1).reshape(levels - 1, -1)
     fresh_code = jnp.where(keep & is_fresh, place_level, -1).reshape(levels - 1, -1)
 
     own_rows, other_rows = [], []
     value, store = first_sum(old_code, color_a + color_b, off_blocks, off_other)
-    sources = [store]
+    solved_levels = []
     for level in range(1, levels):
         partials = [value] + [lax.ppermute(value, "x", xor_pairs(4, k)) for k in (1, 2, 3)]
         last = level == levels - 1
@@ -316,9 +299,9 @@
         if not last:
             next_fresh, sent = lax.optimization_barrier((fresh_code, outs[1]))
             solved = lax.all_to_all(sent, ("z", "y"), 0, 0).reshape(32, half, block)
-            old, listed, near = old_sum(level + 1, old_code, next_fresh, sources, off_blocks, off_other)
+            old, listed, near = old_sum(level + 1, old_code, next_fresh, store, solved_levels, off_blocks, off_other)
             value = fresh_sum(level + 1, listed, solved, old, near, off_blocks, off_other)
-            sources = sources + [solved]
+            solved_levels = solved_levels + [solved]
 
     mine = jnp.stack(own_rows)
     theirs = swap_cores(jnp.stack(other_rows))

time: 248 us -> 219 us (0.88)
  Pallas kernels: 75.8 us -> 48.4 us
  starting transfers between devices: 111 us -> 108 us
    pallas_call x7, Pallas kernels: 64.5 us -> 36.2 us  [sum_call(): pl.pallas_call(kernel, out_shape=[jax.ShapeDtypeStruct((2, rhs_cols, bloc...]
  transfers between devices with their start and end apart: 47 -> 47, of which waited for: 23 -> 27; matrix products, arithmetic and copies ran while one was open for 2% -> 2% of each run, Pallas kernels for 26% -> 17%
where the time goes in v2:
time: 219 us; the launch traced here: 218 us
  starting transfers between devices  108 us (49%)
  Pallas kernels  48.4 us (22%)
  waiting for transfers between devices  40.6 us (19%)
  local copies, waits for them, and re-layouts  16.8 us (8%)
  other arithmetic  2.48 us (1%)
    pallas_call x7, Pallas kernels, sum_call(): pl.pallas_call(kernel, out_shape=[jax.ShapeDtypeStruct((2, rhs_cols, bloc...  36.2 us
    all_to_all x6, starting transfers between devices, on_device(): solved = lax.all_to_all(sent, ('z', 'y'), 0, 0).reshape(32, half, block)  35 us
    ppermute x21, starting transfers between devices, on_device(): lax.ppermute(value, 'x', xor_pairs(4, k))  27.5 us
    ppermute x6, starting transfers between devices, swap_cores(): return lax.ppermute(v, 'core', xor_pairs(2, 1))  21.8 us
    ppermute x21, waiting for transfers between devices, on_device(): lax.ppermute(value, 'x', xor_pairs(4, k))  19.9 us
    unnamed x33, local copies, waits for them, and re-layouts  13.5 us
    ppermute x6, starting transfers between devices, direct_gather(): lax.ppermute(v, axis, xor_pairs(4, k))  12.9 us
    ppermute x2, waiting for transfers between devices, ring_gather(): before = lax.ppermute(v, axis, shift_pairs(4, 1))  8.02 us
  transfers between devices with their start and end apart: 47, of which 27 were waited for; matrix products, arithmetic and copies ran while one was open for 2% of the time, Pallas kernels for 17%

profile of v2, /device:TPU:1, one launch (start us, length us, event | category | flops | bytes accessed | tf_op | source)
XLA Modules:
  0.0 217.7 jit_solution(795226922944630500)
XLA Ops:
  6.2 2.7 %collective-permute-start.10 = (bf16[17,32,128]{2,1,0:T(8,128)(2,1)S(1)}, bf16[17,32,128]{2,1,0:T(8,128)(2,1)S(1)}, u32[]{:S(2)}, u32[]{:S(2)}) collective-permute-start(bf16[17,32,128]{2,1,0:T(8,128)(2,1)S(1)} %collective-permute-done.1), channel_id=1, source_target_pairs={{0,16},{8,24},{16,0},{24,8},{1,17},{9,25},{17,1},{25,9},{2,18},{10... | collective-permute-start | bytes 417800 | tf_op jit(solution)/shard_map/ppermute | solution.py:27
  10.6 3.3 %collective-permute-start.3 = (bf16[17,32,128]{2,1,0:T(8,128)(2,1)S(1)}, bf16[17,32,128]{2,1,0:T(8,128)(2,1)S(1)}, u32[]{:S(2)}, u32[]{:S(2)}) collective-permute-start(bf16[17,32,128]{2,1,0:T(8,128)(2,1)S(1)} %get-tuple-element.54), channel_id=1, source_target_pairs={{0,64},{32,96},{64,0},{96,32},{1,65},{33,97},{65,1},{97,33},{2,66}... | collective-permute-start | bytes 417800 | tf_op jit(solution)/shard_map/ppermute | solution.py:27
  15.5 3.8 %collective-permute-start.4 = (bf16[17,32,128]{2,1,0:T(8,128)(2,1)S(1)}, bf16[17,32,128]{2,1,0:T(8,128)(2,1)S(1)}, u32[]{:S(2)}, u32[]{:S(2)}) collective-permute-start(bf16[17,32,128]{2,1,0:T(8,128)(2,1)S(1)} %get-tuple-element.54), channel_id=1, source_target_pairs={{0,96},{32,64},{64,32},{96,0},{1,97},{33,65},{65,33},{97,1},{2,98}... | collective-permute-start | bytes 417800 | tf_op jit(solution)/shard_map/ppermute | solution.py:27
  27.0 8.0 %collective-permute-done.12.refs_6_ = bf16[68,32,128]{2,1,0:T(8,128)(2,1)S(1)} collective-permute-done((bf16[68,32,128]{2,1,0:T(8,128)(2,1)S(1)}, bf16[68,32,128]{2,1,0:T(8,128)(2,1)S(1)}, u32[]{:S(2)}, u32[]{:S(2)}) %collective-permute-start.12) | collective-permute-done | bytes 557088 | tf_op jit(solution)/shard_map/ppermute | solution.py:31
  37.3 2.7 %collective-permute-start.15 = (bf16[34,32,128]{2,1,0:T(8,128)(2,1)}, bf16[34,32,128]{2,1,0:T(8,128)(2,1)}, u32[]{:S(2)}, u32[]{:S(2)}) collective-permute-start(bf16[34,32,128]{2,1,0:T(8,128)(2,1)} %slice.83), channel_id=1, source_target_pairs={{0,96},{32,0},{64,32},{96,64},{1,97},{33,1},{65,33},{97,65},{2,98}... | collective-permute-start | bytes 835592 | tf_op jit(solution)/shard_map/ppermute | solution.py:35
  47.2 3.6 %collective-permute-done.7.refs_3_ = bf16[34,32,128]{2,1,0:T(8,128)(2,1)} collective-permute-done((bf16[34,32,128]{2,1,0:T(8,128)(2,1)}, bf16[34,32,128]{2,1,0:T(8,128)(2,1)}, u32[]{:S(2)}, u32[]{:S(2)}) %collective-permute-start.7) | collective-permute-done | bytes 278560 | tf_op jit(solution)/shard_map/ppermute | solution.py:34
  52.9 5.6 %first_sum.1 = (f32[2,32,128]{2,1,0:T(8,128)S(1)}, bf16[544,32,128]{2,1,0:T(8,128)(2,1)}) custom-call(s32[7,64]{1,0:T(8,128)S(1)} %get-tuple-element.122.code_ref, bf16[68,32,128]{2,1,0:T(8,128)(2,1)S(1)} %copy-done.7, bf16[68,32,128]{2,1,0:T(8,128)(2,1)S(1)} %collective-permute-done.5.refs_1_, bf16[68,32,128]{2,1,0:T(8,128)(2,1)S(1)} %collective-permute-done.6.refs_2_, ...), custom_call_target="tpu_custom_call" | custom-call | flops 67108864 | bytes 6291456 | tf_op jit(solution)/shard_map/first_sum/pallas_call | solution.py:123
  67.7 4.4 %all-to-all-start = ((bf16[16,2,32,128]{3,2,1,0:T(8,128)(2,1)}), bf16[16,2,32,128]{3,2,1,0:T(8,128)(2,1)S(1)}, u32[]{:S(2)}, u32[]{:S(2)}) async-start(bf16[16,2,32,128]{3,2,1,0:T(8,128)(2,1)} %get-tuple-element.64), calls=%async_computation | async-start | bytes 524288 | tf_op jit(solution)/shard_map/all_to_all | solution.py:301
  74.4 4.8 %old_sum.6 = (f32[2,32,128]{2,1,0:T(8,128)S(1)}, s32[65]{0:T(128)S(1)}, bf16[16,128,128]{2,1,0:T(8,128)(2,1)S(1)}) custom-call(s32[7,64]{1,0:T(8,128)S(1)} %get-tuple-element.122.code_ref, s32[7,64]{1,0:T(8,128)S(1)} %get-tuple-element.96.fresh_ref, bf16[544,32,128]{2,1,0:T(8,128)(2,1)S(1)} %copy-done, bf16[7,1,32,128,128]{4,3,2,1,0:T(8,128)(2,1)} %own_ref.11, ...), custom_call_target="tpu_custom_call" | custom-call | flops 67108864 | bytes 6291456 | tf_op jit(solution)/shard_map/old_sum/pallas_call | solution.py:123
  81.6 3.2 %collective-permute-start.24 = (f32[2,32,128]{2,1,0:T(8,128)S(1)}, f32[2,32,128]{2,1,0:T(8,128)S(1)}, u32[]{:S(2)}, u32[]{:S(2)}) collective-permute-start(f32[2,32,128]{2,1,0:T(8,128)S(1)} %fresh_sum.6.p0), channel_id=1, source_target_pairs={{0,3},{1,2},{2,1},{3,0},{4,7},{5,6},{6,5},{7,4},{8,11},{9,10},{10,... | collective-permute-start | bytes 98312 | tf_op jit(solution)/shard_map/ppermute | solution.py:294
  87.1 6.3 %all-to-all-start.1 = ((bf16[16,2,32,128]{3,2,1,0:T(8,128)(2,1)}), bf16[16,2,32,128]{3,2,1,0:T(8,128)(2,1)S(1)}, u32[]{:S(2)}, u32[]{:S(2)}) async-start(bf16[16,2,32,128]{3,2,1,0:T(8,128)(2,1)} %get-tuple-element.71), calls=%async_computation.1 | async-start | bytes 524288 | tf_op jit(solution)/shard_map/all_to_all | solution.py:301
  95.7 4.8 %old_sum.7 = (f32[2,32,128]{2,1,0:T(8,128)S(1)}, s32[65]{0:T(128)S(1)}, bf16[16,128,128]{2,1,0:T(8,128)(2,1)S(1)}) custom-call(s32[7,64]{1,0:T(8,128)S(1)} %get-tuple-element.122.code_ref, s32[7,64]{1,0:T(8,128)S(1)} %get-tuple-element.96.fresh_ref, bf16[544,32,128]{2,1,0:T(8,128)(2,1)S(1)} %copy-done.1, bf16[32,32,128]{2,1,0:T(8,128)(2,1)S(1)} %bitcast.22, ...), custom_call_target="tpu_custom_call" | custom-call | flops 67108864 | bytes 6291456 | tf_op jit(solution)/shard_map/old_sum/pallas_call | solution.py:123
  102.4 2.9 %collective-permute-start.26 = (f32[2,32,128]{2,1,0:T(8,128)S(1)}, f32[2,32,128]{2,1,0:T(8,128)S(1)}, u32[]{:S(2)}, u32[]{:S(2)}) collective-permute-start(f32[2,32,128]{2,1,0:T(8,128)S(1)} %fresh_sum.7.p0), channel_id=1, source_target_pairs={{0,2},{1,3},{2,0},{3,1},{4,6},{5,7},{6,4},{7,5},{8,10},{9,11},{10,... | collective-permute-start | bytes 98312 | tf_op jit(solution)/shard_map/ppermute | solution.py:294
  110.3 6.4 %all-to-all-start.2 = ((bf16[16,2,32,128]{3,2,1,0:T(8,128)(2,1)}), bf16[16,2,32,128]{3,2,1,0:T(8,128)(2,1)S(1)}, u32[]{:S(2)}, u32[]{:S(2)}) async-start(bf16[16,2,32,128]{3,2,1,0:T(8,128)(2,1)} %get-tuple-element.78), calls=%async_computation.2 | async-start | bytes 524288 | tf_op jit(solution)/shard_map/all_to_all | solution.py:301
  118.9 4.8 %old_sum.8 = (f32[2,32,128]{2,1,0:T(8,128)S(1)}, s32[65]{0:T(128)S(1)}, bf16[16,128,128]{2,1,0:T(8,128)(2,1)S(1)}) custom-call(s32[7,64]{1,0:T(8,128)S(1)} %get-tuple-element.122.code_ref, s32[7,64]{1,0:T(8,128)S(1)} %get-tuple-element.96.fresh_ref, bf16[544,32,128]{2,1,0:T(8,128)(2,1)S(1)} %copy-done.2, bf16[32,32,128]{2,1,0:T(8,128)(2,1)S(1)} %bitcast.23, ...), custom_call_target="tpu_custom_call" | custom-call | flops 67108864 | bytes 6291456 | tf_op jit(solution)/shard_map/old_sum/pallas_call | solution.py:123
  132.2 6.1 %all-to-all-start.3 = ((bf16[16,2,32,128]{3,2,1,0:T(8,128)(2,1)}), bf16[16,2,32,128]{3,2,1,0:T(8,128)(2,1)S(1)}, u32[]{:S(2)}, u32[]{:S(2)}) async-start(bf16[16,2,32,128]{3,2,1,0:T(8,128)(2,1)} %get-tuple-element.85), calls=%async_computation.3 | async-start | bytes 524288 | tf_op jit(solution)/shard_map/all_to_all | solution.py:301
  140.5 4.8 %old_sum.9 = (f32[2,32,128]{2,1,0:T(8,128)S(1)}, s32[65]{0:T(128)S(1)}, bf16[16,128,128]{2,1,0:T(8,128)(2,1)S(1)}) custom-call(s32[7,64]{1,0:T(8,128)S(1)} %get-tuple-element.122.code_ref, s32[7,64]{1,0:T(8,128)S(1)} %get-tuple-element.96.fresh_ref, bf16[544,32,128]{2,1,0:T(8,128)(2,1)S(1)} %copy-done.3, bf16[32,32,128]{2,1,0:T(8,128)(2,1)S(1)} %bitcast.24, ...), custom_call_target="tpu_custom_call" | custom-call | flops 67108864 | bytes 6291456 | tf_op jit(solution)/shard_map/old_sum/pallas_call | solution.py:123
  147.2 2.9 %collective-permute-start.32 = (f32[2,32,128]{2,1,0:T(8,128)S(1)}, f32[2,32,128]{2,1,0:T(8,128)S(1)}, u32[]{:S(2)}, u32[]{:S(2)}) collective-permute-start(f32[2,32,128]{2,1,0:T(8,128)S(1)} %fresh_sum.9.p0), channel_id=1, source_target_pairs={{0,2},{1,3},{2,0},{3,1},{4,6},{5,7},{6,4},{7,5},{8,10},{9,11},{10,... | collective-permute-start | bytes 98312 | tf_op jit(solution)/shard_map/ppermute | solution.py:294
  155.4 5.7 %all-to-all-start.4 = ((bf16[16,2,32,128]{3,2,1,0:T(8,128)(2,1)}), bf16[16,2,32,128]{3,2,1,0:T(8,128)(2,1)S(1)}, u32[]{:S(2)}, u32[]{:S(2)}) async-start(bf16[16,2,32,128]{3,2,1,0:T(8,128)(2,1)} %get-tuple-element.92), calls=%async_computation.4 | async-start | bytes 524288 | tf_op jit(solution)/shard_map/all_to_all | solution.py:301
  163.3 4.8 %old_sum.10 = (f32[2,32,128]{2,1,0:T(8,128)S(1)}, s32[65]{0:T(128)S(1)}, bf16[16,128,128]{2,1,0:T(8,128)(2,1)S(1)}) custom-call(s32[7,64]{1,0:T(8,128)S(1)} %get-tuple-element.122.code_ref, s32[7,64]{1,0:T(8,128)S(1)} %get-tuple-element.96.fresh_ref, bf16[544,32,128]{2,1,0:T(8,128)(2,1)S(1)} %copy-done.4, bf16[32,32,128]{2,1,0:T(8,128)(2,1)S(1)} %bitcast.25, ...), custom_call_target="tpu_custom_call" | custom-call | flops 67108864 | bytes 6291456 | tf_op jit(solution)/shard_map/old_sum/pallas_call | solution.py:123
  177.0 6.1 %all-to-all-start.5 = ((bf16[16,2,32,128]{3,2,1,0:T(8,128)(2,1)}), bf16[16,2,32,128]{3,2,1,0:T(8,128)(2,1)S(1)}, u32[]{:S(2)}, u32[]{:S(2)}) async-start(bf16[16,2,32,128]{3,2,1,0:T(8,128)(2,1)} %get-tuple-element.99), calls=%async_computation.5 | async-start | bytes 524288 | tf_op jit(solution)/shard_map/all_to_all | solution.py:301
  183.2 6.4 %old_sum.11 = (f32[2,32,128]{2,1,0:T(8,128)S(1)}, s32[65]{0:T(128)S(1)}, bf16[16,128,128]{2,1,0:T(8,128)(2,1)S(1)}) custom-call(s32[7,64]{1,0:T(8,128)S(1)} %get-tuple-element.122.code_ref, s32[7,64]{1,0:T(8,128)S(1)} %get-tuple-element.96.fresh_ref, bf16[544,32,128]{2,1,0:T(8,128)(2,1)} %get-tuple-element.61.store_ref, bf16[32,32,128]{2,1,0:T(8,128)(2,1)S(1)} %bitcast.26, ...), custom_call_target="tpu_custom_call" | custom-call | flops 67108864 | bytes 6291456 | tf_op jit(solution)/shard_map/old_sum/pallas_call | solution.py:123
  191.5 3.2 %collective-permute-start.38 = (f32[2,32,128]{2,1,0:T(8,128)S(1)}, f32[2,32,128]{2,1,0:T(8,128)S(1)}, u32[]{:S(2)}, u32[]{:S(2)}) collective-permute-start(f32[2,32,128]{2,1,0:T(8,128)S(1)} %fresh_sum.11.p0), channel_id=1, source_target_pairs={{0,2},{1,3},{2,0},{3,1},{4,6},{5,7},{6,4},{7,5},{8,10},{9,11},{10,... | collective-permute-start | bytes 98312 | tf_op jit(solution)/shard_map/ppermute | solution.py:294
  198.8 17.4 %collective-permute-start.40 = (bf16[7,32,128]{2,1,0:T(8,128)(2,1)S(1)}, bf16[7,32,128]{2,1,0:T(8,128)(2,1)S(1)}, u32[]{:S(2)}, u32[]{:S(2)}) collective-permute-start(bf16[7,32,128]{2,1,0:T(8,128)(2,1)S(1)} %get-tuple-element.108), channel_id=1, source_target_pairs={{0,4},{4,0},{1,5},{5,1},{2,6},{6,2},{3,7},{7,3},{8,12},{12,8},{9,1... | collective-permute-start | bytes 172040 | tf_op jit(solution)/shard_map/ppermute | solution.py:23
  (141 shorter events, 92.5 us)
Async XLA Ops:
  4.4 46.4 %collective-permute-start.16 = (bf16[7,1,32,128,128]{4,3,2,1,0:T(8,128)(2,1)}, bf16[7,1,32,128,128]{4,3,2,1,0:T(8,128)(2,1)}, u32[]{:S(2)}, u32[]{:S(2)}) collective-permute-start(bf16[7,1,32,128,128]{4,3,2,1,0:T(8,128)(2,1)} %own_ref.11), channel_id=1, source_target_pairs={{0,4},{4,0},{1,5},{5,1},{2,6},{6,2},{3,7},{7,3},{8,12},{12,8},{9,1... | collective-permute-start | bytes 22020104 | tf_op jit(solution)/shard_map/ppermute | solution.py:23
  4.8 5.8 %collective-permute-start.9 = (bf16[17,32,128]{2,1,0:T(8,128)(2,1)S(1)}, bf16[17,32,128]{2,1,0:T(8,128)(2,1)S(1)}, u32[]{:S(2)}, u32[]{:S(2)}) collective-permute-start(bf16[17,32,128]{2,1,0:T(8,128)(2,1)S(1)} %collective-permute-done.1), channel_id=1, source_target_pairs={{0,8},{8,0},{16,24},{24,16},{1,9},{9,1},{17,25},{25,17},{2,10},{10... | collective-permute-start | bytes 417800 | tf_op jit(solution)/shard_map/ppermute | solution.py:27
  6.2 9.3 %collective-permute-start.10 = (bf16[17,32,128]{2,1,0:T(8,128)(2,1)S(1)}, bf16[17,32,128]{2,1,0:T(8,128)(2,1)S(1)}, u32[]{:S(2)}, u32[]{:S(2)}) collective-permute-start(bf16[17,32,128]{2,1,0:T(8,128)(2,1)S(1)} %collective-permute-done.1), channel_id=1, source_target_pairs={{0,16},{8,24},{16,0},{24,8},{1,17},{9,25},{17,1},{25,9},{2,18},{10... | collective-permute-start | bytes 417800 | tf_op jit(solution)/shard_map/ppermute | solution.py:27
  8.9 10.4 %collective-permute-start.11 = (bf16[17,32,128]{2,1,0:T(8,128)(2,1)S(1)}, bf16[17,32,128]{2,1,0:T(8,128)(2,1)S(1)}, u32[]{:S(2)}, u32[]{:S(2)}) collective-permute-start(bf16[17,32,128]{2,1,0:T(8,128)(2,1)S(1)} %collective-permute-done.1), channel_id=1, source_target_pairs={{0,24},{8,16},{16,8},{24,0},{1,25},{9,17},{17,9},{25,1},{2,26},{10... | collective-permute-start | bytes 417800 | tf_op jit(solution)/shard_map/ppermute | solution.py:27
  8.9 10.9 %collective-permute-start.2 = (bf16[17,32,128]{2,1,0:T(8,128)(2,1)S(1)}, bf16[17,32,128]{2,1,0:T(8,128)(2,1)S(1)}, u32[]{:S(2)}, u32[]{:S(2)}) collective-permute-start(bf16[17,32,128]{2,1,0:T(8,128)(2,1)S(1)} %get-tuple-element.54), channel_id=1, source_target_pairs={{0,32},{32,0},{64,96},{96,64},{1,33},{33,1},{65,97},{97,65},{2,34}... | collective-permute-start | bytes 417800 | tf_op jit(solution)/shard_map/ppermute | solution.py:27
  10.6 11.5 %collective-permute-start.3 = (bf16[17,32,128]{2,1,0:T(8,128)(2,1)S(1)}, bf16[17,32,128]{2,1,0:T(8,128)(2,1)S(1)}, u32[]{:S(2)}, u32[]{:S(2)}) collective-permute-start(bf16[17,32,128]{2,1,0:T(8,128)(2,1)S(1)} %get-tuple-element.54), channel_id=1, source_target_pairs={{0,64},{32,96},{64,0},{96,32},{1,65},{33,97},{65,1},{97,33},{2,66}... | collective-permute-start | bytes 417800 | tf_op jit(solution)/shard_map/ppermute | solution.py:27
  15.5 8.0 %collective-permute-start.4 = (bf16[17,32,128]{2,1,0:T(8,128)(2,1)S(1)}, bf16[17,32,128]{2,1,0:T(8,128)(2,1)S(1)}, u32[]{:S(2)}, u32[]{:S(2)}) collective-permute-start(bf16[17,32,128]{2,1,0:T(8,128)(2,1)S(1)} %get-tuple-element.54), channel_id=1, source_target_pairs={{0,96},{32,64},{64,32},{96,0},{1,97},{33,65},{65,33},{97,1},{2,98}... | collective-permute-start | bytes 417800 | tf_op jit(solution)/shard_map/ppermute | solution.py:27
  19.3 15.7 %collective-permute-start.12 = (bf16[68,32,128]{2,1,0:T(8,128)(2,1)S(1)}, bf16[68,32,128]{2,1,0:T(8,128)(2,1)S(1)}, u32[]{:S(2)}, u32[]{:S(2)}) collective-permute-start(bf16[68,32,128]{2,1,0:T(8,128)(2,1)S(1)} %constant_dynamic-update-slice_fusion.4.refs_5_), channel_id=1, source_target_pairs={{0,32},{32,64},{64,96},{96,0},{1,33},{33,65},{65,97},{97,1},{2,34}... | collective-permute-start | bytes 1671176 | tf_op jit(solution)/shard_map/ppermute | solution.py:31
  19.8 16.7 %collective-permute-start.13 = (bf16[68,32,128]{2,1,0:T(8,128)(2,1)S(1)}, bf16[68,32,128]{2,1,0:T(8,128)(2,1)S(1)}, u32[]{:S(2)}, u32[]{:S(2)}) collective-permute-start(bf16[68,32,128]{2,1,0:T(8,128)(2,1)S(1)} %constant_dynamic-update-slice_fusion.4.refs_5_), channel_id=1, source_target_pairs={{0,96},{32,0},{64,32},{96,64},{1,97},{33,1},{65,33},{97,65},{2,98}... | collective-permute-start | bytes 1671176 | tf_op jit(solution)/shard_map/ppermute | solution.py:32
  23.6 17.3 %collective-permute-start.5 = (bf16[68,32,128]{2,1,0:T(8,128)(2,1)S(1)}, bf16[68,32,128]{2,1,0:T(8,128)(2,1)S(1)}, u32[]{:S(2)}, u32[]{:S(2)}) collective-permute-start(bf16[68,32,128]{2,1,0:T(8,128)(2,1)S(1)} %constant_dynamic-update-slice_fusion.refs_0_), channel_id=1, source_target_pairs={{0,8},{8,16},{16,24},{24,0},{1,9},{9,17},{17,25},{25,1},{2,10},{10... | collective-permute-start | bytes 1671176 | tf_op jit(solution)/shard_map/ppermute | solution.py:31
  23.8 17.8 %collective-permute-start.6 = (bf16[68,32,128]{2,1,0:T(8,128)(2,1)S(1)}, bf16[68,32,128]{2,1,0:T(8,128)(2,1)S(1)}, u32[]{:S(2)}, u32[]{:S(2)}) collective-permute-start(bf16[68,32,128]{2,1,0:T(8,128)(2,1)S(1)} %constant_dynamic-update-slice_fusion.refs_0_), channel_id=1, source_target_pairs={{0,24},{8,0},{16,8},{24,16},{1,25},{9,1},{17,9},{25,17},{2,26},{10... | collective-permute-start | bytes 1671176 | tf_op jit(solution)/shard_map/ppermute | solution.py:32
  36.5 9.6 %collective-permute-start.14 = (bf16[34,32,128]{2,1,0:T(8,128)(2,1)S(1)}, bf16[34,32,128]{2,1,0:T(8,128)(2,1)S(1)}, u32[]{:S(2)}, u32[]{:S(2)}) collective-permute-start(bf16[34,32,128]{2,1,0:T(8,128)(2,1)S(1)} %slice.82), channel_id=1, source_target_pairs={{0,32},{32,64},{64,96},{96,0},{1,33},{33,65},{65,97},{97,1},{2,34}... | collective-permute-start | bytes 835592 | tf_op jit(solution)/shard_map/ppermute | solution.py:34
  37.3 9.5 %collective-permute-start.15 = (bf16[34,32,128]{2,1,0:T(8,128)(2,1)}, bf16[34,32,128]{2,1,0:T(8,128)(2,1)}, u32[]{:S(2)}, u32[]{:S(2)}) collective-permute-start(bf16[34,32,128]{2,1,0:T(8,128)(2,1)} %slice.83), channel_id=1, source_target_pairs={{0,96},{32,0},{64,32},{96,64},{1,97},{33,1},{65,33},{97,65},{2,98}... | collective-permute-start | bytes 835592 | tf_op jit(solution)/shard_map/ppermute | solution.py:35
  41.6 9.2 %collective-permute-start.7 = (bf16[34,32,128]{2,1,0:T(8,128)(2,1)}, bf16[34,32,128]{2,1,0:T(8,128)(2,1)}, u32[]{:S(2)}, u32[]{:S(2)}) collective-permute-start(bf16[34,32,128]{2,1,0:T(8,128)(2,1)} %slice.80), channel_id=1, source_target_pairs={{0,8},{8,16},{16,24},{24,0},{1,9},{9,17},{17,25},{25,1},{2,10},{10... | collective-permute-start | bytes 835592 | tf_op jit(solution)/shard_map/ppermute | solution.py:34
  42.4 8.4 %collective-permute-start.8 = (bf16[34,32,128]{2,1,0:T(8,128)(2,1)}, bf16[34,32,128]{2,1,0:T(8,128)(2,1)}, u32[]{:S(2)}, u32[]{:S(2)}) collective-permute-start(bf16[34,32,128]{2,1,0:T(8,128)(2,1)} %slice.81), channel_id=1, source_target_pairs={{0,24},{8,0},{16,8},{24,16},{1,25},{9,1},{17,9},{25,17},{2,26},{10... | collective-permute-start | bytes 835592 | tf_op jit(solution)/shard_map/ppermute | solution.py:35
  46.1 16.5 %collective-permute-start.21 = (bf16[8,1,128,128]{3,2,1,0:T(8,128)(2,1)}, bf16[8,1,128,128]{3,2,1,0:T(8,128)(2,1)S(1)}, u32[]{:S(2)}, u32[]{:S(2)}) collective-permute-start(bf16[8,1,128,128]{3,2,1,0:T(8,128)(2,1)} %own_d_ref.13), channel_id=1, source_target_pairs={{0,4},{4,0},{1,5},{5,1},{2,6},{6,2},{3,7},{7,3},{8,12},{12,8},{9,1... | collective-permute-start | bytes 786440 | tf_op jit(solution)/shard_map/ppermute | solution.py:23
  46.8 15.6 %collective-permute-start.20 = (bf16[8,1,32,128]{3,2,1,0:T(8,128)(2,1)S(1)}, bf16[8,1,32,128]{3,2,1,0:T(8,128)(2,1)S(1)}, u32[]{:S(2)}, u32[]{:S(2)}) collective-permute-start(bf16[8,1,32,128]{3,2,1,0:T(8,128)(2,1)S(1)} %get-tuple-element.104), channel_id=1, source_target_pairs={{0,4},{4,0},{1,5},{5,1},{2,6},{6,2},{3,7},{7,3},{8,12},{12,8},{9,1... | collective-permute-start | bytes 196616 | tf_op jit(solution)/shard_map/ppermute | solution.py:23
  67.7 12.0 %all-to-all-start = ((bf16[16,2,32,128]{3,2,1,0:T(8,128)(2,1)}), bf16[16,2,32,128]{3,2,1,0:T(8,128)(2,1)S(1)}, u32[]{:S(2)}, u32[]{:S(2)}) async-start(bf16[16,2,32,128]{3,2,1,0:T(8,128)(2,1)} %get-tuple-element.64), calls=%async_computation | async-start | bytes 524288 | tf_op jit(solution)/shard_map/all_to_all | solution.py:301
  87.1 13.9 %all-to-all-start.1 = ((bf16[16,2,32,128]{3,2,1,0:T(8,128)(2,1)}), bf16[16,2,32,128]{3,2,1,0:T(8,128)(2,1)S(1)}, u32[]{:S(2)}, u32[]{:S(2)}) async-start(bf16[16,2,32,128]{3,2,1,0:T(8,128)(2,1)} %get-tuple-element.71), calls=%async_computation.1 | async-start | bytes 524288 | tf_op jit(solution)/shard_map/all_to_all | solution.py:301
  110.3 13.9 %all-to-all-start.2 = ((bf16[16,2,32,128]{3,2,1,0:T(8,128)(2,1)}), bf16[16,2,32,128]{3,2,1,0:T(8,128)(2,1)S(1)}, u32[]{:S(2)}, u32[]{:S(2)}) async-start(bf16[16,2,32,128]{3,2,1,0:T(8,128)(2,1)} %get-tuple-element.78), calls=%async_computation.2 | async-start | bytes 524288 | tf_op jit(solution)/shard_map/all_to_all | solution.py:301
  132.2 13.6 %all-to-all-start.3 = ((bf16[16,2,32,128]{3,2,1,0:T(8,128)(2,1)}), bf16[16,2,32,128]{3,2,1,0:T(8,128)(2,1)S(1)}, u32[]{:S(2)}, u32[]{:S(2)}) async-start(bf16[16,2,32,128]{3,2,1,0:T(8,128)(2,1)} %get-tuple-element.85), calls=%async_computation.3 | async-start | bytes 524288 | tf_op jit(solution)/shard_map/all_to_all | solution.py:301
  155.4 13.2 %all-to-all-start.4 = ((bf16[16,2,32,128]{3,2,1,0:T(8,128)(2,1)}), bf16[16,2,32,128]{3,2,1,0:T(8,128)(2,1)S(1)}, u32[]{:S(2)}, u32[]{:S(2)}) async-start(bf16[16,2,32,128]{3,2,1,0:T(8,128)(2,1)} %get-tuple-element.92), calls=%async_computation.4 | async-start | bytes 524288 | tf_op jit(solution)/shard_map/all_to_all | solution.py:301
  177.0 13.7 %all-to-all-start.5 = ((bf16[16,2,32,128]{3,2,1,0:T(8,128)(2,1)}), bf16[16,2,32,128]{3,2,1,0:T(8,128)(2,1)S(1)}, u32[]{:S(2)}, u32[]{:S(2)}) async-start(bf16[16,2,32,128]{3,2,1,0:T(8,128)(2,1)} %get-tuple-element.99), calls=%async_computation.5 | async-start | bytes 524288 | tf_op jit(solution)/shard_map/all_to_all | solution.py:301
  198.8 18.3 %collective-permute-start.40 = (bf16[7,32,128]{2,1,0:T(8,128)(2,1)S(1)}, bf16[7,32,128]{2,1,0:T(8,128)(2,1)S(1)}, u32[]{:S(2)}, u32[]{:S(2)}) collective-permute-start(bf16[7,32,128]{2,1,0:T(8,128)(2,1)S(1)} %get-tuple-element.108), channel_id=1, source_target_pairs={{0,4},{4,0},{1,5},{5,1},{2,6},{6,2},{3,7},{7,3},{8,12},{12,8},{9,1... | collective-permute-start | bytes 172040 | tf_op jit(solution)/shard_map/ppermute | solution.py:23
  (33 other events, 159.3 us)

commit v3 on v2

--- a/solution.py
+++ b/solution.py
@@ -44,9 +44,8 @@
 NEAR = 16
 
 
-def gather_sum(level, code_ref, store_ref, solved_ref, own_ref, other_ref, out_ref, blocks, block_sems, between=None):
+def gather_sum(level, code_ref, picks, known, solved_ref, own_ref, other_ref, out_ref, blocks, block_sems, between):
     slots = code_ref.shape[1]
-    known = store_ref.shape[0]
     per_row = slots // 2
     loads = [
         pltpu.make_async_copy(a_ref.at[level - 1, 0], blocks.at[pl.ds(r * per_row, per_row)], block_sems.at[r])
@@ -54,8 +53,7 @@
     ]
     for load in loads:
         load.start()
-    if between is not None:
-        between()
+    between()
     for r in range(2):
         loads[r].wait()
         total = None
@@ -64,7 +62,7 @@
             for k in range(g, g + GROUP):
                 code = code_ref[level - 1, k]
                 kept = (code >= 0).astype(jnp.float32)
-                picked = store_ref[jnp.clip(code, 0, known - 1)]
+                picked = picks(k, jnp.clip(code, 0, known - 1))
                 if solved_ref is not None:
                     picked = jnp.where(code >= known, solved_ref[jnp.maximum(code - known, 0)], picked)
                 xs.append((picked.astype(jnp.float32) * kept).astype(jnp.bfloat16))
@@ -75,32 +73,42 @@
 
 
 def first_kernel(code_ref, *refs):
-    sources, refs = refs[:-7], refs[-7:]
-    own_ref, other_ref, out_ref, store_ref, blocks, block_sems, pack_sems = refs
+    sources, refs = refs[:-9], refs[-9:]
+    own_ref, other_ref, out_ref, store_ref, blocks, block_sems, pack_sems, packed, store_sem = refs
     packs, start = [], 0
     for i, source in enumerate(sources):
-        packs.append(pltpu.make_async_copy(source, store_ref.at[pl.ds(start, source.shape[0])], pack_sems.at[i]))
+        packs.append(pltpu.make_async_copy(source, packed.at[pl.ds(start, source.shape[0])], pack_sems.at[i]))
         start += source.shape[0]
+    keep = pltpu.make_async_copy(packed, store_ref.at[pl.ds(0, start)], store_sem)
 
     def between():
         for pack in packs:
             pack.start()
         for pack in packs:
             pack.wait()
-
-    gather_sum(1, code_ref, store_ref, None, own_ref, other_ref, out_ref, blocks, block_sems, between)
-
-
-def old_kernel(level, code_ref, fresh_ref, store_ref, *refs):
+        keep.start()
+
+    picks = lambda k, code: packed[code]
+    gather_sum(1, code_ref, picks, start, None, own_ref, other_ref, out_ref, blocks, block_sems, between)
+    keep.wait()
+
+
+def old_kernel(level, known, code_ref, fresh_ref, store_ref, *refs):
     solved, refs = refs[: level - 2], refs[level - 2 :]
-    own_ref, other_ref, out_ref, list_ref, near_ref, blocks, block_sems = refs[:7]
-    solved_ref = refs[7] if solved else None
+    own_ref, other_ref, out_ref, list_ref, near_ref, blocks, block_sems, picked, pick_sem = refs[:9]
+    solved_ref = refs[9] if solved else None
+    slots = code_ref.shape[1]
 
     def between():
+        for k in range(slots):
+            place = jnp.clip(code_ref[level - 1, k], 0, known - 1)
+            pltpu.make_async_copy(store_ref.at[place], picked.at[k], pick_sem).start()
         for i, one in enumerate(solved):
             solved_ref[i * one.shape[0] : (i + 1) * one.shape[0]] = one[...]
-
-    gather_sum(level, code_ref, store_ref, solved_ref, own_ref, other_ref, out_ref, blocks, block_sems, between)
+        pltpu.make_async_copy(store_ref.at[pl.ds(0, slots)], picked, pick_sem).wait()
+
+    picks = lambda k, code: picked[k]
+    gather_sum(level, code_ref, picks, known, solved_ref, own_ref, other_ref, out_ref, blocks, block_sems, between)
 
     def note(slot, count):
         code = fresh_ref[level - 1, slot]
@@ -118,13 +126,13 @@
     list_ref[0] = lax.fori_loop(0, fresh_ref.shape[1], note, jnp.int32(0))
 
 
-def sum_call(kernel, codes, sources, source_space, own, other, outs, out_spaces, extra, name):
+def sum_call(kernel, codes, sources, source_spaces, own, other, outs, out_spaces, extra, name):
     slots, (rhs_cols, block) = codes[0].shape[1], sources[0].shape[1:]
     return pl.pallas_call(
         kernel,
         out_shape=[jax.ShapeDtypeStruct((2, rhs_cols, block), jnp.float32)] + outs,
         in_specs=[pl.BlockSpec(memory_space=pltpu.SMEM)] * len(codes)
-        + [pl.BlockSpec(memory_space=source_space)] * len(sources)
+        + [pl.BlockSpec(memory_space=space) for space in source_spaces]
         + [pl.BlockSpec(memory_space=pltpu.HBM)] * 2,
         out_specs=[pl.BlockSpec(memory_space=space) for space in [pltpu.VMEM] + out_spaces],
         scratch_shapes=[pltpu.VMEM((slots, block, block), jnp.bfloat16), pltpu.SemaphoreType.DMA((2,))] + extra,
@@ -139,21 +147,31 @@
 
 
 def first_sum(code, sources, own, other):
-    store = jax.ShapeDtypeStruct((sum(v.shape[0] for v in sources),) + sources[0].shape[1:], jnp.bfloat16)
-    extra = [pltpu.SemaphoreType.DMA((len(sources),))]
-    return sum_call(first_kernel, [code], sources, pl.ANY, own, other, [store], [pltpu.VMEM], extra, "first_sum")
-
-
-def old_sum(level, code, fresh, store, solved, own, other):
-    block = store.shape[-1]
+    one = sources[0].shape[1:]
+    known = sum(v.shape[0] for v in sources)
+    store = jax.ShapeDtypeStruct((2048,) + one, jnp.bfloat16)
+    extra = [
+        pltpu.SemaphoreType.DMA((len(sources),)),
+        pltpu.VMEM((known,) + one, jnp.bfloat16),
+        pltpu.SemaphoreType.DMA,
+    ]
+    spaces = [pl.ANY] * len(sources)
+    return sum_call(first_kernel, [code], sources, spaces, own, other, [store], [pltpu.HBM], extra, "first_sum")
+
+
+def old_sum(level, known, code, fresh, store, solved, own, other):
+    one = store.shape[1:]
     outs = [
         jax.ShapeDtypeStruct((code.shape[1] + 1,), jnp.int32),
-        jax.ShapeDtypeStruct((NEAR, block, block), jnp.bfloat16),
+        jax.ShapeDtypeStruct((NEAR, one[1], one[1]), jnp.bfloat16),
     ]
-    kernel = functools.partial(old_kernel, level)
-    spaces = [pltpu.SMEM, pltpu.VMEM]
-    extra = [pltpu.VMEM((sum(v.shape[0] for v in solved),) + store.shape[1:], jnp.bfloat16)] if solved else []
-    return sum_call(kernel, [code, fresh], [store] + solved, pltpu.VMEM, own, other, outs, spaces, extra, "old_sum")
+    kernel = functools.partial(old_kernel, level, known)
+    extra = [pltpu.VMEM((code.shape[1],) + one, jnp.bfloat16), pltpu.SemaphoreType.DMA]
+    if solved:
+        extra.append(pltpu.VMEM((sum(v.shape[0] for v in solved),) + one, jnp.bfloat16))
+    spaces = [pl.ANY] + [pltpu.VMEM] * len(solved)
+    out_spaces = [pltpu.SMEM, pltpu.VMEM]
+    return sum_call(kernel, [code, fresh], [store] + solved, spaces, own, other, outs, out_spaces, extra, "old_sum")
 
 
 def fresh_kernel(level, list_ref, old_ref, x_ref, near_ref, own_ref, other_ref, out_ref, far, sem):
@@ -299,7 +317,9 @@
         if not last:
             next_fresh, sent = lax.optimization_barrier((fresh_code, outs[1]))
             solved = lax.all_to_all(sent, ("z", "y"), 0, 0).reshape(32, half, block)
-            old, listed, near = old_sum(level + 1, old_code, next_fresh, store, solved_levels, off_blocks, off_other)
+            old, listed, near = old_sum(
+                level + 1, 32 * each, old_code, next_fresh, store, solved_levels, off_blocks, off_other
+            )
             value = fresh_sum(level + 1, listed, solved, old, near, off_blocks, off_other)
             solved_levels = solved_levels + [solved]
 

time: 219 us -> 211 us (0.963)
  local copies, waits for them, and re-layouts: 16.8 us -> 5.5 us
  waiting for transfers between devices: 40.6 us -> 49.3 us
  starting transfers between devices: 108 us -> 101 us
    unnamed x33 -> x23, local copies, waits for them, and re-layouts: 13.5 us -> 2.27 us
    all_to_all x6, waiting for transfers between devices: 3.26 us -> 12.1 us  [on_device(): solved = lax.all_to_all(sent, ('z', 'y'), 0, 0).reshape(32, half, block)]
    all_to_all x6, starting transfers between devices: 35 us -> 28.5 us  [on_device(): solved = lax.all_to_all(sent, ('z', 'y'), 0, 0).reshape(32, half, block)]
  transfers between devices with their start and end apart: 47 -> 47, of which waited for: 27 -> 27; matrix products, arithmetic and copies ran while one was open for 2% -> 2% of each run, Pallas kernels for 17% -> 18%
where the time goes in v3:
time: 211 us; the launch traced here: 210 us
  starting transfers between devices  101 us (48%)
  Pallas kernels  49.6 us (24%)
  waiting for transfers between devices  49.3 us (23%)
  local copies, waits for them, and re-layouts  5.5 us (3%)
  other arithmetic  2.48 us (1%)
    pallas_call x7, Pallas kernels, sum_call(): pl.pallas_call(kernel, out_shape=[jax.ShapeDtypeStruct((2, rhs_cols, bloc...  37.7 us
    all_to_all x6, starting transfers between devices, on_device(): solved = lax.all_to_all(sent, ('z', 'y'), 0, 0).reshape(32, half, block)  28.5 us
    ppermute x21, starting transfers between devices, on_device(): lax.ppermute(value, 'x', xor_pairs(4, k))  27.5 us
    ppermute x6, starting transfers between devices, swap_cores(): return lax.ppermute(v, 'core', xor_pairs(2, 1))  21.6 us
    ppermute x21, waiting for transfers between devices, on_device(): lax.ppermute(value, 'x', xor_pairs(4, k))  19.8 us
    ppermute x6, starting transfers between devices, direct_gather(): lax.ppermute(v, axis, xor_pairs(4, k))  12.9 us
    all_to_all x6, waiting for transfers between devices, on_device(): solved = lax.all_to_all(sent, ('z', 'y'), 0, 0).reshape(32, half, block)  12.1 us
    ppermute x2, waiting for transfers between devices, ring_gather(): before = lax.ppermute(v, axis, shift_pairs(4, 1))  8.02 us
  transfers between devices with their start and end apart: 47, of which 27 were waited for; matrix products, arithmetic and copies ran while one was open for 2% of the time, Pallas kernels for 18%

profile of v3, /device:TPU:1, one launch (start us, length us, event | category | flops | bytes accessed | tf_op | source)
XLA Modules:
  0.0 209.6 jit_solution(1489874392676902983)
XLA Ops:
  6.2 2.7 %collective-permute-start.10 = (bf16[17,32,128]{2,1,0:T(8,128)(2,1)S(1)}, bf16[17,32,128]{2,1,0:T(8,128)(2,1)S(1)}, u32[]{:S(2)}, u32[]{:S(2)}) collective-permute-start(bf16[17,32,128]{2,1,0:T(8,128)(2,1)S(1)} %collective-permute-done.1), channel_id=1, source_target_pairs={{0,16},{8,24},{16,0},{24,8},{1,17},{9,25},{17,1},{25,9},{2,18},{10... | collective-permute-start | bytes 417800 | tf_op jit(solution)/shard_map/ppermute | solution.py:27
  10.6 3.3 %collective-permute-start.3 = (bf16[17,32,128]{2,1,0:T(8,128)(2,1)S(1)}, bf16[17,32,128]{2,1,0:T(8,128)(2,1)S(1)}, u32[]{:S(2)}, u32[]{:S(2)}) collective-permute-start(bf16[17,32,128]{2,1,0:T(8,128)(2,1)S(1)} %get-tuple-element.54), channel_id=1, source_target_pairs={{0,64},{32,96},{64,0},{96,32},{1,65},{33,97},{65,1},{97,33},{2,66}... | collective-permute-start | bytes 417800 | tf_op jit(solution)/shard_map/ppermute | solution.py:27
  15.5 3.8 %collective-permute-start.4 = (bf16[17,32,128]{2,1,0:T(8,128)(2,1)S(1)}, bf16[17,32,128]{2,1,0:T(8,128)(2,1)S(1)}, u32[]{:S(2)}, u32[]{:S(2)}) collective-permute-start(bf16[17,32,128]{2,1,0:T(8,128)(2,1)S(1)} %get-tuple-element.54), channel_id=1, source_target_pairs={{0,96},{32,64},{64,32},{96,0},{1,97},{33,65},{65,33},{97,1},{2,98}... | collective-permute-start | bytes 417800 | tf_op jit(solution)/shard_map/ppermute | solution.py:27
  27.0 8.0 %collective-permute-done.12.refs_6_ = bf16[68,32,128]{2,1,0:T(8,128)(2,1)S(1)} collective-permute-done((bf16[68,32,128]{2,1,0:T(8,128)(2,1)S(1)}, bf16[68,32,128]{2,1,0:T(8,128)(2,1)S(1)}, u32[]{:S(2)}, u32[]{:S(2)}) %collective-permute-start.12) | collective-permute-done | bytes 557088 | tf_op jit(solution)/shard_map/ppermute | solution.py:31
  47.2 3.6 %collective-permute-done.7.refs_3_ = bf16[34,32,128]{2,1,0:T(8,128)(2,1)} collective-permute-done((bf16[34,32,128]{2,1,0:T(8,128)(2,1)}, bf16[34,32,128]{2,1,0:T(8,128)(2,1)}, u32[]{:S(2)}, u32[]{:S(2)}) %collective-permute-start.7) | collective-permute-done | bytes 278560 | tf_op jit(solution)/shard_map/ppermute | solution.py:34
  52.9 4.7 %first_sum.1 = (f32[2,32,128]{2,1,0:T(8,128)S(1)}, bf16[2048,32,128]{2,1,0:T(8,128)(2,1)}) custom-call(s32[7,64]{1,0:T(8,128)S(1)} %get-tuple-element.122.code_ref, bf16[68,32,128]{2,1,0:T(8,128)(2,1)S(1)} %copy-done.2, bf16[68,32,128]{2,1,0:T(8,128)(2,1)S(1)} %collective-permute-done.5.refs_1_, bf16[68,32,128]{2,1,0:T(8,128)(2,1)S(1)} %collective-permute-done.6.refs_2_, ...), custom_call_target="tpu_custom_call" | custom-call | flops 67108864 | bytes 6291456 | tf_op jit(solution)/shard_map/first_sum/pallas_call | solution.py:131
  66.7 4.4 %all-to-all-start = ((bf16[16,2,32,128]{3,2,1,0:T(8,128)(2,1)}), bf16[16,2,32,128]{3,2,1,0:T(8,128)(2,1)S(1)}, u32[]{:S(2)}, u32[]{:S(2)}) async-start(bf16[16,2,32,128]{3,2,1,0:T(8,128)(2,1)} %get-tuple-element.64), calls=%async_computation | async-start | bytes 524288 | tf_op jit(solution)/shard_map/all_to_all | solution.py:319
  71.1 5.8 %old_sum.6 = (f32[2,32,128]{2,1,0:T(8,128)S(1)}, s32[65]{0:T(128)S(1)}, bf16[16,128,128]{2,1,0:T(8,128)(2,1)S(1)}) custom-call(s32[7,64]{1,0:T(8,128)S(1)} %get-tuple-element.122.code_ref, s32[7,64]{1,0:T(8,128)S(1)} %get-tuple-element.96.fresh_ref, bf16[2048,32,128]{2,1,0:T(8,128)(2,1)} %get-tuple-element.61.store_ref, ...), custom_call_target="tpu_custom_call" | custom-call | flops 67108864 | bytes 6291456 | tf_op jit(solution)/shard_map/old_sum/pallas_call | solution.py:131
  80.6 3.2 %collective-permute-start.24 = (f32[2,32,128]{2,1,0:T(8,128)S(1)}, f32[2,32,128]{2,1,0:T(8,128)S(1)}, u32[]{:S(2)}, u32[]{:S(2)}) collective-permute-start(f32[2,32,128]{2,1,0:T(8,128)S(1)} %fresh_sum.6.p0), channel_id=1, source_target_pairs={{0,3},{1,2},{2,1},{3,0},{4,7},{5,6},{6,5},{7,4},{8,11},{9,10},{10,... | collective-permute-start | bytes 98312 | tf_op jit(solution)/shard_map/ppermute | solution.py:312
  86.1 4.8 %all-to-all-start.1 = ((bf16[16,2,32,128]{3,2,1,0:T(8,128)(2,1)}), bf16[16,2,32,128]{3,2,1,0:T(8,128)(2,1)S(1)}, u32[]{:S(2)}, u32[]{:S(2)}) async-start(bf16[16,2,32,128]{3,2,1,0:T(8,128)(2,1)} %get-tuple-element.71), calls=%async_computation.1 | async-start | bytes 524288 | tf_op jit(solution)/shard_map/all_to_all | solution.py:319
  90.9 5.5 %old_sum.7 = (f32[2,32,128]{2,1,0:T(8,128)S(1)}, s32[65]{0:T(128)S(1)}, bf16[16,128,128]{2,1,0:T(8,128)(2,1)S(1)}) custom-call(s32[7,64]{1,0:T(8,128)S(1)} %get-tuple-element.122.code_ref, s32[7,64]{1,0:T(8,128)S(1)} %get-tuple-element.96.fresh_ref, bf16[2048,32,128]{2,1,0:T(8,128)(2,1)} %get-tuple-element.61.store_ref, bf16[32,32,128]{2,1,0:T(8,128)(2,1)S(1)} %bitcast.22, ...), custom_call_target="tpu_custom_call" | custom-call | flops 67108864 | bytes 6291456 | tf_op jit(solution)/shard_map/old_sum/pallas_call | solution.py:131
  100.1 3.1 %collective-permute-start.26 = (f32[2,32,128]{2,1,0:T(8,128)S(1)}, f32[2,32,128]{2,1,0:T(8,128)S(1)}, u32[]{:S(2)}, u32[]{:S(2)}) collective-permute-start(f32[2,32,128]{2,1,0:T(8,128)S(1)} %fresh_sum.7.p0), channel_id=1, source_target_pairs={{0,2},{1,3},{2,0},{3,1},{4,6},{5,7},{6,4},{7,5},{8,10},{9,11},{10,... | collective-permute-start | bytes 98312 | tf_op jit(solution)/shard_map/ppermute | solution.py:312
  108.2 5.0 %all-to-all-start.2 = ((bf16[16,2,32,128]{3,2,1,0:T(8,128)(2,1)}), bf16[16,2,32,128]{3,2,1,0:T(8,128)(2,1)S(1)}, u32[]{:S(2)}, u32[]{:S(2)}) async-start(bf16[16,2,32,128]{3,2,1,0:T(8,128)(2,1)} %get-tuple-element.78), calls=%async_computation.2 | async-start | bytes 524288 | tf_op jit(solution)/shard_map/all_to_all | solution.py:319
  113.2 5.4 %old_sum.8 = (f32[2,32,128]{2,1,0:T(8,128)S(1)}, s32[65]{0:T(128)S(1)}, bf16[16,128,128]{2,1,0:T(8,128)(2,1)S(1)}) custom-call(s32[7,64]{1,0:T(8,128)S(1)} %get-tuple-element.122.code_ref, s32[7,64]{1,0:T(8,128)S(1)} %get-tuple-element.96.fresh_ref, bf16[2048,32,128]{2,1,0:T(8,128)(2,1)} %get-tuple-element.61.store_ref, bf16[32,32,128]{2,1,0:T(8,128)(2,1)S(1)} %bitcast.23, ...), custom_call_target="tpu_custom_call" | custom-call | flops 67108864 | bytes 6291456 | tf_op jit(solution)/shard_map/old_sum/pallas_call | solution.py:131
  122.9 2.8 %collective-permute-start.30 = (f32[2,32,128]{2,1,0:T(8,128)S(1)}, f32[2,32,128]{2,1,0:T(8,128)S(1)}, u32[]{:S(2)}, u32[]{:S(2)}) collective-permute-start(f32[2,32,128]{2,1,0:T(8,128)S(1)} %fresh_sum.8.p0), channel_id=1, source_target_pairs={{0,3},{1,2},{2,1},{3,0},{4,7},{5,6},{6,5},{7,4},{8,11},{9,10},{10,... | collective-permute-start | bytes 98312 | tf_op jit(solution)/shard_map/ppermute | solution.py:312
  128.3 5.2 %all-to-all-start.3 = ((bf16[16,2,32,128]{3,2,1,0:T(8,128)(2,1)}), bf16[16,2,32,128]{3,2,1,0:T(8,128)(2,1)S(1)}, u32[]{:S(2)}, u32[]{:S(2)}) async-start(bf16[16,2,32,128]{3,2,1,0:T(8,128)(2,1)} %get-tuple-element.85), calls=%async_computation.3 | async-start | bytes 524288 | tf_op jit(solution)/shard_map/all_to_all | solution.py:319
  133.6 5.4 %old_sum.9 = (f32[2,32,128]{2,1,0:T(8,128)S(1)}, s32[65]{0:T(128)S(1)}, bf16[16,128,128]{2,1,0:T(8,128)(2,1)S(1)}) custom-call(s32[7,64]{1,0:T(8,128)S(1)} %get-tuple-element.122.code_ref, s32[7,64]{1,0:T(8,128)S(1)} %get-tuple-element.96.fresh_ref, bf16[2048,32,128]{2,1,0:T(8,128)(2,1)} %get-tuple-element.61.store_ref, bf16[32,32,128]{2,1,0:T(8,128)(2,1)S(1)} %bitcast.24, ...), custom_call_target="tpu_custom_call" | custom-call | flops 67108864 | bytes 6291456 | tf_op jit(solution)/shard_map/old_sum/pallas_call | solution.py:131
  142.2 3.1 %collective-permute-start.32 = (f32[2,32,128]{2,1,0:T(8,128)S(1)}, f32[2,32,128]{2,1,0:T(8,128)S(1)}, u32[]{:S(2)}, u32[]{:S(2)}) collective-permute-start(f32[2,32,128]{2,1,0:T(8,128)S(1)} %fresh_sum.9.p0), channel_id=1, source_target_pairs={{0,2},{1,3},{2,0},{3,1},{4,6},{5,7},{6,4},{7,5},{8,10},{9,11},{10,... | collective-permute-start | bytes 98312 | tf_op jit(solution)/shard_map/ppermute | solution.py:312
  150.6 4.4 %all-to-all-start.4 = ((bf16[16,2,32,128]{3,2,1,0:T(8,128)(2,1)}), bf16[16,2,32,128]{3,2,1,0:T(8,128)(2,1)S(1)}, u32[]{:S(2)}, u32[]{:S(2)}) async-start(bf16[16,2,32,128]{3,2,1,0:T(8,128)(2,1)} %get-tuple-element.92), calls=%async_computation.4 | async-start | bytes 524288 | tf_op jit(solution)/shard_map/all_to_all | solution.py:319
  155.0 5.5 %old_sum.10 = (f32[2,32,128]{2,1,0:T(8,128)S(1)}, s32[65]{0:T(128)S(1)}, bf16[16,128,128]{2,1,0:T(8,128)(2,1)S(1)}) custom-call(s32[7,64]{1,0:T(8,128)S(1)} %get-tuple-element.122.code_ref, s32[7,64]{1,0:T(8,128)S(1)} %get-tuple-element.96.fresh_ref, bf16[2048,32,128]{2,1,0:T(8,128)(2,1)} %get-tuple-element.61.store_ref, bf16[32,32,128]{2,1,0:T(8,128)(2,1)S(1)} %bitcast.25, ...), custom_call_target="tpu_custom_call" | custom-call | flops 67108864 | bytes 6291456 | tf_op jit(solution)/shard_map/old_sum/pallas_call | solution.py:131
  171.0 4.6 %all-to-all-start.5 = ((bf16[16,2,32,128]{3,2,1,0:T(8,128)(2,1)}), bf16[16,2,32,128]{3,2,1,0:T(8,128)(2,1)S(1)}, u32[]{:S(2)}, u32[]{:S(2)}) async-start(bf16[16,2,32,128]{3,2,1,0:T(8,128)(2,1)} %get-tuple-element.99), calls=%async_computation.5 | async-start | bytes 524288 | tf_op jit(solution)/shard_map/all_to_all | solution.py:319
  175.7 5.5 %old_sum.11 = (f32[2,32,128]{2,1,0:T(8,128)S(1)}, s32[65]{0:T(128)S(1)}, bf16[16,128,128]{2,1,0:T(8,128)(2,1)S(1)}) custom-call(s32[7,64]{1,0:T(8,128)S(1)} %get-tuple-element.122.code_ref, s32[7,64]{1,0:T(8,128)S(1)} %get-tuple-element.96.fresh_ref, bf16[2048,32,128]{2,1,0:T(8,128)(2,1)} %get-tuple-element.61.store_ref, bf16[32,32,128]{2,1,0:T(8,128)(2,1)S(1)} %bitcast.26, ...), custom_call_target="tpu_custom_call" | custom-call | flops 67108864 | bytes 6291456 | tf_op jit(solution)/shard_map/old_sum/pallas_call | solution.py:131
  183.9 2.8 %collective-permute-start.38 = (f32[2,32,128]{2,1,0:T(8,128)S(1)}, f32[2,32,128]{2,1,0:T(8,128)S(1)}, u32[]{:S(2)}, u32[]{:S(2)}) collective-permute-start(f32[2,32,128]{2,1,0:T(8,128)S(1)} %fresh_sum.11.p0), channel_id=1, source_target_pairs={{0,2},{1,3},{2,0},{3,1},{4,6},{5,7},{6,4},{7,5},{8,10},{9,11},{10,... | collective-permute-start | bytes 98312 | tf_op jit(solution)/shard_map/ppermute | solution.py:312
  190.8 17.3 %collective-permute-start.40 = (bf16[7,32,128]{2,1,0:T(8,128)(2,1)S(1)}, bf16[7,32,128]{2,1,0:T(8,128)(2,1)S(1)}, u32[]{:S(2)}, u32[]{:S(2)}) collective-permute-start(bf16[7,32,128]{2,1,0:T(8,128)(2,1)S(1)} %get-tuple-element.108), channel_id=1, source_target_pairs={{0,4},{4,0},{1,5},{5,1},{2,6},{6,2},{3,7},{7,3},{8,12},{12,8},{9,1... | collective-permute-start | bytes 172040 | tf_op jit(solution)/shard_map/ppermute | solution.py:23
  (131 shorter events, 89.3 us)
Async XLA Ops:
  4.4 46.4 %collective-permute-start.16 = (bf16[7,1,32,128,128]{4,3,2,1,0:T(8,128)(2,1)}, bf16[7,1,32,128,128]{4,3,2,1,0:T(8,128)(2,1)}, u32[]{:S(2)}, u32[]{:S(2)}) collective-permute-start(bf16[7,1,32,128,128]{4,3,2,1,0:T(8,128)(2,1)} %own_ref.11), channel_id=1, source_target_pairs={{0,4},{4,0},{1,5},{5,1},{2,6},{6,2},{3,7},{7,3},{8,12},{12,8},{9,1... | collective-permute-start | bytes 22020104 | tf_op jit(solution)/shard_map/ppermute | solution.py:23
  4.8 5.8 %collective-permute-start.9 = (bf16[17,32,128]{2,1,0:T(8,128)(2,1)S(1)}, bf16[17,32,128]{2,1,0:T(8,128)(2,1)S(1)}, u32[]{:S(2)}, u32[]{:S(2)}) collective-permute-start(bf16[17,32,128]{2,1,0:T(8,128)(2,1)S(1)} %collective-permute-done.1), channel_id=1, source_target_pairs={{0,8},{8,0},{16,24},{24,16},{1,9},{9,1},{17,25},{25,17},{2,10},{10... | collective-permute-start | bytes 417800 | tf_op jit(solution)/shard_map/ppermute | solution.py:27
  6.2 9.3 %collective-permute-start.10 = (bf16[17,32,128]{2,1,0:T(8,128)(2,1)S(1)}, bf16[17,32,128]{2,1,0:T(8,128)(2,1)S(1)}, u32[]{:S(2)}, u32[]{:S(2)}) collective-permute-start(bf16[17,32,128]{2,1,0:T(8,128)(2,1)S(1)} %collective-permute-done.1), channel_id=1, source_target_pairs={{0,16},{8,24},{16,0},{24,8},{1,17},{9,25},{17,1},{25,9},{2,18},{10... | collective-permute-start | bytes 417800 | tf_op jit(solution)/shard_map/ppermute | solution.py:27
  8.9 10.4 %collective-permute-start.11 = (bf16[17,32,128]{2,1,0:T(8,128)(2,1)S(1)}, bf16[17,32,128]{2,1,0:T(8,128)(2,1)S(1)}, u32[]{:S(2)}, u32[]{:S(2)}) collective-permute-start(bf16[17,32,128]{2,1,0:T(8,128)(2,1)S(1)} %collective-permute-done.1), channel_id=1, source_target_pairs={{0,24},{8,16},{16,8},{24,0},{1,25},{9,17},{17,9},{25,1},{2,26},{10... | collective-permute-start | bytes 417800 | tf_op jit(solution)/shard_map/ppermute | solution.py:27
  8.9 10.9 %collective-permute-start.2 = (bf16[17,32,128]{2,1,0:T(8,128)(2,1)S(1)}, bf16[17,32,128]{2,1,0:T(8,128)(2,1)S(1)}, u32[]{:S(2)}, u32[]{:S(2)}) collective-permute-start(bf16[17,32,128]{2,1,0:T(8,128)(2,1)S(1)} %get-tuple-element.54), channel_id=1, source_target_pairs={{0,32},{32,0},{64,96},{96,64},{1,33},{33,1},{65,97},{97,65},{2,34}... | collective-permute-start | bytes 417800 | tf_op jit(solution)/shard_map/ppermute | solution.py:27
  10.6 11.5 %collective-permute-start.3 = (bf16[17,32,128]{2,1,0:T(8,128)(2,1)S(1)}, bf16[17,32,128]{2,1,0:T(8,128)(2,1)S(1)}, u32[]{:S(2)}, u32[]{:S(2)}) collective-permute-start(bf16[17,32,128]{2,1,0:T(8,128)(2,1)S(1)} %get-tuple-element.54), channel_id=1, source_target_pairs={{0,64},{32,96},{64,0},{96,32},{1,65},{33,97},{65,1},{97,33},{2,66}... | collective-permute-start | bytes 417800 | tf_op jit(solution)/shard_map/ppermute | solution.py:27
  15.5 8.0 %collective-permute-start.4 = (bf16[17,32,128]{2,1,0:T(8,128)(2,1)S(1)}, bf16[17,32,128]{2,1,0:T(8,128)(2,1)S(1)}, u32[]{:S(2)}, u32[]{:S(2)}) collective-permute-start(bf16[17,32,128]{2,1,0:T(8,128)(2,1)S(1)} %get-tuple-element.54), channel_id=1, source_target_pairs={{0,96},{32,64},{64,32},{96,0},{1,97},{33,65},{65,33},{97,1},{2,98}... | collective-permute-start | bytes 417800 | tf_op jit(solution)/shard_map/ppermute | solution.py:27
  19.3 15.7 %collective-permute-start.12 = (bf16[68,32,128]{2,1,0:T(8,128)(2,1)S(1)}, bf16[68,32,128]{2,1,0:T(8,128)(2,1)S(1)}, u32[]{:S(2)}, u32[]{:S(2)}) collective-permute-start(bf16[68,32,128]{2,1,0:T(8,128)(2,1)S(1)} %constant_dynamic-update-slice_fusion.4.refs_5_), channel_id=1, source_target_pairs={{0,32},{32,64},{64,96},{96,0},{1,33},{33,65},{65,97},{97,1},{2,34}... | collective-permute-start | bytes 1671176 | tf_op jit(solution)/shard_map/ppermute | solution.py:31
  19.8 16.7 %collective-permute-start.13 = (bf16[68,32,128]{2,1,0:T(8,128)(2,1)S(1)}, bf16[68,32,128]{2,1,0:T(8,128)(2,1)S(1)}, u32[]{:S(2)}, u32[]{:S(2)}) collective-permute-start(bf16[68,32,128]{2,1,0:T(8,128)(2,1)S(1)} %constant_dynamic-update-slice_fusion.4.refs_5_), channel_id=1, source_target_pairs={{0,96},{32,0},{64,32},{96,64},{1,97},{33,1},{65,33},{97,65},{2,98}... | collective-permute-start | bytes 1671176 | tf_op jit(solution)/shard_map/ppermute | solution.py:32
  23.6 17.3 %collective-permute-start.5 = (bf16[68,32,128]{2,1,0:T(8,128)(2,1)S(1)}, bf16[68,32,128]{2,1,0:T(8,128)(2,1)S(1)}, u32[]{:S(2)}, u32[]{:S(2)}) collective-permute-start(bf16[68,32,128]{2,1,0:T(8,128)(2,1)S(1)} %constant_dynamic-update-slice_fusion.refs_0_), channel_id=1, source_target_pairs={{0,8},{8,16},{16,24},{24,0},{1,9},{9,17},{17,25},{25,1},{2,10},{10... | collective-permute-start | bytes 1671176 | tf_op jit(solution)/shard_map/ppermute | solution.py:31
  23.8 17.8 %collective-permute-start.6 = (bf16[68,32,128]{2,1,0:T(8,128)(2,1)S(1)}, bf16[68,32,128]{2,1,0:T(8,128)(2,1)S(1)}, u32[]{:S(2)}, u32[]{:S(2)}) collective-permute-start(bf16[68,32,128]{2,1,0:T(8,128)(2,1)S(1)} %constant_dynamic-update-slice_fusion.refs_0_), channel_id=1, source_target_pairs={{0,24},{8,0},{16,8},{24,16},{1,25},{9,1},{17,9},{25,17},{2,26},{10... | collective-permute-start | bytes 1671176 | tf_op jit(solution)/shard_map/ppermute | solution.py:32
  36.5 9.6 %collective-permute-start.14 = (bf16[34,32,128]{2,1,0:T(8,128)(2,1)S(1)}, bf16[34,32,128]{2,1,0:T(8,128)(2,1)S(1)}, u32[]{:S(2)}, u32[]{:S(2)}) collective-permute-start(bf16[34,32,128]{2,1,0:T(8,128)(2,1)S(1)} %slice.82), channel_id=1, source_target_pairs={{0,32},{32,64},{64,96},{96,0},{1,33},{33,65},{65,97},{97,1},{2,34}... | collective-permute-start | bytes 835592 | tf_op jit(solution)/shard_map/ppermute | solution.py:34
  37.3 9.5 %collective-permute-start.15 = (bf16[34,32,128]{2,1,0:T(8,128)(2,1)}, bf16[34,32,128]{2,1,0:T(8,128)(2,1)}, u32[]{:S(2)}, u32[]{:S(2)}) collective-permute-start(bf16[34,32,128]{2,1,0:T(8,128)(2,1)} %slice.83), channel_id=1, source_target_pairs={{0,96},{32,0},{64,32},{96,64},{1,97},{33,1},{65,33},{97,65},{2,98}... | collective-permute-start | bytes 835592 | tf_op jit(solution)/shard_map/ppermute | solution.py:35
  41.6 9.2 %collective-permute-start.7 = (bf16[34,32,128]{2,1,0:T(8,128)(2,1)}, bf16[34,32,128]{2,1,0:T(8,128)(2,1)}, u32[]{:S(2)}, u32[]{:S(2)}) collective-permute-start(bf16[34,32,128]{2,1,0:T(8,128)(2,1)} %slice.80), channel_id=1, source_target_pairs={{0,8},{8,16},{16,24},{24,0},{1,9},{9,17},{17,25},{25,1},{2,10},{10... | collective-permute-start | bytes 835592 | tf_op jit(solution)/shard_map/ppermute | solution.py:34
  42.4 8.4 %collective-permute-start.8 = (bf16[34,32,128]{2,1,0:T(8,128)(2,1)}, bf16[34,32,128]{2,1,0:T(8,128)(2,1)}, u32[]{:S(2)}, u32[]{:S(2)}) collective-permute-start(bf16[34,32,128]{2,1,0:T(8,128)(2,1)} %slice.81), channel_id=1, source_target_pairs={{0,24},{8,0},{16,8},{24,16},{1,25},{9,1},{17,9},{25,17},{2,26},{10... | collective-permute-start | bytes 835592 | tf_op jit(solution)/shard_map/ppermute | solution.py:35
  46.1 15.5 %collective-permute-start.21 = (bf16[8,1,128,128]{3,2,1,0:T(8,128)(2,1)}, bf16[8,1,128,128]{3,2,1,0:T(8,128)(2,1)S(1)}, u32[]{:S(2)}, u32[]{:S(2)}) collective-permute-start(bf16[8,1,128,128]{3,2,1,0:T(8,128)(2,1)} %own_d_ref.13), channel_id=1, source_target_pairs={{0,4},{4,0},{1,5},{5,1},{2,6},{6,2},{3,7},{7,3},{8,12},{12,8},{9,1... | collective-permute-start | bytes 786440 | tf_op jit(solution)/shard_map/ppermute | solution.py:23
  46.8 14.7 %collective-permute-start.20 = (bf16[8,1,32,128]{3,2,1,0:T(8,128)(2,1)S(1)}, bf16[8,1,32,128]{3,2,1,0:T(8,128)(2,1)S(1)}, u32[]{:S(2)}, u32[]{:S(2)}) collective-permute-start(bf16[8,1,32,128]{3,2,1,0:T(8,128)(2,1)S(1)} %get-tuple-element.104), channel_id=1, source_target_pairs={{0,4},{4,0},{1,5},{5,1},{2,6},{6,2},{3,7},{7,3},{8,12},{12,8},{9,1... | collective-permute-start | bytes 196616 | tf_op jit(solution)/shard_map/ppermute | solution.py:23
  66.7 12.0 %all-to-all-start = ((bf16[16,2,32,128]{3,2,1,0:T(8,128)(2,1)}), bf16[16,2,32,128]{3,2,1,0:T(8,128)(2,1)S(1)}, u32[]{:S(2)}, u32[]{:S(2)}) async-start(bf16[16,2,32,128]{3,2,1,0:T(8,128)(2,1)} %get-tuple-element.64), calls=%async_computation | async-start | bytes 524288 | tf_op jit(solution)/shard_map/all_to_all | solution.py:319
  86.1 12.3 %all-to-all-start.1 = ((bf16[16,2,32,128]{3,2,1,0:T(8,128)(2,1)}), bf16[16,2,32,128]{3,2,1,0:T(8,128)(2,1)S(1)}, u32[]{:S(2)}, u32[]{:S(2)}) async-start(bf16[16,2,32,128]{3,2,1,0:T(8,128)(2,1)} %get-tuple-element.71), calls=%async_computation.1 | async-start | bytes 524288 | tf_op jit(solution)/shard_map/all_to_all | solution.py:319
  108.2 12.6 %all-to-all-start.2 = ((bf16[16,2,32,128]{3,2,1,0:T(8,128)(2,1)}), bf16[16,2,32,128]{3,2,1,0:T(8,128)(2,1)S(1)}, u32[]{:S(2)}, u32[]{:S(2)}) async-start(bf16[16,2,32,128]{3,2,1,0:T(8,128)(2,1)} %get-tuple-element.78), calls=%async_computation.2 | async-start | bytes 524288 | tf_op jit(solution)/shard_map/all_to_all | solution.py:319
  128.3 12.8 %all-to-all-start.3 = ((bf16[16,2,32,128]{3,2,1,0:T(8,128)(2,1)}), bf16[16,2,32,128]{3,2,1,0:T(8,128)(2,1)S(1)}, u32[]{:S(2)}, u32[]{:S(2)}) async-start(bf16[16,2,32,128]{3,2,1,0:T(8,128)(2,1)} %get-tuple-element.85), calls=%async_computation.3 | async-start | bytes 524288 | tf_op jit(solution)/shard_map/all_to_all | solution.py:319
  150.6 11.9 %all-to-all-start.4 = ((bf16[16,2,32,128]{3,2,1,0:T(8,128)(2,1)}), bf16[16,2,32,128]{3,2,1,0:T(8,128)(2,1)S(1)}, u32[]{:S(2)}, u32[]{:S(2)}) async-start(bf16[16,2,32,128]{3,2,1,0:T(8,128)(2,1)} %get-tuple-element.92), calls=%async_computation.4 | async-start | bytes 524288 | tf_op jit(solution)/shard_map/all_to_all | solution.py:319
  171.0 12.2 %all-to-all-start.5 = ((bf16[16,2,32,128]{3,2,1,0:T(8,128)(2,1)}), bf16[16,2,32,128]{3,2,1,0:T(8,128)(2,1)S(1)}, u32[]{:S(2)}, u32[]{:S(2)}) async-start(bf16[16,2,32,128]{3,2,1,0:T(8,128)(2,1)} %get-tuple-element.99), calls=%async_computation.5 | async-start | bytes 524288 | tf_op jit(solution)/shard_map/all_to_all | solution.py:319
  190.8 18.2 %collective-permute-start.40 = (bf16[7,32,128]{2,1,0:T(8,128)(2,1)S(1)}, bf16[7,32,128]{2,1,0:T(8,128)(2,1)S(1)}, u32[]{:S(2)}, u32[]{:S(2)}) collective-permute-start(bf16[7,32,128]{2,1,0:T(8,128)(2,1)S(1)} %get-tuple-element.108), channel_id=1, source_target_pairs={{0,4},{4,0},{1,5},{5,1},{2,6},{6,2},{3,7},{7,3},{8,12},{12,8},{9,1... | collective-permute-start | bytes 172040 | tf_op jit(solution)/shard_map/ppermute | solution.py:23
  (28 other events, 147.3 us)

commit v4 on v3

--- a/solution.py
+++ b/solution.py
@@ -23,17 +23,25 @@
     return lax.ppermute(v, "core", xor_pairs(2, 1))
 
 
-def direct_gather(v, axis):
-    return jnp.concatenate([v] + [lax.ppermute(v, axis, xor_pairs(4, k)) for k in (1, 2, 3)])
-
-
-def ring_gather(v, axis):
-    before = lax.ppermute(v, axis, shift_pairs(4, 1))
-    after = lax.ppermute(v, axis, shift_pairs(4, 3))
+def pairs(stage, move):
+    result = []
+    for z in range(4):
+        for y in range(4):
+            for core in range(2):
+                to_z, to_y = (move(z), y) if core + 1 == stage else (z, move(y))
+                result.append(((z * 4 + y) * 2 + core, (to_z * 4 + to_y) * 2 + core))
+    return result
+
+
+def direct_gather(v):
+    return jnp.stack([v] + [lax.ppermute(v, ROWS, pairs(1, lambda i, k=k: i ^ k)) for k in (1, 2, 3)])
+
+
+def ring_gather(v):
+    up, down = pairs(2, lambda i: (i + 1) % 4), pairs(2, lambda i: (i + 3) % 4)
+    before, after = lax.ppermute(v, ROWS, up), lax.ppermute(v, ROWS, down)
     half = v.shape[0] // 2
-    far_a = lax.ppermute(before[:half], axis, shift_pairs(4, 1))
-    far_b = lax.ppermute(after[half:], axis, shift_pairs(4, 3))
-    return [v, before, after, far_a, far_b]
+    return [v, before, after, lax.ppermute(before[:half], ROWS, up), lax.ppermute(after[half:], ROWS, down)]
 
 
 def nt_dot(x, a):
@@ -77,8 +85,11 @@
     own_ref, other_ref, out_ref, store_ref, blocks, block_sems, pack_sems, packed, store_sem = refs
     packs, start = [], 0
     for i, source in enumerate(sources):
-        packs.append(pltpu.make_async_copy(source, packed.at[pl.ds(start, source.shape[0])], pack_sems.at[i]))
-        start += source.shape[0]
+        which = 0 if i < len(sources) // 2 else 1
+        for part in range(source.shape[0]):
+            target = packed.at[pl.ds(start, source.shape[2])]
+            packs.append(pltpu.make_async_copy(source.at[part, which], target, pack_sems.at[len(packs)]))
+            start += source.shape[2]
     keep = pltpu.make_async_copy(packed, store_ref.at[pl.ds(0, start)], store_sem)
 
     def between():
@@ -127,7 +138,7 @@
 
 
 def sum_call(kernel, codes, sources, source_spaces, own, other, outs, out_spaces, extra, name):
-    slots, (rhs_cols, block) = codes[0].shape[1], sources[0].shape[1:]
+    slots, (rhs_cols, block) = codes[0].shape[1], sources[0].shape[-2:]
     return pl.pallas_call(
         kernel,
         out_shape=[jax.ShapeDtypeStruct((2, rhs_cols, block), jnp.float32)] + outs,
@@ -147,11 +158,12 @@
 
 
 def first_sum(code, sources, own, other):
-    one = sources[0].shape[1:]
-    known = sum(v.shape[0] for v in sources)
+    one = sources[0].shape[3:]
+    parts = sum(v.shape[0] for v in sources)
+    known = parts * sources[0].shape[2]
     store = jax.ShapeDtypeStruct((2048,) + one, jnp.bfloat16)
     extra = [
-        pltpu.SemaphoreType.DMA((len(sources),)),
+        pltpu.SemaphoreType.DMA((parts,)),
         pltpu.VMEM((known,) + one, jnp.bfloat16),
         pltpu.SemaphoreType.DMA,
     ]
@@ -272,17 +284,16 @@
 
     first = jnp.einsum("rb,ab->ra", rhs[0, 0], diag_inv[0, 0], preferred_element_type=jnp.float32).astype(jnp.bfloat16)
     known = jnp.concatenate([boundary, first[None]])
-    known_own = my_half(known, 1)
-    known_own, known_other = lax.optimization_barrier((known_own, swap_cores(their_half(known, 1))))
+    known = jnp.stack([my_half(known, 1), their_half(known, 1)])
     code_own = (coupling + 1024 * present)[:, 0]
     code_both = jnp.stack([code_own, swap_cores(code_own)], axis=1)
     rhs_both = jnp.concatenate([my_half(rhs, 2), swap_cores(their_half(rhs, 2))], axis=1)
     diag_other = swap_cores(diag_inv)
-    off_sent, known_own = lax.optimization_barrier((off_blocks, known_own))
+    off_sent, known = lax.optimization_barrier((off_blocks, known))
     off_other = swap_cores(off_sent)
 
-    color_a = ring_gather(direct_gather(known_own, "z"), "y")
-    color_b = ring_gather(direct_gather(known_other, "y"), "z")
+    pieces = ring_gather(direct_gather(known))
+    pieces = pieces + [swap_cores(piece) for piece in pieces]
 
     keep, index = code_both >= 1024, code_both % 1024
     in_outer = index < outer
@@ -290,13 +301,10 @@
     member = jnp.where(in_outer, index % outer_each, outer_each)
     src_z, src_y, src_core = row // 8, (row // 2) % 4, row % 2
     each = outer_each + 1
-    mine_too = src_core == core
-    away = jnp.where(mine_too, src_y - y, src_z - z) % 4
-    place = jnp.where(mine_too, src_z ^ z, src_y ^ y) * each + member
-    far_half = (away == 2) & (place >= 2 * each)
-    piece = jnp.where(away == 3, 1, jnp.where(away == 1, 2, jnp.where(away == 2, 3, 0))) + far_half
-    place = jnp.where(far_half, place - 2 * each, place)
-    known_place = jnp.where(mine_too, 0, 16 * each) + piece * (4 * each) - jnp.where(piece == 4, 2 * each, 0) + place
+    away = jnp.where(src_core == 0, src_y - y, src_z - z) % 4
+    part = jnp.where(away == 3, 1, jnp.where(away == 1, 2, jnp.where(away == 2, 3, 0))) * 4
+    part = part + jnp.where(src_core == 0, src_z ^ z, src_y ^ y) + jnp.where(src_core == core, 0, 16)
+    known_place = part * each + member
     level_of = jnp.maximum(index - outer, 0) // 32
     this = jnp.arange(levels - 1)[:, None, None]
     is_fresh = (level_of == this) & (level_of > 0)
@@ -306,7 +314,7 @@
     fresh_code = jnp.where(keep & is_fresh, place_level, -1).reshape(levels - 1, -1)
 
     own_rows, other_rows = [], []
-    value, store = first_sum(old_code, color_a + color_b, off_blocks, off_other)
+    value, store = first_sum(old_code, pieces, off_blocks, off_other)
     solved_levels = []
     for level in range(1, levels):
         partials = [value] + [lax.ppermute(value, "x", xor_pairs(4, k)) for k in (1, 2, 3)]

time: 211 us -> 210 us (level)
  waiting for transfers between devices: 49.3 us -> 57.2 us
  starting transfers between devices: 101 us -> 95.7 us
  local copies, waits for them, and re-layouts: 5.5 us -> 2.32 us
    ppermute x14 -> x7, starting transfers between devices: 23.8 us -> 10.4 us  [the longest x3 4 us: direct_gather(): lax.ppermute(v, ROWS, pairs(1, lambda i, k=k: i ^ k))]
    ppermute x6 -> x10, starting transfers between devices: 21.6 us -> 28 us  [swap_cores(): return lax.ppermute(v, 'core', xor_pairs(2, 1))]
    ppermute x14 -> x7, waiting for transfers between devices: 15.5 us -> 21.8 us  [the longest x2 11.1 us: ring_gather(): before, after = (lax.ppermute(v, ROWS, up), lax.ppermute(v, ROWS, down))]
  transfers between devices with their start and end apart: 47 -> 44, of which waited for: 27 -> 29; matrix products, arithmetic and copies ran while one was open for 2% -> 1% of each run, Pallas kernels for 18% -> 19%
where the time goes in v4:
time: 210 us; the launch traced here: 209 us
  starting transfers between devices  95.7 us (46%)
  waiting for transfers between devices  57.2 us (27%)
  Pallas kernels  50.6 us (24%)
  local copies, waits for them, and re-layouts  2.32 us (1%)
    pallas_call x7, Pallas kernels, sum_call(): pl.pallas_call(kernel, out_shape=[jax.ShapeDtypeStruct((2, rhs_cols, bloc...  39.5 us
    all_to_all x6, starting transfers between devices, on_device(): solved = lax.all_to_all(sent, ('z', 'y'), 0, 0).reshape(32, half, block)  29 us
    ppermute x21, starting transfers between devices, on_device(): lax.ppermute(value, 'x', xor_pairs(4, k))  28.3 us
    ppermute x10, starting transfers between devices, swap_cores(): return lax.ppermute(v, 'core', xor_pairs(2, 1))  28 us
    ppermute x21, waiting for transfers between devices, on_device(): lax.ppermute(value, 'x', xor_pairs(4, k))  20.1 us
    all_to_all x6, waiting for transfers between devices, on_device(): solved = lax.all_to_all(sent, ('z', 'y'), 0, 0).reshape(32, half, block)  12 us
    ppermute x2, waiting for transfers between devices, ring_gather(): before, after = (lax.ppermute(v, ROWS, up), lax.ppermute(v, ROWS, down))  11.1 us
    ppermute x3, waiting for transfers between devices, direct_gather(): lax.ppermute(v, ROWS, pairs(1, lambda i, k=k: i ^ k))  9.88 us
  transfers between devices with their start and end apart: 44, of which 29 were waited for; matrix products, arithmetic and copies ran while one was open for 1% of the time, Pallas kernels for 19%

profile of v4, /device:TPU:1, one launch (start us, length us, event | category | flops | bytes accessed | tf_op | source)
XLA Modules:
  0.0 209.1 jit_solution(6937125455005336554)
XLA Ops:
  4.8 2.6 %collective-permute-start.2 = (bf16[2,17,32,128]{3,2,1,0:T(8,128)(2,1)S(1)}, bf16[2,17,32,128]{3,2,1,0:T(8,128)(2,1)S(1)}, u32[]{:S(2)}, u32[]{:S(2)}) collective-permute-start(bf16[2,17,32,128]{3,2,1,0:T(8,128)(2,1)S(1)} %pad_maximum_fusion.1), channel_id=1, source_target_pairs={{0,64},{4,20},{8,72},{12,28},{16,80},{20,4},{24,88},{28,12},{32,96... | collective-permute-start | bytes 835592 | tf_op jit(solution)/shard_map/ppermute | solution.py:37
  9.2 5.6 %collective-permute-done.2 = bf16[2,17,32,128]{3,2,1,0:T(8,128)(2,1)S(1)} collective-permute-done((bf16[2,17,32,128]{3,2,1,0:T(8,128)(2,1)S(1)}, bf16[2,17,32,128]{3,2,1,0:T(8,128)(2,1)S(1)}, u32[]{:S(2)}, u32[]{:S(2)}) %collective-permute-start.2) | collective-permute-done | bytes 278560 | tf_op jit(solution)/shard_map/ppermute | solution.py:37
  14.7 2.6 %collective-permute-done.3 = bf16[2,17,32,128]{3,2,1,0:T(8,128)(2,1)S(1)} collective-permute-done((bf16[2,17,32,128]{3,2,1,0:T(8,128)(2,1)S(1)}, bf16[2,17,32,128]{3,2,1,0:T(8,128)(2,1)S(1)}, u32[]{:S(2)}, u32[]{:S(2)}) %collective-permute-start.3) | collective-permute-done | bytes 278560 | tf_op jit(solution)/shard_map/ppermute | solution.py:37
  23.1 11.1 %collective-permute-done.4.refs_1_ = bf16[4,2,17,32,128]{4,3,2,1,0:T(8,128)(2,1)S(1)} collective-permute-done((bf16[4,2,17,32,128]{4,3,2,1,0:T(8,128)(2,1)S(1)}, bf16[4,2,17,32,128]{4,3,2,1,0:T(8,128)(2,1)S(1)}, u32[]{:S(2)}, u32[]{:S(2)}) %collective-permute-start.4) | collective-permute-done | bytes 1114144 | tf_op jit(solution)/shard_map/ppermute | solution.py:42
  35.5 2.7 %collective-permute-start.7 = (bf16[2,2,17,32,128]{4,3,2,1,0:T(8,128)(2,1)S(1)}, bf16[2,2,17,32,128]{4,3,2,1,0:T(8,128)(2,1)}, u32[]{:S(2)}, u32[]{:S(2)}) collective-permute-start(bf16[2,2,17,32,128]{4,3,2,1,0:T(8,128)(2,1)S(1)} %slice.73), channel_id=1, source_target_pairs={{0,24},{4,100},{8,0},{12,108},{16,8},{20,116},{24,16},{28,124},{32... | collective-permute-start | bytes 1671176 | tf_op jit(solution)/shard_map/ppermute | solution.py:44
  38.2 3.0 %collective-permute-start = (s32[7,32]{1,0:T(8,128)S(1)}, s32[7,32]{1,0:T(8,128)S(1)}, u32[]{:S(2)}, u32[]{:S(2)}) collective-permute-start(s32[7,32]{1,0:T(8,128)S(1)} %bitcast.54), channel_id=1, source_target_pairs={{0,4},{4,0},{1,5},{5,1},{2,6},{6,2},{3,7},{7,3},{8,12},{12,8},{9,1... | collective-permute-start | bytes 2696 | tf_op jit(solution)/shard_map/ppermute | solution.py:23
  44.4 3.2 %collective-permute-start.11 = (bf16[2,2,17,32,128]{4,3,2,1,0:T(8,128)(2,1)}, bf16[2,2,17,32,128]{4,3,2,1,0:T(8,128)(2,1)}, u32[]{:S(2)}, u32[]{:S(2)}) collective-permute-start(bf16[2,2,17,32,128]{4,3,2,1,0:T(8,128)(2,1)} %collective-permute-done.6.refs_3_), channel_id=1, source_target_pairs={{0,4},{4,0},{1,5},{5,1},{2,6},{6,2},{3,7},{7,3},{8,12},{12,8},{9,1... | collective-permute-start | bytes 1671176 | tf_op jit(solution)/shard_map/ppermute | solution.py:23
  50.7 6.3 %first_sum.1 = (f32[2,32,128]{2,1,0:T(8,128)S(1)}, bf16[2048,32,128]{2,1,0:T(8,128)(2,1)}) custom-call(s32[7,64]{1,0:T(8,128)S(1)} %get-tuple-element.118.code_ref, bf16[4,2,17,32,128]{4,3,2,1,0:T(8,128)(2,1)S(1)} %pad_maximum_fusion.refs_0_, bf16[4,2,17,32,128]{4,3,2,1,0:T(8,128)(2,1)S(1)} %collective-permute-done.4.refs_1_, ...), custom_call_target="tpu_custom_call" | custom-call | flops 67108864 | bytes 6291456 | tf_op jit(solution)/shard_map/first_sum/pallas_call | solution.py:142
  65.8 4.7 %all-to-all-start = ((bf16[16,2,32,128]{3,2,1,0:T(8,128)(2,1)}), bf16[16,2,32,128]{3,2,1,0:T(8,128)(2,1)S(1)}, u32[]{:S(2)}, u32[]{:S(2)}) async-start(bf16[16,2,32,128]{3,2,1,0:T(8,128)(2,1)} %get-tuple-element.60), calls=%async_computation | async-start | bytes 524288 | tf_op jit(solution)/shard_map/all_to_all | solution.py:327
  70.5 5.4 %old_sum.6 = (f32[2,32,128]{2,1,0:T(8,128)S(1)}, s32[65]{0:T(128)S(1)}, bf16[16,128,128]{2,1,0:T(8,128)(2,1)S(1)}) custom-call(s32[7,64]{1,0:T(8,128)S(1)} %get-tuple-element.118.code_ref, s32[7,64]{1,0:T(8,128)S(1)} %get-tuple-element.92.fresh_ref, bf16[2048,32,128]{2,1,0:T(8,128)(2,1)} %get-tuple-element.57.store_ref, ...), custom_call_target="tpu_custom_call" | custom-call | flops 67108864 | bytes 6291456 | tf_op jit(solution)/shard_map/old_sum/pallas_call | solution.py:142
  85.8 5.1 %all-to-all-start.1 = ((bf16[16,2,32,128]{3,2,1,0:T(8,128)(2,1)}), bf16[16,2,32,128]{3,2,1,0:T(8,128)(2,1)S(1)}, u32[]{:S(2)}, u32[]{:S(2)}) async-start(bf16[16,2,32,128]{3,2,1,0:T(8,128)(2,1)} %get-tuple-element.67), calls=%async_computation.1 | async-start | bytes 524288 | tf_op jit(solution)/shard_map/all_to_all | solution.py:327
  90.9 5.6 %old_sum.7 = (f32[2,32,128]{2,1,0:T(8,128)S(1)}, s32[65]{0:T(128)S(1)}, bf16[16,128,128]{2,1,0:T(8,128)(2,1)S(1)}) custom-call(s32[7,64]{1,0:T(8,128)S(1)} %get-tuple-element.118.code_ref, s32[7,64]{1,0:T(8,128)S(1)} %get-tuple-element.92.fresh_ref, bf16[2048,32,128]{2,1,0:T(8,128)(2,1)} %get-tuple-element.57.store_ref, bf16[32,32,128]{2,1,0:T(8,128)(2,1)S(1)} %bitcast.30, ...), custom_call_target="tpu_custom_call" | custom-call | flops 67108864 | bytes 6291456 | tf_op jit(solution)/shard_map/old_sum/pallas_call | solution.py:142
  99.4 2.7 %collective-permute-start.23 = (f32[2,32,128]{2,1,0:T(8,128)S(1)}, f32[2,32,128]{2,1,0:T(8,128)S(1)}, u32[]{:S(2)}, u32[]{:S(2)}) collective-permute-start(f32[2,32,128]{2,1,0:T(8,128)S(1)} %fresh_sum.7.p0), channel_id=1, source_target_pairs={{0,2},{1,3},{2,0},{3,1},{4,6},{5,7},{6,4},{7,5},{8,10},{9,11},{10,... | collective-permute-start | bytes 98312 | tf_op jit(solution)/shard_map/ppermute | solution.py:320
  107.1 4.9 %all-to-all-start.2 = ((bf16[16,2,32,128]{3,2,1,0:T(8,128)(2,1)}), bf16[16,2,32,128]{3,2,1,0:T(8,128)(2,1)S(1)}, u32[]{:S(2)}, u32[]{:S(2)}) async-start(bf16[16,2,32,128]{3,2,1,0:T(8,128)(2,1)} %get-tuple-element.74), calls=%async_computation.2 | async-start | bytes 524288 | tf_op jit(solution)/shard_map/all_to_all | solution.py:327
  112.0 5.6 %old_sum.8 = (f32[2,32,128]{2,1,0:T(8,128)S(1)}, s32[65]{0:T(128)S(1)}, bf16[16,128,128]{2,1,0:T(8,128)(2,1)S(1)}) custom-call(s32[7,64]{1,0:T(8,128)S(1)} %get-tuple-element.118.code_ref, s32[7,64]{1,0:T(8,128)S(1)} %get-tuple-element.92.fresh_ref, bf16[2048,32,128]{2,1,0:T(8,128)(2,1)} %get-tuple-element.57.store_ref, bf16[32,32,128]{2,1,0:T(8,128)(2,1)S(1)} %bitcast.31, ...), custom_call_target="tpu_custom_call" | custom-call | flops 67108864 | bytes 6291456 | tf_op jit(solution)/shard_map/old_sum/pallas_call | solution.py:142
  127.7 4.5 %all-to-all-start.3 = ((bf16[16,2,32,128]{3,2,1,0:T(8,128)(2,1)}), bf16[16,2,32,128]{3,2,1,0:T(8,128)(2,1)S(1)}, u32[]{:S(2)}, u32[]{:S(2)}) async-start(bf16[16,2,32,128]{3,2,1,0:T(8,128)(2,1)} %get-tuple-element.81), calls=%async_computation.3 | async-start | bytes 524288 | tf_op jit(solution)/shard_map/all_to_all | solution.py:327
  132.2 5.9 %old_sum.9 = (f32[2,32,128]{2,1,0:T(8,128)S(1)}, s32[65]{0:T(128)S(1)}, bf16[16,128,128]{2,1,0:T(8,128)(2,1)S(1)}) custom-call(s32[7,64]{1,0:T(8,128)S(1)} %get-tuple-element.118.code_ref, s32[7,64]{1,0:T(8,128)S(1)} %get-tuple-element.92.fresh_ref, bf16[2048,32,128]{2,1,0:T(8,128)(2,1)} %get-tuple-element.57.store_ref, bf16[32,32,128]{2,1,0:T(8,128)(2,1)S(1)} %bitcast.32, ...), custom_call_target="tpu_custom_call" | custom-call | flops 67108864 | bytes 6291456 | tf_op jit(solution)/shard_map/old_sum/pallas_call | solution.py:142
  141.0 2.7 %collective-permute-start.29 = (f32[2,32,128]{2,1,0:T(8,128)S(1)}, f32[2,32,128]{2,1,0:T(8,128)S(1)}, u32[]{:S(2)}, u32[]{:S(2)}) collective-permute-start(f32[2,32,128]{2,1,0:T(8,128)S(1)} %fresh_sum.9.p0), channel_id=1, source_target_pairs={{0,2},{1,3},{2,0},{3,1},{4,6},{5,7},{6,4},{7,5},{8,10},{9,11},{10,... | collective-permute-start | bytes 98312 | tf_op jit(solution)/shard_map/ppermute | solution.py:320
  149.0 5.3 %all-to-all-start.4 = ((bf16[16,2,32,128]{3,2,1,0:T(8,128)(2,1)}), bf16[16,2,32,128]{3,2,1,0:T(8,128)(2,1)S(1)}, u32[]{:S(2)}, u32[]{:S(2)}) async-start(bf16[16,2,32,128]{3,2,1,0:T(8,128)(2,1)} %get-tuple-element.88), calls=%async_computation.4 | async-start | bytes 524288 | tf_op jit(solution)/shard_map/all_to_all | solution.py:327
  154.4 5.4 %old_sum.10 = (f32[2,32,128]{2,1,0:T(8,128)S(1)}, s32[65]{0:T(128)S(1)}, bf16[16,128,128]{2,1,0:T(8,128)(2,1)S(1)}) custom-call(s32[7,64]{1,0:T(8,128)S(1)} %get-tuple-element.118.code_ref, s32[7,64]{1,0:T(8,128)S(1)} %get-tuple-element.92.fresh_ref, bf16[2048,32,128]{2,1,0:T(8,128)(2,1)} %get-tuple-element.57.store_ref, bf16[32,32,128]{2,1,0:T(8,128)(2,1)S(1)} %bitcast.33, ...), custom_call_target="tpu_custom_call" | custom-call | flops 67108864 | bytes 6291456 | tf_op jit(solution)/shard_map/old_sum/pallas_call | solution.py:142
  169.5 4.5 %all-to-all-start.5 = ((bf16[16,2,32,128]{3,2,1,0:T(8,128)(2,1)}), bf16[16,2,32,128]{3,2,1,0:T(8,128)(2,1)S(1)}, u32[]{:S(2)}, u32[]{:S(2)}) async-start(bf16[16,2,32,128]{3,2,1,0:T(8,128)(2,1)} %get-tuple-element.95), calls=%async_computation.5 | async-start | bytes 524288 | tf_op jit(solution)/shard_map/all_to_all | solution.py:327
  174.1 5.4 %old_sum.11 = (f32[2,32,128]{2,1,0:T(8,128)S(1)}, s32[65]{0:T(128)S(1)}, bf16[16,128,128]{2,1,0:T(8,128)(2,1)S(1)}) custom-call(s32[7,64]{1,0:T(8,128)S(1)} %get-tuple-element.118.code_ref, s32[7,64]{1,0:T(8,128)S(1)} %get-tuple-element.92.fresh_ref, bf16[2048,32,128]{2,1,0:T(8,128)(2,1)} %get-tuple-element.57.store_ref, bf16[32,32,128]{2,1,0:T(8,128)(2,1)S(1)} %bitcast.34, ...), custom_call_target="tpu_custom_call" | custom-call | flops 67108864 | bytes 6291456 | tf_op jit(solution)/shard_map/old_sum/pallas_call | solution.py:142
  183.7 3.3 %collective-permute-start.35 = (f32[2,32,128]{2,1,0:T(8,128)S(1)}, f32[2,32,128]{2,1,0:T(8,128)S(1)}, u32[]{:S(2)}, u32[]{:S(2)}) collective-permute-start(f32[2,32,128]{2,1,0:T(8,128)S(1)} %fresh_sum.11.p0), channel_id=1, source_target_pairs={{0,2},{1,3},{2,0},{3,1},{4,6},{5,7},{6,4},{7,5},{8,10},{9,11},{10,... | collective-permute-start | bytes 98312 | tf_op jit(solution)/shard_map/ppermute | solution.py:320
  191.1 16.5 %collective-permute-start.37 = (bf16[7,32,128]{2,1,0:T(8,128)(2,1)S(1)}, bf16[7,32,128]{2,1,0:T(8,128)(2,1)S(1)}, u32[]{:S(2)}, u32[]{:S(2)}) collective-permute-start(bf16[7,32,128]{2,1,0:T(8,128)(2,1)S(1)} %get-tuple-element.104), channel_id=1, source_target_pairs={{0,4},{4,0},{1,5},{5,1},{2,6},{6,2},{3,7},{7,3},{8,12},{12,8},{9,1... | collective-permute-start | bytes 172040 | tf_op jit(solution)/shard_map/ppermute | solution.py:23
  (117 shorter events, 84.2 us)
Async XLA Ops:
  2.0 48.8 %collective-permute-start.13 = (bf16[7,1,32,128,128]{4,3,2,1,0:T(8,128)(2,1)}, bf16[7,1,32,128,128]{4,3,2,1,0:T(8,128)(2,1)}, u32[]{:S(2)}, u32[]{:S(2)}) collective-permute-start(bf16[7,1,32,128,128]{4,3,2,1,0:T(8,128)(2,1)} %own_ref.11), channel_id=1, source_target_pairs={{0,4},{4,0},{1,5},{5,1},{2,6},{6,2},{3,7},{7,3},{8,12},{12,8},{9,1... | collective-permute-start | bytes 22020104 | tf_op jit(solution)/shard_map/ppermute | solution.py:23
  3.5 5.7 %collective-permute-start.1 = (bf16[2,17,32,128]{3,2,1,0:T(8,128)(2,1)S(1)}, bf16[2,17,32,128]{3,2,1,0:T(8,128)(2,1)S(1)}, u32[]{:S(2)}, u32[]{:S(2)}) collective-permute-start(bf16[2,17,32,128]{3,2,1,0:T(8,128)(2,1)S(1)} %pad_maximum_fusion.1), channel_id=1, source_target_pairs={{0,32},{4,12},{8,40},{12,4},{16,48},{20,28},{24,56},{28,20},{32,0}... | collective-permute-start | bytes 835592 | tf_op jit(solution)/shard_map/ppermute | solution.py:37
  4.8 9.9 %collective-permute-start.2 = (bf16[2,17,32,128]{3,2,1,0:T(8,128)(2,1)S(1)}, bf16[2,17,32,128]{3,2,1,0:T(8,128)(2,1)S(1)}, u32[]{:S(2)}, u32[]{:S(2)}) collective-permute-start(bf16[2,17,32,128]{3,2,1,0:T(8,128)(2,1)S(1)} %pad_maximum_fusion.1), channel_id=1, source_target_pairs={{0,64},{4,20},{8,72},{12,28},{16,80},{20,4},{24,88},{28,12},{32,96... | collective-permute-start | bytes 835592 | tf_op jit(solution)/shard_map/ppermute | solution.py:37
  7.5 9.9 %collective-permute-start.3 = (bf16[2,17,32,128]{3,2,1,0:T(8,128)(2,1)S(1)}, bf16[2,17,32,128]{3,2,1,0:T(8,128)(2,1)S(1)}, u32[]{:S(2)}, u32[]{:S(2)}) collective-permute-start(bf16[2,17,32,128]{3,2,1,0:T(8,128)(2,1)S(1)} %pad_maximum_fusion.1), channel_id=1, source_target_pairs={{0,96},{4,28},{8,104},{12,20},{16,112},{20,12},{24,120},{28,4},{32... | collective-permute-start | bytes 835592 | tf_op jit(solution)/shard_map/ppermute | solution.py:37
  17.5 16.7 %collective-permute-start.4 = (bf16[4,2,17,32,128]{4,3,2,1,0:T(8,128)(2,1)S(1)}, bf16[4,2,17,32,128]{4,3,2,1,0:T(8,128)(2,1)S(1)}, u32[]{:S(2)}, u32[]{:S(2)}) collective-permute-start(bf16[4,2,17,32,128]{4,3,2,1,0:T(8,128)(2,1)S(1)} %pad_maximum_fusion.refs_0_), channel_id=1, source_target_pairs={{0,8},{4,36},{8,16},{12,44},{16,24},{20,52},{24,0},{28,60},{32,40}... | collective-permute-start | bytes 3342344 | tf_op jit(solution)/shard_map/ppermute | solution.py:42
  19.0 15.4 %collective-permute-start.5 = (bf16[4,2,17,32,128]{4,3,2,1,0:T(8,128)(2,1)S(1)}, bf16[4,2,17,32,128]{4,3,2,1,0:T(8,128)(2,1)}, u32[]{:S(2)}, u32[]{:S(2)}) collective-permute-start(bf16[4,2,17,32,128]{4,3,2,1,0:T(8,128)(2,1)S(1)} %pad_maximum_fusion.refs_0_), channel_id=1, source_target_pairs={{0,24},{4,100},{8,0},{12,108},{16,8},{20,116},{24,16},{28,124},{32... | collective-permute-start | bytes 3342344 | tf_op jit(solution)/shard_map/ppermute | solution.py:42
  21.2 21.2 %collective-permute-start.8 = (bf16[4,2,17,32,128]{4,3,2,1,0:T(8,128)(2,1)S(1)}, bf16[4,2,17,32,128]{4,3,2,1,0:T(8,128)(2,1)S(1)}, u32[]{:S(2)}, u32[]{:S(2)}) collective-permute-start(bf16[4,2,17,32,128]{4,3,2,1,0:T(8,128)(2,1)S(1)} %pad_maximum_fusion.refs_0_), channel_id=1, source_target_pairs={{0,4},{4,0},{1,5},{5,1},{2,6},{6,2},{3,7},{7,3},{8,12},{12,8},{9,1... | collective-permute-start | bytes 3342344 | tf_op jit(solution)/shard_map/ppermute | solution.py:23
  34.3 10.1 %collective-permute-start.6 = (bf16[2,2,17,32,128]{4,3,2,1,0:T(8,128)(2,1)S(1)}, bf16[2,2,17,32,128]{4,3,2,1,0:T(8,128)(2,1)}, u32[]{:S(2)}, u32[]{:S(2)}) collective-permute-start(bf16[2,2,17,32,128]{4,3,2,1,0:T(8,128)(2,1)S(1)} %slice.72), channel_id=1, source_target_pairs={{0,8},{4,36},{8,16},{12,44},{16,24},{20,52},{24,0},{28,60},{32,40}... | collective-permute-start | bytes 1671176 | tf_op jit(solution)/shard_map/ppermute | solution.py:44
  35.5 12.1 %collective-permute-start.7 = (bf16[2,2,17,32,128]{4,3,2,1,0:T(8,128)(2,1)S(1)}, bf16[2,2,17,32,128]{4,3,2,1,0:T(8,128)(2,1)}, u32[]{:S(2)}, u32[]{:S(2)}) collective-permute-start(bf16[2,2,17,32,128]{4,3,2,1,0:T(8,128)(2,1)S(1)} %slice.73), channel_id=1, source_target_pairs={{0,24},{4,100},{8,0},{12,108},{16,8},{20,116},{24,16},{28,124},{32... | collective-permute-start | bytes 1671176 | tf_op jit(solution)/shard_map/ppermute | solution.py:44
  42.1 8.7 %collective-permute-start.10 = (bf16[4,2,17,32,128]{4,3,2,1,0:T(8,128)(2,1)}, bf16[4,2,17,32,128]{4,3,2,1,0:T(8,128)(2,1)}, u32[]{:S(2)}, u32[]{:S(2)}) collective-permute-start(bf16[4,2,17,32,128]{4,3,2,1,0:T(8,128)(2,1)} %collective-permute-done.5.refs_2_), channel_id=1, source_target_pairs={{0,4},{4,0},{1,5},{5,1},{2,6},{6,2},{3,7},{7,3},{8,12},{12,8},{9,1... | collective-permute-start | bytes 3342344 | tf_op jit(solution)/shard_map/ppermute | solution.py:23
  43.4 7.3 %collective-permute-start.9 = (bf16[4,2,17,32,128]{4,3,2,1,0:T(8,128)(2,1)S(1)}, bf16[4,2,17,32,128]{4,3,2,1,0:T(8,128)(2,1)}, u32[]{:S(2)}, u32[]{:S(2)}) collective-permute-start(bf16[4,2,17,32,128]{4,3,2,1,0:T(8,128)(2,1)S(1)} %collective-permute-done.4.refs_1_), channel_id=1, source_target_pairs={{0,4},{4,0},{1,5},{5,1},{2,6},{6,2},{3,7},{7,3},{8,12},{12,8},{9,1... | collective-permute-start | bytes 3342344 | tf_op jit(solution)/shard_map/ppermute | solution.py:23
  44.4 5.1 %collective-permute-start.11 = (bf16[2,2,17,32,128]{4,3,2,1,0:T(8,128)(2,1)}, bf16[2,2,17,32,128]{4,3,2,1,0:T(8,128)(2,1)}, u32[]{:S(2)}, u32[]{:S(2)}) collective-permute-start(bf16[2,2,17,32,128]{4,3,2,1,0:T(8,128)(2,1)} %collective-permute-done.6.refs_3_), channel_id=1, source_target_pairs={{0,4},{4,0},{1,5},{5,1},{2,6},{6,2},{3,7},{7,3},{8,12},{12,8},{9,1... | collective-permute-start | bytes 1671176 | tf_op jit(solution)/shard_map/ppermute | solution.py:23
  49.5 11.5 %collective-permute-start.18 = (bf16[8,1,128,128]{3,2,1,0:T(8,128)(2,1)S(1)}, bf16[8,1,128,128]{3,2,1,0:T(8,128)(2,1)S(1)}, u32[]{:S(2)}, u32[]{:S(2)}) collective-permute-start(bf16[8,1,128,128]{3,2,1,0:T(8,128)(2,1)S(1)} %copy-done), channel_id=1, source_target_pairs={{0,4},{4,0},{1,5},{5,1},{2,6},{6,2},{3,7},{7,3},{8,12},{12,8},{9,1... | collective-permute-start | bytes 786440 | tf_op jit(solution)/shard_map/ppermute | solution.py:23
  50.3 10.7 %collective-permute-start.17 = (bf16[8,1,32,128]{3,2,1,0:T(8,128)(2,1)S(1)}, bf16[8,1,32,128]{3,2,1,0:T(8,128)(2,1)S(1)}, u32[]{:S(2)}, u32[]{:S(2)}) collective-permute-start(bf16[8,1,32,128]{3,2,1,0:T(8,128)(2,1)S(1)} %get-tuple-element.100), channel_id=1, source_target_pairs={{0,4},{4,0},{1,5},{5,1},{2,6},{6,2},{3,7},{7,3},{8,12},{12,8},{9,1... | collective-permute-start | bytes 196616 | tf_op jit(solution)/shard_map/ppermute | solution.py:23
  65.8 12.3 %all-to-all-start = ((bf16[16,2,32,128]{3,2,1,0:T(8,128)(2,1)}), bf16[16,2,32,128]{3,2,1,0:T(8,128)(2,1)S(1)}, u32[]{:S(2)}, u32[]{:S(2)}) async-start(bf16[16,2,32,128]{3,2,1,0:T(8,128)(2,1)} %get-tuple-element.60), calls=%async_computation | async-start | bytes 524288 | tf_op jit(solution)/shard_map/all_to_all | solution.py:327
  85.8 12.6 %all-to-all-start.1 = ((bf16[16,2,32,128]{3,2,1,0:T(8,128)(2,1)}), bf16[16,2,32,128]{3,2,1,0:T(8,128)(2,1)S(1)}, u32[]{:S(2)}, u32[]{:S(2)}) async-start(bf16[16,2,32,128]{3,2,1,0:T(8,128)(2,1)} %get-tuple-element.67), calls=%async_computation.1 | async-start | bytes 524288 | tf_op jit(solution)/shard_map/all_to_all | solution.py:327
  107.1 12.5 %all-to-all-start.2 = ((bf16[16,2,32,128]{3,2,1,0:T(8,128)(2,1)}), bf16[16,2,32,128]{3,2,1,0:T(8,128)(2,1)S(1)}, u32[]{:S(2)}, u32[]{:S(2)}) async-start(bf16[16,2,32,128]{3,2,1,0:T(8,128)(2,1)} %get-tuple-element.74), calls=%async_computation.2 | async-start | bytes 524288 | tf_op jit(solution)/shard_map/all_to_all | solution.py:327
  120.4 4.6 %collective-permute-start.26 = (f32[2,32,128]{2,1,0:T(8,128)S(1)}, f32[2,32,128]{2,1,0:T(8,128)S(1)}, u32[]{:S(2)}, u32[]{:S(2)}) collective-permute-start(f32[2,32,128]{2,1,0:T(8,128)S(1)} %fresh_sum.8.p0), channel_id=1, source_target_pairs={{0,2},{1,3},{2,0},{3,1},{4,6},{5,7},{6,4},{7,5},{8,10},{9,11},{10,... | collective-permute-start | bytes 98312 | tf_op jit(solution)/shard_map/ppermute | solution.py:320
  127.7 12.1 %all-to-all-start.3 = ((bf16[16,2,32,128]{3,2,1,0:T(8,128)(2,1)}), bf16[16,2,32,128]{3,2,1,0:T(8,128)(2,1)S(1)}, u32[]{:S(2)}, u32[]{:S(2)}) async-start(bf16[16,2,32,128]{3,2,1,0:T(8,128)(2,1)} %get-tuple-element.81), calls=%async_computation.3 | async-start | bytes 524288 | tf_op jit(solution)/shard_map/all_to_all | solution.py:327
  149.0 12.9 %all-to-all-start.4 = ((bf16[16,2,32,128]{3,2,1,0:T(8,128)(2,1)}), bf16[16,2,32,128]{3,2,1,0:T(8,128)(2,1)S(1)}, u32[]{:S(2)}, u32[]{:S(2)}) async-start(bf16[16,2,32,128]{3,2,1,0:T(8,128)(2,1)} %get-tuple-element.88), calls=%async_computation.4 | async-start | bytes 524288 | tf_op jit(solution)/shard_map/all_to_all | solution.py:327
  169.5 12.0 %all-to-all-start.5 = ((bf16[16,2,32,128]{3,2,1,0:T(8,128)(2,1)}), bf16[16,2,32,128]{3,2,1,0:T(8,128)(2,1)S(1)}, u32[]{:S(2)}, u32[]{:S(2)}) async-start(bf16[16,2,32,128]{3,2,1,0:T(8,128)(2,1)} %get-tuple-element.95), calls=%async_computation.5 | async-start | bytes 524288 | tf_op jit(solution)/shard_map/all_to_all | solution.py:327
  182.3 4.7 %collective-permute-start.34 = (f32[2,32,128]{2,1,0:T(8,128)S(1)}, f32[2,32,128]{2,1,0:T(8,128)S(1)}, u32[]{:S(2)}, u32[]{:S(2)}) collective-permute-start(f32[2,32,128]{2,1,0:T(8,128)S(1)} %fresh_sum.11.p0), channel_id=1, source_target_pairs={{0,1},{1,0},{2,3},{3,2},{4,5},{5,4},{6,7},{7,6},{8,9},{9,8},{10,11... | collective-permute-start | bytes 98312 | tf_op jit(solution)/shard_map/ppermute | solution.py:320
  183.7 4.9 %collective-permute-start.35 = (f32[2,32,128]{2,1,0:T(8,128)S(1)}, f32[2,32,128]{2,1,0:T(8,128)S(1)}, u32[]{:S(2)}, u32[]{:S(2)}) collective-permute-start(f32[2,32,128]{2,1,0:T(8,128)S(1)} %fresh_sum.11.p0), channel_id=1, source_target_pairs={{0,2},{1,3},{2,0},{3,1},{4,6},{5,7},{6,4},{7,5},{8,10},{9,11},{10,... | collective-permute-start | bytes 98312 | tf_op jit(solution)/shard_map/ppermute | solution.py:320
  191.1 17.3 %collective-permute-start.37 = (bf16[7,32,128]{2,1,0:T(8,128)(2,1)S(1)}, bf16[7,32,128]{2,1,0:T(8,128)(2,1)S(1)}, u32[]{:S(2)}, u32[]{:S(2)}) collective-permute-start(bf16[7,32,128]{2,1,0:T(8,128)(2,1)S(1)} %get-tuple-element.104), channel_id=1, source_target_pairs={{0,4},{4,0},{1,5},{5,1},{2,6},{6,2},{3,7},{7,3},{8,12},{12,8},{9,1... | collective-permute-start | bytes 172040 | tf_op jit(solution)/shard_map/ppermute | solution.py:23
  (25 other events, 185.6 us)

commit v5 on v4

--- a/solution.py
+++ b/solution.py
@@ -33,15 +33,14 @@
     return result
 
 
-def direct_gather(v):
-    return jnp.stack([v] + [lax.ppermute(v, ROWS, pairs(1, lambda i, k=k: i ^ k)) for k in (1, 2, 3)])
-
-
-def ring_gather(v):
+def gather_parts(v):
+    near = [lax.ppermute(v, ROWS, pairs(1, lambda i, k=k: i ^ k)) for k in (1, 2, 3)]
+    low, high = jnp.stack([v, near[0]]), jnp.stack(near[1:])
     up, down = pairs(2, lambda i: (i + 1) % 4), pairs(2, lambda i: (i + 3) % 4)
-    before, after = lax.ppermute(v, ROWS, up), lax.ppermute(v, ROWS, down)
-    half = v.shape[0] // 2
-    return [v, before, after, lax.ppermute(before[:half], ROWS, up), lax.ppermute(after[half:], ROWS, down)]
+    before_low, after_high = lax.ppermute(low, ROWS, up), lax.ppermute(high, ROWS, down)
+    before_high, after_low = lax.ppermute(high, ROWS, up), lax.ppermute(low, ROWS, down)
+    far = [lax.ppermute(before_low, ROWS, up), lax.ppermute(after_high, ROWS, down)]
+    return [low, high, before_low, before_high, after_low, after_high] + far
 
 
 def nt_dot(x, a):
@@ -77,7 +76,7 @@
                 group.append(blocks[k])
             part = nt_dot(jnp.concatenate(xs, axis=1), jnp.concatenate(group, axis=1))
             total = part if total is None else total + part
-        out_ref[r] = total
+        out_ref[r] = total.astype(out_ref.dtype)
 
 
 def first_kernel(code_ref, *refs):
@@ -137,11 +136,11 @@
     list_ref[0] = lax.fori_loop(0, fresh_ref.shape[1], note, jnp.int32(0))
 
 
-def sum_call(kernel, codes, sources, source_spaces, own, other, outs, out_spaces, extra, name):
+def sum_call(kernel, codes, sources, source_spaces, own, other, outs, out_spaces, extra, name, kind):
     slots, (rhs_cols, block) = codes[0].shape[1], sources[0].shape[-2:]
     return pl.pallas_call(
         kernel,
-        out_shape=[jax.ShapeDtypeStruct((2, rhs_cols, block), jnp.float32)] + outs,
+        out_shape=[jax.ShapeDtypeStruct((2, rhs_cols, block), kind)] + outs,
         in_specs=[pl.BlockSpec(memory_space=pltpu.SMEM)] * len(codes)
         + [pl.BlockSpec(memory_space=space) for space in source_spaces]
         + [pl.BlockSpec(memory_space=pltpu.HBM)] * 2,
@@ -168,7 +167,7 @@
         pltpu.SemaphoreType.DMA,
     ]
     spaces = [pl.ANY] * len(sources)
-    return sum_call(first_kernel, [code], sources, spaces, own, other, [store], [pltpu.HBM], extra, "first_sum")
+    return sum_call(first_kernel, [code], sources, spaces, own, other, [store], [pltpu.HBM], extra, "first_sum", jnp.bfloat16)
 
 
 def old_sum(level, known, code, fresh, store, solved, own, other):
@@ -183,17 +182,17 @@
         extra.append(pltpu.VMEM((sum(v.shape[0] for v in solved),) + one, jnp.bfloat16))
     spaces = [pl.ANY] + [pltpu.VMEM] * len(solved)
     out_spaces = [pltpu.SMEM, pltpu.VMEM]
-    return sum_call(kernel, [code, fresh], [store] + solved, spaces, own, other, outs, out_spaces, extra, "old_sum")
-
-
-def fresh_kernel(level, list_ref, old_ref, x_ref, near_ref, own_ref, other_ref, out_ref, far, sem):
+    return sum_call(kernel, [code, fresh], [store] + solved, spaces, own, other, outs, out_spaces, extra, "old_sum", jnp.float32)
+
+
+def fresh_kernel(level, list_ref, old_ref, x_ref, near_ref, own_ref, other_ref, out_ref, total, far, sem):
     per_row = own_ref.shape[2]
-    out_ref[...] = old_ref[...]
+    total[...] = old_ref[...]
     count = list_ref[0]
 
     def add(block, entry):
         row = ((entry & 1023) >= per_row).astype(jnp.int32)
-        out_ref[row] += nt_dot(x_ref[entry >> 10], block)
+        total[row] += nt_dot(x_ref[entry >> 10], block)
 
     def add_near(n, carry):
         add(near_ref[n], list_ref[1 + n])
@@ -216,6 +215,7 @@
 
     lax.fori_loop(0, jnp.minimum(count, NEAR), add_near, 0)
     lax.fori_loop(NEAR, count, add_far, 0)
+    out_ref[...] = total[...].astype(out_ref.dtype)
 
 
 def fresh_sum(level, listed, solved, old, near, own, other):
@@ -223,10 +223,14 @@
     vmem = pl.BlockSpec(memory_space=pltpu.VMEM)
     return pl.pallas_call(
         functools.partial(fresh_kernel, level),
-        out_shape=jax.ShapeDtypeStruct(old.shape, jnp.float32),
+        out_shape=jax.ShapeDtypeStruct(old.shape, jnp.bfloat16),
         in_specs=[pl.BlockSpec(memory_space=pltpu.SMEM)] + [vmem] * 3 + [pl.BlockSpec(memory_space=pltpu.HBM)] * 2,
         out_specs=vmem,
-        scratch_shapes=[pltpu.VMEM((block, block), jnp.bfloat16), pltpu.SemaphoreType.DMA],
+        scratch_shapes=[
+            pltpu.VMEM(old.shape, jnp.float32),
+            pltpu.VMEM((block, block), jnp.bfloat16),
+            pltpu.SemaphoreType.DMA,
+        ],
         compiler_params=pltpu.CompilerParams(vmem_limit_bytes=VMEM_LIMIT),
         name="fresh_sum",
     )(listed, old, solved, near, own, other)
@@ -235,7 +239,8 @@
 def solve_kernel(level, p0, p1, p2, p3, rhs_ref, own_d_ref, other_d_ref, out_ref, *refs):
     core = lax.axis_index("core")
     for r, d_ref in enumerate((own_d_ref, other_d_ref)):
-        coupled = (p0[r] + p1[r]) + (p2[r] + p3[r])
+        q0, q1, q2, q3 = (p[r].astype(jnp.float32) for p in (p0, p1, p2, p3))
+        coupled = (q0 + q1) + (q2 + q3)
         reduced = (rhs_ref[level, r].astype(jnp.float32) - coupled).astype(jnp.bfloat16)
         solved = nt_dot(reduced, d_ref[level, 0]).astype(jnp.bfloat16)
         out_ref[r] = solved
@@ -292,7 +297,7 @@
     off_sent, known = lax.optimization_barrier((off_blocks, known))
     off_other = swap_cores(off_sent)
 
-    pieces = ring_gather(direct_gather(known))
+    pieces = gather_parts(known)
     pieces = pieces + [swap_cores(piece) for piece in pieces]
 
     keep, index = code_both >= 1024, code_both % 1024

time: 210 us -> 213 us (1.014)
  waiting for transfers between devices: 57.2 us -> 50.4 us
  local copies, waits for them, and re-layouts: 2.32 us -> 8.55 us
    unnamed x17 -> x27, local copies, waits for them, and re-layouts: 1.08 us -> 7.57 us
    ppermute x7 -> x9, waiting for transfers between devices: 21.8 us -> 17.1 us  [the longest x3 6.44 us: gather_parts(): lax.ppermute(v, ROWS, pairs(1, lambda i, k=k: i ^ k))]
    ppermute x7 -> x9, starting transfers between devices: 10.4 us -> 13.2 us  [the longest x1 3.88 us: gather_parts(): lax.ppermute(high, ROWS, down)]
    ppermute x10 -> x13, starting transfers between devices: 28 us -> 27.6 us  [swap_cores(): return lax.ppermute(v, 'core', xor_pairs(2, 1))]
  transfers between devices with their start and end apart: 44 -> 49, of which waited for: 29 -> 28; matrix products, arithmetic and copies ran while one was open for 1% -> 1% of each run, Pallas kernels for 19% -> 19%
where the time goes in v5:
time: 213 us; the launch traced here: 212 us
  starting transfers between devices  97 us (46%)
  Pallas kernels  52.3 us (25%)
  waiting for transfers between devices  50.4 us (24%)
  local copies, waits for them, and re-layouts  8.55 us (4%)
  other arithmetic  2.62 us (1%)
    pallas_call x7, Pallas kernels, sum_call(): pl.pallas_call(kernel, out_shape=[jax.ShapeDtypeStruct((2, rhs_cols, bloc...  39.9 us
    ppermute x21, starting transfers between devices, on_device(): lax.ppermute(value, 'x', xor_pairs(4, k))  28.2 us
    all_to_all x6, starting transfers between devices, on_device(): solved = lax.all_to_all(sent, ('z', 'y'), 0, 0).reshape(32, half, block)  28 us
    ppermute x13, starting transfers between devices, swap_cores(): return lax.ppermute(v, 'core', xor_pairs(2, 1))  27.6 us
    ppermute x21, waiting for transfers between devices, on_device(): lax.ppermute(value, 'x', xor_pairs(4, k))  19 us
    all_to_all x6, waiting for transfers between devices, on_device(): solved = lax.all_to_all(sent, ('z', 'y'), 0, 0).reshape(32, half, block)  12.8 us
    unnamed x27, local copies, waits for them, and re-layouts  7.57 us
    ppermute x3, waiting for transfers between devices, gather_parts(): lax.ppermute(v, ROWS, pairs(1, lambda i, k=k: i ^ k))  6.44 us
  transfers between devices with their start and end apart: 49, of which 28 were waited for; matrix products, arithmetic and copies ran while one was open for 1% of the time, Pallas kernels for 19%

profile of v5, /device:TPU:1, one launch (start us, length us, event | category | flops | bytes accessed | tf_op | source)
XLA Modules:
  0.0 212.1 jit_solution(3367607517988169064)
XLA Ops:
  3.5 3.0 %collective-permute-start.2 = (bf16[2,17,32,128]{3,2,1,0:T(8,128)(2,1)S(1)}, bf16[2,17,32,128]{3,2,1,0:T(8,128)(2,1)S(1)}, u32[]{:S(2)}, u32[]{:S(2)}) collective-permute-start(bf16[2,17,32,128]{3,2,1,0:T(8,128)(2,1)S(1)} %pad_maximum_fusion.2), channel_id=1, source_target_pairs={{0,64},{4,20},{8,72},{12,28},{16,80},{20,4},{24,88},{28,12},{32,96... | collective-permute-start | bytes 835592 | tf_op jit(solution)/shard_map/ppermute | solution.py:37
  7.2 3.5 %collective-permute-done.2 = bf16[2,17,32,128]{3,2,1,0:T(8,128)(2,1)S(1)} collective-permute-done((bf16[2,17,32,128]{3,2,1,0:T(8,128)(2,1)S(1)}, bf16[2,17,32,128]{3,2,1,0:T(8,128)(2,1)S(1)}, u32[]{:S(2)}, u32[]{:S(2)}) %collective-permute-start.2) | collective-permute-done | bytes 278560 | tf_op jit(solution)/shard_map/ppermute | solution.py:37
  10.7 3.0 %collective-permute-done.3 = bf16[2,17,32,128]{3,2,1,0:T(8,128)(2,1)S(1)} collective-permute-done((bf16[2,17,32,128]{3,2,1,0:T(8,128)(2,1)S(1)}, bf16[2,17,32,128]{3,2,1,0:T(8,128)(2,1)S(1)}, u32[]{:S(2)}, u32[]{:S(2)}) %collective-permute-start.3) | collective-permute-done | bytes 278560 | tf_op jit(solution)/shard_map/ppermute | solution.py:37
  13.7 3.9 %collective-permute-start.7 = (bf16[2,2,17,32,128]{4,3,2,1,0:T(8,128)(2,1)S(1)}, bf16[2,2,17,32,128]{4,3,2,1,0:T(8,128)(2,1)S(1)}, u32[]{:S(2)}, u32[]{:S(2)}) collective-permute-start(bf16[2,2,17,32,128]{4,3,2,1,0:T(8,128)(2,1)S(1)} %pad_maximum_fusion.1.refs_1_), channel_id=1, source_target_pairs={{0,24},{4,100},{8,0},{12,108},{16,8},{20,116},{24,16},{28,124},{32... | collective-permute-start | bytes 1671176 | tf_op jit(solution)/shard_map/ppermute | solution.py:40
  29.3 4.3 %collective-permute-done.5.refs_3_ = bf16[2,2,17,32,128]{4,3,2,1,0:T(8,128)(2,1)S(1)} collective-permute-done((bf16[2,2,17,32,128]{4,3,2,1,0:T(8,128)(2,1)S(1)}, bf16[2,2,17,32,128]{4,3,2,1,0:T(8,128)(2,1)S(1)}, u32[]{:S(2)}, u32[]{:S(2)}) %collective-permute-start.5) | collective-permute-done | bytes 557088 | tf_op jit(solution)/shard_map/ppermute | solution.py:41
  38.9 3.5 %collective-permute-done.9.refs_7_ = bf16[2,2,17,32,128]{4,3,2,1,0:T(8,128)(2,1)} collective-permute-done((bf16[2,2,17,32,128]{4,3,2,1,0:T(8,128)(2,1)S(1)}, bf16[2,2,17,32,128]{4,3,2,1,0:T(8,128)(2,1)}, u32[]{:S(2)}, u32[]{:S(2)}) %collective-permute-start.9) | collective-permute-done | bytes 557088 | tf_op jit(solution)/shard_map/ppermute | solution.py:42
  53.9 7.5 %first_sum.1 = (bf16[2,32,128]{2,1,0:T(8,128)(2,1)S(1)}, bf16[2048,32,128]{2,1,0:T(8,128)(2,1)}) custom-call(s32[7,64]{1,0:T(8,128)S(1)} %get-tuple-element.118.code_ref, bf16[2,2,17,32,128]{4,3,2,1,0:T(8,128)(2,1)S(1)} %pad_maximum_fusion.refs_0_, bf16[2,2,17,32,128]{4,3,2,1,0:T(8,128)(2,1)S(1)} %pad_maximum_fusion.1.refs_1_, ...), custom_call_target="tpu_custom_call" | custom-call | flops 67108864 | bytes 6291456 | tf_op jit(solution)/shard_map/first_sum/pallas_call | solution.py:141
  70.0 5.2 %all-to-all-start = ((bf16[16,2,32,128]{3,2,1,0:T(8,128)(2,1)}), bf16[16,2,32,128]{3,2,1,0:T(8,128)(2,1)S(1)}, u32[]{:S(2)}, u32[]{:S(2)}) async-start(bf16[16,2,32,128]{3,2,1,0:T(8,128)(2,1)} %get-tuple-element.60), calls=%async_computation | async-start | bytes 524288 | tf_op jit(solution)/shard_map/all_to_all | solution.py:332
  75.2 5.4 %old_sum.6 = (f32[2,32,128]{2,1,0:T(8,128)S(1)}, s32[65]{0:T(128)S(1)}, bf16[16,128,128]{2,1,0:T(8,128)(2,1)S(1)}) custom-call(s32[7,64]{1,0:T(8,128)S(1)} %get-tuple-element.118.code_ref, s32[7,64]{1,0:T(8,128)S(1)} %get-tuple-element.92.fresh_ref, bf16[2048,32,128]{2,1,0:T(8,128)(2,1)} %get-tuple-element.57.store_ref, ...), custom_call_target="tpu_custom_call" | custom-call | flops 67108864 | bytes 6291456 | tf_op jit(solution)/shard_map/old_sum/pallas_call | solution.py:141
  90.4 4.6 %all-to-all-start.1 = ((bf16[16,2,32,128]{3,2,1,0:T(8,128)(2,1)}), bf16[16,2,32,128]{3,2,1,0:T(8,128)(2,1)S(1)}, u32[]{:S(2)}, u32[]{:S(2)}) async-start(bf16[16,2,32,128]{3,2,1,0:T(8,128)(2,1)} %get-tuple-element.67), calls=%async_computation.1 | async-start | bytes 524288 | tf_op jit(solution)/shard_map/all_to_all | solution.py:332
  95.0 5.3 %old_sum.7 = (f32[2,32,128]{2,1,0:T(8,128)S(1)}, s32[65]{0:T(128)S(1)}, bf16[16,128,128]{2,1,0:T(8,128)(2,1)S(1)}) custom-call(s32[7,64]{1,0:T(8,128)S(1)} %get-tuple-element.118.code_ref, s32[7,64]{1,0:T(8,128)S(1)} %get-tuple-element.92.fresh_ref, bf16[2048,32,128]{2,1,0:T(8,128)(2,1)} %get-tuple-element.57.store_ref, bf16[32,32,128]{2,1,0:T(8,128)(2,1)S(1)} %bitcast.30, ...), custom_call_target="tpu_custom_call" | custom-call | flops 67108864 | bytes 6291456 | tf_op jit(solution)/shard_map/old_sum/pallas_call | solution.py:141
  103.9 3.7 %collective-permute-start.28 = (bf16[2,32,128]{2,1,0:T(8,128)(2,1)S(1)}, bf16[2,32,128]{2,1,0:T(8,128)(2,1)S(1)}, u32[]{:S(2)}, u32[]{:S(2)}) collective-permute-start(bf16[2,32,128]{2,1,0:T(8,128)(2,1)S(1)} %fresh_sum.7.p0), channel_id=1, source_target_pairs={{0,2},{1,3},{2,0},{3,1},{4,6},{5,7},{6,4},{7,5},{8,10},{9,11},{10,... | collective-permute-start | bytes 49160 | tf_op jit(solution)/shard_map/ppermute | solution.py:325
  112.5 4.5 %all-to-all-start.2 = ((bf16[16,2,32,128]{3,2,1,0:T(8,128)(2,1)}), bf16[16,2,32,128]{3,2,1,0:T(8,128)(2,1)S(1)}, u32[]{:S(2)}, u32[]{:S(2)}) async-start(bf16[16,2,32,128]{3,2,1,0:T(8,128)(2,1)} %get-tuple-element.74), calls=%async_computation.2 | async-start | bytes 524288 | tf_op jit(solution)/shard_map/all_to_all | solution.py:332
  116.9 5.3 %old_sum.8 = (f32[2,32,128]{2,1,0:T(8,128)S(1)}, s32[65]{0:T(128)S(1)}, bf16[16,128,128]{2,1,0:T(8,128)(2,1)S(1)}) custom-call(s32[7,64]{1,0:T(8,128)S(1)} %get-tuple-element.118.code_ref, s32[7,64]{1,0:T(8,128)S(1)} %get-tuple-element.92.fresh_ref, bf16[2048,32,128]{2,1,0:T(8,128)(2,1)} %get-tuple-element.57.store_ref, bf16[32,32,128]{2,1,0:T(8,128)(2,1)S(1)} %bitcast.31, ...), custom_call_target="tpu_custom_call" | custom-call | flops 67108864 | bytes 6291456 | tf_op jit(solution)/shard_map/old_sum/pallas_call | solution.py:141
  132.0 4.4 %all-to-all-start.3 = ((bf16[16,2,32,128]{3,2,1,0:T(8,128)(2,1)}), bf16[16,2,32,128]{3,2,1,0:T(8,128)(2,1)S(1)}, u32[]{:S(2)}, u32[]{:S(2)}) async-start(bf16[16,2,32,128]{3,2,1,0:T(8,128)(2,1)} %get-tuple-element.81), calls=%async_computation.3 | async-start | bytes 524288 | tf_op jit(solution)/shard_map/all_to_all | solution.py:332
  136.4 5.3 %old_sum.9 = (f32[2,32,128]{2,1,0:T(8,128)S(1)}, s32[65]{0:T(128)S(1)}, bf16[16,128,128]{2,1,0:T(8,128)(2,1)S(1)}) custom-call(s32[7,64]{1,0:T(8,128)S(1)} %get-tuple-element.118.code_ref, s32[7,64]{1,0:T(8,128)S(1)} %get-tuple-element.92.fresh_ref, bf16[2048,32,128]{2,1,0:T(8,128)(2,1)} %get-tuple-element.57.store_ref, bf16[32,32,128]{2,1,0:T(8,128)(2,1)S(1)} %bitcast.32, ...), custom_call_target="tpu_custom_call" | custom-call | flops 67108864 | bytes 6291456 | tf_op jit(solution)/shard_map/old_sum/pallas_call | solution.py:141
  145.5 3.0 %collective-permute-start.34 = (bf16[2,32,128]{2,1,0:T(8,128)(2,1)S(1)}, bf16[2,32,128]{2,1,0:T(8,128)(2,1)S(1)}, u32[]{:S(2)}, u32[]{:S(2)}) collective-permute-start(bf16[2,32,128]{2,1,0:T(8,128)(2,1)S(1)} %fresh_sum.9.p0), channel_id=1, source_target_pairs={{0,2},{1,3},{2,0},{3,1},{4,6},{5,7},{6,4},{7,5},{8,10},{9,11},{10,... | collective-permute-start | bytes 49160 | tf_op jit(solution)/shard_map/ppermute | solution.py:325
  153.6 4.9 %all-to-all-start.4 = ((bf16[16,2,32,128]{3,2,1,0:T(8,128)(2,1)}), bf16[16,2,32,128]{3,2,1,0:T(8,128)(2,1)S(1)}, u32[]{:S(2)}, u32[]{:S(2)}) async-start(bf16[16,2,32,128]{3,2,1,0:T(8,128)(2,1)} %get-tuple-element.88), calls=%async_computation.4 | async-start | bytes 524288 | tf_op jit(solution)/shard_map/all_to_all | solution.py:332
  158.5 5.6 %old_sum.10 = (f32[2,32,128]{2,1,0:T(8,128)S(1)}, s32[65]{0:T(128)S(1)}, bf16[16,128,128]{2,1,0:T(8,128)(2,1)S(1)}) custom-call(s32[7,64]{1,0:T(8,128)S(1)} %get-tuple-element.118.code_ref, s32[7,64]{1,0:T(8,128)S(1)} %get-tuple-element.92.fresh_ref, bf16[2048,32,128]{2,1,0:T(8,128)(2,1)} %get-tuple-element.57.store_ref, bf16[32,32,128]{2,1,0:T(8,128)(2,1)S(1)} %bitcast.33, ...), custom_call_target="tpu_custom_call" | custom-call | flops 67108864 | bytes 6291456 | tf_op jit(solution)/shard_map/old_sum/pallas_call | solution.py:141
  168.3 3.0 %collective-permute-start.38 = (bf16[2,32,128]{2,1,0:T(8,128)(2,1)S(1)}, bf16[2,32,128]{2,1,0:T(8,128)(2,1)S(1)}, u32[]{:S(2)}, u32[]{:S(2)}) collective-permute-start(bf16[2,32,128]{2,1,0:T(8,128)(2,1)S(1)} %fresh_sum.10.p0), channel_id=1, source_target_pairs={{0,3},{1,2},{2,1},{3,0},{4,7},{5,6},{6,5},{7,4},{8,11},{9,10},{10,... | collective-permute-start | bytes 49160 | tf_op jit(solution)/shard_map/ppermute | solution.py:325
  173.4 4.4 %all-to-all-start.5 = ((bf16[16,2,32,128]{3,2,1,0:T(8,128)(2,1)}), bf16[16,2,32,128]{3,2,1,0:T(8,128)(2,1)S(1)}, u32[]{:S(2)}, u32[]{:S(2)}) async-start(bf16[16,2,32,128]{3,2,1,0:T(8,128)(2,1)} %get-tuple-element.95), calls=%async_computation.5 | async-start | bytes 524288 | tf_op jit(solution)/shard_map/all_to_all | solution.py:332
  177.9 5.3 %old_sum.11 = (f32[2,32,128]{2,1,0:T(8,128)S(1)}, s32[65]{0:T(128)S(1)}, bf16[16,128,128]{2,1,0:T(8,128)(2,1)S(1)}) custom-call(s32[7,64]{1,0:T(8,128)S(1)} %get-tuple-element.118.code_ref, s32[7,64]{1,0:T(8,128)S(1)} %get-tuple-element.92.fresh_ref, bf16[2048,32,128]{2,1,0:T(8,128)(2,1)} %get-tuple-element.57.store_ref, bf16[32,32,128]{2,1,0:T(8,128)(2,1)S(1)} %bitcast.34, ...), custom_call_target="tpu_custom_call" | custom-call | flops 67108864 | bytes 6291456 | tf_op jit(solution)/shard_map/old_sum/pallas_call | solution.py:141
  187.4 3.1 %collective-permute-start.40 = (bf16[2,32,128]{2,1,0:T(8,128)(2,1)S(1)}, bf16[2,32,128]{2,1,0:T(8,128)(2,1)S(1)}, u32[]{:S(2)}, u32[]{:S(2)}) collective-permute-start(bf16[2,32,128]{2,1,0:T(8,128)(2,1)S(1)} %fresh_sum.11.p0), channel_id=1, source_target_pairs={{0,2},{1,3},{2,0},{3,1},{4,6},{5,7},{6,4},{7,5},{8,10},{9,11},{10,... | collective-permute-start | bytes 49160 | tf_op jit(solution)/shard_map/ppermute | solution.py:325
  194.5 16.1 %collective-permute-start.42 = (bf16[7,32,128]{2,1,0:T(8,128)(2,1)S(1)}, bf16[7,32,128]{2,1,0:T(8,128)(2,1)S(1)}, u32[]{:S(2)}, u32[]{:S(2)}) collective-permute-start(bf16[7,32,128]{2,1,0:T(8,128)(2,1)S(1)} %get-tuple-element.104), channel_id=1, source_target_pairs={{0,4},{4,0},{1,5},{5,1},{2,6},{6,2},{3,7},{7,3},{8,12},{12,8},{9,1... | collective-permute-start | bytes 172040 | tf_op jit(solution)/shard_map/ppermute | solution.py:23
  (136 shorter events, 93.9 us)
Async XLA Ops:
  2.0 47.7 %collective-permute-start.18 = (bf16[7,1,32,128,128]{4,3,2,1,0:T(8,128)(2,1)}, bf16[7,1,32,128,128]{4,3,2,1,0:T(8,128)(2,1)}, u32[]{:S(2)}, u32[]{:S(2)}) collective-permute-start(bf16[7,1,32,128,128]{4,3,2,1,0:T(8,128)(2,1)} %own_ref.11), channel_id=1, source_target_pairs={{0,4},{4,0},{1,5},{5,1},{2,6},{6,2},{3,7},{7,3},{8,12},{12,8},{9,1... | collective-permute-start | bytes 22020104 | tf_op jit(solution)/shard_map/ppermute | solution.py:23
  3.5 7.2 %collective-permute-start.2 = (bf16[2,17,32,128]{3,2,1,0:T(8,128)(2,1)S(1)}, bf16[2,17,32,128]{3,2,1,0:T(8,128)(2,1)S(1)}, u32[]{:S(2)}, u32[]{:S(2)}) collective-permute-start(bf16[2,17,32,128]{3,2,1,0:T(8,128)(2,1)S(1)} %pad_maximum_fusion.2), channel_id=1, source_target_pairs={{0,64},{4,20},{8,72},{12,28},{16,80},{20,4},{24,88},{28,12},{32,96... | collective-permute-start | bytes 835592 | tf_op jit(solution)/shard_map/ppermute | solution.py:37
  6.5 7.2 %collective-permute-start.3 = (bf16[2,17,32,128]{3,2,1,0:T(8,128)(2,1)S(1)}, bf16[2,17,32,128]{3,2,1,0:T(8,128)(2,1)S(1)}, u32[]{:S(2)}, u32[]{:S(2)}) collective-permute-start(bf16[2,17,32,128]{3,2,1,0:T(8,128)(2,1)S(1)} %pad_maximum_fusion.2), channel_id=1, source_target_pairs={{0,96},{4,28},{8,104},{12,20},{16,112},{20,12},{24,120},{28,4},{32... | collective-permute-start | bytes 835592 | tf_op jit(solution)/shard_map/ppermute | solution.py:37
  7.2 10.4 %collective-permute-start.1 = (bf16[2,17,32,128]{3,2,1,0:T(8,128)(2,1)S(1)}, bf16[2,17,32,128]{3,2,1,0:T(8,128)(2,1)S(1)}, u32[]{:S(2)}, u32[]{:S(2)}) collective-permute-start(bf16[2,17,32,128]{3,2,1,0:T(8,128)(2,1)S(1)} %pad_maximum_fusion.2), channel_id=1, source_target_pairs={{0,32},{4,12},{8,40},{12,4},{16,48},{20,28},{24,56},{28,20},{32,0}... | collective-permute-start | bytes 835592 | tf_op jit(solution)/shard_map/ppermute | solution.py:37
  13.7 10.4 %collective-permute-start.7 = (bf16[2,2,17,32,128]{4,3,2,1,0:T(8,128)(2,1)S(1)}, bf16[2,2,17,32,128]{4,3,2,1,0:T(8,128)(2,1)S(1)}, u32[]{:S(2)}, u32[]{:S(2)}) collective-permute-start(bf16[2,2,17,32,128]{4,3,2,1,0:T(8,128)(2,1)S(1)} %pad_maximum_fusion.1.refs_1_), channel_id=1, source_target_pairs={{0,24},{4,100},{8,0},{12,108},{16,8},{20,116},{24,16},{28,124},{32... | collective-permute-start | bytes 1671176 | tf_op jit(solution)/shard_map/ppermute | solution.py:40
  17.7 10.0 %collective-permute-start.4 = (bf16[2,2,17,32,128]{4,3,2,1,0:T(8,128)(2,1)S(1)}, bf16[2,2,17,32,128]{4,3,2,1,0:T(8,128)(2,1)S(1)}, u32[]{:S(2)}, u32[]{:S(2)}) collective-permute-start(bf16[2,2,17,32,128]{4,3,2,1,0:T(8,128)(2,1)S(1)} %pad_maximum_fusion.refs_0_), channel_id=1, source_target_pairs={{0,8},{4,36},{8,16},{12,44},{16,24},{20,52},{24,0},{28,60},{32,40}... | collective-permute-start | bytes 1671176 | tf_op jit(solution)/shard_map/ppermute | solution.py:40
  19.4 14.2 %collective-permute-start.5 = (bf16[2,2,17,32,128]{4,3,2,1,0:T(8,128)(2,1)S(1)}, bf16[2,2,17,32,128]{4,3,2,1,0:T(8,128)(2,1)S(1)}, u32[]{:S(2)}, u32[]{:S(2)}) collective-permute-start(bf16[2,2,17,32,128]{4,3,2,1,0:T(8,128)(2,1)S(1)} %pad_maximum_fusion.1.refs_1_), channel_id=1, source_target_pairs={{0,8},{4,36},{8,16},{12,44},{16,24},{20,52},{24,0},{28,60},{32,40}... | collective-permute-start | bytes 1671176 | tf_op jit(solution)/shard_map/ppermute | solution.py:41
  20.4 13.2 %collective-permute-start.6 = (bf16[2,2,17,32,128]{4,3,2,1,0:T(8,128)(2,1)S(1)}, bf16[2,2,17,32,128]{4,3,2,1,0:T(8,128)(2,1)}, u32[]{:S(2)}, u32[]{:S(2)}) collective-permute-start(bf16[2,2,17,32,128]{4,3,2,1,0:T(8,128)(2,1)S(1)} %pad_maximum_fusion.refs_0_), channel_id=1, source_target_pairs={{0,24},{4,100},{8,0},{12,108},{16,8},{20,116},{24,16},{28,124},{32... | collective-permute-start | bytes 1671176 | tf_op jit(solution)/shard_map/ppermute | solution.py:41
  24.1 11.0 %collective-permute-start.11 = (bf16[2,2,17,32,128]{4,3,2,1,0:T(8,128)(2,1)S(1)}, bf16[2,2,17,32,128]{4,3,2,1,0:T(8,128)(2,1)S(1)}, u32[]{:S(2)}, u32[]{:S(2)}) collective-permute-start(bf16[2,2,17,32,128]{4,3,2,1,0:T(8,128)(2,1)S(1)} %pad_maximum_fusion.1.refs_1_), channel_id=1, source_target_pairs={{0,4},{4,0},{1,5},{5,1},{2,6},{6,2},{3,7},{7,3},{8,12},{12,8},{9,1... | collective-permute-start | bytes 1671176 | tf_op jit(solution)/shard_map/ppermute | solution.py:23
  27.6 10.5 %collective-permute-start.10 = (bf16[2,2,17,32,128]{4,3,2,1,0:T(8,128)(2,1)S(1)}, bf16[2,2,17,32,128]{4,3,2,1,0:T(8,128)(2,1)S(1)}, u32[]{:S(2)}, u32[]{:S(2)}) collective-permute-start(bf16[2,2,17,32,128]{4,3,2,1,0:T(8,128)(2,1)S(1)} %pad_maximum_fusion.refs_0_), channel_id=1, source_target_pairs={{0,4},{4,0},{1,5},{5,1},{2,6},{6,2},{3,7},{7,3},{8,12},{12,8},{9,1... | collective-permute-start | bytes 1671176 | tf_op jit(solution)/shard_map/ppermute | solution.py:23
  33.6 8.8 %collective-permute-start.9 = (bf16[2,2,17,32,128]{4,3,2,1,0:T(8,128)(2,1)S(1)}, bf16[2,2,17,32,128]{4,3,2,1,0:T(8,128)(2,1)}, u32[]{:S(2)}, u32[]{:S(2)}) collective-permute-start(bf16[2,2,17,32,128]{4,3,2,1,0:T(8,128)(2,1)S(1)} %collective-permute-done.7.refs_5_), channel_id=1, source_target_pairs={{0,24},{4,100},{8,0},{12,108},{16,8},{20,116},{24,16},{28,124},{32... | collective-permute-start | bytes 1671176 | tf_op jit(solution)/shard_map/ppermute | solution.py:42
  33.6 12.1 %collective-permute-start.8 = (bf16[2,2,17,32,128]{4,3,2,1,0:T(8,128)(2,1)S(1)}, bf16[2,2,17,32,128]{4,3,2,1,0:T(8,128)(2,1)}, u32[]{:S(2)}, u32[]{:S(2)}) collective-permute-start(bf16[2,2,17,32,128]{4,3,2,1,0:T(8,128)(2,1)S(1)} %collective-permute-done.4.refs_2_), channel_id=1, source_target_pairs={{0,8},{4,36},{8,16},{12,44},{16,24},{20,52},{24,0},{28,60},{32,40}... | collective-permute-start | bytes 1671176 | tf_op jit(solution)/shard_map/ppermute | solution.py:42
  35.9 10.3 %collective-permute-start.15 = (bf16[2,2,17,32,128]{4,3,2,1,0:T(8,128)(2,1)S(1)}, bf16[2,2,17,32,128]{4,3,2,1,0:T(8,128)(2,1)S(1)}, u32[]{:S(2)}, u32[]{:S(2)}) collective-permute-start(bf16[2,2,17,32,128]{4,3,2,1,0:T(8,128)(2,1)S(1)} %collective-permute-done.7.refs_5_), channel_id=1, source_target_pairs={{0,4},{4,0},{1,5},{5,1},{2,6},{6,2},{3,7},{7,3},{8,12},{12,8},{9,1... | collective-permute-start | bytes 1671176 | tf_op jit(solution)/shard_map/ppermute | solution.py:23
  38.9 7.3 %collective-permute-start.12 = (bf16[2,2,17,32,128]{4,3,2,1,0:T(8,128)(2,1)S(1)}, bf16[2,2,17,32,128]{4,3,2,1,0:T(8,128)(2,1)S(1)}, u32[]{:S(2)}, u32[]{:S(2)}) collective-permute-start(bf16[2,2,17,32,128]{4,3,2,1,0:T(8,128)(2,1)S(1)} %collective-permute-done.4.refs_2_), channel_id=1, source_target_pairs={{0,4},{4,0},{1,5},{5,1},{2,6},{6,2},{3,7},{7,3},{8,12},{12,8},{9,1... | collective-permute-start | bytes 1671176 | tf_op jit(solution)/shard_map/ppermute | solution.py:23
  42.4 6.1 %collective-permute-start.13 = (bf16[2,2,17,32,128]{4,3,2,1,0:T(8,128)(2,1)S(1)}, bf16[2,2,17,32,128]{4,3,2,1,0:T(8,128)(2,1)}, u32[]{:S(2)}, u32[]{:S(2)}) collective-permute-start(bf16[2,2,17,32,128]{4,3,2,1,0:T(8,128)(2,1)S(1)} %collective-permute-done.5.refs_3_), channel_id=1, source_target_pairs={{0,4},{4,0},{1,5},{5,1},{2,6},{6,2},{3,7},{7,3},{8,12},{12,8},{9,1... | collective-permute-start | bytes 1671176 | tf_op jit(solution)/shard_map/ppermute | solution.py:23
  48.4 16.9 %collective-permute-start.23 = (bf16[8,1,128,128]{3,2,1,0:T(8,128)(2,1)}, bf16[8,1,128,128]{3,2,1,0:T(8,128)(2,1)S(1)}, u32[]{:S(2)}, u32[]{:S(2)}) collective-permute-start(bf16[8,1,128,128]{3,2,1,0:T(8,128)(2,1)} %own_d_ref.13), channel_id=1, source_target_pairs={{0,4},{4,0},{1,5},{5,1},{2,6},{6,2},{3,7},{7,3},{8,12},{12,8},{9,1... | collective-permute-start | bytes 786440 | tf_op jit(solution)/shard_map/ppermute | solution.py:23
  48.6 16.7 %collective-permute-start.22 = (bf16[8,1,32,128]{3,2,1,0:T(8,128)(2,1)S(1)}, bf16[8,1,32,128]{3,2,1,0:T(8,128)(2,1)S(1)}, u32[]{:S(2)}, u32[]{:S(2)}) collective-permute-start(bf16[8,1,32,128]{3,2,1,0:T(8,128)(2,1)S(1)} %get-tuple-element.100), channel_id=1, source_target_pairs={{0,4},{4,0},{1,5},{5,1},{2,6},{6,2},{3,7},{7,3},{8,12},{12,8},{9,1... | collective-permute-start | bytes 196616 | tf_op jit(solution)/shard_map/ppermute | solution.py:23
  70.0 12.7 %all-to-all-start = ((bf16[16,2,32,128]{3,2,1,0:T(8,128)(2,1)}), bf16[16,2,32,128]{3,2,1,0:T(8,128)(2,1)S(1)}, u32[]{:S(2)}, u32[]{:S(2)}) async-start(bf16[16,2,32,128]{3,2,1,0:T(8,128)(2,1)} %get-tuple-element.60), calls=%async_computation | async-start | bytes 524288 | tf_op jit(solution)/shard_map/all_to_all | solution.py:332
  90.4 12.2 %all-to-all-start.1 = ((bf16[16,2,32,128]{3,2,1,0:T(8,128)(2,1)}), bf16[16,2,32,128]{3,2,1,0:T(8,128)(2,1)S(1)}, u32[]{:S(2)}, u32[]{:S(2)}) async-start(bf16[16,2,32,128]{3,2,1,0:T(8,128)(2,1)} %get-tuple-element.67), calls=%async_computation.1 | async-start | bytes 524288 | tf_op jit(solution)/shard_map/all_to_all | solution.py:332
  112.5 12.0 %all-to-all-start.2 = ((bf16[16,2,32,128]{3,2,1,0:T(8,128)(2,1)}), bf16[16,2,32,128]{3,2,1,0:T(8,128)(2,1)S(1)}, u32[]{:S(2)}, u32[]{:S(2)}) async-start(bf16[16,2,32,128]{3,2,1,0:T(8,128)(2,1)} %get-tuple-element.74), calls=%async_computation.2 | async-start | bytes 524288 | tf_op jit(solution)/shard_map/all_to_all | solution.py:332
  132.0 12.0 %all-to-all-start.3 = ((bf16[16,2,32,128]{3,2,1,0:T(8,128)(2,1)}), bf16[16,2,32,128]{3,2,1,0:T(8,128)(2,1)S(1)}, u32[]{:S(2)}, u32[]{:S(2)}) async-start(bf16[16,2,32,128]{3,2,1,0:T(8,128)(2,1)} %get-tuple-element.81), calls=%async_computation.3 | async-start | bytes 524288 | tf_op jit(solution)/shard_map/all_to_all | solution.py:332
  153.6 12.4 %all-to-all-start.4 = ((bf16[16,2,32,128]{3,2,1,0:T(8,128)(2,1)}), bf16[16,2,32,128]{3,2,1,0:T(8,128)(2,1)S(1)}, u32[]{:S(2)}, u32[]{:S(2)}) async-start(bf16[16,2,32,128]{3,2,1,0:T(8,128)(2,1)} %get-tuple-element.88), calls=%async_computation.4 | async-start | bytes 524288 | tf_op jit(solution)/shard_map/all_to_all | solution.py:332
  173.4 12.0 %all-to-all-start.5 = ((bf16[16,2,32,128]{3,2,1,0:T(8,128)(2,1)}), bf16[16,2,32,128]{3,2,1,0:T(8,128)(2,1)S(1)}, u32[]{:S(2)}, u32[]{:S(2)}) async-start(bf16[16,2,32,128]{3,2,1,0:T(8,128)(2,1)} %get-tuple-element.95), calls=%async_computation.5 | async-start | bytes 524288 | tf_op jit(solution)/shard_map/all_to_all | solution.py:332
  194.5 16.9 %collective-permute-start.42 = (bf16[7,32,128]{2,1,0:T(8,128)(2,1)S(1)}, bf16[7,32,128]{2,1,0:T(8,128)(2,1)S(1)}, u32[]{:S(2)}, u32[]{:S(2)}) collective-permute-start(bf16[7,32,128]{2,1,0:T(8,128)(2,1)S(1)} %get-tuple-element.104), channel_id=1, source_target_pairs={{0,4},{4,0},{1,5},{5,1},{2,6},{6,2},{3,7},{7,3},{8,12},{12,8},{9,1... | collective-permute-start | bytes 172040 | tf_op jit(solution)/shard_map/ppermute | solution.py:23
  (35 other events, 122.8 us)

commit v6 on v5

--- a/solution.py
+++ b/solution.py
@@ -76,7 +76,7 @@
                 group.append(blocks[k])
             part = nt_dot(jnp.concatenate(xs, axis=1), jnp.concatenate(group, axis=1))
             total = part if total is None else total + part
-        out_ref[r] = total.astype(out_ref.dtype)
+        out_ref[r] = total
 
 
 def first_kernel(code_ref, *refs):
@@ -136,17 +136,17 @@
     list_ref[0] = lax.fori_loop(0, fresh_ref.shape[1], note, jnp.int32(0))
 
 
-def sum_call(kernel, codes, sources, source_spaces, own, other, outs, out_spaces, extra, name, kind):
+def sum_call(kernel, codes, sources, source_spaces, own, other, outs, out_spaces, extra, name, limit):
     slots, (rhs_cols, block) = codes[0].shape[1], sources[0].shape[-2:]
     return pl.pallas_call(
         kernel,
-        out_shape=[jax.ShapeDtypeStruct((2, rhs_cols, block), kind)] + outs,
+        out_shape=[jax.ShapeDtypeStruct((2, rhs_cols, block), jnp.float32)] + outs,
         in_specs=[pl.BlockSpec(memory_space=pltpu.SMEM)] * len(codes)
         + [pl.BlockSpec(memory_space=space) for space in source_spaces]
         + [pl.BlockSpec(memory_space=pltpu.HBM)] * 2,
         out_specs=[pl.BlockSpec(memory_space=space) for space in [pltpu.VMEM] + out_spaces],
         scratch_shapes=[pltpu.VMEM((slots, block, block), jnp.bfloat16), pltpu.SemaphoreType.DMA((2,))] + extra,
-        compiler_params=pltpu.CompilerParams(vmem_limit_bytes=VMEM_LIMIT),
+        compiler_params=pltpu.CompilerParams(vmem_limit_bytes=limit),
         cost_estimate=pl.CostEstimate(
             flops=2 * slots * rhs_cols * block * block,
             bytes_accessed=slots * block * (block + 2 * rhs_cols) * 4,
@@ -167,7 +167,7 @@
         pltpu.SemaphoreType.DMA,
     ]
     spaces = [pl.ANY] * len(sources)
-    return sum_call(first_kernel, [code], sources, spaces, own, other, [store], [pltpu.HBM], extra, "first_sum", jnp.bfloat16)
+    return sum_call(first_kernel, [code], sources, spaces, own, other, [store], [pltpu.HBM], extra, "first_sum", 12 * 1024 * 1024)
 
 
 def old_sum(level, known, code, fresh, store, solved, own, other):
@@ -182,17 +182,17 @@
         extra.append(pltpu.VMEM((sum(v.shape[0] for v in solved),) + one, jnp.bfloat16))
     spaces = [pl.ANY] + [pltpu.VMEM] * len(solved)
     out_spaces = [pltpu.SMEM, pltpu.VMEM]
-    return sum_call(kernel, [code, fresh], [store] + solved, spaces, own, other, outs, out_spaces, extra, "old_sum", jnp.float32)
-
-
-def fresh_kernel(level, list_ref, old_ref, x_ref, near_ref, own_ref, other_ref, out_ref, total, far, sem):
+    return sum_call(kernel, [code, fresh], [store] + solved, spaces, own, other, outs, out_spaces, extra, "old_sum", VMEM_LIMIT)
+
+
+def fresh_kernel(level, list_ref, old_ref, x_ref, near_ref, own_ref, other_ref, out_ref, far, sem):
     per_row = own_ref.shape[2]
-    total[...] = old_ref[...]
+    out_ref[...] = old_ref[...]
     count = list_ref[0]
 
     def add(block, entry):
         row = ((entry & 1023) >= per_row).astype(jnp.int32)
-        total[row] += nt_dot(x_ref[entry >> 10], block)
+        out_ref[row] += nt_dot(x_ref[entry >> 10], block)
 
     def add_near(n, carry):
         add(near_ref[n], list_ref[1 + n])
@@ -215,7 +215,6 @@
 
     lax.fori_loop(0, jnp.minimum(count, NEAR), add_near, 0)
     lax.fori_loop(NEAR, count, add_far, 0)
-    out_ref[...] = total[...].astype(out_ref.dtype)
 
 
 def fresh_sum(level, listed, solved, old, near, own, other):
@@ -223,11 +222,10 @@
     vmem = pl.BlockSpec(memory_space=pltpu.VMEM)
     return pl.pallas_call(
         functools.partial(fresh_kernel, level),
-        out_shape=jax.ShapeDtypeStruct(old.shape, jnp.bfloat16),
+        out_shape=jax.ShapeDtypeStruct(old.shape, jnp.float32),
         in_specs=[pl.BlockSpec(memory_space=pltpu.SMEM)] + [vmem] * 3 + [pl.BlockSpec(memory_space=pltpu.HBM)] * 2,
         out_specs=vmem,
         scratch_shapes=[
-            pltpu.VMEM(old.shape, jnp.float32),
             pltpu.VMEM((block, block), jnp.bfloat16),
             pltpu.SemaphoreType.DMA,
         ],
@@ -239,8 +237,7 @@
 def solve_kernel(level, p0, p1, p2, p3, rhs_ref, own_d_ref, other_d_ref, out_ref, *refs):
     core = lax.axis_index("core")
     for r, d_ref in enumerate((own_d_ref, other_d_ref)):
-        q0, q1, q2, q3 = (p[r].astype(jnp.float32) for p in (p0, p1, p2, p3))
-        coupled = (q0 + q1) + (q2 + q3)
+        coupled = (p0[r] + p1[r]) + (p2[r] + p3[r])
         reduced = (rhs_ref[level, r].astype(jnp.float32) - coupled).astype(jnp.bfloat16)
         solved = nt_dot(reduced, d_ref[level, 0]).astype(jnp.bfloat16)
         out_ref[r] = solved
@@ -296,6 +293,8 @@
     diag_other = swap_cores(diag_inv)
     off_sent, known = lax.optimization_barrier((off_blocks, known))
     off_other = swap_cores(off_sent)
+    off_first = off_sent[:1]
+    off_first_other = swap_cores(off_first)
 
     pieces = gather_parts(known)
     pieces = pieces + [swap_cores(piece) for piece in pieces]
@@ -319,7 +318,7 @@
     fresh_code = jnp.where(keep & is_fresh, place_level, -1).reshape(levels - 1, -1)
 
     own_rows, other_rows = [], []
-    value, store = first_sum(old_code, pieces, off_blocks, off_other)
+    value, store = first_sum(old_code, pieces, off_first, off_first_other)
     solved_levels = []
     for level in range(1, levels):
         partials = [value] + [lax.ppermute(value, "x", xor_pairs(4, k)) for k in (1, 2, 3)]

time: 213 us -> 228 us (1.070)
  local copies, waits for them, and re-layouts: 8.55 us -> 19.7 us
  starting transfers between devices: 97 us -> 99.5 us
    unnamed x27 -> x35, local copies, waits for them, and re-layouts: 7.57 us -> 17.5 us
    ppermute x1, starting transfers between devices: 0.01 us -> 3.16 us  [gather_parts(): lax.ppermute(after_high, ROWS, down)]
    ppermute x13 -> x14, starting transfers between devices: 27.6 us -> 29.5 us  [swap_cores(): return lax.ppermute(v, 'core', xor_pairs(2, 1))]
  transfers between devices with their start and end apart: 49 -> 50, of which waited for: 28 -> 29; matrix products, arithmetic and copies ran while one was open for 1% -> 1% of each run, Pallas kernels for 19% -> 18%
where the time goes in v6:
time: 228 us; the launch traced here: 226 us
  starting transfers between devices  99.5 us (44%)
  Pallas kernels  52.8 us (23%)
  waiting for transfers between devices  49.9 us (22%)
  local copies, waits for them, and re-layouts  19.7 us (9%)
  other arithmetic  2.62 us (1%)
    pallas_call x7, Pallas kernels, sum_call(): pl.pallas_call(kernel, out_shape=[jax.ShapeDtypeStruct((2, rhs_cols, bloc...  40.6 us
    ppermute x14, starting transfers between devices, swap_cores(): return lax.ppermute(v, 'core', xor_pairs(2, 1))  29.5 us
    all_to_all x6, starting transfers between devices, on_device(): solved = lax.all_to_all(sent, ('z', 'y'), 0, 0).reshape(32, half, block)  28.1 us
    ppermute x21, starting transfers between devices, on_device(): lax.ppermute(value, 'x', xor_pairs(4, k))  27.6 us
    ppermute x21, waiting for transfers between devices, on_device(): lax.ppermute(value, 'x', xor_pairs(4, k))  19.9 us
    unnamed x35, local copies, waits for them, and re-layouts  17.5 us
    all_to_all x6, waiting for transfers between devices, on_device(): solved = lax.all_to_all(sent, ('z', 'y'), 0, 0).reshape(32, half, block)  11.4 us
    ppermute x3, waiting for transfers between devices, gather_parts(): lax.ppermute(v, ROWS, pairs(1, lambda i, k=k: i ^ k))  6.44 us
  transfers between devices with their start and end apart: 50, of which 29 were waited for; matrix products, arithmetic and copies ran while one was open for 1% of the time, Pallas kernels for 18%

profile of v6, /device:TPU:1, one launch (start us, length us, event | category | flops | bytes accessed | tf_op | source)
XLA Modules:
  0.0 225.9 jit_solution(15006871722546488505)
XLA Ops:
  7.2 3.5 %collective-permute-done.2 = bf16[2,17,32,128]{3,2,1,0:T(8,128)(2,1)S(1)} collective-permute-done((bf16[2,17,32,128]{3,2,1,0:T(8,128)(2,1)S(1)}, bf16[2,17,32,128]{3,2,1,0:T(8,128)(2,1)S(1)}, u32[]{:S(2)}, u32[]{:S(2)}) %collective-permute-start.2) | collective-permute-done | bytes 278560 | tf_op jit(solution)/shard_map/ppermute | solution.py:37
  13.7 3.9 %collective-permute-start.7 = (bf16[2,2,17,32,128]{4,3,2,1,0:T(8,128)(2,1)S(1)}, bf16[2,2,17,32,128]{4,3,2,1,0:T(8,128)(2,1)S(1)}, u32[]{:S(2)}, u32[]{:S(2)}) collective-permute-start(bf16[2,2,17,32,128]{4,3,2,1,0:T(8,128)(2,1)S(1)} %pad_maximum_fusion.1.refs_1_), channel_id=1, source_target_pairs={{0,24},{4,100},{8,0},{12,108},{16,8},{20,116},{24,16},{28,124},{32... | collective-permute-start | bytes 1671176 | tf_op jit(solution)/shard_map/ppermute | solution.py:40
  24.1 3.4 %collective-permute-start.6 = (bf16[2,2,17,32,128]{4,3,2,1,0:T(8,128)(2,1)S(1)}, bf16[2,2,17,32,128]{4,3,2,1,0:T(8,128)(2,1)}, u32[]{:S(2)}, u32[]{:S(2)}) collective-permute-start(bf16[2,2,17,32,128]{4,3,2,1,0:T(8,128)(2,1)S(1)} %pad_maximum_fusion.refs_0_), channel_id=1, source_target_pairs={{0,24},{4,100},{8,0},{12,108},{16,8},{20,116},{24,16},{28,124},{32... | collective-permute-start | bytes 1671176 | tf_op jit(solution)/shard_map/ppermute | solution.py:41
  29.3 4.4 %collective-permute-done.5.refs_3_ = bf16[2,2,17,32,128]{4,3,2,1,0:T(8,128)(2,1)} collective-permute-done((bf16[2,2,17,32,128]{4,3,2,1,0:T(8,128)(2,1)S(1)}, bf16[2,2,17,32,128]{4,3,2,1,0:T(8,128)(2,1)}, u32[]{:S(2)}, u32[]{:S(2)}) %collective-permute-start.5) | collective-permute-done | bytes 557088 | tf_op jit(solution)/shard_map/ppermute | solution.py:41
  35.4 3.2 %collective-permute-start.9 = (bf16[2,2,17,32,128]{4,3,2,1,0:T(8,128)(2,1)S(1)}, bf16[2,2,17,32,128]{4,3,2,1,0:T(8,128)(2,1)}, u32[]{:S(2)}, u32[]{:S(2)}) collective-permute-start(bf16[2,2,17,32,128]{4,3,2,1,0:T(8,128)(2,1)S(1)} %collective-permute-done.7.refs_5_), channel_id=1, source_target_pairs={{0,24},{4,100},{8,0},{12,108},{16,8},{20,116},{24,16},{28,124},{32... | collective-permute-start | bytes 1671176 | tf_op jit(solution)/shard_map/ppermute | solution.py:42
  62.3 6.9 %first_sum.1 = (f32[2,32,128]{2,1,0:T(8,128)S(1)}, bf16[2048,32,128]{2,1,0:T(8,128)(2,1)S(1)}) custom-call(s32[7,64]{1,0:T(8,128)S(1)} %get-tuple-element.118.code_ref, bf16[2,2,17,32,128]{4,3,2,1,0:T(8,128)(2,1)S(1)} %pad_maximum_fusion.refs_0_, bf16[2,2,17,32,128]{4,3,2,1,0:T(8,128)(2,1)S(1)} %pad_maximum_fusion.1.refs_1_, ...), custom_call_target="tpu_custom_call" | custom-call | flops 67108864 | bytes 6291456 | tf_op jit(solution)/shard_map/first_sum/pallas_call | solution.py:141
  69.2 5.8 %copy-done = bf16[2048,32,128]{2,1,0:T(8,128)(2,1)} copy-done((bf16[2048,32,128]{2,1,0:T(8,128)(2,1)}, bf16[2048,32,128]{2,1,0:T(8,128)(2,1)S(1)}, u32[]{:S(2)}) %copy-start) | copy-done | bytes 16777240
  83.7 4.5 %all-to-all-start = ((bf16[16,2,32,128]{3,2,1,0:T(8,128)(2,1)}), bf16[16,2,32,128]{3,2,1,0:T(8,128)(2,1)S(1)}, u32[]{:S(2)}, u32[]{:S(2)}) async-start(bf16[16,2,32,128]{3,2,1,0:T(8,128)(2,1)} %get-tuple-element.60), calls=%async_computation | async-start | bytes 524288 | tf_op jit(solution)/shard_map/all_to_all | solution.py:331
  88.2 5.6 %old_sum.6 = (f32[2,32,128]{2,1,0:T(8,128)S(1)}, s32[65]{0:T(128)S(1)}, bf16[16,128,128]{2,1,0:T(8,128)(2,1)S(1)}) custom-call(s32[7,64]{1,0:T(8,128)S(1)} %get-tuple-element.118.code_ref, s32[7,64]{1,0:T(8,128)S(1)} %get-tuple-element.92.fresh_ref, bf16[2048,32,128]{2,1,0:T(8,128)(2,1)} %copy-done, bf16[7,1,32,128,128]{4,3,2,1,0:T(8,128)(2,1)} %own_ref.11, ...), custom_call_target="tpu_custom_call" | custom-call | flops 67108864 | bytes 6291456 | tf_op jit(solution)/shard_map/old_sum/pallas_call | solution.py:141
  103.1 4.9 %all-to-all-start.1 = ((bf16[16,2,32,128]{3,2,1,0:T(8,128)(2,1)}), bf16[16,2,32,128]{3,2,1,0:T(8,128)(2,1)S(1)}, u32[]{:S(2)}, u32[]{:S(2)}) async-start(bf16[16,2,32,128]{3,2,1,0:T(8,128)(2,1)} %get-tuple-element.67), calls=%async_computation.1 | async-start | bytes 524288 | tf_op jit(solution)/shard_map/all_to_all | solution.py:331
  108.0 5.4 %old_sum.7 = (f32[2,32,128]{2,1,0:T(8,128)S(1)}, s32[65]{0:T(128)S(1)}, bf16[16,128,128]{2,1,0:T(8,128)(2,1)S(1)}) custom-call(s32[7,64]{1,0:T(8,128)S(1)} %get-tuple-element.118.code_ref, s32[7,64]{1,0:T(8,128)S(1)} %get-tuple-element.92.fresh_ref, bf16[2048,32,128]{2,1,0:T(8,128)(2,1)} %copy-done, bf16[32,32,128]{2,1,0:T(8,128)(2,1)S(1)} %bitcast.30, ...), custom_call_target="tpu_custom_call" | custom-call | flops 67108864 | bytes 6291456 | tf_op jit(solution)/shard_map/old_sum/pallas_call | solution.py:141
  117.1 3.6 %collective-permute-start.29 = (f32[2,32,128]{2,1,0:T(8,128)S(1)}, f32[2,32,128]{2,1,0:T(8,128)S(1)}, u32[]{:S(2)}, u32[]{:S(2)}) collective-permute-start(f32[2,32,128]{2,1,0:T(8,128)S(1)} %fresh_sum.7.p0), channel_id=1, source_target_pairs={{0,2},{1,3},{2,0},{3,1},{4,6},{5,7},{6,4},{7,5},{8,10},{9,11},{10,... | collective-permute-start | bytes 98312 | tf_op jit(solution)/shard_map/ppermute | solution.py:324
  125.7 4.8 %all-to-all-start.2 = ((bf16[16,2,32,128]{3,2,1,0:T(8,128)(2,1)}), bf16[16,2,32,128]{3,2,1,0:T(8,128)(2,1)S(1)}, u32[]{:S(2)}, u32[]{:S(2)}) async-start(bf16[16,2,32,128]{3,2,1,0:T(8,128)(2,1)} %get-tuple-element.74), calls=%async_computation.2 | async-start | bytes 524288 | tf_op jit(solution)/shard_map/all_to_all | solution.py:331
  130.5 5.8 %old_sum.8 = (f32[2,32,128]{2,1,0:T(8,128)S(1)}, s32[65]{0:T(128)S(1)}, bf16[16,128,128]{2,1,0:T(8,128)(2,1)S(1)}) custom-call(s32[7,64]{1,0:T(8,128)S(1)} %get-tuple-element.118.code_ref, s32[7,64]{1,0:T(8,128)S(1)} %get-tuple-element.92.fresh_ref, bf16[2048,32,128]{2,1,0:T(8,128)(2,1)} %copy-done, bf16[32,32,128]{2,1,0:T(8,128)(2,1)S(1)} %bitcast.31, ...), custom_call_target="tpu_custom_call" | custom-call | flops 67108864 | bytes 6291456 | tf_op jit(solution)/shard_map/old_sum/pallas_call | solution.py:141
  139.8 3.1 %collective-permute-start.33 = (f32[2,32,128]{2,1,0:T(8,128)S(1)}, f32[2,32,128]{2,1,0:T(8,128)S(1)}, u32[]{:S(2)}, u32[]{:S(2)}) collective-permute-start(f32[2,32,128]{2,1,0:T(8,128)S(1)} %fresh_sum.8.p0), channel_id=1, source_target_pairs={{0,3},{1,2},{2,1},{3,0},{4,7},{5,6},{6,5},{7,4},{8,11},{9,10},{10,... | collective-permute-start | bytes 98312 | tf_op jit(solution)/shard_map/ppermute | solution.py:324
  145.6 4.4 %all-to-all-start.3 = ((bf16[16,2,32,128]{3,2,1,0:T(8,128)(2,1)}), bf16[16,2,32,128]{3,2,1,0:T(8,128)(2,1)S(1)}, u32[]{:S(2)}, u32[]{:S(2)}) async-start(bf16[16,2,32,128]{3,2,1,0:T(8,128)(2,1)} %get-tuple-element.81), calls=%async_computation.3 | async-start | bytes 524288 | tf_op jit(solution)/shard_map/all_to_all | solution.py:331
  150.0 5.5 %old_sum.9 = (f32[2,32,128]{2,1,0:T(8,128)S(1)}, s32[65]{0:T(128)S(1)}, bf16[16,128,128]{2,1,0:T(8,128)(2,1)S(1)}) custom-call(s32[7,64]{1,0:T(8,128)S(1)} %get-tuple-element.118.code_ref, s32[7,64]{1,0:T(8,128)S(1)} %get-tuple-element.92.fresh_ref, bf16[2048,32,128]{2,1,0:T(8,128)(2,1)} %copy-done, bf16[32,32,128]{2,1,0:T(8,128)(2,1)S(1)} %bitcast.32, ...), custom_call_target="tpu_custom_call" | custom-call | flops 67108864 | bytes 6291456 | tf_op jit(solution)/shard_map/old_sum/pallas_call | solution.py:141
  159.1 3.3 %collective-permute-start.35 = (f32[2,32,128]{2,1,0:T(8,128)S(1)}, f32[2,32,128]{2,1,0:T(8,128)S(1)}, u32[]{:S(2)}, u32[]{:S(2)}) collective-permute-start(f32[2,32,128]{2,1,0:T(8,128)S(1)} %fresh_sum.9.p0), channel_id=1, source_target_pairs={{0,2},{1,3},{2,0},{3,1},{4,6},{5,7},{6,4},{7,5},{8,10},{9,11},{10,... | collective-permute-start | bytes 98312 | tf_op jit(solution)/shard_map/ppermute | solution.py:324
  167.7 4.0 %all-to-all-start.4 = ((bf16[16,2,32,128]{3,2,1,0:T(8,128)(2,1)}), bf16[16,2,32,128]{3,2,1,0:T(8,128)(2,1)S(1)}, u32[]{:S(2)}, u32[]{:S(2)}) async-start(bf16[16,2,32,128]{3,2,1,0:T(8,128)(2,1)} %get-tuple-element.88), calls=%async_computation.4 | async-start | bytes 524288 | tf_op jit(solution)/shard_map/all_to_all | solution.py:331
  171.8 5.8 %old_sum.10 = (f32[2,32,128]{2,1,0:T(8,128)S(1)}, s32[65]{0:T(128)S(1)}, bf16[16,128,128]{2,1,0:T(8,128)(2,1)S(1)}) custom-call(s32[7,64]{1,0:T(8,128)S(1)} %get-tuple-element.118.code_ref, s32[7,64]{1,0:T(8,128)S(1)} %get-tuple-element.92.fresh_ref, bf16[2048,32,128]{2,1,0:T(8,128)(2,1)} %copy-done, bf16[32,32,128]{2,1,0:T(8,128)(2,1)S(1)} %bitcast.33, ...), custom_call_target="tpu_custom_call" | custom-call | flops 67108864 | bytes 6291456 | tf_op jit(solution)/shard_map/old_sum/pallas_call | solution.py:141
  187.1 5.4 %all-to-all-start.5 = ((bf16[16,2,32,128]{3,2,1,0:T(8,128)(2,1)}), bf16[16,2,32,128]{3,2,1,0:T(8,128)(2,1)S(1)}, u32[]{:S(2)}, u32[]{:S(2)}) async-start(bf16[16,2,32,128]{3,2,1,0:T(8,128)(2,1)} %get-tuple-element.95), calls=%async_computation.5 | async-start | bytes 524288 | tf_op jit(solution)/shard_map/all_to_all | solution.py:331
  192.5 5.7 %old_sum.11 = (f32[2,32,128]{2,1,0:T(8,128)S(1)}, s32[65]{0:T(128)S(1)}, bf16[16,128,128]{2,1,0:T(8,128)(2,1)S(1)}) custom-call(s32[7,64]{1,0:T(8,128)S(1)} %get-tuple-element.118.code_ref, s32[7,64]{1,0:T(8,128)S(1)} %get-tuple-element.92.fresh_ref, bf16[2048,32,128]{2,1,0:T(8,128)(2,1)} %copy-done, bf16[32,32,128]{2,1,0:T(8,128)(2,1)S(1)} %bitcast.34, ...), custom_call_target="tpu_custom_call" | custom-call | flops 67108864 | bytes 6291456 | tf_op jit(solution)/shard_map/old_sum/pallas_call | solution.py:141
  201.1 3.0 %collective-permute-start.41 = (f32[2,32,128]{2,1,0:T(8,128)S(1)}, f32[2,32,128]{2,1,0:T(8,128)S(1)}, u32[]{:S(2)}, u32[]{:S(2)}) collective-permute-start(f32[2,32,128]{2,1,0:T(8,128)S(1)} %fresh_sum.11.p0), channel_id=1, source_target_pairs={{0,2},{1,3},{2,0},{3,1},{4,6},{5,7},{6,4},{7,5},{8,10},{9,11},{10,... | collective-permute-start | bytes 98312 | tf_op jit(solution)/shard_map/ppermute | solution.py:324
  208.3 16.1 %collective-permute-start.43 = (bf16[7,32,128]{2,1,0:T(8,128)(2,1)S(1)}, bf16[7,32,128]{2,1,0:T(8,128)(2,1)S(1)}, u32[]{:S(2)}, u32[]{:S(2)}) collective-permute-start(bf16[7,32,128]{2,1,0:T(8,128)(2,1)S(1)} %get-tuple-element.104), channel_id=1, source_target_pairs={{0,4},{4,0},{1,5},{5,1},{2,6},{6,2},{3,7},{7,3},{8,12},{12,8},{9,1... | collective-permute-start | bytes 172040 | tf_op jit(solution)/shard_map/ppermute | solution.py:23
  (147 shorter events, 103.6 us)
Async XLA Ops:
  2.0 86.3 %collective-permute-start.24 = (bf16[7,1,32,128,128]{4,3,2,1,0:T(8,128)(2,1)}, bf16[7,1,32,128,128]{4,3,2,1,0:T(8,128)(2,1)}, u32[]{:S(2)}, u32[]{:S(2)}) collective-permute-start(bf16[7,1,32,128,128]{4,3,2,1,0:T(8,128)(2,1)} %own_ref.11), channel_id=1, source_target_pairs={{0,4},{4,0},{1,5},{5,1},{2,6},{6,2},{3,7},{7,3},{8,12},{12,8},{9,1... | collective-permute-start | bytes 22020104 | tf_op jit(solution)/shard_map/ppermute | solution.py:23
  3.5 7.2 %collective-permute-start.2 = (bf16[2,17,32,128]{3,2,1,0:T(8,128)(2,1)S(1)}, bf16[2,17,32,128]{3,2,1,0:T(8,128)(2,1)S(1)}, u32[]{:S(2)}, u32[]{:S(2)}) collective-permute-start(bf16[2,17,32,128]{3,2,1,0:T(8,128)(2,1)S(1)} %pad_maximum_fusion.2), channel_id=1, source_target_pairs={{0,64},{4,20},{8,72},{12,28},{16,80},{20,4},{24,88},{28,12},{32,96... | collective-permute-start | bytes 835592 | tf_op jit(solution)/shard_map/ppermute | solution.py:37
  6.5 7.2 %collective-permute-start.3 = (bf16[2,17,32,128]{3,2,1,0:T(8,128)(2,1)S(1)}, bf16[2,17,32,128]{3,2,1,0:T(8,128)(2,1)S(1)}, u32[]{:S(2)}, u32[]{:S(2)}) collective-permute-start(bf16[2,17,32,128]{3,2,1,0:T(8,128)(2,1)S(1)} %pad_maximum_fusion.2), channel_id=1, source_target_pairs={{0,96},{4,28},{8,104},{12,20},{16,112},{20,12},{24,120},{28,4},{32... | collective-permute-start | bytes 835592 | tf_op jit(solution)/shard_map/ppermute | solution.py:37
  7.2 10.4 %collective-permute-start.1 = (bf16[2,17,32,128]{3,2,1,0:T(8,128)(2,1)S(1)}, bf16[2,17,32,128]{3,2,1,0:T(8,128)(2,1)S(1)}, u32[]{:S(2)}, u32[]{:S(2)}) collective-permute-start(bf16[2,17,32,128]{3,2,1,0:T(8,128)(2,1)S(1)} %pad_maximum_fusion.2), channel_id=1, source_target_pairs={{0,32},{4,12},{8,40},{12,4},{16,48},{20,28},{24,56},{28,20},{32,0}... | collective-permute-start | bytes 835592 | tf_op jit(solution)/shard_map/ppermute | solution.py:37
  13.7 10.4 %collective-permute-start.7 = (bf16[2,2,17,32,128]{4,3,2,1,0:T(8,128)(2,1)S(1)}, bf16[2,2,17,32,128]{4,3,2,1,0:T(8,128)(2,1)S(1)}, u32[]{:S(2)}, u32[]{:S(2)}) collective-permute-start(bf16[2,2,17,32,128]{4,3,2,1,0:T(8,128)(2,1)S(1)} %pad_maximum_fusion.1.refs_1_), channel_id=1, source_target_pairs={{0,24},{4,100},{8,0},{12,108},{16,8},{20,116},{24,16},{28,124},{32... | collective-permute-start | bytes 1671176 | tf_op jit(solution)/shard_map/ppermute | solution.py:40
  17.7 10.0 %collective-permute-start.4 = (bf16[2,2,17,32,128]{4,3,2,1,0:T(8,128)(2,1)S(1)}, bf16[2,2,17,32,128]{4,3,2,1,0:T(8,128)(2,1)S(1)}, u32[]{:S(2)}, u32[]{:S(2)}) collective-permute-start(bf16[2,2,17,32,128]{4,3,2,1,0:T(8,128)(2,1)S(1)} %pad_maximum_fusion.refs_0_), channel_id=1, source_target_pairs={{0,8},{4,36},{8,16},{12,44},{16,24},{20,52},{24,0},{28,60},{32,40}... | collective-permute-start | bytes 1671176 | tf_op jit(solution)/shard_map/ppermute | solution.py:40
  17.8 15.9 %collective-permute-start.5 = (bf16[2,2,17,32,128]{4,3,2,1,0:T(8,128)(2,1)S(1)}, bf16[2,2,17,32,128]{4,3,2,1,0:T(8,128)(2,1)}, u32[]{:S(2)}, u32[]{:S(2)}) collective-permute-start(bf16[2,2,17,32,128]{4,3,2,1,0:T(8,128)(2,1)S(1)} %pad_maximum_fusion.1.refs_1_), channel_id=1, source_target_pairs={{0,8},{4,36},{8,16},{12,44},{16,24},{20,52},{24,0},{28,60},{32,40}... | collective-permute-start | bytes 1671176 | tf_op jit(solution)/shard_map/ppermute | solution.py:41
  21.5 20.2 %collective-permute-start.18 = (bf16[1,1,32,128,128]{4,3,2,1,0:T(8,128)(2,1)S(1)}, bf16[1,1,32,128,128]{4,3,2,1,0:T(8,128)(2,1)S(1)}, u32[]{:S(2)}, u32[]{:S(2)}) collective-permute-start(bf16[1,1,32,128,128]{4,3,2,1,0:T(8,128)(2,1)S(1)} %slice.53.refs_16_), channel_id=1, source_target_pairs={{0,4},{4,0},{1,5},{5,1},{2,6},{6,2},{3,7},{7,3},{8,12},{12,8},{9,1... | collective-permute-start | bytes 3145736 | tf_op jit(solution)/shard_map/ppermute | solution.py:23
  24.1 11.3 %collective-permute-start.6 = (bf16[2,2,17,32,128]{4,3,2,1,0:T(8,128)(2,1)S(1)}, bf16[2,2,17,32,128]{4,3,2,1,0:T(8,128)(2,1)}, u32[]{:S(2)}, u32[]{:S(2)}) collective-permute-start(bf16[2,2,17,32,128]{4,3,2,1,0:T(8,128)(2,1)S(1)} %pad_maximum_fusion.refs_0_), channel_id=1, source_target_pairs={{0,24},{4,100},{8,0},{12,108},{16,8},{20,116},{24,16},{28,124},{32... | collective-permute-start | bytes 1671176 | tf_op jit(solution)/shard_map/ppermute | solution.py:41
  27.6 10.9 %collective-permute-start.11 = (bf16[2,2,17,32,128]{4,3,2,1,0:T(8,128)(2,1)S(1)}, bf16[2,2,17,32,128]{4,3,2,1,0:T(8,128)(2,1)S(1)}, u32[]{:S(2)}, u32[]{:S(2)}) collective-permute-start(bf16[2,2,17,32,128]{4,3,2,1,0:T(8,128)(2,1)S(1)} %pad_maximum_fusion.1.refs_1_), channel_id=1, source_target_pairs={{0,4},{4,0},{1,5},{5,1},{2,6},{6,2},{3,7},{7,3},{8,12},{12,8},{9,1... | collective-permute-start | bytes 1671176 | tf_op jit(solution)/shard_map/ppermute | solution.py:23
  35.4 9.6 %collective-permute-start.9 = (bf16[2,2,17,32,128]{4,3,2,1,0:T(8,128)(2,1)S(1)}, bf16[2,2,17,32,128]{4,3,2,1,0:T(8,128)(2,1)}, u32[]{:S(2)}, u32[]{:S(2)}) collective-permute-start(bf16[2,2,17,32,128]{4,3,2,1,0:T(8,128)(2,1)S(1)} %collective-permute-done.7.refs_5_), channel_id=1, source_target_pairs={{0,24},{4,100},{8,0},{12,108},{16,8},{20,116},{24,16},{28,124},{32... | collective-permute-start | bytes 1671176 | tf_op jit(solution)/shard_map/ppermute | solution.py:42
  39.3 10.0 %collective-permute-start.8 = (bf16[2,2,17,32,128]{4,3,2,1,0:T(8,128)(2,1)S(1)}, bf16[2,2,17,32,128]{4,3,2,1,0:T(8,128)(2,1)}, u32[]{:S(2)}, u32[]{:S(2)}) collective-permute-start(bf16[2,2,17,32,128]{4,3,2,1,0:T(8,128)(2,1)S(1)} %collective-permute-done.4.refs_2_), channel_id=1, source_target_pairs={{0,8},{4,36},{8,16},{12,44},{16,24},{20,52},{24,0},{28,60},{32,40}... | collective-permute-start | bytes 1671176 | tf_op jit(solution)/shard_map/ppermute | solution.py:42
  40.1 11.5 %collective-permute-start.15 = (bf16[2,2,17,32,128]{4,3,2,1,0:T(8,128)(2,1)S(1)}, bf16[2,2,17,32,128]{4,3,2,1,0:T(8,128)(2,1)S(1)}, u32[]{:S(2)}, u32[]{:S(2)}) collective-permute-start(bf16[2,2,17,32,128]{4,3,2,1,0:T(8,128)(2,1)S(1)} %collective-permute-done.7.refs_5_), channel_id=1, source_target_pairs={{0,4},{4,0},{1,5},{5,1},{2,6},{6,2},{3,7},{7,3},{8,12},{12,8},{9,1... | collective-permute-start | bytes 1671176 | tf_op jit(solution)/shard_map/ppermute | solution.py:23
  42.6 9.9 %collective-permute-start.12 = (bf16[2,2,17,32,128]{4,3,2,1,0:T(8,128)(2,1)S(1)}, bf16[2,2,17,32,128]{4,3,2,1,0:T(8,128)(2,1)S(1)}, u32[]{:S(2)}, u32[]{:S(2)}) collective-permute-start(bf16[2,2,17,32,128]{4,3,2,1,0:T(8,128)(2,1)S(1)} %collective-permute-done.4.refs_2_), channel_id=1, source_target_pairs={{0,4},{4,0},{1,5},{5,1},{2,6},{6,2},{3,7},{7,3},{8,12},{12,8},{9,1... | collective-permute-start | bytes 1671176 | tf_op jit(solution)/shard_map/ppermute | solution.py:23
  45.0 9.9 %collective-permute-start.13 = (bf16[2,2,17,32,128]{4,3,2,1,0:T(8,128)(2,1)}, bf16[2,2,17,32,128]{4,3,2,1,0:T(8,128)(2,1)}, u32[]{:S(2)}, u32[]{:S(2)}) collective-permute-start(bf16[2,2,17,32,128]{4,3,2,1,0:T(8,128)(2,1)} %collective-permute-done.5.refs_3_), channel_id=1, source_target_pairs={{0,4},{4,0},{1,5},{5,1},{2,6},{6,2},{3,7},{7,3},{8,12},{12,8},{9,1... | collective-permute-start | bytes 1671176 | tf_op jit(solution)/shard_map/ppermute | solution.py:23
  54.9 24.0 %collective-permute-start.23 = (bf16[8,1,128,128]{3,2,1,0:T(8,128)(2,1)}, bf16[8,1,128,128]{3,2,1,0:T(8,128)(2,1)S(1)}, u32[]{:S(2)}, u32[]{:S(2)}) collective-permute-start(bf16[8,1,128,128]{3,2,1,0:T(8,128)(2,1)} %own_d_ref.13), channel_id=1, source_target_pairs={{0,4},{4,0},{1,5},{5,1},{2,6},{6,2},{3,7},{7,3},{8,12},{12,8},{9,1... | collective-permute-start | bytes 786440 | tf_op jit(solution)/shard_map/ppermute | solution.py:23
  54.9 23.7 %collective-permute-start.22 = (bf16[8,1,32,128]{3,2,1,0:T(8,128)(2,1)S(1)}, bf16[8,1,32,128]{3,2,1,0:T(8,128)(2,1)S(1)}, u32[]{:S(2)}, u32[]{:S(2)}) collective-permute-start(bf16[8,1,32,128]{3,2,1,0:T(8,128)(2,1)S(1)} %get-tuple-element.100), channel_id=1, source_target_pairs={{0,4},{4,0},{1,5},{5,1},{2,6},{6,2},{3,7},{7,3},{8,12},{12,8},{9,1... | collective-permute-start | bytes 196616 | tf_op jit(solution)/shard_map/ppermute | solution.py:23
  83.7 12.1 %all-to-all-start = ((bf16[16,2,32,128]{3,2,1,0:T(8,128)(2,1)}), bf16[16,2,32,128]{3,2,1,0:T(8,128)(2,1)S(1)}, u32[]{:S(2)}, u32[]{:S(2)}) async-start(bf16[16,2,32,128]{3,2,1,0:T(8,128)(2,1)} %get-tuple-element.60), calls=%async_computation | async-start | bytes 524288 | tf_op jit(solution)/shard_map/all_to_all | solution.py:331
  103.1 12.5 %all-to-all-start.1 = ((bf16[16,2,32,128]{3,2,1,0:T(8,128)(2,1)}), bf16[16,2,32,128]{3,2,1,0:T(8,128)(2,1)S(1)}, u32[]{:S(2)}, u32[]{:S(2)}) async-start(bf16[16,2,32,128]{3,2,1,0:T(8,128)(2,1)} %get-tuple-element.67), calls=%async_computation.1 | async-start | bytes 524288 | tf_op jit(solution)/shard_map/all_to_all | solution.py:331
  125.7 12.3 %all-to-all-start.2 = ((bf16[16,2,32,128]{3,2,1,0:T(8,128)(2,1)}), bf16[16,2,32,128]{3,2,1,0:T(8,128)(2,1)S(1)}, u32[]{:S(2)}, u32[]{:S(2)}) async-start(bf16[16,2,32,128]{3,2,1,0:T(8,128)(2,1)} %get-tuple-element.74), calls=%async_computation.2 | async-start | bytes 524288 | tf_op jit(solution)/shard_map/all_to_all | solution.py:331
  145.6 12.0 %all-to-all-start.3 = ((bf16[16,2,32,128]{3,2,1,0:T(8,128)(2,1)}), bf16[16,2,32,128]{3,2,1,0:T(8,128)(2,1)S(1)}, u32[]{:S(2)}, u32[]{:S(2)}) async-start(bf16[16,2,32,128]{3,2,1,0:T(8,128)(2,1)} %get-tuple-element.81), calls=%async_computation.3 | async-start | bytes 524288 | tf_op jit(solution)/shard_map/all_to_all | solution.py:331
  167.7 11.6 %all-to-all-start.4 = ((bf16[16,2,32,128]{3,2,1,0:T(8,128)(2,1)}), bf16[16,2,32,128]{3,2,1,0:T(8,128)(2,1)S(1)}, u32[]{:S(2)}, u32[]{:S(2)}) async-start(bf16[16,2,32,128]{3,2,1,0:T(8,128)(2,1)} %get-tuple-element.88), calls=%async_computation.4 | async-start | bytes 524288 | tf_op jit(solution)/shard_map/all_to_all | solution.py:331
  187.1 12.9 %all-to-all-start.5 = ((bf16[16,2,32,128]{3,2,1,0:T(8,128)(2,1)}), bf16[16,2,32,128]{3,2,1,0:T(8,128)(2,1)S(1)}, u32[]{:S(2)}, u32[]{:S(2)}) async-start(bf16[16,2,32,128]{3,2,1,0:T(8,128)(2,1)} %get-tuple-element.95), calls=%async_computation.5 | async-start | bytes 524288 | tf_op jit(solution)/shard_map/all_to_all | solution.py:331
  208.3 17.0 %collective-permute-start.43 = (bf16[7,32,128]{2,1,0:T(8,128)(2,1)S(1)}, bf16[7,32,128]{2,1,0:T(8,128)(2,1)S(1)}, u32[]{:S(2)}, u32[]{:S(2)}) collective-permute-start(bf16[7,32,128]{2,1,0:T(8,128)(2,1)S(1)} %get-tuple-element.104), channel_id=1, source_target_pairs={{0,4},{4,0},{1,5},{5,1},{2,6},{6,2},{3,7},{7,3},{8,12},{12,8},{9,1... | collective-permute-start | bytes 172040 | tf_op jit(solution)/shard_map/ppermute | solution.py:23
  (40 other events, 191.3 us)

commit v7 on v6

--- a/solution.py
+++ b/solution.py
@@ -167,7 +167,7 @@
         pltpu.SemaphoreType.DMA,
     ]
     spaces = [pl.ANY] * len(sources)
-    return sum_call(first_kernel, [code], sources, spaces, own, other, [store], [pltpu.HBM], extra, "first_sum", 12 * 1024 * 1024)
+    return sum_call(first_kernel, [code], sources, spaces, own, other, [store], [pltpu.HBM], extra, "first_sum", 61 * 1024 * 1024)
 
 
 def old_sum(level, known, code, fresh, store, solved, own, other):
@@ -293,8 +293,6 @@
     diag_other = swap_cores(diag_inv)
     off_sent, known = lax.optimization_barrier((off_blocks, known))
     off_other = swap_cores(off_sent)
-    off_first = off_sent[:1]
-    off_first_other = swap_cores(off_first)
 
     pieces = gather_parts(known)
     pieces = pieces + [swap_cores(piece) for piece in pieces]
@@ -318,7 +316,7 @@
     fresh_code = jnp.where(keep & is_fresh, place_level, -1).reshape(levels - 1, -1)
 
     own_rows, other_rows = [], []
-    value, store = first_sum(old_code, pieces, off_first, off_first_other)
+    value, store = first_sum(old_code, pieces, off_blocks, off_other)
     solved_levels = []
     for level in range(1, levels):
         partials = [value] + [lax.ppermute(value, "x", xor_pairs(4, k)) for k in (1, 2, 3)]

time: 228 us -> 211 us (0.925)
  local copies, waits for them, and re-layouts: 19.7 us -> 3.33 us
    unnamed x35 -> x31, local copies, waits for them, and re-layouts: 17.5 us -> 2.36 us
    ppermute x1, waiting for transfers between devices: 1.56 us -> 4.98 us  [gather_parts(): lax.ppermute(after_high, ROWS, down)]
    ppermute x1, starting transfers between devices: 3.16 us -> 0.01 us  [gather_parts(): lax.ppermute(after_high, ROWS, down)]
    ppermute x14 -> x13, starting transfers between devices: 29.5 us -> 28.9 us  [swap_cores(): return lax.ppermute(v, 'core', xor_pairs(2, 1))]
  transfers between devices with their start and end apart: 50 -> 49, of which waited for: 29 -> 27; matrix products, arithmetic and copies ran while one was open for 1% -> 1% of each run, Pallas kernels for 18% -> 19%
where the time goes in v7:
time: 211 us; the launch traced here: 209 us
  starting transfers between devices  98.2 us (47%)
  Pallas kernels  52.8 us (25%)
  waiting for transfers between devices  50.4 us (24%)
  local copies, waits for them, and re-layouts  3.33 us (2%)
  other arithmetic  3.29 us (2%)
    pallas_call x7, Pallas kernels, sum_call(): pl.pallas_call(kernel, out_shape=[jax.ShapeDtypeStruct((2, rhs_cols, bloc...  40.3 us
    ppermute x13, starting transfers between devices, swap_cores(): return lax.ppermute(v, 'core', xor_pairs(2, 1))  28.9 us
    ppermute x21, starting transfers between devices, on_device(): lax.ppermute(value, 'x', xor_pairs(4, k))  28.2 us
    all_to_all x6, starting transfers between devices, on_device(): solved = lax.all_to_all(sent, ('z', 'y'), 0, 0).reshape(32, half, block)  27.9 us
    ppermute x21, waiting for transfers between devices, on_device(): lax.ppermute(value, 'x', xor_pairs(4, k))  19.5 us
    all_to_all x6, waiting for transfers between devices, on_device(): solved = lax.all_to_all(sent, ('z', 'y'), 0, 0).reshape(32, half, block)  11.4 us
    ppermute x3, waiting for transfers between devices, gather_parts(): lax.ppermute(v, ROWS, pairs(1, lambda i, k=k: i ^ k))  6.44 us
    pallas_call x6, Pallas kernels, fresh_sum(): pl.pallas_call(functools.partial(fresh_kernel, level), out_shape=jax.Shap...  6.35 us
  transfers between devices with their start and end apart: 49, of which 27 were waited for; matrix products, arithmetic and copies ran while one was open for 1% of the time, Pallas kernels for 19%

profile of v7, /device:TPU:1, one launch (start us, length us, event | category | flops | bytes accessed | tf_op | source)
XLA Modules:
  0.0 209.4 jit_solution(3803231007773674967)
XLA Ops:
  3.5 3.0 %collective-permute-start.2 = (bf16[2,17,32,128]{3,2,1,0:T(8,128)(2,1)S(1)}, bf16[2,17,32,128]{3,2,1,0:T(8,128)(2,1)S(1)}, u32[]{:S(2)}, u32[]{:S(2)}) collective-permute-start(bf16[2,17,32,128]{3,2,1,0:T(8,128)(2,1)S(1)} %pad_maximum_fusion.2), channel_id=1, source_target_pairs={{0,64},{4,20},{8,72},{12,28},{16,80},{20,4},{24,88},{28,12},{32,96... | collective-permute-start | bytes 835592 | tf_op jit(solution)/shard_map/ppermute | solution.py:37
  7.2 3.5 %collective-permute-done.2 = bf16[2,17,32,128]{3,2,1,0:T(8,128)(2,1)S(1)} collective-permute-done((bf16[2,17,32,128]{3,2,1,0:T(8,128)(2,1)S(1)}, bf16[2,17,32,128]{3,2,1,0:T(8,128)(2,1)S(1)}, u32[]{:S(2)}, u32[]{:S(2)}) %collective-permute-start.2) | collective-permute-done | bytes 278560 | tf_op jit(solution)/shard_map/ppermute | solution.py:37
  10.7 3.0 %collective-permute-done.3 = bf16[2,17,32,128]{3,2,1,0:T(8,128)(2,1)S(1)} collective-permute-done((bf16[2,17,32,128]{3,2,1,0:T(8,128)(2,1)S(1)}, bf16[2,17,32,128]{3,2,1,0:T(8,128)(2,1)S(1)}, u32[]{:S(2)}, u32[]{:S(2)}) %collective-permute-start.3) | collective-permute-done | bytes 278560 | tf_op jit(solution)/shard_map/ppermute | solution.py:37
  13.7 3.9 %collective-permute-start.7 = (bf16[2,2,17,32,128]{4,3,2,1,0:T(8,128)(2,1)S(1)}, bf16[2,2,17,32,128]{4,3,2,1,0:T(8,128)(2,1)S(1)}, u32[]{:S(2)}, u32[]{:S(2)}) collective-permute-start(bf16[2,2,17,32,128]{4,3,2,1,0:T(8,128)(2,1)S(1)} %pad_maximum_fusion.1.refs_1_), channel_id=1, source_target_pairs={{0,24},{4,100},{8,0},{12,108},{16,8},{20,116},{24,16},{28,124},{32... | collective-permute-start | bytes 1671176 | tf_op jit(solution)/shard_map/ppermute | solution.py:40
  20.5 2.9 %collective-permute-start.6 = (bf16[2,2,17,32,128]{4,3,2,1,0:T(8,128)(2,1)S(1)}, bf16[2,2,17,32,128]{4,3,2,1,0:T(8,128)(2,1)}, u32[]{:S(2)}, u32[]{:S(2)}) collective-permute-start(bf16[2,2,17,32,128]{4,3,2,1,0:T(8,128)(2,1)S(1)} %pad_maximum_fusion.refs_0_), channel_id=1, source_target_pairs={{0,24},{4,100},{8,0},{12,108},{16,8},{20,116},{24,16},{28,124},{32... | collective-permute-start | bytes 1671176 | tf_op jit(solution)/shard_map/ppermute | solution.py:41
  29.3 4.3 %collective-permute-done.5.refs_3_ = bf16[2,2,17,32,128]{4,3,2,1,0:T(8,128)(2,1)S(1)} collective-permute-done((bf16[2,2,17,32,128]{4,3,2,1,0:T(8,128)(2,1)S(1)}, bf16[2,2,17,32,128]{4,3,2,1,0:T(8,128)(2,1)S(1)}, u32[]{:S(2)}, u32[]{:S(2)}) %collective-permute-start.5) | collective-permute-done | bytes 557088 | tf_op jit(solution)/shard_map/ppermute | solution.py:41
  37.4 5.0 %collective-permute-done.9.refs_7_ = bf16[2,2,17,32,128]{4,3,2,1,0:T(8,128)(2,1)} collective-permute-done((bf16[2,2,17,32,128]{4,3,2,1,0:T(8,128)(2,1)S(1)}, bf16[2,2,17,32,128]{4,3,2,1,0:T(8,128)(2,1)}, u32[]{:S(2)}, u32[]{:S(2)}) %collective-permute-start.9) | collective-permute-done | bytes 557088 | tf_op jit(solution)/shard_map/ppermute | solution.py:42
  50.2 6.5 %first_sum.1 = (f32[2,32,128]{2,1,0:T(8,128)}, bf16[2048,32,128]{2,1,0:T(8,128)(2,1)}) custom-call(s32[7,64]{1,0:T(8,128)} %get-tuple-element.118.code_ref, bf16[2,2,17,32,128]{4,3,2,1,0:T(8,128)(2,1)} %copy-done.4, bf16[2,2,17,32,128]{4,3,2,1,0:T(8,128)(2,1)} %copy-done.3, bf16[2,2,17,32,128]{4,3,2,1,0:T(8,128)(2,1)} %copy-done.6, ...), custom_call_target="tpu_custom_call" | custom-call | flops 67108864 | bytes 6291456 | tf_op jit(solution)/shard_map/first_sum/pallas_call | solution.py:141
  66.4 4.8 %all-to-all-start = ((bf16[16,2,32,128]{3,2,1,0:T(8,128)(2,1)}), bf16[16,2,32,128]{3,2,1,0:T(8,128)(2,1)S(1)}, u32[]{:S(2)}, u32[]{:S(2)}) async-start(bf16[16,2,32,128]{3,2,1,0:T(8,128)(2,1)} %get-tuple-element.60), calls=%async_computation | async-start | bytes 524288 | tf_op jit(solution)/shard_map/all_to_all | solution.py:329
  71.2 5.6 %old_sum.6 = (f32[2,32,128]{2,1,0:T(8,128)S(1)}, s32[65]{0:T(128)S(1)}, bf16[16,128,128]{2,1,0:T(8,128)(2,1)S(1)}) custom-call(s32[7,64]{1,0:T(8,128)S(1)} %copy-done.1, s32[7,64]{1,0:T(8,128)S(1)} %get-tuple-element.92.fresh_ref, bf16[2048,32,128]{2,1,0:T(8,128)(2,1)} %get-tuple-element.57.store_ref, bf16[7,1,32,128,128]{4,3,2,1,0:T(8,128)(2,1)} %own_ref.11, ...), custom_call_target="tpu_custom_call" | custom-call | flops 67108864 | bytes 6291456 | tf_op jit(solution)/shard_map/old_sum/pallas_call | solution.py:141
  86.2 5.1 %all-to-all-start.1 = ((bf16[16,2,32,128]{3,2,1,0:T(8,128)(2,1)}), bf16[16,2,32,128]{3,2,1,0:T(8,128)(2,1)S(1)}, u32[]{:S(2)}, u32[]{:S(2)}) async-start(bf16[16,2,32,128]{3,2,1,0:T(8,128)(2,1)} %get-tuple-element.67), calls=%async_computation.1 | async-start | bytes 524288 | tf_op jit(solution)/shard_map/all_to_all | solution.py:329
  91.3 5.6 %old_sum.7 = (f32[2,32,128]{2,1,0:T(8,128)S(1)}, s32[65]{0:T(128)S(1)}, bf16[16,128,128]{2,1,0:T(8,128)(2,1)S(1)}) custom-call(s32[7,64]{1,0:T(8,128)S(1)} %copy-done.1, s32[7,64]{1,0:T(8,128)S(1)} %get-tuple-element.92.fresh_ref, bf16[2048,32,128]{2,1,0:T(8,128)(2,1)} %get-tuple-element.57.store_ref, bf16[32,32,128]{2,1,0:T(8,128)(2,1)S(1)} %bitcast.30, ...), custom_call_target="tpu_custom_call" | custom-call | flops 67108864 | bytes 6291456 | tf_op jit(solution)/shard_map/old_sum/pallas_call | solution.py:141
  100.1 3.5 %collective-permute-start.28 = (f32[2,32,128]{2,1,0:T(8,128)S(1)}, f32[2,32,128]{2,1,0:T(8,128)S(1)}, u32[]{:S(2)}, u32[]{:S(2)}) collective-permute-start(f32[2,32,128]{2,1,0:T(8,128)S(1)} %fresh_sum.7.p0), channel_id=1, source_target_pairs={{0,2},{1,3},{2,0},{3,1},{4,6},{5,7},{6,4},{7,5},{8,10},{9,11},{10,... | collective-permute-start | bytes 98312 | tf_op jit(solution)/shard_map/ppermute | solution.py:322
  108.6 4.9 %all-to-all-start.2 = ((bf16[16,2,32,128]{3,2,1,0:T(8,128)(2,1)}), bf16[16,2,32,128]{3,2,1,0:T(8,128)(2,1)S(1)}, u32[]{:S(2)}, u32[]{:S(2)}) async-start(bf16[16,2,32,128]{3,2,1,0:T(8,128)(2,1)} %get-tuple-element.74), calls=%async_computation.2 | async-start | bytes 524288 | tf_op jit(solution)/shard_map/all_to_all | solution.py:329
  113.5 5.7 %old_sum.8 = (f32[2,32,128]{2,1,0:T(8,128)S(1)}, s32[65]{0:T(128)S(1)}, bf16[16,128,128]{2,1,0:T(8,128)(2,1)S(1)}) custom-call(s32[7,64]{1,0:T(8,128)S(1)} %copy-done.1, s32[7,64]{1,0:T(8,128)S(1)} %get-tuple-element.92.fresh_ref, bf16[2048,32,128]{2,1,0:T(8,128)(2,1)} %get-tuple-element.57.store_ref, bf16[32,32,128]{2,1,0:T(8,128)(2,1)S(1)} %bitcast.31, ...), custom_call_target="tpu_custom_call" | custom-call | flops 67108864 | bytes 6291456 | tf_op jit(solution)/shard_map/old_sum/pallas_call | solution.py:141
  128.8 4.3 %all-to-all-start.3 = ((bf16[16,2,32,128]{3,2,1,0:T(8,128)(2,1)}), bf16[16,2,32,128]{3,2,1,0:T(8,128)(2,1)S(1)}, u32[]{:S(2)}, u32[]{:S(2)}) async-start(bf16[16,2,32,128]{3,2,1,0:T(8,128)(2,1)} %get-tuple-element.81), calls=%async_computation.3 | async-start | bytes 524288 | tf_op jit(solution)/shard_map/all_to_all | solution.py:329
  133.1 5.6 %old_sum.9 = (f32[2,32,128]{2,1,0:T(8,128)S(1)}, s32[65]{0:T(128)S(1)}, bf16[16,128,128]{2,1,0:T(8,128)(2,1)S(1)}) custom-call(s32[7,64]{1,0:T(8,128)S(1)} %copy-done.1, s32[7,64]{1,0:T(8,128)S(1)} %get-tuple-element.92.fresh_ref, bf16[2048,32,128]{2,1,0:T(8,128)(2,1)} %get-tuple-element.57.store_ref, bf16[32,32,128]{2,1,0:T(8,128)(2,1)S(1)} %bitcast.32, ...), custom_call_target="tpu_custom_call" | custom-call | flops 67108864 | bytes 6291456 | tf_op jit(solution)/shard_map/old_sum/pallas_call | solution.py:141
  142.3 3.4 %collective-permute-start.34 = (f32[2,32,128]{2,1,0:T(8,128)S(1)}, f32[2,32,128]{2,1,0:T(8,128)S(1)}, u32[]{:S(2)}, u32[]{:S(2)}) collective-permute-start(f32[2,32,128]{2,1,0:T(8,128)S(1)} %fresh_sum.9.p0), channel_id=1, source_target_pairs={{0,2},{1,3},{2,0},{3,1},{4,6},{5,7},{6,4},{7,5},{8,10},{9,11},{10,... | collective-permute-start | bytes 98312 | tf_op jit(solution)/shard_map/ppermute | solution.py:322
  151.0 3.9 %all-to-all-start.4 = ((bf16[16,2,32,128]{3,2,1,0:T(8,128)(2,1)}), bf16[16,2,32,128]{3,2,1,0:T(8,128)(2,1)S(1)}, u32[]{:S(2)}, u32[]{:S(2)}) async-start(bf16[16,2,32,128]{3,2,1,0:T(8,128)(2,1)} %get-tuple-element.88), calls=%async_computation.4 | async-start | bytes 524288 | tf_op jit(solution)/shard_map/all_to_all | solution.py:329
  155.0 5.7 %old_sum.10 = (f32[2,32,128]{2,1,0:T(8,128)S(1)}, s32[65]{0:T(128)S(1)}, bf16[16,128,128]{2,1,0:T(8,128)(2,1)S(1)}) custom-call(s32[7,64]{1,0:T(8,128)S(1)} %copy-done.1, s32[7,64]{1,0:T(8,128)S(1)} %get-tuple-element.92.fresh_ref, bf16[2048,32,128]{2,1,0:T(8,128)(2,1)} %get-tuple-element.57.store_ref, bf16[32,32,128]{2,1,0:T(8,128)(2,1)S(1)} %bitcast.33, ...), custom_call_target="tpu_custom_call" | custom-call | flops 67108864 | bytes 6291456 | tf_op jit(solution)/shard_map/old_sum/pallas_call | solution.py:141
  169.8 4.9 %all-to-all-start.5 = ((bf16[16,2,32,128]{3,2,1,0:T(8,128)(2,1)}), bf16[16,2,32,128]{3,2,1,0:T(8,128)(2,1)S(1)}, u32[]{:S(2)}, u32[]{:S(2)}) async-start(bf16[16,2,32,128]{3,2,1,0:T(8,128)(2,1)} %get-tuple-element.95), calls=%async_computation.5 | async-start | bytes 524288 | tf_op jit(solution)/shard_map/all_to_all | solution.py:329
  174.7 5.6 %old_sum.11 = (f32[2,32,128]{2,1,0:T(8,128)S(1)}, s32[65]{0:T(128)S(1)}, bf16[16,128,128]{2,1,0:T(8,128)(2,1)S(1)}) custom-call(s32[7,64]{1,0:T(8,128)S(1)} %copy-done.1, s32[7,64]{1,0:T(8,128)S(1)} %get-tuple-element.92.fresh_ref, bf16[2048,32,128]{2,1,0:T(8,128)(2,1)} %get-tuple-element.57.store_ref, bf16[32,32,128]{2,1,0:T(8,128)(2,1)S(1)} %bitcast.34, ...), custom_call_target="tpu_custom_call" | custom-call | flops 67108864 | bytes 6291456 | tf_op jit(solution)/shard_map/old_sum/pallas_call | solution.py:141
  183.9 3.0 %collective-permute-start.40 = (f32[2,32,128]{2,1,0:T(8,128)S(1)}, f32[2,32,128]{2,1,0:T(8,128)S(1)}, u32[]{:S(2)}, u32[]{:S(2)}) collective-permute-start(f32[2,32,128]{2,1,0:T(8,128)S(1)} %fresh_sum.11.p0), channel_id=1, source_target_pairs={{0,2},{1,3},{2,0},{3,1},{4,6},{5,7},{6,4},{7,5},{8,10},{9,11},{10,... | collective-permute-start | bytes 98312 | tf_op jit(solution)/shard_map/ppermute | solution.py:322
  191.1 16.7 %collective-permute-start.42 = (bf16[7,32,128]{2,1,0:T(8,128)(2,1)S(1)}, bf16[7,32,128]{2,1,0:T(8,128)(2,1)S(1)}, u32[]{:S(2)}, u32[]{:S(2)}) collective-permute-start(bf16[7,32,128]{2,1,0:T(8,128)(2,1)S(1)} %get-tuple-element.104), channel_id=1, source_target_pairs={{0,4},{4,0},{1,5},{5,1},{2,6},{6,2},{3,7},{7,3},{8,12},{12,8},{9,1... | collective-permute-start | bytes 172040 | tf_op jit(solution)/shard_map/ppermute | solution.py:23
  (140 shorter events, 88.5 us)
Async XLA Ops:
  2.0 48.2 %collective-permute-start.18 = (bf16[7,1,32,128,128]{4,3,2,1,0:T(8,128)(2,1)}, bf16[7,1,32,128,128]{4,3,2,1,0:T(8,128)(2,1)}, u32[]{:S(2)}, u32[]{:S(2)}) collective-permute-start(bf16[7,1,32,128,128]{4,3,2,1,0:T(8,128)(2,1)} %own_ref.11), channel_id=1, source_target_pairs={{0,4},{4,0},{1,5},{5,1},{2,6},{6,2},{3,7},{7,3},{8,12},{12,8},{9,1... | collective-permute-start | bytes 22020104 | tf_op jit(solution)/shard_map/ppermute | solution.py:23
  3.5 7.2 %collective-permute-start.2 = (bf16[2,17,32,128]{3,2,1,0:T(8,128)(2,1)S(1)}, bf16[2,17,32,128]{3,2,1,0:T(8,128)(2,1)S(1)}, u32[]{:S(2)}, u32[]{:S(2)}) collective-permute-start(bf16[2,17,32,128]{3,2,1,0:T(8,128)(2,1)S(1)} %pad_maximum_fusion.2), channel_id=1, source_target_pairs={{0,64},{4,20},{8,72},{12,28},{16,80},{20,4},{24,88},{28,12},{32,96... | collective-permute-start | bytes 835592 | tf_op jit(solution)/shard_map/ppermute | solution.py:37
  6.5 7.2 %collective-permute-start.3 = (bf16[2,17,32,128]{3,2,1,0:T(8,128)(2,1)S(1)}, bf16[2,17,32,128]{3,2,1,0:T(8,128)(2,1)S(1)}, u32[]{:S(2)}, u32[]{:S(2)}) collective-permute-start(bf16[2,17,32,128]{3,2,1,0:T(8,128)(2,1)S(1)} %pad_maximum_fusion.2), channel_id=1, source_target_pairs={{0,96},{4,28},{8,104},{12,20},{16,112},{20,12},{24,120},{28,4},{32... | collective-permute-start | bytes 835592 | tf_op jit(solution)/shard_map/ppermute | solution.py:37
  7.2 10.4 %collective-permute-start.1 = (bf16[2,17,32,128]{3,2,1,0:T(8,128)(2,1)S(1)}, bf16[2,17,32,128]{3,2,1,0:T(8,128)(2,1)S(1)}, u32[]{:S(2)}, u32[]{:S(2)}) collective-permute-start(bf16[2,17,32,128]{3,2,1,0:T(8,128)(2,1)S(1)} %pad_maximum_fusion.2), channel_id=1, source_target_pairs={{0,32},{4,12},{8,40},{12,4},{16,48},{20,28},{24,56},{28,20},{32,0}... | collective-permute-start | bytes 835592 | tf_op jit(solution)/shard_map/ppermute | solution.py:37
  13.7 10.4 %collective-permute-start.7 = (bf16[2,2,17,32,128]{4,3,2,1,0:T(8,128)(2,1)S(1)}, bf16[2,2,17,32,128]{4,3,2,1,0:T(8,128)(2,1)S(1)}, u32[]{:S(2)}, u32[]{:S(2)}) collective-permute-start(bf16[2,2,17,32,128]{4,3,2,1,0:T(8,128)(2,1)S(1)} %pad_maximum_fusion.1.refs_1_), channel_id=1, source_target_pairs={{0,24},{4,100},{8,0},{12,108},{16,8},{20,116},{24,16},{28,124},{32... | collective-permute-start | bytes 1671176 | tf_op jit(solution)/shard_map/ppermute | solution.py:40
  17.7 10.0 %collective-permute-start.4 = (bf16[2,2,17,32,128]{4,3,2,1,0:T(8,128)(2,1)S(1)}, bf16[2,2,17,32,128]{4,3,2,1,0:T(8,128)(2,1)S(1)}, u32[]{:S(2)}, u32[]{:S(2)}) collective-permute-start(bf16[2,2,17,32,128]{4,3,2,1,0:T(8,128)(2,1)S(1)} %pad_maximum_fusion.refs_0_), channel_id=1, source_target_pairs={{0,8},{4,36},{8,16},{12,44},{16,24},{20,52},{24,0},{28,60},{32,40}... | collective-permute-start | bytes 1671176 | tf_op jit(solution)/shard_map/ppermute | solution.py:40
  19.5 14.2 %collective-permute-start.5 = (bf16[2,2,17,32,128]{4,3,2,1,0:T(8,128)(2,1)S(1)}, bf16[2,2,17,32,128]{4,3,2,1,0:T(8,128)(2,1)S(1)}, u32[]{:S(2)}, u32[]{:S(2)}) collective-permute-start(bf16[2,2,17,32,128]{4,3,2,1,0:T(8,128)(2,1)S(1)} %pad_maximum_fusion.1.refs_1_), channel_id=1, source_target_pairs={{0,8},{4,36},{8,16},{12,44},{16,24},{20,52},{24,0},{28,60},{32,40}... | collective-permute-start | bytes 1671176 | tf_op jit(solution)/shard_map/ppermute | solution.py:41
  20.5 13.1 %collective-permute-start.6 = (bf16[2,2,17,32,128]{4,3,2,1,0:T(8,128)(2,1)S(1)}, bf16[2,2,17,32,128]{4,3,2,1,0:T(8,128)(2,1)}, u32[]{:S(2)}, u32[]{:S(2)}) collective-permute-start(bf16[2,2,17,32,128]{4,3,2,1,0:T(8,128)(2,1)S(1)} %pad_maximum_fusion.refs_0_), channel_id=1, source_target_pairs={{0,24},{4,100},{8,0},{12,108},{16,8},{20,116},{24,16},{28,124},{32... | collective-permute-start | bytes 1671176 | tf_op jit(solution)/shard_map/ppermute | solution.py:41
  24.1 11.0 %collective-permute-start.11 = (bf16[2,2,17,32,128]{4,3,2,1,0:T(8,128)(2,1)S(1)}, bf16[2,2,17,32,128]{4,3,2,1,0:T(8,128)(2,1)S(1)}, u32[]{:S(2)}, u32[]{:S(2)}) collective-permute-start(bf16[2,2,17,32,128]{4,3,2,1,0:T(8,128)(2,1)S(1)} %pad_maximum_fusion.1.refs_1_), channel_id=1, source_target_pairs={{0,4},{4,0},{1,5},{5,1},{2,6},{6,2},{3,7},{7,3},{8,12},{12,8},{9,1... | collective-permute-start | bytes 1671176 | tf_op jit(solution)/shard_map/ppermute | solution.py:23
  27.6 9.7 %collective-permute-start.10 = (bf16[2,2,17,32,128]{4,3,2,1,0:T(8,128)(2,1)S(1)}, bf16[2,2,17,32,128]{4,3,2,1,0:T(8,128)(2,1)S(1)}, u32[]{:S(2)}, u32[]{:S(2)}) collective-permute-start(bf16[2,2,17,32,128]{4,3,2,1,0:T(8,128)(2,1)S(1)} %pad_maximum_fusion.refs_0_), channel_id=1, source_target_pairs={{0,4},{4,0},{1,5},{5,1},{2,6},{6,2},{3,7},{7,3},{8,12},{12,8},{9,1... | collective-permute-start | bytes 1671176 | tf_op jit(solution)/shard_map/ppermute | solution.py:23
  33.6 8.8 %collective-permute-start.9 = (bf16[2,2,17,32,128]{4,3,2,1,0:T(8,128)(2,1)S(1)}, bf16[2,2,17,32,128]{4,3,2,1,0:T(8,128)(2,1)}, u32[]{:S(2)}, u32[]{:S(2)}) collective-permute-start(bf16[2,2,17,32,128]{4,3,2,1,0:T(8,128)(2,1)S(1)} %collective-permute-done.7.refs_5_), channel_id=1, source_target_pairs={{0,24},{4,100},{8,0},{12,108},{16,8},{20,116},{24,16},{28,124},{32... | collective-permute-start | bytes 1671176 | tf_op jit(solution)/shard_map/ppermute | solution.py:42
  33.6 11.3 %collective-permute-start.8 = (bf16[2,2,17,32,128]{4,3,2,1,0:T(8,128)(2,1)S(1)}, bf16[2,2,17,32,128]{4,3,2,1,0:T(8,128)(2,1)}, u32[]{:S(2)}, u32[]{:S(2)}) collective-permute-start(bf16[2,2,17,32,128]{4,3,2,1,0:T(8,128)(2,1)S(1)} %collective-permute-done.4.refs_2_), channel_id=1, source_target_pairs={{0,8},{4,36},{8,16},{12,44},{16,24},{20,52},{24,0},{28,60},{32,40}... | collective-permute-start | bytes 1671176 | tf_op jit(solution)/shard_map/ppermute | solution.py:42
  35.1 11.1 %collective-permute-start.15 = (bf16[2,2,17,32,128]{4,3,2,1,0:T(8,128)(2,1)S(1)}, bf16[2,2,17,32,128]{4,3,2,1,0:T(8,128)(2,1)S(1)}, u32[]{:S(2)}, u32[]{:S(2)}) collective-permute-start(bf16[2,2,17,32,128]{4,3,2,1,0:T(8,128)(2,1)S(1)} %collective-permute-done.7.refs_5_), channel_id=1, source_target_pairs={{0,4},{4,0},{1,5},{5,1},{2,6},{6,2},{3,7},{7,3},{8,12},{12,8},{9,1... | collective-permute-start | bytes 1671176 | tf_op jit(solution)/shard_map/ppermute | solution.py:23
  37.3 9.0 %collective-permute-start.12 = (bf16[2,2,17,32,128]{4,3,2,1,0:T(8,128)(2,1)S(1)}, bf16[2,2,17,32,128]{4,3,2,1,0:T(8,128)(2,1)S(1)}, u32[]{:S(2)}, u32[]{:S(2)}) collective-permute-start(bf16[2,2,17,32,128]{4,3,2,1,0:T(8,128)(2,1)S(1)} %collective-permute-done.4.refs_2_), channel_id=1, source_target_pairs={{0,4},{4,0},{1,5},{5,1},{2,6},{6,2},{3,7},{7,3},{8,12},{12,8},{9,1... | collective-permute-start | bytes 1671176 | tf_op jit(solution)/shard_map/ppermute | solution.py:23
  42.4 6.4 %collective-permute-start.13 = (bf16[2,2,17,32,128]{4,3,2,1,0:T(8,128)(2,1)S(1)}, bf16[2,2,17,32,128]{4,3,2,1,0:T(8,128)(2,1)}, u32[]{:S(2)}, u32[]{:S(2)}) collective-permute-start(bf16[2,2,17,32,128]{4,3,2,1,0:T(8,128)(2,1)S(1)} %collective-permute-done.5.refs_3_), channel_id=1, source_target_pairs={{0,4},{4,0},{1,5},{5,1},{2,6},{6,2},{3,7},{7,3},{8,12},{12,8},{9,1... | collective-permute-start | bytes 1671176 | tf_op jit(solution)/shard_map/ppermute | solution.py:23
  48.8 11.8 %collective-permute-start.23 = (bf16[8,1,128,128]{3,2,1,0:T(8,128)(2,1)}, bf16[8,1,128,128]{3,2,1,0:T(8,128)(2,1)S(1)}, u32[]{:S(2)}, u32[]{:S(2)}) collective-permute-start(bf16[8,1,128,128]{3,2,1,0:T(8,128)(2,1)} %own_d_ref.13), channel_id=1, source_target_pairs={{0,4},{4,0},{1,5},{5,1},{2,6},{6,2},{3,7},{7,3},{8,12},{12,8},{9,1... | collective-permute-start | bytes 786440 | tf_op jit(solution)/shard_map/ppermute | solution.py:23
  49.4 11.3 %collective-permute-start.22 = (bf16[8,1,32,128]{3,2,1,0:T(8,128)(2,1)S(1)}, bf16[8,1,32,128]{3,2,1,0:T(8,128)(2,1)S(1)}, u32[]{:S(2)}, u32[]{:S(2)}) collective-permute-start(bf16[8,1,32,128]{3,2,1,0:T(8,128)(2,1)S(1)} %get-tuple-element.100), channel_id=1, source_target_pairs={{0,4},{4,0},{1,5},{5,1},{2,6},{6,2},{3,7},{7,3},{8,12},{12,8},{9,1... | collective-permute-start | bytes 196616 | tf_op jit(solution)/shard_map/ppermute | solution.py:23
  66.4 12.3 %all-to-all-start = ((bf16[16,2,32,128]{3,2,1,0:T(8,128)(2,1)}), bf16[16,2,32,128]{3,2,1,0:T(8,128)(2,1)S(1)}, u32[]{:S(2)}, u32[]{:S(2)}) async-start(bf16[16,2,32,128]{3,2,1,0:T(8,128)(2,1)} %get-tuple-element.60), calls=%async_computation | async-start | bytes 524288 | tf_op jit(solution)/shard_map/all_to_all | solution.py:329
  86.2 12.6 %all-to-all-start.1 = ((bf16[16,2,32,128]{3,2,1,0:T(8,128)(2,1)}), bf16[16,2,32,128]{3,2,1,0:T(8,128)(2,1)S(1)}, u32[]{:S(2)}, u32[]{:S(2)}) async-start(bf16[16,2,32,128]{3,2,1,0:T(8,128)(2,1)} %get-tuple-element.67), calls=%async_computation.1 | async-start | bytes 524288 | tf_op jit(solution)/shard_map/all_to_all | solution.py:329
  108.6 12.5 %all-to-all-start.2 = ((bf16[16,2,32,128]{3,2,1,0:T(8,128)(2,1)}), bf16[16,2,32,128]{3,2,1,0:T(8,128)(2,1)S(1)}, u32[]{:S(2)}, u32[]{:S(2)}) async-start(bf16[16,2,32,128]{3,2,1,0:T(8,128)(2,1)} %get-tuple-element.74), calls=%async_computation.2 | async-start | bytes 524288 | tf_op jit(solution)/shard_map/all_to_all | solution.py:329
  128.8 11.9 %all-to-all-start.3 = ((bf16[16,2,32,128]{3,2,1,0:T(8,128)(2,1)}), bf16[16,2,32,128]{3,2,1,0:T(8,128)(2,1)S(1)}, u32[]{:S(2)}, u32[]{:S(2)}) async-start(bf16[16,2,32,128]{3,2,1,0:T(8,128)(2,1)} %get-tuple-element.81), calls=%async_computation.3 | async-start | bytes 524288 | tf_op jit(solution)/shard_map/all_to_all | solution.py:329
  151.0 11.5 %all-to-all-start.4 = ((bf16[16,2,32,128]{3,2,1,0:T(8,128)(2,1)}), bf16[16,2,32,128]{3,2,1,0:T(8,128)(2,1)S(1)}, u32[]{:S(2)}, u32[]{:S(2)}) async-start(bf16[16,2,32,128]{3,2,1,0:T(8,128)(2,1)} %get-tuple-element.88), calls=%async_computation.4 | async-start | bytes 524288 | tf_op jit(solution)/shard_map/all_to_all | solution.py:329
  169.8 12.4 %all-to-all-start.5 = ((bf16[16,2,32,128]{3,2,1,0:T(8,128)(2,1)}), bf16[16,2,32,128]{3,2,1,0:T(8,128)(2,1)S(1)}, u32[]{:S(2)}, u32[]{:S(2)}) async-start(bf16[16,2,32,128]{3,2,1,0:T(8,128)(2,1)} %get-tuple-element.95), calls=%async_computation.5 | async-start | bytes 524288 | tf_op jit(solution)/shard_map/all_to_all | solution.py:329
  191.1 17.6 %collective-permute-start.42 = (bf16[7,32,128]{2,1,0:T(8,128)(2,1)S(1)}, bf16[7,32,128]{2,1,0:T(8,128)(2,1)S(1)}, u32[]{:S(2)}, u32[]{:S(2)}) collective-permute-start(bf16[7,32,128]{2,1,0:T(8,128)(2,1)S(1)} %get-tuple-element.104), channel_id=1, source_target_pairs={{0,4},{4,0},{1,5},{5,1},{2,6},{6,2},{3,7},{7,3},{8,12},{12,8},{9,1... | collective-permute-start | bytes 172040 | tf_op jit(solution)/shard_map/ppermute | solution.py:23
  (37 other events, 293.5 us)

commit v8 on v7

--- a/solution.py
+++ b/solution.py
@@ -38,8 +38,9 @@
     low, high = jnp.stack([v, near[0]]), jnp.stack(near[1:])
     up, down = pairs(2, lambda i: (i + 1) % 4), pairs(2, lambda i: (i + 3) % 4)
     before_low, after_high = lax.ppermute(low, ROWS, up), lax.ppermute(high, ROWS, down)
-    before_high, after_low = lax.ppermute(high, ROWS, up), lax.ppermute(low, ROWS, down)
-    far = [lax.ppermute(before_low, ROWS, up), lax.ppermute(after_high, ROWS, down)]
+    low_now, high_now, sent_up, sent_down = lax.optimization_barrier((low, high, before_low, after_high))
+    before_high, after_low = lax.ppermute(high_now, ROWS, up), lax.ppermute(low_now, ROWS, down)
+    far = [lax.ppermute(sent_up, ROWS, up), lax.ppermute(sent_down, ROWS, down)]
     return [low, high, before_low, before_high, after_low, after_high] + far
 
 
@@ -48,77 +49,86 @@
 
 
 GROUP = 8
+SUM_LIMIT = 61 * 1024 * 1024
 NEAR = 16
 
 
-def gather_sum(level, code_ref, picks, known, solved_ref, own_ref, other_ref, out_ref, blocks, block_sems, between):
+def pick(sources, first, code, target, sem):
+    if len(sources) == 1:
+        source, which = sources[0]
+        pltpu.make_async_copy(source.at[(code >> 5) & 1, which, code & 31], target, sem).start()
+        return
+    middle = len(sources) // 2
+
+    @pl.when((code >> 6) < first + middle)
+    def _():
+        pick(sources[:middle], first, code, target, sem)
+
+    @pl.when((code >> 6) >= first + middle)
+    def _():
+        pick(sources[middle:], first + middle, code, target, sem)
+
+
+def gather_sum(level, code_ref, pieces, solved_ref, base_ref, own_ref, other_ref, out_ref, scratch, between=None):
+    blocks, block_sems, picked, pick_sem = scratch
     slots = code_ref.shape[1]
     per_row = slots // 2
+    row = code_ref.shape[0] - 1 if code_ref.shape[0] < level else level - 1
     loads = [
         pltpu.make_async_copy(a_ref.at[level - 1, 0], blocks.at[pl.ds(r * per_row, per_row)], block_sems.at[r])
         for r, a_ref in enumerate((own_ref, other_ref))
     ]
     for load in loads:
         load.start()
-    between()
+    sources = [(piece, 0 if i < len(pieces) // 2 else 1) for i, piece in enumerate(pieces)]
+
+    def fetch(k, carry):
+        code = code_ref[row, k]
+        pick(sources, 0, jnp.where((code < 0) | (code >= 1024), 0, code), picked.at[k], pick_sem)
+        return carry
+
+    lax.fori_loop(0, slots, fetch, 0)
+    if between is not None:
+        between()
+    pltpu.make_async_copy(picked, picked, pick_sem).wait()
     for r in range(2):
         loads[r].wait()
-        total = None
+        total = None if base_ref is None else base_ref[r]
         for g in range(r * per_row, (r + 1) * per_row, GROUP):
             xs, group = [], []
             for k in range(g, g + GROUP):
-                code = code_ref[level - 1, k]
+                code = code_ref[row, k]
                 kept = (code >= 0).astype(jnp.float32)
-                picked = picks(k, jnp.clip(code, 0, known - 1))
+                x = picked[k]
                 if solved_ref is not None:
-                    picked = jnp.where(code >= known, solved_ref[jnp.maximum(code - known, 0)], picked)
-                xs.append((picked.astype(jnp.float32) * kept).astype(jnp.bfloat16))
+                    x = jnp.where(code >= 1024, solved_ref[jnp.maximum(code - 1024, 0)], x)
+                xs.append((x.astype(jnp.float32) * kept).astype(jnp.bfloat16))
                 group.append(blocks[k])
             part = nt_dot(jnp.concatenate(xs, axis=1), jnp.concatenate(group, axis=1))
             total = part if total is None else total + part
         out_ref[r] = total
 
 
-def first_kernel(code_ref, *refs):
-    sources, refs = refs[:-9], refs[-9:]
-    own_ref, other_ref, out_ref, store_ref, blocks, block_sems, pack_sems, packed, store_sem = refs
-    packs, start = [], 0
-    for i, source in enumerate(sources):
-        which = 0 if i < len(sources) // 2 else 1
-        for part in range(source.shape[0]):
-            target = packed.at[pl.ds(start, source.shape[2])]
-            packs.append(pltpu.make_async_copy(source.at[part, which], target, pack_sems.at[len(packs)]))
-            start += source.shape[2]
-    keep = pltpu.make_async_copy(packed, store_ref.at[pl.ds(0, start)], store_sem)
+def first_kernel(count, based, code_ref, *refs):
+    pieces, refs = refs[:count], refs[count:]
+    base_ref = refs[0] if based else None
+    own_ref, other_ref, out_ref = refs[based : based + 3]
+    gather_sum(1, code_ref, pieces, None, base_ref, own_ref, other_ref, out_ref, refs[based + 3 :])
+
+
+def old_kernel(level, count, code_ref, fresh_ref, *refs):
+    pieces, refs = refs[:count], refs[count:]
+    solved, refs = refs[: level - 2], refs[level - 2 :]
+    own_ref, other_ref, out_ref, list_ref, near_ref = refs[:5]
+    scratch = refs[5:9]
+    blocks = scratch[0]
+    solved_ref = refs[9] if solved else None
 
     def between():
-        for pack in packs:
-            pack.start()
-        for pack in packs:
-            pack.wait()
-        keep.start()
-
-    picks = lambda k, code: packed[code]
-    gather_sum(1, code_ref, picks, start, None, own_ref, other_ref, out_ref, blocks, block_sems, between)
-    keep.wait()
-
-
-def old_kernel(level, known, code_ref, fresh_ref, store_ref, *refs):
-    solved, refs = refs[: level - 2], refs[level - 2 :]
-    own_ref, other_ref, out_ref, list_ref, near_ref, blocks, block_sems, picked, pick_sem = refs[:9]
-    solved_ref = refs[9] if solved else None
-    slots = code_ref.shape[1]
-
-    def between():
-        for k in range(slots):
-            place = jnp.clip(code_ref[level - 1, k], 0, known - 1)
-            pltpu.make_async_copy(store_ref.at[place], picked.at[k], pick_sem).start()
         for i, one in enumerate(solved):
             solved_ref[i * one.shape[0] : (i + 1) * one.shape[0]] = one[...]
-        pltpu.make_async_copy(store_ref.at[pl.ds(0, slots)], picked, pick_sem).wait()
-
-    picks = lambda k, code: picked[k]
-    gather_sum(level, code_ref, picks, known, solved_ref, own_ref, other_ref, out_ref, blocks, block_sems, between)
+
+    gather_sum(level, code_ref, pieces, solved_ref, None, own_ref, other_ref, out_ref, scratch, between)
 
     def note(slot, count):
         code = fresh_ref[level - 1, slot]
@@ -136,8 +146,8 @@
     list_ref[0] = lax.fori_loop(0, fresh_ref.shape[1], note, jnp.int32(0))
 
 
-def sum_call(kernel, codes, sources, source_spaces, own, other, outs, out_spaces, extra, name, limit):
-    slots, (rhs_cols, block) = codes[0].shape[1], sources[0].shape[-2:]
+def sum_call(kernel, codes, sources, source_spaces, own, other, one, outs, out_spaces, extra, name):
+    slots, (rhs_cols, block) = codes[0].shape[1], one
     return pl.pallas_call(
         kernel,
         out_shape=[jax.ShapeDtypeStruct((2, rhs_cols, block), jnp.float32)] + outs,
@@ -145,8 +155,14 @@
         + [pl.BlockSpec(memory_space=space) for space in source_spaces]
         + [pl.BlockSpec(memory_space=pltpu.HBM)] * 2,
         out_specs=[pl.BlockSpec(memory_space=space) for space in [pltpu.VMEM] + out_spaces],
-        scratch_shapes=[pltpu.VMEM((slots, block, block), jnp.bfloat16), pltpu.SemaphoreType.DMA((2,))] + extra,
-        compiler_params=pltpu.CompilerParams(vmem_limit_bytes=limit),
+        scratch_shapes=[
+            pltpu.VMEM((slots, block, block), jnp.bfloat16),
+            pltpu.SemaphoreType.DMA((2,)),
+            pltpu.VMEM((slots, rhs_cols, block), jnp.bfloat16),
+            pltpu.SemaphoreType.DMA,
+        ]
+        + extra,
+        compiler_params=pltpu.CompilerParams(vmem_limit_bytes=SUM_LIMIT),
         cost_estimate=pl.CostEstimate(
             flops=2 * slots * rhs_cols * block * block,
             bytes_accessed=slots * block * (block + 2 * rhs_cols) * 4,
@@ -156,33 +172,27 @@
     )(*codes, *sources, own, other)
 
 
-def first_sum(code, sources, own, other):
-    one = sources[0].shape[3:]
-    parts = sum(v.shape[0] for v in sources)
-    known = parts * sources[0].shape[2]
-    store = jax.ShapeDtypeStruct((2048,) + one, jnp.bfloat16)
-    extra = [
-        pltpu.SemaphoreType.DMA((parts,)),
-        pltpu.VMEM((known,) + one, jnp.bfloat16),
-        pltpu.SemaphoreType.DMA,
-    ]
-    spaces = [pl.ANY] * len(sources)
-    return sum_call(first_kernel, [code], sources, spaces, own, other, [store], [pltpu.HBM], extra, "first_sum", 61 * 1024 * 1024)
-
-
-def old_sum(level, known, code, fresh, store, solved, own, other):
-    one = store.shape[1:]
+def first_sum(code, pieces, base, own, other):
+    spaces = [pl.ANY] * len(pieces) + [pltpu.VMEM] * len(base)
+    kernel = functools.partial(first_kernel, len(pieces), len(base))
+    one = pieces[0].shape[-2:]
+    return sum_call(kernel, [code], [*pieces, *base], spaces, own, other, one, [], [], [], "first_sum")[0]
+
+
+def old_sum(level, code, fresh, pieces, solved, own, other):
+    one = pieces[0].shape[-2:]
     outs = [
         jax.ShapeDtypeStruct((code.shape[1] + 1,), jnp.int32),
         jax.ShapeDtypeStruct((NEAR, one[1], one[1]), jnp.bfloat16),
     ]
-    kernel = functools.partial(old_kernel, level, known)
-    extra = [pltpu.VMEM((code.shape[1],) + one, jnp.bfloat16), pltpu.SemaphoreType.DMA]
+    kernel = functools.partial(old_kernel, level, len(pieces))
+    extra = []
     if solved:
         extra.append(pltpu.VMEM((sum(v.shape[0] for v in solved),) + one, jnp.bfloat16))
-    spaces = [pl.ANY] + [pltpu.VMEM] * len(solved)
+    spaces = [pl.ANY] * len(pieces) + [pltpu.VMEM] * len(solved)
     out_spaces = [pltpu.SMEM, pltpu.VMEM]
-    return sum_call(kernel, [code, fresh], [store] + solved, spaces, own, other, outs, out_spaces, extra, "old_sum", VMEM_LIMIT)
+    sources = [*pieces, *solved]
+    return sum_call(kernel, [code, fresh], sources, spaces, own, other, one, outs, out_spaces, extra, "old_sum")
 
 
 def fresh_kernel(level, list_ref, old_ref, x_ref, near_ref, own_ref, other_ref, out_ref, far, sem):
@@ -242,14 +252,13 @@
         solved = nt_dot(reduced, d_ref[level, 0]).astype(jnp.bfloat16)
         out_ref[r] = solved
         if refs:
-            refs[1][core ^ r] = solved
+            for i in range(refs[1].shape[0]):
+                refs[1][i, core ^ r] = solved
     if refs:
-        all_ref, both, sems = refs
-        sends = [pltpu.make_async_copy(both, all_ref.at[i], sems.at[i]) for i in range(all_ref.shape[0])]
-        for send in sends:
-            send.start()
-        for send in sends:
-            send.wait()
+        all_ref, copies, sem = refs
+        send = pltpu.make_async_copy(copies, all_ref, sem)
+        send.start()
+        send.wait()
 
 
 def solve_level(level, partials, rhs, own_d, other_d, copies):
@@ -259,7 +268,7 @@
     if copies:
         out_shape.append(jax.ShapeDtypeStruct((copies, 2, rhs_cols, block), jnp.bfloat16))
         out_specs.append(pl.BlockSpec(memory_space=pltpu.HBM))
-        scratch = [pltpu.VMEM((2, rhs_cols, block), jnp.bfloat16), pltpu.SemaphoreType.DMA((copies,))]
+        scratch = [pltpu.VMEM((copies, 2, rhs_cols, block), jnp.bfloat16), pltpu.SemaphoreType.DMA]
     return pl.pallas_call(
         functools.partial(solve_kernel, level),
         out_shape=out_shape,
@@ -304,19 +313,32 @@
     src_z, src_y, src_core = row // 8, (row // 2) % 4, row % 2
     each = outer_each + 1
     away = jnp.where(src_core == 0, src_y - y, src_z - z) % 4
-    part = jnp.where(away == 3, 1, jnp.where(away == 1, 2, jnp.where(away == 2, 3, 0))) * 4
-    part = part + jnp.where(src_core == 0, src_z ^ z, src_y ^ y) + jnp.where(src_core == core, 0, 16)
-    known_place = part * each + member
+    part = jnp.where(src_core == 0, src_z ^ z, src_y ^ y)
+    side = jnp.where(away == 3, 1, jnp.where(away == 1, 2, jnp.where(away == 2, 3, 0)))
+    mine = src_core == core
+    piece = side * 2 + part // 2
+    in_piece = (part % 2) * 32 + member
+    known_code = (piece + jnp.where(mine, 0, 8)) * 64 + in_piece
     level_of = jnp.maximum(index - outer, 0) // 32
     this = jnp.arange(levels - 1)[:, None, None]
     is_fresh = (level_of == this) & (level_of > 0)
     place_level = (index - outer) % 32
-    old_code = jnp.where(level_of == 0, known_place, 32 * each + (level_of - 1) * 32 + place_level)
+    old_code = jnp.where(level_of == 0, known_code, 1024 + (level_of - 1) * 32 + place_level)
     old_code = jnp.where(keep & ~is_fresh, old_code, -1).reshape(levels - 1, -1)
     fresh_code = jnp.where(keep & is_fresh, place_level, -1).reshape(levels - 1, -1)
 
     own_rows, other_rows = [], []
-    value, store = first_sum(old_code, pieces, off_blocks, off_other)
+    steps = ((0, 1, 2, 5), (3, 4, 6, 7))
+    early_code, late_code = (
+        sum(jnp.where(keep & (piece == p), (n + jnp.where(mine, 0, 4)) * 64 + in_piece + 1, 0) for n, p in enumerate(some))[
+            0
+        ].reshape(1, -1)
+        - 1
+        for some in steps
+    )
+    early_pieces, late_pieces = ([pieces[p] for p in some] + [pieces[8 + p] for p in some] for some in steps)
+    early = first_sum(early_code, early_pieces, [], off_blocks, off_other)
+    value = first_sum(late_code, late_pieces, [early], off_blocks, off_other)
     solved_levels = []
     for level in range(1, levels):
         partials = [value] + [lax.ppermute(value, "x", xor_pairs(4, k)) for k in (1, 2, 3)]
@@ -328,7 +350,7 @@
             next_fresh, sent = lax.optimization_barrier((fresh_code, outs[1]))
             solved = lax.all_to_all(sent, ("z", "y"), 0, 0).reshape(32, half, block)
             old, listed, near = old_sum(
-                level + 1, 32 * each, old_code, next_fresh, store, solved_levels, off_blocks, off_other
+                level + 1, old_code, next_fresh, pieces, solved_levels, off_blocks, off_other
             )
             value = fresh_sum(level + 1, listed, solved, old, near, off_blocks, off_other)
             solved_levels = solved_levels + [solved]

time: 211 us -> 242 us (1.15)
  local copies, waits for them, and re-layouts: 3.33 us -> 19.6 us
  Pallas kernels: 52.8 us -> 67.8 us
  waiting for transfers between devices: 50.4 us -> 42.1 us
  starting transfers between devices: 98.2 us -> 105 us
    pallas_call x7 -> x8, Pallas kernels: 40.3 us -> 56.8 us  [sum_call(): pl.pallas_call(kernel, out_shape=[jax.ShapeDtypeStruct((2, rhs_cols, bloc...]
    unnamed x31 -> x71, local copies, waits for them, and re-layouts: 2.36 us -> 17.4 us
    all_to_all x6, starting transfers between devices: 27.9 us -> 41.3 us  [on_device(): solved = lax.all_to_all(sent, ('z', 'y'), 0, 0).reshape(32, half, block)]
    all_to_all x6, waiting for transfers between devices: 11.4 us -> 0.21 us  [on_device(): solved = lax.all_to_all(sent, ('z', 'y'), 0, 0).reshape(32, half, block)]
    ppermute x13, starting transfers between devices: 28.9 us -> 22.7 us  [swap_cores(): return lax.ppermute(v, 'core', xor_pairs(2, 1))]
    ppermute x1, waiting for transfers between devices: 0.65 us -> 3.31 us  [gather_parts(): lax.ppermute(high, ROWS, down)]
  transfers between devices with their start and end apart: 49 -> 49, of which waited for: 27 -> 23; matrix products, arithmetic and copies ran while one was open for 1% -> 2% of each run, Pallas kernels for 19% -> 24%
where the time goes in v8:
time: 242 us; the launch traced here: 240 us
  starting transfers between devices  105 us (43%)
  Pallas kernels  67.8 us (28%)
  waiting for transfers between devices  42.1 us (17%)
  local copies, waits for them, and re-layouts  19.6 us (8%)
  other arithmetic  3.46 us (1%)
    pallas_call x8, Pallas kernels, sum_call(): pl.pallas_call(kernel, out_shape=[jax.ShapeDtypeStruct((2, rhs_cols, bloc...  56.8 us
    all_to_all x6, starting transfers between devices, on_device(): solved = lax.all_to_all(sent, ('z', 'y'), 0, 0).reshape(32, half, block)  41.3 us
    ppermute x21, starting transfers between devices, on_device(): lax.ppermute(value, 'x', xor_pairs(4, k))  27.5 us
    ppermute x13, starting transfers between devices, swap_cores(): return lax.ppermute(v, 'core', xor_pairs(2, 1))  22.7 us
    ppermute x21, waiting for transfers between devices, on_device(): lax.ppermute(value, 'x', xor_pairs(4, k))  19.8 us
    unnamed x71, local copies, waits for them, and re-layouts  17.4 us
    ppermute x3, waiting for transfers between devices, gather_parts(): lax.ppermute(v, ROWS, pairs(1, lambda i, k=k: i ^ k))  6.44 us
    pallas_call x7, Pallas kernels, solve_level(): pl.pallas_call(functools.partial(solve_kernel, level), out_shape=out_shap...  5.5 us
  transfers between devices with their start and end apart: 49, of which 23 were waited for; matrix products, arithmetic and copies ran while one was open for 2% of the time, Pallas kernels for 24%

profile of v8, /device:TPU:1, one launch (start us, length us, event | category | flops | bytes accessed | tf_op | source)
XLA Modules:
  0.0 239.7 jit_solution(12662418501940264174)
XLA Ops:
  3.5 3.0 %collective-permute-start.2 = (bf16[2,17,32,128]{3,2,1,0:T(8,128)(2,1)S(1)}, bf16[2,17,32,128]{3,2,1,0:T(8,128)(2,1)S(1)}, u32[]{:S(2)}, u32[]{:S(2)}) collective-permute-start(bf16[2,17,32,128]{3,2,1,0:T(8,128)(2,1)S(1)} %pad_maximum_fusion.2), channel_id=1, source_target_pairs={{0,64},{4,20},{8,72},{12,28},{16,80},{20,4},{24,88},{28,12},{32,96... | collective-permute-start | bytes 835592 | tf_op jit(solution)/shard_map/ppermute | solution.py:37
  7.2 3.5 %collective-permute-done.2 = bf16[2,17,32,128]{3,2,1,0:T(8,128)(2,1)S(1)} collective-permute-done((bf16[2,17,32,128]{3,2,1,0:T(8,128)(2,1)S(1)}, bf16[2,17,32,128]{3,2,1,0:T(8,128)(2,1)S(1)}, u32[]{:S(2)}, u32[]{:S(2)}) %collective-permute-start.2) | collective-permute-done | bytes 278560 | tf_op jit(solution)/shard_map/ppermute | solution.py:37
  10.7 3.0 %collective-permute-done.3 = bf16[2,17,32,128]{3,2,1,0:T(8,128)(2,1)S(1)} collective-permute-done((bf16[2,17,32,128]{3,2,1,0:T(8,128)(2,1)S(1)}, bf16[2,17,32,128]{3,2,1,0:T(8,128)(2,1)S(1)}, u32[]{:S(2)}, u32[]{:S(2)}) %collective-permute-start.3) | collective-permute-done | bytes 278560 | tf_op jit(solution)/shard_map/ppermute | solution.py:37
  13.7 3.9 %collective-permute-start.5 = (bf16[2,2,17,32,128]{4,3,2,1,0:T(8,128)(2,1)S(1)}, bf16[2,2,17,32,128]{4,3,2,1,0:T(8,128)(2,1)S(1)}, u32[]{:S(2)}, u32[]{:S(2)}) collective-permute-start(bf16[2,2,17,32,128]{4,3,2,1,0:T(8,128)(2,1)S(1)} %pad_maximum_fusion.1.refs_1_), channel_id=1, source_target_pairs={{0,24},{4,100},{8,0},{12,108},{16,8},{20,116},{24,16},{28,124},{32... | collective-permute-start | bytes 1671176 | tf_op jit(solution)/shard_map/ppermute | solution.py:40
  20.8 3.3 %collective-permute-done.5.refs_3_.refs_5_ = bf16[2,2,17,32,128]{4,3,2,1,0:T(8,128)(2,1)S(1)} collective-permute-done((bf16[2,2,17,32,128]{4,3,2,1,0:T(8,128)(2,1)S(1)}, bf16[2,2,17,32,128]{4,3,2,1,0:T(8,128)(2,1)S(1)}, u32[]{:S(2)}, u32[]{:S(2)}) %collective-permute-start.5) | collective-permute-done | bytes 557088 | tf_op jit(solution)/shard_map/ppermute | solution.py:40
  37.3 3.4 %collective-permute-done.6.refs_0_.refs_3_ = bf16[2,2,17,32,128]{4,3,2,1,0:T(8,128)(2,1)} collective-permute-done((bf16[2,2,17,32,128]{4,3,2,1,0:T(8,128)(2,1)S(1)}, bf16[2,2,17,32,128]{4,3,2,1,0:T(8,128)(2,1)}, u32[]{:S(2)}, u32[]{:S(2)}) %collective-permute-start.6) | collective-permute-done | bytes 557088 | tf_op jit(solution)/shard_map/ppermute | solution.py:42
  41.8 4.8 %collective-permute-done.8.refs_2_.refs_6_ = bf16[2,2,17,32,128]{4,3,2,1,0:T(8,128)(2,1)} collective-permute-done((bf16[2,2,17,32,128]{4,3,2,1,0:T(8,128)(2,1)S(1)}, bf16[2,2,17,32,128]{4,3,2,1,0:T(8,128)(2,1)}, u32[]{:S(2)}, u32[]{:S(2)}) %collective-permute-start.8) | collective-permute-done | bytes 557088 | tf_op jit(solution)/shard_map/ppermute | solution.py:43
  50.1 5.5 %first_sum.2.refs_8_ = f32[2,32,128]{2,1,0:T(8,128)} custom-call(s32[1,64]{1,0:T(1,128)} %sub.89.code_ref, bf16[2,2,17,32,128]{4,3,2,1,0:T(8,128)(2,1)} %copy-done.26, bf16[2,2,17,32,128]{4,3,2,1,0:T(8,128)(2,1)} %copy-done.25, bf16[2,2,17,32,128]{4,3,2,1,0:T(8,128)(2,1)} %copy-done.28, bf16[2,2,17,32,128]{4,3,2,1,0:T(8,128)(2,1)} %copy-done.27, ...), custom_call_target="tpu_custom_call" | custom-call | flops 67108864 | bytes 6291456 | tf_op jit(solution)/shard_map/first_sum/pallas_call | solution.py:151
  55.6 5.4 %first_sum.3.p0 = f32[2,32,128]{2,1,0:T(8,128)} custom-call(s32[1,64]{1,0:T(1,128)} %sub.86.code_ref, bf16[2,2,17,32,128]{4,3,2,1,0:T(8,128)(2,1)} %collective-permute-done.6.refs_0_.refs_3_, bf16[2,2,17,32,128]{4,3,2,1,0:T(8,128)(2,1)} %collective-permute-done.7.refs_1_.refs_4_, bf16[2,2,17,32,128]{4,3,2,1,0:T(8,128)(2,1)} %collective-permute-done.8.refs_2_.refs_6_, ...), custom_call_target="tpu_custom_call" | custom-call | flops 67108864 | bytes 6291456 | tf_op jit(solution)/shard_map/first_sum/pallas_call | solution.py:151
  70.7 7.7 %all-to-all-start = ((bf16[16,2,32,128]{3,2,1,0:T(8,128)(2,1)}), bf16[16,2,32,128]{3,2,1,0:T(8,128)(2,1)S(1)}, u32[]{:S(2)}, u32[]{:S(2)}) async-start(bf16[16,2,32,128]{3,2,1,0:T(8,128)(2,1)} %get-tuple-element.64), calls=%async_computation | async-start | bytes 524288 | tf_op jit(solution)/shard_map/all_to_all | solution.py:351
  78.4 7.4 %old_sum.6 = (f32[2,32,128]{2,1,0:T(8,128)}, s32[65]{0:T(128)}, bf16[16,128,128]{2,1,0:T(8,128)(2,1)}) custom-call(s32[7,64]{1,0:T(8,128)} %get-tuple-element.134.code_ref, s32[7,64]{1,0:T(8,128)} %get-tuple-element.96.fresh_ref, bf16[2,2,17,32,128]{4,3,2,1,0:T(8,128)(2,1)} %copy-done.26, bf16[2,2,17,32,128]{4,3,2,1,0:T(8,128)(2,1)} %copy-done.25, ...), custom_call_target="tpu_custom_call" | custom-call | flops 67108864 | bytes 6291456 | tf_op jit(solution)/shard_map/old_sum/pallas_call | solution.py:151
  95.9 6.6 %all-to-all-start.1 = ((bf16[16,2,32,128]{3,2,1,0:T(8,128)(2,1)}), bf16[16,2,32,128]{3,2,1,0:T(8,128)(2,1)S(1)}, u32[]{:S(2)}, u32[]{:S(2)}) async-start(bf16[16,2,32,128]{3,2,1,0:T(8,128)(2,1)} %get-tuple-element.71), calls=%async_computation.1 | async-start | bytes 524288 | tf_op jit(solution)/shard_map/all_to_all | solution.py:351
  102.5 7.5 %old_sum.7 = (f32[2,32,128]{2,1,0:T(8,128)}, s32[65]{0:T(128)}, bf16[16,128,128]{2,1,0:T(8,128)(2,1)}) custom-call(s32[7,64]{1,0:T(8,128)} %get-tuple-element.134.code_ref, s32[7,64]{1,0:T(8,128)} %get-tuple-element.96.fresh_ref, bf16[2,2,17,32,128]{4,3,2,1,0:T(8,128)(2,1)} %copy-done.26, bf16[2,2,17,32,128]{4,3,2,1,0:T(8,128)(2,1)} %copy-done.25, ...), custom_call_target="tpu_custom_call" | custom-call | flops 67108864 | bytes 6291456 | tf_op jit(solution)/shard_map/old_sum/pallas_call | solution.py:151
  113.8 3.1 %collective-permute-start.28 = (f32[2,32,128]{2,1,0:T(8,128)S(1)}, f32[2,32,128]{2,1,0:T(8,128)S(1)}, u32[]{:S(2)}, u32[]{:S(2)}) collective-permute-start(f32[2,32,128]{2,1,0:T(8,128)S(1)} %fresh_sum.7.p0), channel_id=1, source_target_pairs={{0,2},{1,3},{2,0},{3,1},{4,6},{5,7},{6,4},{7,5},{8,10},{9,11},{10,... | collective-permute-start | bytes 98312 | tf_op jit(solution)/shard_map/ppermute | solution.py:344
  121.8 7.0 %all-to-all-start.2 = ((bf16[16,2,32,128]{3,2,1,0:T(8,128)(2,1)}), bf16[16,2,32,128]{3,2,1,0:T(8,128)(2,1)S(1)}, u32[]{:S(2)}, u32[]{:S(2)}) async-start(bf16[16,2,32,128]{3,2,1,0:T(8,128)(2,1)} %get-tuple-element.78), calls=%async_computation.2 | async-start | bytes 524288 | tf_op jit(solution)/shard_map/all_to_all | solution.py:351
  128.8 7.6 %old_sum.8 = (f32[2,32,128]{2,1,0:T(8,128)}, s32[65]{0:T(128)}, bf16[16,128,128]{2,1,0:T(8,128)(2,1)}) custom-call(s32[7,64]{1,0:T(8,128)} %get-tuple-element.134.code_ref, s32[7,64]{1,0:T(8,128)} %get-tuple-element.96.fresh_ref, bf16[2,2,17,32,128]{4,3,2,1,0:T(8,128)(2,1)} %copy-done.26, bf16[2,2,17,32,128]{4,3,2,1,0:T(8,128)(2,1)} %copy-done.25, ...), custom_call_target="tpu_custom_call" | custom-call | flops 67108864 | bytes 6291456 | tf_op jit(solution)/shard_map/old_sum/pallas_call | solution.py:151
  146.7 6.7 %all-to-all-start.3 = ((bf16[16,2,32,128]{3,2,1,0:T(8,128)(2,1)}), bf16[16,2,32,128]{3,2,1,0:T(8,128)(2,1)S(1)}, u32[]{:S(2)}, u32[]{:S(2)}) async-start(bf16[16,2,32,128]{3,2,1,0:T(8,128)(2,1)} %get-tuple-element.85), calls=%async_computation.3 | async-start | bytes 524288 | tf_op jit(solution)/shard_map/all_to_all | solution.py:351
  153.4 7.7 %old_sum.9 = (f32[2,32,128]{2,1,0:T(8,128)}, s32[65]{0:T(128)}, bf16[16,128,128]{2,1,0:T(8,128)(2,1)}) custom-call(s32[7,64]{1,0:T(8,128)} %get-tuple-element.134.code_ref, s32[7,64]{1,0:T(8,128)} %get-tuple-element.96.fresh_ref, bf16[2,2,17,32,128]{4,3,2,1,0:T(8,128)(2,1)} %copy-done.26, bf16[2,2,17,32,128]{4,3,2,1,0:T(8,128)(2,1)} %copy-done.25, ...), custom_call_target="tpu_custom_call" | custom-call | flops 67108864 | bytes 6291456 | tf_op jit(solution)/shard_map/old_sum/pallas_call | solution.py:151
  164.5 3.1 %collective-permute-start.34 = (f32[2,32,128]{2,1,0:T(8,128)S(1)}, f32[2,32,128]{2,1,0:T(8,128)S(1)}, u32[]{:S(2)}, u32[]{:S(2)}) collective-permute-start(f32[2,32,128]{2,1,0:T(8,128)S(1)} %fresh_sum.9.p0), channel_id=1, source_target_pairs={{0,2},{1,3},{2,0},{3,1},{4,6},{5,7},{6,4},{7,5},{8,10},{9,11},{10,... | collective-permute-start | bytes 98312 | tf_op jit(solution)/shard_map/ppermute | solution.py:344
  172.5 6.8 %all-to-all-start.4 = ((bf16[16,2,32,128]{3,2,1,0:T(8,128)(2,1)}), bf16[16,2,32,128]{3,2,1,0:T(8,128)(2,1)S(1)}, u32[]{:S(2)}, u32[]{:S(2)}) async-start(bf16[16,2,32,128]{3,2,1,0:T(8,128)(2,1)} %get-tuple-element.92), calls=%async_computation.4 | async-start | bytes 524288 | tf_op jit(solution)/shard_map/all_to_all | solution.py:351
  179.3 7.8 %old_sum.10 = (f32[2,32,128]{2,1,0:T(8,128)}, s32[65]{0:T(128)}, bf16[16,128,128]{2,1,0:T(8,128)(2,1)}) custom-call(s32[7,64]{1,0:T(8,128)} %get-tuple-element.134.code_ref, s32[7,64]{1,0:T(8,128)} %get-tuple-element.96.fresh_ref, bf16[2,2,17,32,128]{4,3,2,1,0:T(8,128)(2,1)} %copy-done.26, bf16[2,2,17,32,128]{4,3,2,1,0:T(8,128)(2,1)} %copy-done.25, ...), custom_call_target="tpu_custom_call" | custom-call | flops 67108864 | bytes 6291456 | tf_op jit(solution)/shard_map/old_sum/pallas_call | solution.py:151
  197.9 6.5 %all-to-all-start.5 = ((bf16[16,2,32,128]{3,2,1,0:T(8,128)(2,1)}), bf16[16,2,32,128]{3,2,1,0:T(8,128)(2,1)S(1)}, u32[]{:S(2)}, u32[]{:S(2)}) async-start(bf16[16,2,32,128]{3,2,1,0:T(8,128)(2,1)} %get-tuple-element.99), calls=%async_computation.5 | async-start | bytes 524288 | tf_op jit(solution)/shard_map/all_to_all | solution.py:351
  204.4 7.9 %old_sum.11 = (f32[2,32,128]{2,1,0:T(8,128)}, s32[65]{0:T(128)}, bf16[16,128,128]{2,1,0:T(8,128)(2,1)}) custom-call(s32[7,64]{1,0:T(8,128)} %get-tuple-element.134.code_ref, s32[7,64]{1,0:T(8,128)} %get-tuple-element.96.fresh_ref, bf16[2,2,17,32,128]{4,3,2,1,0:T(8,128)(2,1)} %copy-done.26, bf16[2,2,17,32,128]{4,3,2,1,0:T(8,128)(2,1)} %copy-done.25, ...), custom_call_target="tpu_custom_call" | custom-call | flops 67108864 | bytes 6291456 | tf_op jit(solution)/shard_map/old_sum/pallas_call | solution.py:151
  222.9 15.1 %collective-permute-start.42 = (bf16[7,32,128]{2,1,0:T(8,128)(2,1)S(1)}, bf16[7,32,128]{2,1,0:T(8,128)(2,1)S(1)}, u32[]{:S(2)}, u32[]{:S(2)}) collective-permute-start(bf16[7,32,128]{2,1,0:T(8,128)(2,1)S(1)} %get-tuple-element.116), channel_id=1, source_target_pairs={{0,4},{4,0},{1,5},{5,1},{2,6},{6,2},{3,7},{7,3},{8,12},{12,8},{9,1... | collective-permute-start | bytes 172040 | tf_op jit(solution)/shard_map/ppermute | solution.py:23
  (187 shorter events, 94.8 us)
Async XLA Ops:
  2.0 46.4 %collective-permute-start.18 = (bf16[7,1,32,128,128]{4,3,2,1,0:T(8,128)(2,1)}, bf16[7,1,32,128,128]{4,3,2,1,0:T(8,128)(2,1)}, u32[]{:S(2)}, u32[]{:S(2)}) collective-permute-start(bf16[7,1,32,128,128]{4,3,2,1,0:T(8,128)(2,1)} %own_ref.11), channel_id=1, source_target_pairs={{0,4},{4,0},{1,5},{5,1},{2,6},{6,2},{3,7},{7,3},{8,12},{12,8},{9,1... | collective-permute-start | bytes 22020104 | tf_op jit(solution)/shard_map/ppermute | solution.py:23
  3.5 7.2 %collective-permute-start.2 = (bf16[2,17,32,128]{3,2,1,0:T(8,128)(2,1)S(1)}, bf16[2,17,32,128]{3,2,1,0:T(8,128)(2,1)S(1)}, u32[]{:S(2)}, u32[]{:S(2)}) collective-permute-start(bf16[2,17,32,128]{3,2,1,0:T(8,128)(2,1)S(1)} %pad_maximum_fusion.2), channel_id=1, source_target_pairs={{0,64},{4,20},{8,72},{12,28},{16,80},{20,4},{24,88},{28,12},{32,96... | collective-permute-start | bytes 835592 | tf_op jit(solution)/shard_map/ppermute | solution.py:37
  7.2 10.4 %collective-permute-start.1 = (bf16[2,17,32,128]{3,2,1,0:T(8,128)(2,1)S(1)}, bf16[2,17,32,128]{3,2,1,0:T(8,128)(2,1)S(1)}, u32[]{:S(2)}, u32[]{:S(2)}) collective-permute-start(bf16[2,17,32,128]{3,2,1,0:T(8,128)(2,1)S(1)} %pad_maximum_fusion.2), channel_id=1, source_target_pairs={{0,32},{4,12},{8,40},{12,4},{16,48},{20,28},{24,56},{28,20},{32,0}... | collective-permute-start | bytes 835592 | tf_op jit(solution)/shard_map/ppermute | solution.py:37
  13.7 10.4 %collective-permute-start.5 = (bf16[2,2,17,32,128]{4,3,2,1,0:T(8,128)(2,1)S(1)}, bf16[2,2,17,32,128]{4,3,2,1,0:T(8,128)(2,1)S(1)}, u32[]{:S(2)}, u32[]{:S(2)}) collective-permute-start(bf16[2,2,17,32,128]{4,3,2,1,0:T(8,128)(2,1)S(1)} %pad_maximum_fusion.1.refs_1_), channel_id=1, source_target_pairs={{0,24},{4,100},{8,0},{12,108},{16,8},{20,116},{24,16},{28,124},{32... | collective-permute-start | bytes 1671176 | tf_op jit(solution)/shard_map/ppermute | solution.py:40
  17.7 10.0 %collective-permute-start.4 = (bf16[2,2,17,32,128]{4,3,2,1,0:T(8,128)(2,1)S(1)}, bf16[2,2,17,32,128]{4,3,2,1,0:T(8,128)(2,1)S(1)}, u32[]{:S(2)}, u32[]{:S(2)}) collective-permute-start(bf16[2,2,17,32,128]{4,3,2,1,0:T(8,128)(2,1)S(1)} %pad_maximum_fusion.refs_0_), channel_id=1, source_target_pairs={{0,8},{4,36},{8,16},{12,44},{16,24},{20,52},{24,0},{28,60},{32,40}... | collective-permute-start | bytes 1671176 | tf_op jit(solution)/shard_map/ppermute | solution.py:40
  17.8 11.5 %collective-permute-start.15 = (bf16[2,2,17,32,128]{4,3,2,1,0:T(8,128)(2,1)S(1)}, bf16[2,2,17,32,128]{4,3,2,1,0:T(8,128)(2,1)S(1)}, u32[]{:S(2)}, u32[]{:S(2)}) collective-permute-start(bf16[2,2,17,32,128]{4,3,2,1,0:T(8,128)(2,1)S(1)} %pad_maximum_fusion.1.refs_1_), channel_id=1, source_target_pairs={{0,4},{4,0},{1,5},{5,1},{2,6},{6,2},{3,7},{7,3},{8,12},{12,8},{9,1... | collective-permute-start | bytes 1671176 | tf_op jit(solution)/shard_map/ppermute | solution.py:23
  20.6 11.5 %collective-permute-start.14 = (bf16[2,2,17,32,128]{4,3,2,1,0:T(8,128)(2,1)S(1)}, bf16[2,2,17,32,128]{4,3,2,1,0:T(8,128)(2,1)S(1)}, u32[]{:S(2)}, u32[]{:S(2)}) collective-permute-start(bf16[2,2,17,32,128]{4,3,2,1,0:T(8,128)(2,1)S(1)} %pad_maximum_fusion.refs_0_), channel_id=1, source_target_pairs={{0,4},{4,0},{1,5},{5,1},{2,6},{6,2},{3,7},{7,3},{8,12},{12,8},{9,1... | collective-permute-start | bytes 1671176 | tf_op jit(solution)/shard_map/ppermute | solution.py:23
  24.1 10.2 %collective-permute-start.17 = (bf16[2,2,17,32,128]{4,3,2,1,0:T(8,128)(2,1)S(1)}, bf16[2,2,17,32,128]{4,3,2,1,0:T(8,128)(2,1)}, u32[]{:S(2)}, u32[]{:S(2)}) collective-permute-start(bf16[2,2,17,32,128]{4,3,2,1,0:T(8,128)(2,1)S(1)} %collective-permute-done.5.refs_3_.refs_5_), channel_id=1, source_target_pairs={{0,4},{4,0},{1,5},{5,1},{2,6},{6,2},{3,7},{7,3},{8,12},{12,8},{9,1... | collective-permute-start | bytes 1671176 | tf_op jit(solution)/shard_map/ppermute | solution.py:23
  30.1 10.5 %collective-permute-start.6 = (bf16[2,2,17,32,128]{4,3,2,1,0:T(8,128)(2,1)S(1)}, bf16[2,2,17,32,128]{4,3,2,1,0:T(8,128)(2,1)}, u32[]{:S(2)}, u32[]{:S(2)}) collective-permute-start(bf16[2,2,17,32,128]{4,3,2,1,0:T(8,128)(2,1)S(1)} %pad_maximum_fusion.1.refs_1_), channel_id=1, source_target_pairs={{0,8},{4,36},{8,16},{12,44},{16,24},{20,52},{24,0},{28,60},{32,40}... | collective-permute-start | bytes 1671176 | tf_op jit(solution)/shard_map/ppermute | solution.py:42
  32.1 9.6 %collective-permute-start.7 = (bf16[2,2,17,32,128]{4,3,2,1,0:T(8,128)(2,1)S(1)}, bf16[2,2,17,32,128]{4,3,2,1,0:T(8,128)(2,1)}, u32[]{:S(2)}, u32[]{:S(2)}) collective-permute-start(bf16[2,2,17,32,128]{4,3,2,1,0:T(8,128)(2,1)S(1)} %pad_maximum_fusion.refs_0_), channel_id=1, source_target_pairs={{0,24},{4,100},{8,0},{12,108},{16,8},{20,116},{24,16},{28,124},{32... | collective-permute-start | bytes 1671176 | tf_op jit(solution)/shard_map/ppermute | solution.py:42
  34.3 12.3 %collective-permute-start.8 = (bf16[2,2,17,32,128]{4,3,2,1,0:T(8,128)(2,1)S(1)}, bf16[2,2,17,32,128]{4,3,2,1,0:T(8,128)(2,1)}, u32[]{:S(2)}, u32[]{:S(2)}) collective-permute-start(bf16[2,2,17,32,128]{4,3,2,1,0:T(8,128)(2,1)S(1)} %collective-permute-done.4.refs_2_), channel_id=1, source_target_pairs={{0,8},{4,36},{8,16},{12,44},{16,24},{20,52},{24,0},{28,60},{32,40}... | collective-permute-start | bytes 1671176 | tf_op jit(solution)/shard_map/ppermute | solution.py:43
  34.3 12.7 %collective-permute-start.9 = (bf16[2,2,17,32,128]{4,3,2,1,0:T(8,128)(2,1)S(1)}, bf16[2,2,17,32,128]{4,3,2,1,0:T(8,128)(2,1)}, u32[]{:S(2)}, u32[]{:S(2)}) collective-permute-start(bf16[2,2,17,32,128]{4,3,2,1,0:T(8,128)(2,1)S(1)} %collective-permute-done.5.refs_3_.refs_5_), channel_id=1, source_target_pairs={{0,24},{4,100},{8,0},{12,108},{16,8},{20,116},{24,16},{28,124},{32... | collective-permute-start | bytes 1671176 | tf_op jit(solution)/shard_map/ppermute | solution.py:43
  41.7 13.9 %collective-permute-start.11 = (bf16[2,2,17,32,128]{4,3,2,1,0:T(8,128)(2,1)}, bf16[2,2,17,32,128]{4,3,2,1,0:T(8,128)(2,1)}, u32[]{:S(2)}, u32[]{:S(2)}) collective-permute-start(bf16[2,2,17,32,128]{4,3,2,1,0:T(8,128)(2,1)} %collective-permute-done.7.refs_1_.refs_4_), channel_id=1, source_target_pairs={{0,4},{4,0},{1,5},{5,1},{2,6},{6,2},{3,7},{7,3},{8,12},{12,8},{9,1... | collective-permute-start | bytes 1671176 | tf_op jit(solution)/shard_map/ppermute | solution.py:23
  46.6 9.1 %collective-permute-start.12 = (bf16[2,2,17,32,128]{4,3,2,1,0:T(8,128)(2,1)}, bf16[2,2,17,32,128]{4,3,2,1,0:T(8,128)(2,1)}, u32[]{:S(2)}, u32[]{:S(2)}) collective-permute-start(bf16[2,2,17,32,128]{4,3,2,1,0:T(8,128)(2,1)} %collective-permute-done.8.refs_2_.refs_6_), channel_id=1, source_target_pairs={{0,4},{4,0},{1,5},{5,1},{2,6},{6,2},{3,7},{7,3},{8,12},{12,8},{9,1... | collective-permute-start | bytes 1671176 | tf_op jit(solution)/shard_map/ppermute | solution.py:23
  47.0 8.6 %collective-permute-start.13 = (bf16[2,2,17,32,128]{4,3,2,1,0:T(8,128)(2,1)}, bf16[2,2,17,32,128]{4,3,2,1,0:T(8,128)(2,1)}, u32[]{:S(2)}, u32[]{:S(2)}) collective-permute-start(bf16[2,2,17,32,128]{4,3,2,1,0:T(8,128)(2,1)} %collective-permute-done.9.refs_3_.refs_7_), channel_id=1, source_target_pairs={{0,4},{4,0},{1,5},{5,1},{2,6},{6,2},{3,7},{7,3},{8,12},{12,8},{9,1... | collective-permute-start | bytes 1671176 | tf_op jit(solution)/shard_map/ppermute | solution.py:23
  48.3 16.7 %collective-permute-start.23 = (bf16[8,1,128,128]{3,2,1,0:T(8,128)(2,1)}, bf16[8,1,128,128]{3,2,1,0:T(8,128)(2,1)S(1)}, u32[]{:S(2)}, u32[]{:S(2)}) collective-permute-start(bf16[8,1,128,128]{3,2,1,0:T(8,128)(2,1)} %own_d_ref.13), channel_id=1, source_target_pairs={{0,4},{4,0},{1,5},{5,1},{2,6},{6,2},{3,7},{7,3},{8,12},{12,8},{9,1... | collective-permute-start | bytes 786440 | tf_op jit(solution)/shard_map/ppermute | solution.py:23
  48.4 16.6 %collective-permute-start.22 = (bf16[8,1,32,128]{3,2,1,0:T(8,128)(2,1)S(1)}, bf16[8,1,32,128]{3,2,1,0:T(8,128)(2,1)S(1)}, u32[]{:S(2)}, u32[]{:S(2)}) collective-permute-start(bf16[8,1,32,128]{3,2,1,0:T(8,128)(2,1)S(1)} %get-tuple-element.110), channel_id=1, source_target_pairs={{0,4},{4,0},{1,5},{5,1},{2,6},{6,2},{3,7},{7,3},{8,12},{12,8},{9,1... | collective-permute-start | bytes 196616 | tf_op jit(solution)/shard_map/ppermute | solution.py:23
  70.7 15.3 %all-to-all-start = ((bf16[16,2,32,128]{3,2,1,0:T(8,128)(2,1)}), bf16[16,2,32,128]{3,2,1,0:T(8,128)(2,1)S(1)}, u32[]{:S(2)}, u32[]{:S(2)}) async-start(bf16[16,2,32,128]{3,2,1,0:T(8,128)(2,1)} %get-tuple-element.64), calls=%async_computation | async-start | bytes 524288 | tf_op jit(solution)/shard_map/all_to_all | solution.py:351
  95.9 14.1 %all-to-all-start.1 = ((bf16[16,2,32,128]{3,2,1,0:T(8,128)(2,1)}), bf16[16,2,32,128]{3,2,1,0:T(8,128)(2,1)S(1)}, u32[]{:S(2)}, u32[]{:S(2)}) async-start(bf16[16,2,32,128]{3,2,1,0:T(8,128)(2,1)} %get-tuple-element.71), calls=%async_computation.1 | async-start | bytes 524288 | tf_op jit(solution)/shard_map/all_to_all | solution.py:351
  121.8 14.6 %all-to-all-start.2 = ((bf16[16,2,32,128]{3,2,1,0:T(8,128)(2,1)}), bf16[16,2,32,128]{3,2,1,0:T(8,128)(2,1)S(1)}, u32[]{:S(2)}, u32[]{:S(2)}) async-start(bf16[16,2,32,128]{3,2,1,0:T(8,128)(2,1)} %get-tuple-element.78), calls=%async_computation.2 | async-start | bytes 524288 | tf_op jit(solution)/shard_map/all_to_all | solution.py:351
  146.7 14.4 %all-to-all-start.3 = ((bf16[16,2,32,128]{3,2,1,0:T(8,128)(2,1)}), bf16[16,2,32,128]{3,2,1,0:T(8,128)(2,1)S(1)}, u32[]{:S(2)}, u32[]{:S(2)}) async-start(bf16[16,2,32,128]{3,2,1,0:T(8,128)(2,1)} %get-tuple-element.85), calls=%async_computation.3 | async-start | bytes 524288 | tf_op jit(solution)/shard_map/all_to_all | solution.py:351
  172.5 14.6 %all-to-all-start.4 = ((bf16[16,2,32,128]{3,2,1,0:T(8,128)(2,1)}), bf16[16,2,32,128]{3,2,1,0:T(8,128)(2,1)S(1)}, u32[]{:S(2)}, u32[]{:S(2)}) async-start(bf16[16,2,32,128]{3,2,1,0:T(8,128)(2,1)} %get-tuple-element.92), calls=%async_computation.4 | async-start | bytes 524288 | tf_op jit(solution)/shard_map/all_to_all | solution.py:351
  197.9 14.4 %all-to-all-start.5 = ((bf16[16,2,32,128]{3,2,1,0:T(8,128)(2,1)}), bf16[16,2,32,128]{3,2,1,0:T(8,128)(2,1)S(1)}, u32[]{:S(2)}, u32[]{:S(2)}) async-start(bf16[16,2,32,128]{3,2,1,0:T(8,128)(2,1)} %get-tuple-element.99), calls=%async_computation.5 | async-start | bytes 524288 | tf_op jit(solution)/shard_map/all_to_all | solution.py:351
  222.9 16.0 %collective-permute-start.42 = (bf16[7,32,128]{2,1,0:T(8,128)(2,1)S(1)}, bf16[7,32,128]{2,1,0:T(8,128)(2,1)S(1)}, u32[]{:S(2)}, u32[]{:S(2)}) collective-permute-start(bf16[7,32,128]{2,1,0:T(8,128)(2,1)S(1)} %get-tuple-element.116), channel_id=1, source_target_pairs={{0,4},{4,0},{1,5},{5,1},{2,6},{6,2},{3,7},{7,3},{8,12},{12,8},{9,1... | collective-permute-start | bytes 172040 | tf_op jit(solution)/shard_map/ppermute | solution.py:23
  (57 other events, 291.2 us)

commit v9 on v7

--- a/solution.py
+++ b/solution.py
@@ -85,10 +85,9 @@
     packs, start = [], 0
     for i, source in enumerate(sources):
         which = 0 if i < len(sources) // 2 else 1
-        for part in range(source.shape[0]):
-            target = packed.at[pl.ds(start, source.shape[2])]
-            packs.append(pltpu.make_async_copy(source.at[part, which], target, pack_sems.at[len(packs)]))
-            start += source.shape[2]
+        target = packed.at[pl.ds(start, source.shape[0])]
+        packs.append(pltpu.make_async_copy(source.at[:, which], target, pack_sems.at[i]))
+        start += source.shape[0]
     keep = pltpu.make_async_copy(packed, store_ref.at[pl.ds(0, start)], store_sem)
 
     def between():
@@ -98,8 +97,9 @@
             pack.wait()
         keep.start()
 
-    picks = lambda k, code: packed[code]
-    gather_sum(1, code_ref, picks, start, None, own_ref, other_ref, out_ref, blocks, block_sems, between)
+    each = packed.shape[1]
+    picks = lambda k, code: packed[code // each, code % each]
+    gather_sum(1, code_ref, picks, start * each, None, own_ref, other_ref, out_ref, blocks, block_sems, between)
     keep.wait()
 
 
@@ -159,15 +159,15 @@
 def first_sum(code, sources, own, other):
     one = sources[0].shape[3:]
     parts = sum(v.shape[0] for v in sources)
-    known = parts * sources[0].shape[2]
-    store = jax.ShapeDtypeStruct((2048,) + one, jnp.bfloat16)
+    each = sources[0].shape[2]
+    store = jax.ShapeDtypeStruct((2048 // each, each) + one, jnp.bfloat16)
     extra = [
-        pltpu.SemaphoreType.DMA((parts,)),
-        pltpu.VMEM((known,) + one, jnp.bfloat16),
+        pltpu.SemaphoreType.DMA((len(sources),)),
+        pltpu.VMEM((parts, each) + one, jnp.bfloat16),
         pltpu.SemaphoreType.DMA,
     ]
     spaces = [pl.ANY] * len(sources)
-    return sum_call(first_kernel, [code], sources, spaces, own, other, [store], [pltpu.HBM], extra, "first_sum", 61 * 1024 * 1024)
+    return sum_call(first_kernel, [code], sources, spaces, own, other, [store], [pltpu.HBM], extra, "first_sum", 60 * 1024 * 1024)
 
 
 def old_sum(level, known, code, fresh, store, solved, own, other):
@@ -242,14 +242,13 @@
         solved = nt_dot(reduced, d_ref[level, 0]).astype(jnp.bfloat16)
         out_ref[r] = solved
         if refs:
-            refs[1][core ^ r] = solved
+            for i in range(refs[1].shape[0]):
+                refs[1][i, core ^ r] = solved
     if refs:
-        all_ref, both, sems = refs
-        sends = [pltpu.make_async_copy(both, all_ref.at[i], sems.at[i]) for i in range(all_ref.shape[0])]
-        for send in sends:
-            send.start()
-        for send in sends:
-            send.wait()
+        all_ref, copies, sem = refs
+        send = pltpu.make_async_copy(copies, all_ref, sem)
+        send.start()
+        send.wait()
 
 
 def solve_level(level, partials, rhs, own_d, other_d, copies):
@@ -259,7 +258,7 @@
     if copies:
         out_shape.append(jax.ShapeDtypeStruct((copies, 2, rhs_cols, block), jnp.bfloat16))
         out_specs.append(pl.BlockSpec(memory_space=pltpu.HBM))
-        scratch = [pltpu.VMEM((2, rhs_cols, block), jnp.bfloat16), pltpu.SemaphoreType.DMA((copies,))]
+        scratch = [pltpu.VMEM((copies, 2, rhs_cols, block), jnp.bfloat16), pltpu.SemaphoreType.DMA]
     return pl.pallas_call(
         functools.partial(solve_kernel, level),
         out_shape=out_shape,
@@ -295,7 +294,8 @@
     off_other = swap_cores(off_sent)
 
     pieces = gather_parts(known)
-    pieces = pieces + [swap_cores(piece) for piece in pieces]
+    arrived = lax.optimization_barrier(tuple(pieces[:6]))
+    pieces = pieces + [swap_cores(piece) for piece in [*arrived, *pieces[6:]]]
 
     keep, index = code_both >= 1024, code_both % 1024
     in_outer = index < outer
@@ -317,6 +317,7 @@
 
     own_rows, other_rows = [], []
     value, store = first_sum(old_code, pieces, off_blocks, off_other)
+    store = store.reshape((-1,) + store.shape[2:])
     solved_levels = []
     for level in range(1, levels):
         partials = [value] + [lax.ppermute(value, "x", xor_pairs(4, k)) for k in (1, 2, 3)]

time: 211 us -> 212 us (level)
  waiting for transfers between devices: 50.4 us -> 62.6 us
  starting transfers between devices: 98.2 us -> 88.4 us
    ppermute x13, starting transfers between devices: 28.9 us -> 22 us  [swap_cores(): return lax.ppermute(v, 'core', xor_pairs(2, 1))]
    ppermute x1, starting transfers between devices: 0.01 us -> 3.16 us  [gather_parts(): lax.ppermute(after_high, ROWS, down)]
    ppermute x1, waiting for transfers between devices: 0.01 us -> 3.09 us  [gather_parts(): lax.ppermute(before_low, ROWS, up)]
    all_to_all x6, starting transfers between devices: 27.9 us -> 25 us  [on_device(): solved = lax.all_to_all(sent, ('z', 'y'), 0, 0).reshape(32, half, block)]
    ppermute x1, waiting for transfers between devices: 0.65 us -> 3.58 us  [gather_parts(): lax.ppermute(high, ROWS, down)]
  transfers between devices with their start and end apart: 49 -> 49, of which waited for: 27 -> 29; matrix products, arithmetic and copies ran while one was open for 1% -> 1% of each run, Pallas kernels for 19% -> 19%
where the time goes in v9:
time: 212 us; the launch traced here: 210 us
  starting transfers between devices  88.4 us (42%)
  waiting for transfers between devices  62.6 us (30%)
  Pallas kernels  53 us (25%)
  other arithmetic  3.2 us (2%)
    pallas_call x7, Pallas kernels, sum_call(): pl.pallas_call(kernel, out_shape=[jax.ShapeDtypeStruct((2, rhs_cols, bloc...  40.4 us
    ppermute x21, starting transfers between devices, on_device(): lax.ppermute(value, 'x', xor_pairs(4, k))  27.7 us
    all_to_all x6, starting transfers between devices, on_device(): solved = lax.all_to_all(sent, ('z', 'y'), 0, 0).reshape(32, half, block)  25 us
    ppermute x13, starting transfers between devices, swap_cores(): return lax.ppermute(v, 'core', xor_pairs(2, 1))  22 us
    ppermute x21, waiting for transfers between devices, on_device(): lax.ppermute(value, 'x', xor_pairs(4, k))  20.9 us
    all_to_all x6, waiting for transfers between devices, on_device(): solved = lax.all_to_all(sent, ('z', 'y'), 0, 0).reshape(32, half, block)  11.3 us
    pallas_call x6, Pallas kernels, fresh_sum(): pl.pallas_call(functools.partial(fresh_kernel, level), out_shape=jax.Shap...  7.1 us
    ppermute x3, waiting for transfers between devices, gather_parts(): lax.ppermute(v, ROWS, pairs(1, lambda i, k=k: i ^ k))  6.44 us
  transfers between devices with their start and end apart: 49, of which 29 were waited for; matrix products, arithmetic and copies ran while one was open for 1% of the time, Pallas kernels for 19%

profile of v9, /device:TPU:1, one launch (start us, length us, event | category | flops | bytes accessed | tf_op | source)
XLA Modules:
  0.0 210.4 jit_solution(5756221692793034554)
XLA Ops:
  7.2 3.5 %collective-permute-done.2 = bf16[2,17,32,128]{3,2,1,0:T(8,128)(2,1)S(1)} collective-permute-done((bf16[2,17,32,128]{3,2,1,0:T(8,128)(2,1)S(1)}, bf16[2,17,32,128]{3,2,1,0:T(8,128)(2,1)S(1)}, u32[]{:S(2)}, u32[]{:S(2)}) %collective-permute-start.2) | collective-permute-done | bytes 278560 | tf_op jit(solution)/shard_map/ppermute | solution.py:37
  13.7 3.9 %collective-permute-start.7 = (bf16[2,2,17,32,128]{4,3,2,1,0:T(8,128)(2,1)S(1)}, bf16[2,2,17,32,128]{4,3,2,1,0:T(8,128)(2,1)S(1)}, u32[]{:S(2)}, u32[]{:S(2)}) collective-permute-start(bf16[2,2,17,32,128]{4,3,2,1,0:T(8,128)(2,1)S(1)} %pad_maximum_fusion.1.refs_1_), channel_id=1, source_target_pairs={{0,24},{4,100},{8,0},{12,108},{16,8},{20,116},{24,16},{28,124},{32... | collective-permute-start | bytes 1671176 | tf_op jit(solution)/shard_map/ppermute | solution.py:40
  20.5 3.6 %collective-permute-done.7.refs_5_ = bf16[2,2,17,32,128]{4,3,2,1,0:T(8,128)(2,1)S(1)} collective-permute-done((bf16[2,2,17,32,128]{4,3,2,1,0:T(8,128)(2,1)S(1)}, bf16[2,2,17,32,128]{4,3,2,1,0:T(8,128)(2,1)S(1)}, u32[]{:S(2)}, u32[]{:S(2)}) %collective-permute-start.7) | collective-permute-done | bytes 557088 | tf_op jit(solution)/shard_map/ppermute | solution.py:40
  24.1 3.5 %collective-permute-done.4.refs_2_ = bf16[2,2,17,32,128]{4,3,2,1,0:T(8,128)(2,1)S(1)} collective-permute-done((bf16[2,2,17,32,128]{4,3,2,1,0:T(8,128)(2,1)S(1)}, bf16[2,2,17,32,128]{4,3,2,1,0:T(8,128)(2,1)S(1)}, u32[]{:S(2)}, u32[]{:S(2)}) %collective-permute-start.4) | collective-permute-done | bytes 557088 | tf_op jit(solution)/shard_map/ppermute | solution.py:40
  27.6 6.0 %collective-permute-done.5.refs_3_ = bf16[2,2,17,32,128]{4,3,2,1,0:T(8,128)(2,1)S(1)} collective-permute-done((bf16[2,2,17,32,128]{4,3,2,1,0:T(8,128)(2,1)S(1)}, bf16[2,2,17,32,128]{4,3,2,1,0:T(8,128)(2,1)S(1)}, u32[]{:S(2)}, u32[]{:S(2)}) %collective-permute-start.5) | collective-permute-done | bytes 557088 | tf_op jit(solution)/shard_map/ppermute | solution.py:41
  38.1 3.2 %collective-permute-start.9 = (bf16[2,2,17,32,128]{4,3,2,1,0:T(8,128)(2,1)S(1)}, bf16[2,2,17,32,128]{4,3,2,1,0:T(8,128)(2,1)}, u32[]{:S(2)}, u32[]{:S(2)}) collective-permute-start(bf16[2,2,17,32,128]{4,3,2,1,0:T(8,128)(2,1)S(1)} %collective-permute-done.7.refs_5_), channel_id=1, source_target_pairs={{0,24},{4,100},{8,0},{12,108},{16,8},{20,116},{24,16},{28,124},{32... | collective-permute-start | bytes 1671176 | tf_op jit(solution)/shard_map/ppermute | solution.py:42
  41.9 5.8 %collective-permute-done.9.refs_7_ = bf16[2,2,17,32,128]{4,3,2,1,0:T(8,128)(2,1)} collective-permute-done((bf16[2,2,17,32,128]{4,3,2,1,0:T(8,128)(2,1)S(1)}, bf16[2,2,17,32,128]{4,3,2,1,0:T(8,128)(2,1)}, u32[]{:S(2)}, u32[]{:S(2)}) %collective-permute-start.9) | collective-permute-done | bytes 557088 | tf_op jit(solution)/shard_map/ppermute | solution.py:42
  53.5 6.6 %first_sum.1 = (f32[2,32,128]{2,1,0:T(8,128)}, bf16[120,17,32,128]{3,2,1,0:T(8,128)(2,1)}) custom-call(s32[7,64]{1,0:T(8,128)} %get-tuple-element.130.code_ref, bf16[2,2,17,32,128]{4,3,2,1,0:T(8,128)(2,1)} %copy-done.4, bf16[2,2,17,32,128]{4,3,2,1,0:T(8,128)(2,1)} %copy-done.3, bf16[2,2,17,32,128]{4,3,2,1,0:T(8,128)(2,1)} %copy-done.6, ...), custom_call_target="tpu_custom_call" | custom-call | flops 67108864 | bytes 6291456 | tf_op jit(solution)/shard_map/first_sum/pallas_call | solution.py:141
  69.6 3.5 %all-to-all-start = ((bf16[16,2,32,128]{3,2,1,0:T(8,128)(2,1)}), bf16[16,2,32,128]{3,2,1,0:T(8,128)(2,1)S(1)}, u32[]{:S(2)}, u32[]{:S(2)}) async-start(bf16[16,2,32,128]{3,2,1,0:T(8,128)(2,1)} %get-tuple-element.72), calls=%async_computation | async-start | bytes 524288 | tf_op jit(solution)/shard_map/all_to_all | solution.py:330
  73.2 5.9 %old_sum.6 = (f32[2,32,128]{2,1,0:T(8,128)S(1)}, s32[65]{0:T(128)S(1)}, bf16[16,128,128]{2,1,0:T(8,128)(2,1)S(1)}) custom-call(s32[7,64]{1,0:T(8,128)S(1)} %copy-done.1, s32[7,64]{1,0:T(8,128)S(1)} %get-tuple-element.104.fresh_ref, bf16[2040,32,128]{2,1,0:T(8,128)(2,1)} %bitcast.51, bf16[7,1,32,128,128]{4,3,2,1,0:T(8,128)(2,1)} %own_ref.11, ...), custom_call_target="tpu_custom_call" | custom-call | flops 67108864 | bytes 6291456 | tf_op jit(solution)/shard_map/old_sum/pallas_call | solution.py:141
  88.4 4.3 %all-to-all-start.1 = ((bf16[16,2,32,128]{3,2,1,0:T(8,128)(2,1)}), bf16[16,2,32,128]{3,2,1,0:T(8,128)(2,1)S(1)}, u32[]{:S(2)}, u32[]{:S(2)}) async-start(bf16[16,2,32,128]{3,2,1,0:T(8,128)(2,1)} %get-tuple-element.79), calls=%async_computation.1 | async-start | bytes 524288 | tf_op jit(solution)/shard_map/all_to_all | solution.py:330
  92.7 5.6 %old_sum.7 = (f32[2,32,128]{2,1,0:T(8,128)S(1)}, s32[65]{0:T(128)S(1)}, bf16[16,128,128]{2,1,0:T(8,128)(2,1)S(1)}) custom-call(s32[7,64]{1,0:T(8,128)S(1)} %copy-done.1, s32[7,64]{1,0:T(8,128)S(1)} %get-tuple-element.104.fresh_ref, bf16[2040,32,128]{2,1,0:T(8,128)(2,1)} %bitcast.52, bf16[32,32,128]{2,1,0:T(8,128)(2,1)S(1)} %bitcast.31, ...), custom_call_target="tpu_custom_call" | custom-call | flops 67108864 | bytes 6291456 | tf_op jit(solution)/shard_map/old_sum/pallas_call | solution.py:141
  102.2 3.8 %collective-permute-start.28 = (f32[2,32,128]{2,1,0:T(8,128)S(1)}, f32[2,32,128]{2,1,0:T(8,128)S(1)}, u32[]{:S(2)}, u32[]{:S(2)}) collective-permute-start(f32[2,32,128]{2,1,0:T(8,128)S(1)} %fresh_sum.7.p0), channel_id=1, source_target_pairs={{0,2},{1,3},{2,0},{3,1},{4,6},{5,7},{6,4},{7,5},{8,10},{9,11},{10,... | collective-permute-start | bytes 98312 | tf_op jit(solution)/shard_map/ppermute | solution.py:323
  110.9 3.8 %all-to-all-start.2 = ((bf16[16,2,32,128]{3,2,1,0:T(8,128)(2,1)}), bf16[16,2,32,128]{3,2,1,0:T(8,128)(2,1)S(1)}, u32[]{:S(2)}, u32[]{:S(2)}) async-start(bf16[16,2,32,128]{3,2,1,0:T(8,128)(2,1)} %get-tuple-element.86), calls=%async_computation.2 | async-start | bytes 524288 | tf_op jit(solution)/shard_map/all_to_all | solution.py:330
  114.7 5.8 %old_sum.8 = (f32[2,32,128]{2,1,0:T(8,128)S(1)}, s32[65]{0:T(128)S(1)}, bf16[16,128,128]{2,1,0:T(8,128)(2,1)S(1)}) custom-call(s32[7,64]{1,0:T(8,128)S(1)} %copy-done.1, s32[7,64]{1,0:T(8,128)S(1)} %get-tuple-element.104.fresh_ref, bf16[2040,32,128]{2,1,0:T(8,128)(2,1)} %bitcast.53, bf16[32,32,128]{2,1,0:T(8,128)(2,1)S(1)} %bitcast.32, ...), custom_call_target="tpu_custom_call" | custom-call | flops 67108864 | bytes 6291456 | tf_op jit(solution)/shard_map/old_sum/pallas_call | solution.py:141
  129.5 4.7 %all-to-all-start.3 = ((bf16[16,2,32,128]{3,2,1,0:T(8,128)(2,1)}), bf16[16,2,32,128]{3,2,1,0:T(8,128)(2,1)S(1)}, u32[]{:S(2)}, u32[]{:S(2)}) async-start(bf16[16,2,32,128]{3,2,1,0:T(8,128)(2,1)} %get-tuple-element.93), calls=%async_computation.3 | async-start | bytes 524288 | tf_op jit(solution)/shard_map/all_to_all | solution.py:330
  134.2 5.7 %old_sum.9 = (f32[2,32,128]{2,1,0:T(8,128)S(1)}, s32[65]{0:T(128)S(1)}, bf16[16,128,128]{2,1,0:T(8,128)(2,1)S(1)}) custom-call(s32[7,64]{1,0:T(8,128)S(1)} %copy-done.1, s32[7,64]{1,0:T(8,128)S(1)} %get-tuple-element.104.fresh_ref, bf16[2040,32,128]{2,1,0:T(8,128)(2,1)} %bitcast.54, bf16[32,32,128]{2,1,0:T(8,128)(2,1)S(1)} %bitcast.33, ...), custom_call_target="tpu_custom_call" | custom-call | flops 67108864 | bytes 6291456 | tf_op jit(solution)/shard_map/old_sum/pallas_call | solution.py:141
  143.3 3.4 %collective-permute-start.34 = (f32[2,32,128]{2,1,0:T(8,128)S(1)}, f32[2,32,128]{2,1,0:T(8,128)S(1)}, u32[]{:S(2)}, u32[]{:S(2)}) collective-permute-start(f32[2,32,128]{2,1,0:T(8,128)S(1)} %fresh_sum.9.p0), channel_id=1, source_target_pairs={{0,2},{1,3},{2,0},{3,1},{4,6},{5,7},{6,4},{7,5},{8,10},{9,11},{10,... | collective-permute-start | bytes 98312 | tf_op jit(solution)/shard_map/ppermute | solution.py:323
  151.9 3.8 %all-to-all-start.4 = ((bf16[16,2,32,128]{3,2,1,0:T(8,128)(2,1)}), bf16[16,2,32,128]{3,2,1,0:T(8,128)(2,1)S(1)}, u32[]{:S(2)}, u32[]{:S(2)}) async-start(bf16[16,2,32,128]{3,2,1,0:T(8,128)(2,1)} %get-tuple-element.100), calls=%async_computation.4 | async-start | bytes 524288 | tf_op jit(solution)/shard_map/all_to_all | solution.py:330
  155.7 5.4 %old_sum.10 = (f32[2,32,128]{2,1,0:T(8,128)S(1)}, s32[65]{0:T(128)S(1)}, bf16[16,128,128]{2,1,0:T(8,128)(2,1)S(1)}) custom-call(s32[7,64]{1,0:T(8,128)S(1)} %copy-done.1, s32[7,64]{1,0:T(8,128)S(1)} %get-tuple-element.104.fresh_ref, bf16[2040,32,128]{2,1,0:T(8,128)(2,1)} %bitcast.55, bf16[32,32,128]{2,1,0:T(8,128)(2,1)S(1)} %bitcast.34, ...), custom_call_target="tpu_custom_call" | custom-call | flops 67108864 | bytes 6291456 | tf_op jit(solution)/shard_map/old_sum/pallas_call | solution.py:141
  171.2 4.8 %all-to-all-start.5 = ((bf16[16,2,32,128]{3,2,1,0:T(8,128)(2,1)}), bf16[16,2,32,128]{3,2,1,0:T(8,128)(2,1)S(1)}, u32[]{:S(2)}, u32[]{:S(2)}) async-start(bf16[16,2,32,128]{3,2,1,0:T(8,128)(2,1)} %get-tuple-element.107), calls=%async_computation.5 | async-start | bytes 524288 | tf_op jit(solution)/shard_map/all_to_all | solution.py:330
  176.0 5.4 %old_sum.11 = (f32[2,32,128]{2,1,0:T(8,128)S(1)}, s32[65]{0:T(128)S(1)}, bf16[16,128,128]{2,1,0:T(8,128)(2,1)S(1)}) custom-call(s32[7,64]{1,0:T(8,128)S(1)} %copy-done.1, s32[7,64]{1,0:T(8,128)S(1)} %get-tuple-element.104.fresh_ref, bf16[2040,32,128]{2,1,0:T(8,128)(2,1)} %bitcast.56, bf16[32,32,128]{2,1,0:T(8,128)(2,1)S(1)} %bitcast.35, ...), custom_call_target="tpu_custom_call" | custom-call | flops 67108864 | bytes 6291456 | tf_op jit(solution)/shard_map/old_sum/pallas_call | solution.py:141
  184.7 3.6 %collective-permute-start.40 = (f32[2,32,128]{2,1,0:T(8,128)S(1)}, f32[2,32,128]{2,1,0:T(8,128)S(1)}, u32[]{:S(2)}, u32[]{:S(2)}) collective-permute-start(f32[2,32,128]{2,1,0:T(8,128)S(1)} %fresh_sum.11.p0), channel_id=1, source_target_pairs={{0,2},{1,3},{2,0},{3,1},{4,6},{5,7},{6,4},{7,5},{8,10},{9,11},{10,... | collective-permute-start | bytes 98312 | tf_op jit(solution)/shard_map/ppermute | solution.py:323
  192.4 16.4 %collective-permute-start.42 = (bf16[7,32,128]{2,1,0:T(8,128)(2,1)S(1)}, bf16[7,32,128]{2,1,0:T(8,128)(2,1)S(1)}, u32[]{:S(2)}, u32[]{:S(2)}) collective-permute-start(bf16[7,32,128]{2,1,0:T(8,128)(2,1)S(1)} %get-tuple-element.116), channel_id=1, source_target_pairs={{0,4},{4,0},{1,5},{5,1},{2,6},{6,2},{3,7},{7,3},{8,12},{12,8},{9,1... | collective-permute-start | bytes 172040 | tf_op jit(solution)/shard_map/ppermute | solution.py:23
  (142 shorter events, 87.9 us)
Async XLA Ops:
  2.0 51.4 %collective-permute-start.18 = (bf16[7,1,32,128,128]{4,3,2,1,0:T(8,128)(2,1)}, bf16[7,1,32,128,128]{4,3,2,1,0:T(8,128)(2,1)}, u32[]{:S(2)}, u32[]{:S(2)}) collective-permute-start(bf16[7,1,32,128,128]{4,3,2,1,0:T(8,128)(2,1)} %own_ref.11), channel_id=1, source_target_pairs={{0,4},{4,0},{1,5},{5,1},{2,6},{6,2},{3,7},{7,3},{8,12},{12,8},{9,1... | collective-permute-start | bytes 22020104 | tf_op jit(solution)/shard_map/ppermute | solution.py:23
  3.5 7.2 %collective-permute-start.2 = (bf16[2,17,32,128]{3,2,1,0:T(8,128)(2,1)S(1)}, bf16[2,17,32,128]{3,2,1,0:T(8,128)(2,1)S(1)}, u32[]{:S(2)}, u32[]{:S(2)}) collective-permute-start(bf16[2,17,32,128]{3,2,1,0:T(8,128)(2,1)S(1)} %pad_maximum_fusion.2), channel_id=1, source_target_pairs={{0,64},{4,20},{8,72},{12,28},{16,80},{20,4},{24,88},{28,12},{32,96... | collective-permute-start | bytes 835592 | tf_op jit(solution)/shard_map/ppermute | solution.py:37
  6.5 7.2 %collective-permute-start.3 = (bf16[2,17,32,128]{3,2,1,0:T(8,128)(2,1)S(1)}, bf16[2,17,32,128]{3,2,1,0:T(8,128)(2,1)S(1)}, u32[]{:S(2)}, u32[]{:S(2)}) collective-permute-start(bf16[2,17,32,128]{3,2,1,0:T(8,128)(2,1)S(1)} %pad_maximum_fusion.2), channel_id=1, source_target_pairs={{0,96},{4,28},{8,104},{12,20},{16,112},{20,12},{24,120},{28,4},{32... | collective-permute-start | bytes 835592 | tf_op jit(solution)/shard_map/ppermute | solution.py:37
  7.2 10.4 %collective-permute-start.1 = (bf16[2,17,32,128]{3,2,1,0:T(8,128)(2,1)S(1)}, bf16[2,17,32,128]{3,2,1,0:T(8,128)(2,1)S(1)}, u32[]{:S(2)}, u32[]{:S(2)}) collective-permute-start(bf16[2,17,32,128]{3,2,1,0:T(8,128)(2,1)S(1)} %pad_maximum_fusion.2), channel_id=1, source_target_pairs={{0,32},{4,12},{8,40},{12,4},{16,48},{20,28},{24,56},{28,20},{32,0}... | collective-permute-start | bytes 835592 | tf_op jit(solution)/shard_map/ppermute | solution.py:37
  13.7 10.4 %collective-permute-start.7 = (bf16[2,2,17,32,128]{4,3,2,1,0:T(8,128)(2,1)S(1)}, bf16[2,2,17,32,128]{4,3,2,1,0:T(8,128)(2,1)S(1)}, u32[]{:S(2)}, u32[]{:S(2)}) collective-permute-start(bf16[2,2,17,32,128]{4,3,2,1,0:T(8,128)(2,1)S(1)} %pad_maximum_fusion.1.refs_1_), channel_id=1, source_target_pairs={{0,24},{4,100},{8,0},{12,108},{16,8},{20,116},{24,16},{28,124},{32... | collective-permute-start | bytes 1671176 | tf_op jit(solution)/shard_map/ppermute | solution.py:40
  17.7 10.0 %collective-permute-start.4 = (bf16[2,2,17,32,128]{4,3,2,1,0:T(8,128)(2,1)S(1)}, bf16[2,2,17,32,128]{4,3,2,1,0:T(8,128)(2,1)S(1)}, u32[]{:S(2)}, u32[]{:S(2)}) collective-permute-start(bf16[2,2,17,32,128]{4,3,2,1,0:T(8,128)(2,1)S(1)} %pad_maximum_fusion.refs_0_), channel_id=1, source_target_pairs={{0,8},{4,36},{8,16},{12,44},{16,24},{20,52},{24,0},{28,60},{32,40}... | collective-permute-start | bytes 1671176 | tf_op jit(solution)/shard_map/ppermute | solution.py:40
  17.8 15.8 %collective-permute-start.5 = (bf16[2,2,17,32,128]{4,3,2,1,0:T(8,128)(2,1)S(1)}, bf16[2,2,17,32,128]{4,3,2,1,0:T(8,128)(2,1)S(1)}, u32[]{:S(2)}, u32[]{:S(2)}) collective-permute-start(bf16[2,2,17,32,128]{4,3,2,1,0:T(8,128)(2,1)S(1)} %pad_maximum_fusion.1.refs_1_), channel_id=1, source_target_pairs={{0,8},{4,36},{8,16},{12,44},{16,24},{20,52},{24,0},{28,60},{32,40}... | collective-permute-start | bytes 1671176 | tf_op jit(solution)/shard_map/ppermute | solution.py:41
  17.9 15.8 %collective-permute-start.6 = (bf16[2,2,17,32,128]{4,3,2,1,0:T(8,128)(2,1)S(1)}, bf16[2,2,17,32,128]{4,3,2,1,0:T(8,128)(2,1)S(1)}, u32[]{:S(2)}, u32[]{:S(2)}) collective-permute-start(bf16[2,2,17,32,128]{4,3,2,1,0:T(8,128)(2,1)S(1)} %pad_maximum_fusion.refs_0_), channel_id=1, source_target_pairs={{0,24},{4,100},{8,0},{12,108},{16,8},{20,116},{24,16},{28,124},{32... | collective-permute-start | bytes 1671176 | tf_op jit(solution)/shard_map/ppermute | solution.py:41
  35.4 5.9 %collective-permute-start.11 = (bf16[2,2,17,32,128]{4,3,2,1,0:T(8,128)(2,1)S(1)}, bf16[2,2,17,32,128]{4,3,2,1,0:T(8,128)(2,1)S(1)}, u32[]{:S(2)}, u32[]{:S(2)}) collective-permute-start(bf16[2,2,17,32,128]{4,3,2,1,0:T(8,128)(2,1)S(1)} %pad_maximum_fusion.1.refs_1_), channel_id=1, source_target_pairs={{0,4},{4,0},{1,5},{5,1},{2,6},{6,2},{3,7},{7,3},{8,12},{12,8},{9,1... | collective-permute-start | bytes 1671176 | tf_op jit(solution)/shard_map/ppermute | solution.py:23
  38.1 9.6 %collective-permute-start.9 = (bf16[2,2,17,32,128]{4,3,2,1,0:T(8,128)(2,1)S(1)}, bf16[2,2,17,32,128]{4,3,2,1,0:T(8,128)(2,1)}, u32[]{:S(2)}, u32[]{:S(2)}) collective-permute-start(bf16[2,2,17,32,128]{4,3,2,1,0:T(8,128)(2,1)S(1)} %collective-permute-done.7.refs_5_), channel_id=1, source_target_pairs={{0,24},{4,100},{8,0},{12,108},{16,8},{20,116},{24,16},{28,124},{32... | collective-permute-start | bytes 1671176 | tf_op jit(solution)/shard_map/ppermute | solution.py:42
  41.3 9.7 %collective-permute-start.8 = (bf16[2,2,17,32,128]{4,3,2,1,0:T(8,128)(2,1)S(1)}, bf16[2,2,17,32,128]{4,3,2,1,0:T(8,128)(2,1)}, u32[]{:S(2)}, u32[]{:S(2)}) collective-permute-start(bf16[2,2,17,32,128]{4,3,2,1,0:T(8,128)(2,1)S(1)} %collective-permute-done.4.refs_2_), channel_id=1, source_target_pairs={{0,8},{4,36},{8,16},{12,44},{16,24},{20,52},{24,0},{28,60},{32,40}... | collective-permute-start | bytes 1671176 | tf_op jit(solution)/shard_map/ppermute | solution.py:42
  41.3 10.8 %collective-permute-start.14 = (bf16[2,2,17,32,128]{4,3,2,1,0:T(8,128)(2,1)S(1)}, bf16[2,2,17,32,128]{4,3,2,1,0:T(8,128)(2,1)}, u32[]{:S(2)}, u32[]{:S(2)}) collective-permute-start(bf16[2,2,17,32,128]{4,3,2,1,0:T(8,128)(2,1)S(1)} %collective-permute-done.6.refs_4_), channel_id=1, source_target_pairs={{0,4},{4,0},{1,5},{5,1},{2,6},{6,2},{3,7},{7,3},{8,12},{12,8},{9,1... | collective-permute-start | bytes 1671176 | tf_op jit(solution)/shard_map/ppermute | solution.py:23
  41.4 11.2 %collective-permute-start.15 = (bf16[2,2,17,32,128]{4,3,2,1,0:T(8,128)(2,1)S(1)}, bf16[2,2,17,32,128]{4,3,2,1,0:T(8,128)(2,1)}, u32[]{:S(2)}, u32[]{:S(2)}) collective-permute-start(bf16[2,2,17,32,128]{4,3,2,1,0:T(8,128)(2,1)S(1)} %collective-permute-done.7.refs_5_), channel_id=1, source_target_pairs={{0,4},{4,0},{1,5},{5,1},{2,6},{6,2},{3,7},{7,3},{8,12},{12,8},{9,1... | collective-permute-start | bytes 1671176 | tf_op jit(solution)/shard_map/ppermute | solution.py:23
  47.8 5.6 %collective-permute-start.17 = (bf16[2,2,17,32,128]{4,3,2,1,0:T(8,128)(2,1)}, bf16[2,2,17,32,128]{4,3,2,1,0:T(8,128)(2,1)}, u32[]{:S(2)}, u32[]{:S(2)}) collective-permute-start(bf16[2,2,17,32,128]{4,3,2,1,0:T(8,128)(2,1)} %collective-permute-done.9.refs_7_), channel_id=1, source_target_pairs={{0,4},{4,0},{1,5},{5,1},{2,6},{6,2},{3,7},{7,3},{8,12},{12,8},{9,1... | collective-permute-start | bytes 1671176 | tf_op jit(solution)/shard_map/ppermute | solution.py:23
  52.1 11.9 %collective-permute-start.23 = (bf16[8,1,128,128]{3,2,1,0:T(8,128)(2,1)}, bf16[8,1,128,128]{3,2,1,0:T(8,128)(2,1)S(1)}, u32[]{:S(2)}, u32[]{:S(2)}) collective-permute-start(bf16[8,1,128,128]{3,2,1,0:T(8,128)(2,1)} %own_d_ref.13), channel_id=1, source_target_pairs={{0,4},{4,0},{1,5},{5,1},{2,6},{6,2},{3,7},{7,3},{8,12},{12,8},{9,1... | collective-permute-start | bytes 786440 | tf_op jit(solution)/shard_map/ppermute | solution.py:23
  52.6 11.3 %collective-permute-start.22 = (bf16[8,1,32,128]{3,2,1,0:T(8,128)(2,1)S(1)}, bf16[8,1,32,128]{3,2,1,0:T(8,128)(2,1)S(1)}, u32[]{:S(2)}, u32[]{:S(2)}) collective-permute-start(bf16[8,1,32,128]{3,2,1,0:T(8,128)(2,1)S(1)} %get-tuple-element.112), channel_id=1, source_target_pairs={{0,4},{4,0},{1,5},{5,1},{2,6},{6,2},{3,7},{7,3},{8,12},{12,8},{9,1... | collective-permute-start | bytes 196616 | tf_op jit(solution)/shard_map/ppermute | solution.py:23
  69.6 11.1 %all-to-all-start = ((bf16[16,2,32,128]{3,2,1,0:T(8,128)(2,1)}), bf16[16,2,32,128]{3,2,1,0:T(8,128)(2,1)S(1)}, u32[]{:S(2)}, u32[]{:S(2)}) async-start(bf16[16,2,32,128]{3,2,1,0:T(8,128)(2,1)} %get-tuple-element.72), calls=%async_computation | async-start | bytes 524288 | tf_op jit(solution)/shard_map/all_to_all | solution.py:330
  88.4 11.8 %all-to-all-start.1 = ((bf16[16,2,32,128]{3,2,1,0:T(8,128)(2,1)}), bf16[16,2,32,128]{3,2,1,0:T(8,128)(2,1)S(1)}, u32[]{:S(2)}, u32[]{:S(2)}) async-start(bf16[16,2,32,128]{3,2,1,0:T(8,128)(2,1)} %get-tuple-element.79), calls=%async_computation.1 | async-start | bytes 524288 | tf_op jit(solution)/shard_map/all_to_all | solution.py:330
  102.2 5.5 %collective-permute-start.28 = (f32[2,32,128]{2,1,0:T(8,128)S(1)}, f32[2,32,128]{2,1,0:T(8,128)S(1)}, u32[]{:S(2)}, u32[]{:S(2)}) collective-permute-start(f32[2,32,128]{2,1,0:T(8,128)S(1)} %fresh_sum.7.p0), channel_id=1, source_target_pairs={{0,2},{1,3},{2,0},{3,1},{4,6},{5,7},{6,4},{7,5},{8,10},{9,11},{10,... | collective-permute-start | bytes 98312 | tf_op jit(solution)/shard_map/ppermute | solution.py:323
  110.9 11.4 %all-to-all-start.2 = ((bf16[16,2,32,128]{3,2,1,0:T(8,128)(2,1)}), bf16[16,2,32,128]{3,2,1,0:T(8,128)(2,1)S(1)}, u32[]{:S(2)}, u32[]{:S(2)}) async-start(bf16[16,2,32,128]{3,2,1,0:T(8,128)(2,1)} %get-tuple-element.86), calls=%async_computation.2 | async-start | bytes 524288 | tf_op jit(solution)/shard_map/all_to_all | solution.py:330
  129.5 12.3 %all-to-all-start.3 = ((bf16[16,2,32,128]{3,2,1,0:T(8,128)(2,1)}), bf16[16,2,32,128]{3,2,1,0:T(8,128)(2,1)S(1)}, u32[]{:S(2)}, u32[]{:S(2)}) async-start(bf16[16,2,32,128]{3,2,1,0:T(8,128)(2,1)} %get-tuple-element.93), calls=%async_computation.3 | async-start | bytes 524288 | tf_op jit(solution)/shard_map/all_to_all | solution.py:330
  151.9 11.4 %all-to-all-start.4 = ((bf16[16,2,32,128]{3,2,1,0:T(8,128)(2,1)}), bf16[16,2,32,128]{3,2,1,0:T(8,128)(2,1)S(1)}, u32[]{:S(2)}, u32[]{:S(2)}) async-start(bf16[16,2,32,128]{3,2,1,0:T(8,128)(2,1)} %get-tuple-element.100), calls=%async_computation.4 | async-start | bytes 524288 | tf_op jit(solution)/shard_map/all_to_all | solution.py:330
  171.2 12.3 %all-to-all-start.5 = ((bf16[16,2,32,128]{3,2,1,0:T(8,128)(2,1)}), bf16[16,2,32,128]{3,2,1,0:T(8,128)(2,1)S(1)}, u32[]{:S(2)}, u32[]{:S(2)}) async-start(bf16[16,2,32,128]{3,2,1,0:T(8,128)(2,1)} %get-tuple-element.107), calls=%async_computation.5 | async-start | bytes 524288 | tf_op jit(solution)/shard_map/all_to_all | solution.py:330
  192.4 17.2 %collective-permute-start.42 = (bf16[7,32,128]{2,1,0:T(8,128)(2,1)S(1)}, bf16[7,32,128]{2,1,0:T(8,128)(2,1)S(1)}, u32[]{:S(2)}, u32[]{:S(2)}) collective-permute-start(bf16[7,32,128]{2,1,0:T(8,128)(2,1)S(1)} %get-tuple-element.116), channel_id=1, source_target_pairs={{0,4},{4,0},{1,5},{5,1},{2,6},{6,2},{3,7},{7,3},{8,12},{12,8},{9,1... | collective-permute-start | bytes 172040 | tf_op jit(solution)/shard_map/ppermute | solution.py:23
  (38 other events, 347.5 us)

commit v10 on v9

--- a/solution.py
+++ b/solution.py
@@ -294,8 +294,7 @@
     off_other = swap_cores(off_sent)
 
     pieces = gather_parts(known)
-    arrived = lax.optimization_barrier(tuple(pieces[:6]))
-    pieces = pieces + [swap_cores(piece) for piece in [*arrived, *pieces[6:]]]
+    pieces = pieces + [swap_cores(piece) for piece in pieces]
 
     keep, index = code_both >= 1024, code_both % 1024
     in_outer = index < outer

time: 212 us -> 209 us (0.986)
  waiting for transfers between devices: 62.6 us -> 52.7 us
  starting transfers between devices: 88.4 us -> 98.2 us
  Pallas kernels: 53 us -> 49.1 us
    ppermute x13, starting transfers between devices: 22 us -> 28.7 us  [swap_cores(): return lax.ppermute(v, 'core', xor_pairs(2, 1))]
    all_to_all x6, starting transfers between devices: 25 us -> 28.7 us  [on_device(): solved = lax.all_to_all(sent, ('z', 'y'), 0, 0).reshape(32, half, block)]
    ppermute x1, starting transfers between devices: 3.16 us -> 0.01 us  [gather_parts(): lax.ppermute(after_high, ROWS, down)]
    ppermute x1, waiting for transfers between devices: 3.09 us -> 0.01 us  [gather_parts(): lax.ppermute(before_low, ROWS, up)]
    ppermute x1, waiting for transfers between devices: 3.58 us -> 0.65 us  [gather_parts(): lax.ppermute(high, ROWS, down)]
    pallas_call x6, Pallas kernels: 7.1 us -> 4.7 us  [fresh_sum(): pl.pallas_call(functools.partial(fresh_kernel, level), out_shape=jax.Shap...]
  transfers between devices with their start and end apart: 49 -> 49, of which waited for: 29 -> 27; matrix products, arithmetic and copies ran while one was open for 1% -> 1% of each run, Pallas kernels for 19% -> 19%
where the time goes in v10:
time: 209 us; the launch traced here: 208 us
  starting transfers between devices  98.2 us (47%)
  waiting for transfers between devices  52.7 us (25%)
  Pallas kernels  49.1 us (23%)
  local copies, waits for them, and re-layouts  3.37 us (2%)
  other arithmetic  3.28 us (2%)
    pallas_call x7, Pallas kernels, sum_call(): pl.pallas_call(kernel, out_shape=[jax.ShapeDtypeStruct((2, rhs_cols, bloc...  38.9 us
    ppermute x13, starting transfers between devices, swap_cores(): return lax.ppermute(v, 'core', xor_pairs(2, 1))  28.7 us
    all_to_all x6, starting transfers between devices, on_device(): solved = lax.all_to_all(sent, ('z', 'y'), 0, 0).reshape(32, half, block)  28.7 us
    ppermute x21, starting transfers between devices, on_device(): lax.ppermute(value, 'x', xor_pairs(4, k))  27.7 us
    ppermute x21, waiting for transfers between devices, on_device(): lax.ppermute(value, 'x', xor_pairs(4, k))  20.4 us
    all_to_all x6, waiting for transfers between devices, on_device(): solved = lax.all_to_all(sent, ('z', 'y'), 0, 0).reshape(32, half, block)  12.8 us
    ppermute x3, waiting for transfers between devices, gather_parts(): lax.ppermute(v, ROWS, pairs(1, lambda i, k=k: i ^ k))  6.44 us
    pallas_call x7, Pallas kernels, solve_level(): pl.pallas_call(functools.partial(solve_kernel, level), out_shape=out_shap...  5.5 us
  transfers between devices with their start and end apart: 49, of which 27 were waited for; matrix products, arithmetic and copies ran while one was open for 1% of the time, Pallas kernels for 19%

profile of v10, /device:TPU:1, one launch (start us, length us, event | category | flops | bytes accessed | tf_op | source)
XLA Modules:
  0.0 208.0 jit_solution(4418889948163121626)
XLA Ops:
  3.5 3.0 %collective-permute-start.2 = (bf16[2,17,32,128]{3,2,1,0:T(8,128)(2,1)S(1)}, bf16[2,17,32,128]{3,2,1,0:T(8,128)(2,1)S(1)}, u32[]{:S(2)}, u32[]{:S(2)}) collective-permute-start(bf16[2,17,32,128]{3,2,1,0:T(8,128)(2,1)S(1)} %pad_maximum_fusion.2), channel_id=1, source_target_pairs={{0,64},{4,20},{8,72},{12,28},{16,80},{20,4},{24,88},{28,12},{32,96... | collective-permute-start | bytes 835592 | tf_op jit(solution)/shard_map/ppermute | solution.py:37
  7.2 3.5 %collective-permute-done.2 = bf16[2,17,32,128]{3,2,1,0:T(8,128)(2,1)S(1)} collective-permute-done((bf16[2,17,32,128]{3,2,1,0:T(8,128)(2,1)S(1)}, bf16[2,17,32,128]{3,2,1,0:T(8,128)(2,1)S(1)}, u32[]{:S(2)}, u32[]{:S(2)}) %collective-permute-start.2) | collective-permute-done | bytes 278560 | tf_op jit(solution)/shard_map/ppermute | solution.py:37
  10.7 3.0 %collective-permute-done.3 = bf16[2,17,32,128]{3,2,1,0:T(8,128)(2,1)S(1)} collective-permute-done((bf16[2,17,32,128]{3,2,1,0:T(8,128)(2,1)S(1)}, bf16[2,17,32,128]{3,2,1,0:T(8,128)(2,1)S(1)}, u32[]{:S(2)}, u32[]{:S(2)}) %collective-permute-start.3) | collective-permute-done | bytes 278560 | tf_op jit(solution)/shard_map/ppermute | solution.py:37
  13.7 3.9 %collective-permute-start.7 = (bf16[2,2,17,32,128]{4,3,2,1,0:T(8,128)(2,1)S(1)}, bf16[2,2,17,32,128]{4,3,2,1,0:T(8,128)(2,1)S(1)}, u32[]{:S(2)}, u32[]{:S(2)}) collective-permute-start(bf16[2,2,17,32,128]{4,3,2,1,0:T(8,128)(2,1)S(1)} %pad_maximum_fusion.1.refs_1_), channel_id=1, source_target_pairs={{0,24},{4,100},{8,0},{12,108},{16,8},{20,116},{24,16},{28,124},{32... | collective-permute-start | bytes 1671176 | tf_op jit(solution)/shard_map/ppermute | solution.py:40
  20.5 2.9 %collective-permute-start.6 = (bf16[2,2,17,32,128]{4,3,2,1,0:T(8,128)(2,1)S(1)}, bf16[2,2,17,32,128]{4,3,2,1,0:T(8,128)(2,1)}, u32[]{:S(2)}, u32[]{:S(2)}) collective-permute-start(bf16[2,2,17,32,128]{4,3,2,1,0:T(8,128)(2,1)S(1)} %pad_maximum_fusion.refs_0_), channel_id=1, source_target_pairs={{0,24},{4,100},{8,0},{12,108},{16,8},{20,116},{24,16},{28,124},{32... | collective-permute-start | bytes 1671176 | tf_op jit(solution)/shard_map/ppermute | solution.py:41
  29.3 4.3 %collective-permute-done.5.refs_3_ = bf16[2,2,17,32,128]{4,3,2,1,0:T(8,128)(2,1)S(1)} collective-permute-done((bf16[2,2,17,32,128]{4,3,2,1,0:T(8,128)(2,1)S(1)}, bf16[2,2,17,32,128]{4,3,2,1,0:T(8,128)(2,1)S(1)}, u32[]{:S(2)}, u32[]{:S(2)}) %collective-permute-start.5) | collective-permute-done | bytes 557088 | tf_op jit(solution)/shard_map/ppermute | solution.py:41
  37.4 5.0 %collective-permute-done.9.refs_7_ = bf16[2,2,17,32,128]{4,3,2,1,0:T(8,128)(2,1)} collective-permute-done((bf16[2,2,17,32,128]{4,3,2,1,0:T(8,128)(2,1)S(1)}, bf16[2,2,17,32,128]{4,3,2,1,0:T(8,128)(2,1)}, u32[]{:S(2)}, u32[]{:S(2)}) %collective-permute-start.9) | collective-permute-done | bytes 557088 | tf_op jit(solution)/shard_map/ppermute | solution.py:42
  50.2 6.6 %first_sum.1 = (f32[2,32,128]{2,1,0:T(8,128)}, bf16[120,17,32,128]{3,2,1,0:T(8,128)(2,1)}) custom-call(s32[7,64]{1,0:T(8,128)} %get-tuple-element.118.code_ref, bf16[2,2,17,32,128]{4,3,2,1,0:T(8,128)(2,1)} %copy-done.4, bf16[2,2,17,32,128]{4,3,2,1,0:T(8,128)(2,1)} %copy-done.3, bf16[2,2,17,32,128]{4,3,2,1,0:T(8,128)(2,1)} %copy-done.6, ...), custom_call_target="tpu_custom_call" | custom-call | flops 67108864 | bytes 6291456 | tf_op jit(solution)/shard_map/first_sum/pallas_call | solution.py:141
  66.4 4.8 %all-to-all-start = ((bf16[16,2,32,128]{3,2,1,0:T(8,128)(2,1)}), bf16[16,2,32,128]{3,2,1,0:T(8,128)(2,1)S(1)}, u32[]{:S(2)}, u32[]{:S(2)}) async-start(bf16[16,2,32,128]{3,2,1,0:T(8,128)(2,1)} %get-tuple-element.60), calls=%async_computation | async-start | bytes 524288 | tf_op jit(solution)/shard_map/all_to_all | solution.py:329
  71.2 5.3 %old_sum.6 = (f32[2,32,128]{2,1,0:T(8,128)S(1)}, s32[65]{0:T(128)S(1)}, bf16[16,128,128]{2,1,0:T(8,128)(2,1)S(1)}) custom-call(s32[7,64]{1,0:T(8,128)S(1)} %copy-done.1, s32[7,64]{1,0:T(8,128)S(1)} %get-tuple-element.92.fresh_ref, bf16[2040,32,128]{2,1,0:T(8,128)(2,1)} %bitcast.51, bf16[7,1,32,128,128]{4,3,2,1,0:T(8,128)(2,1)} %own_ref.11, ...), custom_call_target="tpu_custom_call" | custom-call | flops 67108864 | bytes 6291456 | tf_op jit(solution)/shard_map/old_sum/pallas_call | solution.py:141
  85.8 5.4 %all-to-all-start.1 = ((bf16[16,2,32,128]{3,2,1,0:T(8,128)(2,1)}), bf16[16,2,32,128]{3,2,1,0:T(8,128)(2,1)S(1)}, u32[]{:S(2)}, u32[]{:S(2)}) async-start(bf16[16,2,32,128]{3,2,1,0:T(8,128)(2,1)} %get-tuple-element.67), calls=%async_computation.1 | async-start | bytes 524288 | tf_op jit(solution)/shard_map/all_to_all | solution.py:329
  91.2 5.4 %old_sum.7 = (f32[2,32,128]{2,1,0:T(8,128)S(1)}, s32[65]{0:T(128)S(1)}, bf16[16,128,128]{2,1,0:T(8,128)(2,1)S(1)}) custom-call(s32[7,64]{1,0:T(8,128)S(1)} %copy-done.1, s32[7,64]{1,0:T(8,128)S(1)} %get-tuple-element.92.fresh_ref, bf16[2040,32,128]{2,1,0:T(8,128)(2,1)} %bitcast.52, bf16[32,32,128]{2,1,0:T(8,128)(2,1)S(1)} %bitcast.31, ...), custom_call_target="tpu_custom_call" | custom-call | flops 67108864 | bytes 6291456 | tf_op jit(solution)/shard_map/old_sum/pallas_call | solution.py:141
  99.9 3.1 %collective-permute-start.28 = (f32[2,32,128]{2,1,0:T(8,128)S(1)}, f32[2,32,128]{2,1,0:T(8,128)S(1)}, u32[]{:S(2)}, u32[]{:S(2)}) collective-permute-start(f32[2,32,128]{2,1,0:T(8,128)S(1)} %fresh_sum.7.p0), channel_id=1, source_target_pairs={{0,2},{1,3},{2,0},{3,1},{4,6},{5,7},{6,4},{7,5},{8,10},{9,11},{10,... | collective-permute-start | bytes 98312 | tf_op jit(solution)/shard_map/ppermute | solution.py:322
  107.8 4.7 %all-to-all-start.2 = ((bf16[16,2,32,128]{3,2,1,0:T(8,128)(2,1)}), bf16[16,2,32,128]{3,2,1,0:T(8,128)(2,1)S(1)}, u32[]{:S(2)}, u32[]{:S(2)}) async-start(bf16[16,2,32,128]{3,2,1,0:T(8,128)(2,1)} %get-tuple-element.74), calls=%async_computation.2 | async-start | bytes 524288 | tf_op jit(solution)/shard_map/all_to_all | solution.py:329
  112.5 5.6 %old_sum.8 = (f32[2,32,128]{2,1,0:T(8,128)S(1)}, s32[65]{0:T(128)S(1)}, bf16[16,128,128]{2,1,0:T(8,128)(2,1)S(1)}) custom-call(s32[7,64]{1,0:T(8,128)S(1)} %copy-done.1, s32[7,64]{1,0:T(8,128)S(1)} %get-tuple-element.92.fresh_ref, bf16[2040,32,128]{2,1,0:T(8,128)(2,1)} %bitcast.53, bf16[32,32,128]{2,1,0:T(8,128)(2,1)S(1)} %bitcast.32, ...), custom_call_target="tpu_custom_call" | custom-call | flops 67108864 | bytes 6291456 | tf_op jit(solution)/shard_map/old_sum/pallas_call | solution.py:141
  127.8 4.5 %all-to-all-start.3 = ((bf16[16,2,32,128]{3,2,1,0:T(8,128)(2,1)}), bf16[16,2,32,128]{3,2,1,0:T(8,128)(2,1)S(1)}, u32[]{:S(2)}, u32[]{:S(2)}) async-start(bf16[16,2,32,128]{3,2,1,0:T(8,128)(2,1)} %get-tuple-element.81), calls=%async_computation.3 | async-start | bytes 524288 | tf_op jit(solution)/shard_map/all_to_all | solution.py:329
  132.4 5.3 %old_sum.9 = (f32[2,32,128]{2,1,0:T(8,128)S(1)}, s32[65]{0:T(128)S(1)}, bf16[16,128,128]{2,1,0:T(8,128)(2,1)S(1)}) custom-call(s32[7,64]{1,0:T(8,128)S(1)} %copy-done.1, s32[7,64]{1,0:T(8,128)S(1)} %get-tuple-element.92.fresh_ref, bf16[2040,32,128]{2,1,0:T(8,128)(2,1)} %bitcast.54, bf16[32,32,128]{2,1,0:T(8,128)(2,1)S(1)} %bitcast.33, ...), custom_call_target="tpu_custom_call" | custom-call | flops 67108864 | bytes 6291456 | tf_op jit(solution)/shard_map/old_sum/pallas_call | solution.py:141
  141.0 3.1 %collective-permute-start.34 = (f32[2,32,128]{2,1,0:T(8,128)S(1)}, f32[2,32,128]{2,1,0:T(8,128)S(1)}, u32[]{:S(2)}, u32[]{:S(2)}) collective-permute-start(f32[2,32,128]{2,1,0:T(8,128)S(1)} %fresh_sum.9.p0), channel_id=1, source_target_pairs={{0,2},{1,3},{2,0},{3,1},{4,6},{5,7},{6,4},{7,5},{8,10},{9,11},{10,... | collective-permute-start | bytes 98312 | tf_op jit(solution)/shard_map/ppermute | solution.py:322
  149.3 4.6 %all-to-all-start.4 = ((bf16[16,2,32,128]{3,2,1,0:T(8,128)(2,1)}), bf16[16,2,32,128]{3,2,1,0:T(8,128)(2,1)S(1)}, u32[]{:S(2)}, u32[]{:S(2)}) async-start(bf16[16,2,32,128]{3,2,1,0:T(8,128)(2,1)} %get-tuple-element.88), calls=%async_computation.4 | async-start | bytes 524288 | tf_op jit(solution)/shard_map/all_to_all | solution.py:329
  153.9 5.4 %old_sum.10 = (f32[2,32,128]{2,1,0:T(8,128)S(1)}, s32[65]{0:T(128)S(1)}, bf16[16,128,128]{2,1,0:T(8,128)(2,1)S(1)}) custom-call(s32[7,64]{1,0:T(8,128)S(1)} %copy-done.1, s32[7,64]{1,0:T(8,128)S(1)} %get-tuple-element.92.fresh_ref, bf16[2040,32,128]{2,1,0:T(8,128)(2,1)} %bitcast.55, bf16[32,32,128]{2,1,0:T(8,128)(2,1)S(1)} %bitcast.34, ...), custom_call_target="tpu_custom_call" | custom-call | flops 67108864 | bytes 6291456 | tf_op jit(solution)/shard_map/old_sum/pallas_call | solution.py:141
  169.1 4.6 %all-to-all-start.5 = ((bf16[16,2,32,128]{3,2,1,0:T(8,128)(2,1)}), bf16[16,2,32,128]{3,2,1,0:T(8,128)(2,1)S(1)}, u32[]{:S(2)}, u32[]{:S(2)}) async-start(bf16[16,2,32,128]{3,2,1,0:T(8,128)(2,1)} %get-tuple-element.95), calls=%async_computation.5 | async-start | bytes 524288 | tf_op jit(solution)/shard_map/all_to_all | solution.py:329
  173.8 5.3 %old_sum.11 = (f32[2,32,128]{2,1,0:T(8,128)S(1)}, s32[65]{0:T(128)S(1)}, bf16[16,128,128]{2,1,0:T(8,128)(2,1)S(1)}) custom-call(s32[7,64]{1,0:T(8,128)S(1)} %copy-done.1, s32[7,64]{1,0:T(8,128)S(1)} %get-tuple-element.92.fresh_ref, bf16[2040,32,128]{2,1,0:T(8,128)(2,1)} %bitcast.56, bf16[32,32,128]{2,1,0:T(8,128)(2,1)S(1)} %bitcast.35, ...), custom_call_target="tpu_custom_call" | custom-call | flops 67108864 | bytes 6291456 | tf_op jit(solution)/shard_map/old_sum/pallas_call | solution.py:141
  182.6 3.3 %collective-permute-start.40 = (f32[2,32,128]{2,1,0:T(8,128)S(1)}, f32[2,32,128]{2,1,0:T(8,128)S(1)}, u32[]{:S(2)}, u32[]{:S(2)}) collective-permute-start(f32[2,32,128]{2,1,0:T(8,128)S(1)} %fresh_sum.11.p0), channel_id=1, source_target_pairs={{0,2},{1,3},{2,0},{3,1},{4,6},{5,7},{6,4},{7,5},{8,10},{9,11},{10,... | collective-permute-start | bytes 98312 | tf_op jit(solution)/shard_map/ppermute | solution.py:322
  190.0 16.4 %collective-permute-start.42 = (bf16[7,32,128]{2,1,0:T(8,128)(2,1)S(1)}, bf16[7,32,128]{2,1,0:T(8,128)(2,1)S(1)}, u32[]{:S(2)}, u32[]{:S(2)}) collective-permute-start(bf16[7,32,128]{2,1,0:T(8,128)(2,1)S(1)} %get-tuple-element.104), channel_id=1, source_target_pairs={{0,4},{4,0},{1,5},{5,1},{2,6},{6,2},{3,7},{7,3},{8,12},{12,8},{9,1... | collective-permute-start | bytes 172040 | tf_op jit(solution)/shard_map/ppermute | solution.py:23
  (140 shorter events, 88.6 us)
Async XLA Ops:
  2.0 48.2 %collective-permute-start.18 = (bf16[7,1,32,128,128]{4,3,2,1,0:T(8,128)(2,1)}, bf16[7,1,32,128,128]{4,3,2,1,0:T(8,128)(2,1)}, u32[]{:S(2)}, u32[]{:S(2)}) collective-permute-start(bf16[7,1,32,128,128]{4,3,2,1,0:T(8,128)(2,1)} %own_ref.11), channel_id=1, source_target_pairs={{0,4},{4,0},{1,5},{5,1},{2,6},{6,2},{3,7},{7,3},{8,12},{12,8},{9,1... | collective-permute-start | bytes 22020104 | tf_op jit(solution)/shard_map/ppermute | solution.py:23
  3.5 7.2 %collective-permute-start.2 = (bf16[2,17,32,128]{3,2,1,0:T(8,128)(2,1)S(1)}, bf16[2,17,32,128]{3,2,1,0:T(8,128)(2,1)S(1)}, u32[]{:S(2)}, u32[]{:S(2)}) collective-permute-start(bf16[2,17,32,128]{3,2,1,0:T(8,128)(2,1)S(1)} %pad_maximum_fusion.2), channel_id=1, source_target_pairs={{0,64},{4,20},{8,72},{12,28},{16,80},{20,4},{24,88},{28,12},{32,96... | collective-permute-start | bytes 835592 | tf_op jit(solution)/shard_map/ppermute | solution.py:37
  6.5 7.2 %collective-permute-start.3 = (bf16[2,17,32,128]{3,2,1,0:T(8,128)(2,1)S(1)}, bf16[2,17,32,128]{3,2,1,0:T(8,128)(2,1)S(1)}, u32[]{:S(2)}, u32[]{:S(2)}) collective-permute-start(bf16[2,17,32,128]{3,2,1,0:T(8,128)(2,1)S(1)} %pad_maximum_fusion.2), channel_id=1, source_target_pairs={{0,96},{4,28},{8,104},{12,20},{16,112},{20,12},{24,120},{28,4},{32... | collective-permute-start | bytes 835592 | tf_op jit(solution)/shard_map/ppermute | solution.py:37
  7.2 10.4 %collective-permute-start.1 = (bf16[2,17,32,128]{3,2,1,0:T(8,128)(2,1)S(1)}, bf16[2,17,32,128]{3,2,1,0:T(8,128)(2,1)S(1)}, u32[]{:S(2)}, u32[]{:S(2)}) collective-permute-start(bf16[2,17,32,128]{3,2,1,0:T(8,128)(2,1)S(1)} %pad_maximum_fusion.2), channel_id=1, source_target_pairs={{0,32},{4,12},{8,40},{12,4},{16,48},{20,28},{24,56},{28,20},{32,0}... | collective-permute-start | bytes 835592 | tf_op jit(solution)/shard_map/ppermute | solution.py:37
  13.7 10.4 %collective-permute-start.7 = (bf16[2,2,17,32,128]{4,3,2,1,0:T(8,128)(2,1)S(1)}, bf16[2,2,17,32,128]{4,3,2,1,0:T(8,128)(2,1)S(1)}, u32[]{:S(2)}, u32[]{:S(2)}) collective-permute-start(bf16[2,2,17,32,128]{4,3,2,1,0:T(8,128)(2,1)S(1)} %pad_maximum_fusion.1.refs_1_), channel_id=1, source_target_pairs={{0,24},{4,100},{8,0},{12,108},{16,8},{20,116},{24,16},{28,124},{32... | collective-permute-start | bytes 1671176 | tf_op jit(solution)/shard_map/ppermute | solution.py:40
  17.7 10.0 %collective-permute-start.4 = (bf16[2,2,17,32,128]{4,3,2,1,0:T(8,128)(2,1)S(1)}, bf16[2,2,17,32,128]{4,3,2,1,0:T(8,128)(2,1)S(1)}, u32[]{:S(2)}, u32[]{:S(2)}) collective-permute-start(bf16[2,2,17,32,128]{4,3,2,1,0:T(8,128)(2,1)S(1)} %pad_maximum_fusion.refs_0_), channel_id=1, source_target_pairs={{0,8},{4,36},{8,16},{12,44},{16,24},{20,52},{24,0},{28,60},{32,40}... | collective-permute-start | bytes 1671176 | tf_op jit(solution)/shard_map/ppermute | solution.py:40
  19.5 14.2 %collective-permute-start.5 = (bf16[2,2,17,32,128]{4,3,2,1,0:T(8,128)(2,1)S(1)}, bf16[2,2,17,32,128]{4,3,2,1,0:T(8,128)(2,1)S(1)}, u32[]{:S(2)}, u32[]{:S(2)}) collective-permute-start(bf16[2,2,17,32,128]{4,3,2,1,0:T(8,128)(2,1)S(1)} %pad_maximum_fusion.1.refs_1_), channel_id=1, source_target_pairs={{0,8},{4,36},{8,16},{12,44},{16,24},{20,52},{24,0},{28,60},{32,40}... | collective-permute-start | bytes 1671176 | tf_op jit(solution)/shard_map/ppermute | solution.py:41
  20.5 13.1 %collective-permute-start.6 = (bf16[2,2,17,32,128]{4,3,2,1,0:T(8,128)(2,1)S(1)}, bf16[2,2,17,32,128]{4,3,2,1,0:T(8,128)(2,1)}, u32[]{:S(2)}, u32[]{:S(2)}) collective-permute-start(bf16[2,2,17,32,128]{4,3,2,1,0:T(8,128)(2,1)S(1)} %pad_maximum_fusion.refs_0_), channel_id=1, source_target_pairs={{0,24},{4,100},{8,0},{12,108},{16,8},{20,116},{24,16},{28,124},{32... | collective-permute-start | bytes 1671176 | tf_op jit(solution)/shard_map/ppermute | solution.py:41
  24.1 11.0 %collective-permute-start.11 = (bf16[2,2,17,32,128]{4,3,2,1,0:T(8,128)(2,1)S(1)}, bf16[2,2,17,32,128]{4,3,2,1,0:T(8,128)(2,1)S(1)}, u32[]{:S(2)}, u32[]{:S(2)}) collective-permute-start(bf16[2,2,17,32,128]{4,3,2,1,0:T(8,128)(2,1)S(1)} %pad_maximum_fusion.1.refs_1_), channel_id=1, source_target_pairs={{0,4},{4,0},{1,5},{5,1},{2,6},{6,2},{3,7},{7,3},{8,12},{12,8},{9,1... | collective-permute-start | bytes 1671176 | tf_op jit(solution)/shard_map/ppermute | solution.py:23
  27.6 9.7 %collective-permute-start.10 = (bf16[2,2,17,32,128]{4,3,2,1,0:T(8,128)(2,1)S(1)}, bf16[2,2,17,32,128]{4,3,2,1,0:T(8,128)(2,1)S(1)}, u32[]{:S(2)}, u32[]{:S(2)}) collective-permute-start(bf16[2,2,17,32,128]{4,3,2,1,0:T(8,128)(2,1)S(1)} %pad_maximum_fusion.refs_0_), channel_id=1, source_target_pairs={{0,4},{4,0},{1,5},{5,1},{2,6},{6,2},{3,7},{7,3},{8,12},{12,8},{9,1... | collective-permute-start | bytes 1671176 | tf_op jit(solution)/shard_map/ppermute | solution.py:23
  33.6 8.8 %collective-permute-start.9 = (bf16[2,2,17,32,128]{4,3,2,1,0:T(8,128)(2,1)S(1)}, bf16[2,2,17,32,128]{4,3,2,1,0:T(8,128)(2,1)}, u32[]{:S(2)}, u32[]{:S(2)}) collective-permute-start(bf16[2,2,17,32,128]{4,3,2,1,0:T(8,128)(2,1)S(1)} %collective-permute-done.7.refs_5_), channel_id=1, source_target_pairs={{0,24},{4,100},{8,0},{12,108},{16,8},{20,116},{24,16},{28,124},{32... | collective-permute-start | bytes 1671176 | tf_op jit(solution)/shard_map/ppermute | solution.py:42
  33.6 11.3 %collective-permute-start.8 = (bf16[2,2,17,32,128]{4,3,2,1,0:T(8,128)(2,1)S(1)}, bf16[2,2,17,32,128]{4,3,2,1,0:T(8,128)(2,1)}, u32[]{:S(2)}, u32[]{:S(2)}) collective-permute-start(bf16[2,2,17,32,128]{4,3,2,1,0:T(8,128)(2,1)S(1)} %collective-permute-done.4.refs_2_), channel_id=1, source_target_pairs={{0,8},{4,36},{8,16},{12,44},{16,24},{20,52},{24,0},{28,60},{32,40}... | collective-permute-start | bytes 1671176 | tf_op jit(solution)/shard_map/ppermute | solution.py:42
  35.1 11.1 %collective-permute-start.15 = (bf16[2,2,17,32,128]{4,3,2,1,0:T(8,128)(2,1)S(1)}, bf16[2,2,17,32,128]{4,3,2,1,0:T(8,128)(2,1)S(1)}, u32[]{:S(2)}, u32[]{:S(2)}) collective-permute-start(bf16[2,2,17,32,128]{4,3,2,1,0:T(8,128)(2,1)S(1)} %collective-permute-done.7.refs_5_), channel_id=1, source_target_pairs={{0,4},{4,0},{1,5},{5,1},{2,6},{6,2},{3,7},{7,3},{8,12},{12,8},{9,1... | collective-permute-start | bytes 1671176 | tf_op jit(solution)/shard_map/ppermute | solution.py:23
  37.3 9.0 %collective-permute-start.12 = (bf16[2,2,17,32,128]{4,3,2,1,0:T(8,128)(2,1)S(1)}, bf16[2,2,17,32,128]{4,3,2,1,0:T(8,128)(2,1)S(1)}, u32[]{:S(2)}, u32[]{:S(2)}) collective-permute-start(bf16[2,2,17,32,128]{4,3,2,1,0:T(8,128)(2,1)S(1)} %collective-permute-done.4.refs_2_), channel_id=1, source_target_pairs={{0,4},{4,0},{1,5},{5,1},{2,6},{6,2},{3,7},{7,3},{8,12},{12,8},{9,1... | collective-permute-start | bytes 1671176 | tf_op jit(solution)/shard_map/ppermute | solution.py:23
  42.4 6.5 %collective-permute-start.13 = (bf16[2,2,17,32,128]{4,3,2,1,0:T(8,128)(2,1)S(1)}, bf16[2,2,17,32,128]{4,3,2,1,0:T(8,128)(2,1)}, u32[]{:S(2)}, u32[]{:S(2)}) collective-permute-start(bf16[2,2,17,32,128]{4,3,2,1,0:T(8,128)(2,1)S(1)} %collective-permute-done.5.refs_3_), channel_id=1, source_target_pairs={{0,4},{4,0},{1,5},{5,1},{2,6},{6,2},{3,7},{7,3},{8,12},{12,8},{9,1... | collective-permute-start | bytes 1671176 | tf_op jit(solution)/shard_map/ppermute | solution.py:23
  48.9 11.9 %collective-permute-start.23 = (bf16[8,1,128,128]{3,2,1,0:T(8,128)(2,1)}, bf16[8,1,128,128]{3,2,1,0:T(8,128)(2,1)S(1)}, u32[]{:S(2)}, u32[]{:S(2)}) collective-permute-start(bf16[8,1,128,128]{3,2,1,0:T(8,128)(2,1)} %own_d_ref.13), channel_id=1, source_target_pairs={{0,4},{4,0},{1,5},{5,1},{2,6},{6,2},{3,7},{7,3},{8,12},{12,8},{9,1... | collective-permute-start | bytes 786440 | tf_op jit(solution)/shard_map/ppermute | solution.py:23
  49.4 11.3 %collective-permute-start.22 = (bf16[8,1,32,128]{3,2,1,0:T(8,128)(2,1)S(1)}, bf16[8,1,32,128]{3,2,1,0:T(8,128)(2,1)S(1)}, u32[]{:S(2)}, u32[]{:S(2)}) collective-permute-start(bf16[8,1,32,128]{3,2,1,0:T(8,128)(2,1)S(1)} %get-tuple-element.100), channel_id=1, source_target_pairs={{0,4},{4,0},{1,5},{5,1},{2,6},{6,2},{3,7},{7,3},{8,12},{12,8},{9,1... | collective-permute-start | bytes 196616 | tf_op jit(solution)/shard_map/ppermute | solution.py:23
  66.4 12.3 %all-to-all-start = ((bf16[16,2,32,128]{3,2,1,0:T(8,128)(2,1)}), bf16[16,2,32,128]{3,2,1,0:T(8,128)(2,1)S(1)}, u32[]{:S(2)}, u32[]{:S(2)}) async-start(bf16[16,2,32,128]{3,2,1,0:T(8,128)(2,1)} %get-tuple-element.60), calls=%async_computation | async-start | bytes 524288 | tf_op jit(solution)/shard_map/all_to_all | solution.py:329
  85.8 13.0 %all-to-all-start.1 = ((bf16[16,2,32,128]{3,2,1,0:T(8,128)(2,1)}), bf16[16,2,32,128]{3,2,1,0:T(8,128)(2,1)S(1)}, u32[]{:S(2)}, u32[]{:S(2)}) async-start(bf16[16,2,32,128]{3,2,1,0:T(8,128)(2,1)} %get-tuple-element.67), calls=%async_computation.1 | async-start | bytes 524288 | tf_op jit(solution)/shard_map/all_to_all | solution.py:329
  107.8 12.2 %all-to-all-start.2 = ((bf16[16,2,32,128]{3,2,1,0:T(8,128)(2,1)}), bf16[16,2,32,128]{3,2,1,0:T(8,128)(2,1)S(1)}, u32[]{:S(2)}, u32[]{:S(2)}) async-start(bf16[16,2,32,128]{3,2,1,0:T(8,128)(2,1)} %get-tuple-element.74), calls=%async_computation.2 | async-start | bytes 524288 | tf_op jit(solution)/shard_map/all_to_all | solution.py:329
  127.8 12.1 %all-to-all-start.3 = ((bf16[16,2,32,128]{3,2,1,0:T(8,128)(2,1)}), bf16[16,2,32,128]{3,2,1,0:T(8,128)(2,1)S(1)}, u32[]{:S(2)}, u32[]{:S(2)}) async-start(bf16[16,2,32,128]{3,2,1,0:T(8,128)(2,1)} %get-tuple-element.81), calls=%async_computation.3 | async-start | bytes 524288 | tf_op jit(solution)/shard_map/all_to_all | solution.py:329
  149.3 12.2 %all-to-all-start.4 = ((bf16[16,2,32,128]{3,2,1,0:T(8,128)(2,1)}), bf16[16,2,32,128]{3,2,1,0:T(8,128)(2,1)S(1)}, u32[]{:S(2)}, u32[]{:S(2)}) async-start(bf16[16,2,32,128]{3,2,1,0:T(8,128)(2,1)} %get-tuple-element.88), calls=%async_computation.4 | async-start | bytes 524288 | tf_op jit(solution)/shard_map/all_to_all | solution.py:329
  169.1 12.2 %all-to-all-start.5 = ((bf16[16,2,32,128]{3,2,1,0:T(8,128)(2,1)}), bf16[16,2,32,128]{3,2,1,0:T(8,128)(2,1)S(1)}, u32[]{:S(2)}, u32[]{:S(2)}) async-start(bf16[16,2,32,128]{3,2,1,0:T(8,128)(2,1)} %get-tuple-element.95), calls=%async_computation.5 | async-start | bytes 524288 | tf_op jit(solution)/shard_map/all_to_all | solution.py:329
  190.0 17.3 %collective-permute-start.42 = (bf16[7,32,128]{2,1,0:T(8,128)(2,1)S(1)}, bf16[7,32,128]{2,1,0:T(8,128)(2,1)S(1)}, u32[]{:S(2)}, u32[]{:S(2)}) collective-permute-start(bf16[7,32,128]{2,1,0:T(8,128)(2,1)S(1)} %get-tuple-element.104), channel_id=1, source_target_pairs={{0,4},{4,0},{1,5},{5,1},{2,6},{6,2},{3,7},{7,3},{8,12},{12,8},{9,1... | collective-permute-start | bytes 172040 | tf_op jit(solution)/shard_map/ppermute | solution.py:23
  (37 other events, 296.0 us)

commit v11 on v10

--- a/solution.py
+++ b/solution.py
@@ -23,24 +23,31 @@
     return lax.ppermute(v, "core", xor_pairs(2, 1))
 
 
-def pairs(stage, move):
+def pairs(stage, move, cross=False):
     result = []
     for z in range(4):
         for y in range(4):
             for core in range(2):
                 to_z, to_y = (move(z), y) if core + 1 == stage else (z, move(y))
-                result.append(((z * 4 + y) * 2 + core, (to_z * 4 + to_y) * 2 + core))
+                to_core = 1 - core if cross else core
+                result.append(((z * 4 + y) * 2 + core, (to_z * 4 + to_y) * 2 + to_core))
     return result
 
 
 def gather_parts(v):
-    near = [lax.ppermute(v, ROWS, pairs(1, lambda i, k=k: i ^ k)) for k in (1, 2, 3)]
-    low, high = jnp.stack([v, near[0]]), jnp.stack(near[1:])
-    up, down = pairs(2, lambda i: (i + 1) % 4), pairs(2, lambda i: (i + 3) % 4)
-    before_low, after_high = lax.ppermute(low, ROWS, up), lax.ppermute(high, ROWS, down)
-    before_high, after_low = lax.ppermute(high, ROWS, up), lax.ppermute(low, ROWS, down)
-    far = [lax.ppermute(before_low, ROWS, up), lax.ppermute(after_high, ROWS, down)]
-    return [low, high, before_low, before_high, after_low, after_high] + far
+    after_one, before_one = lambda i: (i + 1) % 4, lambda i: (i + 3) % 4
+    near = [v] + [lax.ppermute(v, ROWS, pairs(1, lambda i, k=k: i ^ k)) for k in (1, 2, 3)]
+    mine, theirs = jnp.stack([one[0] for one in near]), jnp.stack([one[1] for one in near])
+
+    def spread(part, cross):
+        again = 1 if cross else 2
+        before = lax.ppermute(part, ROWS, pairs(2, after_one, cross))
+        after = lax.ppermute(part, ROWS, pairs(2, before_one, cross))
+        far_low = lax.ppermute(before[:2], ROWS, pairs(again, after_one))
+        far_high = lax.ppermute(after[2:], ROWS, pairs(again, before_one))
+        return [before, after, far_low, far_high]
+
+    return [mine, *spread(mine, False), swap_cores(theirs), *spread(theirs, True)]
 
 
 def nt_dot(x, a):
@@ -84,9 +91,8 @@
     own_ref, other_ref, out_ref, store_ref, blocks, block_sems, pack_sems, packed, store_sem = refs
     packs, start = [], 0
     for i, source in enumerate(sources):
-        which = 0 if i < len(sources) // 2 else 1
         target = packed.at[pl.ds(start, source.shape[0])]
-        packs.append(pltpu.make_async_copy(source.at[:, which], target, pack_sems.at[i]))
+        packs.append(pltpu.make_async_copy(source, target, pack_sems.at[i]))
         start += source.shape[0]
     keep = pltpu.make_async_copy(packed, store_ref.at[pl.ds(0, start)], store_sem)
 
@@ -157,9 +163,9 @@
 
 
 def first_sum(code, sources, own, other):
-    one = sources[0].shape[3:]
+    one = sources[0].shape[2:]
     parts = sum(v.shape[0] for v in sources)
-    each = sources[0].shape[2]
+    each = sources[0].shape[1]
     store = jax.ShapeDtypeStruct((2048 // each, each) + one, jnp.bfloat16)
     extra = [
         pltpu.SemaphoreType.DMA((len(sources),)),
@@ -294,7 +300,6 @@
     off_other = swap_cores(off_sent)
 
     pieces = gather_parts(known)
-    pieces = pieces + [swap_cores(piece) for piece in pieces]
 
     keep, index = code_both >= 1024, code_both % 1024
     in_outer = index < outer

time: 209 us -> 205 us (0.981)
  waiting for transfers between devices: 52.7 us -> 47.8 us
  starting transfers between devices: 98.2 us -> 95.5 us
  Pallas kernels: 49.1 us -> 51.4 us
    ppermute x13 -> x6, starting transfers between devices: 28.7 us -> 21.1 us  [swap_cores(): return lax.ppermute(v, 'core', xor_pairs(2, 1))]
    ppermute x6 -> x8, starting transfers between devices: 9.4 us -> 14.5 us  [the longest x2 5.36 us: spread(): far_high = lax.ppermute(after[2:], ROWS, pairs(again, before_one))]
    ppermute x6 -> x8, waiting for transfers between devices: 12.1 us -> 8.07 us  [the longest x2 6.37 us: spread(): before = lax.ppermute(part, ROWS, pairs(2, after_one, cross))]
    slice x0 -> x8, local copies, waits for them, and re-layouts: none -> 2.33 us  [the longest x2 1.51 us: spread(): far_high = lax.ppermute(after[2:], ROWS, pairs(again, before_one))]
  transfers between devices with their start and end apart: 49 -> 44, of which waited for: 27 -> 28; matrix products, arithmetic and copies ran while one was open for 1% -> 3% of each run, Pallas kernels for 19% -> 20%
where the time goes in v11:
time: 205 us; the launch traced here: 204 us
  starting transfers between devices  95.5 us (47%)
  Pallas kernels  51.4 us (25%)
  waiting for transfers between devices  47.8 us (23%)
  local copies, waits for them, and re-layouts  4.14 us (2%)
  other arithmetic  4.06 us (2%)
    pallas_call x7, Pallas kernels, sum_call(): pl.pallas_call(kernel, out_shape=[jax.ShapeDtypeStruct((2, rhs_cols, bloc...  39.9 us
    all_to_all x6, starting transfers between devices, on_device(): solved = lax.all_to_all(sent, ('z', 'y'), 0, 0).reshape(32, half, block)  28.6 us
    ppermute x21, starting transfers between devices, on_device(): lax.ppermute(value, 'x', xor_pairs(4, k))  27.5 us
    ppermute x6, starting transfers between devices, swap_cores(): return lax.ppermute(v, 'core', xor_pairs(2, 1))  21.1 us
    ppermute x21, waiting for transfers between devices, on_device(): lax.ppermute(value, 'x', xor_pairs(4, k))  20.1 us
    all_to_all x6, waiting for transfers between devices, on_device(): solved = lax.all_to_all(sent, ('z', 'y'), 0, 0).reshape(32, half, block)  11.7 us
    ppermute x3, waiting for transfers between devices, gather_parts(): lax.ppermute(v, ROWS, pairs(1, lambda i, k=k: i ^ k))  6.8 us
    ppermute x2, waiting for transfers between devices, spread(): before = lax.ppermute(part, ROWS, pairs(2, after_one, cross))  6.37 us
  transfers between devices with their start and end apart: 44, of which 28 were waited for; matrix products, arithmetic and copies ran while one was open for 3% of the time, Pallas kernels for 20%

profile of v11, /device:TPU:1, one launch (start us, length us, event | category | flops | bytes accessed | tf_op | source)
XLA Modules:
  0.0 204.3 jit_solution(9519238626994300291)
XLA Ops:
  3.5 3.0 %collective-permute-start.2 = (bf16[2,17,32,128]{3,2,1,0:T(8,128)(2,1)S(1)}, bf16[2,17,32,128]{3,2,1,0:T(8,128)(2,1)S(1)}, u32[]{:S(2)}, u32[]{:S(2)}) collective-permute-start(bf16[2,17,32,128]{3,2,1,0:T(8,128)(2,1)S(1)} %pad_maximum_fusion.2), channel_id=1, source_target_pairs={{0,64},{4,20},{8,72},{12,28},{16,80},{20,4},{24,88},{28,12},{32,96... | collective-permute-start | bytes 835592 | tf_op jit(solution)/shard_map/ppermute | solution.py:39
  7.3 3.4 %collective-permute-done.2 = bf16[2,17,32,128]{3,2,1,0:T(8,128)(2,1)S(1)} collective-permute-done((bf16[2,17,32,128]{3,2,1,0:T(8,128)(2,1)S(1)}, bf16[2,17,32,128]{3,2,1,0:T(8,128)(2,1)S(1)}, u32[]{:S(2)}, u32[]{:S(2)}) %collective-permute-start.2) | collective-permute-done | bytes 278560 | tf_op jit(solution)/shard_map/ppermute | solution.py:39
  10.8 3.0 %collective-permute-done.3 = bf16[2,17,32,128]{3,2,1,0:T(8,128)(2,1)S(1)} collective-permute-done((bf16[2,17,32,128]{3,2,1,0:T(8,128)(2,1)S(1)}, bf16[2,17,32,128]{3,2,1,0:T(8,128)(2,1)S(1)}, u32[]{:S(2)}, u32[]{:S(2)}) %collective-permute-start.3) | collective-permute-done | bytes 278560 | tf_op jit(solution)/shard_map/ppermute | solution.py:39
  20.4 2.7 %collective-permute-start.5 = (bf16[4,17,32,128]{3,2,1,0:T(8,128)(2,1)S(1)}, bf16[4,17,32,128]{3,2,1,0:T(8,128)(2,1)S(1)}, u32[]{:S(2)}, u32[]{:S(2)}) collective-permute-start(bf16[4,17,32,128]{3,2,1,0:T(8,128)(2,1)S(1)} %pad_maximum_fusion.refs_0_), channel_id=1, source_target_pairs={{0,24},{4,100},{8,0},{12,108},{16,8},{20,116},{24,16},{28,124},{32... | collective-permute-start | bytes 1671176 | tf_op jit(solution)/shard_map/ppermute | solution.py:45
  23.0 4.1 %collective-permute-done.9.refs_6_ = bf16[4,17,32,128]{3,2,1,0:T(8,128)(2,1)S(1)} collective-permute-done((bf16[4,17,32,128]{3,2,1,0:T(8,128)(2,1)}, bf16[4,17,32,128]{3,2,1,0:T(8,128)(2,1)S(1)}, u32[]{:S(2)}, u32[]{:S(2)}) %collective-permute-start.9) | collective-permute-done | bytes 557088 | tf_op jit(solution)/shard_map/ppermute | solution.py:44
  33.0 2.7 %collective-permute-start.12 = (bf16[2,17,32,128]{3,2,1,0:T(8,128)(2,1)}, bf16[2,17,32,128]{3,2,1,0:T(8,128)(2,1)}, u32[]{:S(2)}, u32[]{:S(2)}) collective-permute-start(bf16[2,17,32,128]{3,2,1,0:T(8,128)(2,1)} %slice.121), channel_id=1, source_target_pairs={{0,96},{4,28},{8,104},{12,4},{16,112},{20,12},{24,120},{28,20},{32... | collective-permute-start | bytes 835592 | tf_op jit(solution)/shard_map/ppermute | solution.py:47
  38.2 2.6 %collective-permute-start.7 = (bf16[2,17,32,128]{3,2,1,0:T(8,128)(2,1)}, bf16[2,17,32,128]{3,2,1,0:T(8,128)(2,1)}, u32[]{:S(2)}, u32[]{:S(2)}) collective-permute-start(bf16[2,17,32,128]{3,2,1,0:T(8,128)(2,1)} %slice.116), channel_id=1, source_target_pairs={{0,24},{4,100},{8,0},{12,108},{16,8},{20,116},{24,16},{28,124},{32... | collective-permute-start | bytes 835592 | tf_op jit(solution)/shard_map/ppermute | solution.py:47
  44.7 6.4 %first_sum.1 = (f32[2,32,128]{2,1,0:T(8,128)}, bf16[120,17,32,128]{3,2,1,0:T(8,128)(2,1)}) custom-call(s32[7,64]{1,0:T(8,128)} %get-tuple-element.126.code_ref, bf16[4,17,32,128]{3,2,1,0:T(8,128)(2,1)} %copy-done.3, bf16[4,17,32,128]{3,2,1,0:T(8,128)(2,1)} %copy-done.6, bf16[4,17,32,128]{3,2,1,0:T(8,128)(2,1)} %copy-done.7, ...), custom_call_target="tpu_custom_call" | custom-call | flops 67108864 | bytes 6291456 | tf_op jit(solution)/shard_map/first_sum/pallas_call | solution.py:147
  61.0 4.8 %all-to-all-start = ((bf16[16,2,32,128]{3,2,1,0:T(8,128)(2,1)}), bf16[16,2,32,128]{3,2,1,0:T(8,128)(2,1)S(1)}, u32[]{:S(2)}, u32[]{:S(2)}) async-start(bf16[16,2,32,128]{3,2,1,0:T(8,128)(2,1)} %get-tuple-element.60), calls=%async_computation | async-start | bytes 524288 | tf_op jit(solution)/shard_map/all_to_all | solution.py:334
  65.8 5.6 %old_sum.6 = (f32[2,32,128]{2,1,0:T(8,128)S(1)}, s32[65]{0:T(128)S(1)}, bf16[16,128,128]{2,1,0:T(8,128)(2,1)S(1)}) custom-call(s32[7,64]{1,0:T(8,128)S(1)} %copy-done.1, s32[7,64]{1,0:T(8,128)S(1)} %get-tuple-element.92.fresh_ref, bf16[2040,32,128]{2,1,0:T(8,128)(2,1)} %bitcast.47, bf16[7,1,32,128,128]{4,3,2,1,0:T(8,128)(2,1)} %own_ref.11, ...), custom_call_target="tpu_custom_call" | custom-call | flops 67108864 | bytes 6291456 | tf_op jit(solution)/shard_map/old_sum/pallas_call | solution.py:147
  75.3 3.2 %collective-permute-start.21 = (f32[2,32,128]{2,1,0:T(8,128)S(1)}, f32[2,32,128]{2,1,0:T(8,128)S(1)}, u32[]{:S(2)}, u32[]{:S(2)}) collective-permute-start(f32[2,32,128]{2,1,0:T(8,128)S(1)} %fresh_sum.6.p0), channel_id=1, source_target_pairs={{0,3},{1,2},{2,1},{3,0},{4,7},{5,6},{6,5},{7,4},{8,11},{9,10},{10,... | collective-permute-start | bytes 98312 | tf_op jit(solution)/shard_map/ppermute | solution.py:327
  80.7 4.6 %all-to-all-start.1 = ((bf16[16,2,32,128]{3,2,1,0:T(8,128)(2,1)}), bf16[16,2,32,128]{3,2,1,0:T(8,128)(2,1)S(1)}, u32[]{:S(2)}, u32[]{:S(2)}) async-start(bf16[16,2,32,128]{3,2,1,0:T(8,128)(2,1)} %get-tuple-element.67), calls=%async_computation.1 | async-start | bytes 524288 | tf_op jit(solution)/shard_map/all_to_all | solution.py:334
  85.3 5.5 %old_sum.7 = (f32[2,32,128]{2,1,0:T(8,128)S(1)}, s32[65]{0:T(128)S(1)}, bf16[16,128,128]{2,1,0:T(8,128)(2,1)S(1)}) custom-call(s32[7,64]{1,0:T(8,128)S(1)} %copy-done.1, s32[7,64]{1,0:T(8,128)S(1)} %get-tuple-element.92.fresh_ref, bf16[2040,32,128]{2,1,0:T(8,128)(2,1)} %bitcast.48, bf16[32,32,128]{2,1,0:T(8,128)(2,1)S(1)} %bitcast.27, ...), custom_call_target="tpu_custom_call" | custom-call | flops 67108864 | bytes 6291456 | tf_op jit(solution)/shard_map/old_sum/pallas_call | solution.py:147
  94.5 3.5 %collective-permute-start.23 = (f32[2,32,128]{2,1,0:T(8,128)S(1)}, f32[2,32,128]{2,1,0:T(8,128)S(1)}, u32[]{:S(2)}, u32[]{:S(2)}) collective-permute-start(f32[2,32,128]{2,1,0:T(8,128)S(1)} %fresh_sum.7.p0), channel_id=1, source_target_pairs={{0,2},{1,3},{2,0},{3,1},{4,6},{5,7},{6,4},{7,5},{8,10},{9,11},{10,... | collective-permute-start | bytes 98312 | tf_op jit(solution)/shard_map/ppermute | solution.py:327
  102.9 4.7 %all-to-all-start.2 = ((bf16[16,2,32,128]{3,2,1,0:T(8,128)(2,1)}), bf16[16,2,32,128]{3,2,1,0:T(8,128)(2,1)S(1)}, u32[]{:S(2)}, u32[]{:S(2)}) async-start(bf16[16,2,32,128]{3,2,1,0:T(8,128)(2,1)} %get-tuple-element.74), calls=%async_computation.2 | async-start | bytes 524288 | tf_op jit(solution)/shard_map/all_to_all | solution.py:334
  107.6 5.5 %old_sum.8 = (f32[2,32,128]{2,1,0:T(8,128)S(1)}, s32[65]{0:T(128)S(1)}, bf16[16,128,128]{2,1,0:T(8,128)(2,1)S(1)}) custom-call(s32[7,64]{1,0:T(8,128)S(1)} %copy-done.1, s32[7,64]{1,0:T(8,128)S(1)} %get-tuple-element.92.fresh_ref, bf16[2040,32,128]{2,1,0:T(8,128)(2,1)} %bitcast.49, bf16[32,32,128]{2,1,0:T(8,128)(2,1)S(1)} %bitcast.28, ...), custom_call_target="tpu_custom_call" | custom-call | flops 67108864 | bytes 6291456 | tf_op jit(solution)/shard_map/old_sum/pallas_call | solution.py:147
  122.6 5.2 %all-to-all-start.3 = ((bf16[16,2,32,128]{3,2,1,0:T(8,128)(2,1)}), bf16[16,2,32,128]{3,2,1,0:T(8,128)(2,1)S(1)}, u32[]{:S(2)}, u32[]{:S(2)}) async-start(bf16[16,2,32,128]{3,2,1,0:T(8,128)(2,1)} %get-tuple-element.81), calls=%async_computation.3 | async-start | bytes 524288 | tf_op jit(solution)/shard_map/all_to_all | solution.py:334
  127.8 5.7 %old_sum.9 = (f32[2,32,128]{2,1,0:T(8,128)S(1)}, s32[65]{0:T(128)S(1)}, bf16[16,128,128]{2,1,0:T(8,128)(2,1)S(1)}) custom-call(s32[7,64]{1,0:T(8,128)S(1)} %copy-done.1, s32[7,64]{1,0:T(8,128)S(1)} %get-tuple-element.92.fresh_ref, bf16[2040,32,128]{2,1,0:T(8,128)(2,1)} %bitcast.50, bf16[32,32,128]{2,1,0:T(8,128)(2,1)S(1)} %bitcast.29, ...), custom_call_target="tpu_custom_call" | custom-call | flops 67108864 | bytes 6291456 | tf_op jit(solution)/shard_map/old_sum/pallas_call | solution.py:147
  143.9 4.9 %all-to-all-start.4 = ((bf16[16,2,32,128]{3,2,1,0:T(8,128)(2,1)}), bf16[16,2,32,128]{3,2,1,0:T(8,128)(2,1)S(1)}, u32[]{:S(2)}, u32[]{:S(2)}) async-start(bf16[16,2,32,128]{3,2,1,0:T(8,128)(2,1)} %get-tuple-element.88), calls=%async_computation.4 | async-start | bytes 524288 | tf_op jit(solution)/shard_map/all_to_all | solution.py:334
  148.9 5.8 %old_sum.10 = (f32[2,32,128]{2,1,0:T(8,128)S(1)}, s32[65]{0:T(128)S(1)}, bf16[16,128,128]{2,1,0:T(8,128)(2,1)S(1)}) custom-call(s32[7,64]{1,0:T(8,128)S(1)} %copy-done.1, s32[7,64]{1,0:T(8,128)S(1)} %get-tuple-element.92.fresh_ref, bf16[2040,32,128]{2,1,0:T(8,128)(2,1)} %bitcast.51, bf16[32,32,128]{2,1,0:T(8,128)(2,1)S(1)} %bitcast.30, ...), custom_call_target="tpu_custom_call" | custom-call | flops 67108864 | bytes 6291456 | tf_op jit(solution)/shard_map/old_sum/pallas_call | solution.py:147
  164.9 4.3 %all-to-all-start.5 = ((bf16[16,2,32,128]{3,2,1,0:T(8,128)(2,1)}), bf16[16,2,32,128]{3,2,1,0:T(8,128)(2,1)S(1)}, u32[]{:S(2)}, u32[]{:S(2)}) async-start(bf16[16,2,32,128]{3,2,1,0:T(8,128)(2,1)} %get-tuple-element.95), calls=%async_computation.5 | async-start | bytes 524288 | tf_op jit(solution)/shard_map/all_to_all | solution.py:334
  169.3 5.4 %old_sum.11 = (f32[2,32,128]{2,1,0:T(8,128)S(1)}, s32[65]{0:T(128)S(1)}, bf16[16,128,128]{2,1,0:T(8,128)(2,1)S(1)}) custom-call(s32[7,64]{1,0:T(8,128)S(1)} %copy-done.1, s32[7,64]{1,0:T(8,128)S(1)} %get-tuple-element.92.fresh_ref, bf16[2040,32,128]{2,1,0:T(8,128)(2,1)} %bitcast.52, bf16[32,32,128]{2,1,0:T(8,128)(2,1)S(1)} %bitcast.31, ...), custom_call_target="tpu_custom_call" | custom-call | flops 67108864 | bytes 6291456 | tf_op jit(solution)/shard_map/old_sum/pallas_call | solution.py:147
  177.8 3.2 %collective-permute-start.35 = (f32[2,32,128]{2,1,0:T(8,128)S(1)}, f32[2,32,128]{2,1,0:T(8,128)S(1)}, u32[]{:S(2)}, u32[]{:S(2)}) collective-permute-start(f32[2,32,128]{2,1,0:T(8,128)S(1)} %fresh_sum.11.p0), channel_id=1, source_target_pairs={{0,2},{1,3},{2,0},{3,1},{4,6},{5,7},{6,4},{7,5},{8,10},{9,11},{10,... | collective-permute-start | bytes 98312 | tf_op jit(solution)/shard_map/ppermute | solution.py:327
  185.1 17.6 %collective-permute-start.37 = (bf16[7,32,128]{2,1,0:T(8,128)(2,1)S(1)}, bf16[7,32,128]{2,1,0:T(8,128)(2,1)S(1)}, u32[]{:S(2)}, u32[]{:S(2)}) collective-permute-start(bf16[7,32,128]{2,1,0:T(8,128)(2,1)S(1)} %get-tuple-element.112), channel_id=1, source_target_pairs={{0,4},{4,0},{1,5},{5,1},{2,6},{6,2},{3,7},{7,3},{8,12},{12,8},{9,1... | collective-permute-start | bytes 172040 | tf_op jit(solution)/shard_map/ppermute | solution.py:23
  (130 shorter events, 86.4 us)
Async XLA Ops:
  2.0 42.6 %collective-permute-start.13 = (bf16[7,1,32,128,128]{4,3,2,1,0:T(8,128)(2,1)}, bf16[7,1,32,128,128]{4,3,2,1,0:T(8,128)(2,1)}, u32[]{:S(2)}, u32[]{:S(2)}) collective-permute-start(bf16[7,1,32,128,128]{4,3,2,1,0:T(8,128)(2,1)} %own_ref.11), channel_id=1, source_target_pairs={{0,4},{4,0},{1,5},{5,1},{2,6},{6,2},{3,7},{7,3},{8,12},{12,8},{9,1... | collective-permute-start | bytes 22020104 | tf_op jit(solution)/shard_map/ppermute | solution.py:23
  3.5 7.2 %collective-permute-start.2 = (bf16[2,17,32,128]{3,2,1,0:T(8,128)(2,1)S(1)}, bf16[2,17,32,128]{3,2,1,0:T(8,128)(2,1)S(1)}, u32[]{:S(2)}, u32[]{:S(2)}) collective-permute-start(bf16[2,17,32,128]{3,2,1,0:T(8,128)(2,1)S(1)} %pad_maximum_fusion.2), channel_id=1, source_target_pairs={{0,64},{4,20},{8,72},{12,28},{16,80},{20,4},{24,88},{28,12},{32,96... | collective-permute-start | bytes 835592 | tf_op jit(solution)/shard_map/ppermute | solution.py:39
  6.5 7.2 %collective-permute-start.3 = (bf16[2,17,32,128]{3,2,1,0:T(8,128)(2,1)S(1)}, bf16[2,17,32,128]{3,2,1,0:T(8,128)(2,1)S(1)}, u32[]{:S(2)}, u32[]{:S(2)}) collective-permute-start(bf16[2,17,32,128]{3,2,1,0:T(8,128)(2,1)S(1)} %pad_maximum_fusion.2), channel_id=1, source_target_pairs={{0,96},{4,28},{8,104},{12,20},{16,112},{20,12},{24,120},{28,4},{32... | collective-permute-start | bytes 835592 | tf_op jit(solution)/shard_map/ppermute | solution.py:39
  7.3 6.9 %collective-permute-start.1 = (bf16[2,17,32,128]{3,2,1,0:T(8,128)(2,1)S(1)}, bf16[2,17,32,128]{3,2,1,0:T(8,128)(2,1)S(1)}, u32[]{:S(2)}, u32[]{:S(2)}) collective-permute-start(bf16[2,17,32,128]{3,2,1,0:T(8,128)(2,1)S(1)} %pad_maximum_fusion.2), channel_id=1, source_target_pairs={{0,32},{4,12},{8,40},{12,4},{16,48},{20,28},{24,56},{28,20},{32,0}... | collective-permute-start | bytes 835592 | tf_op jit(solution)/shard_map/ppermute | solution.py:39
  15.1 12.0 %collective-permute-start.9 = (bf16[4,17,32,128]{3,2,1,0:T(8,128)(2,1)}, bf16[4,17,32,128]{3,2,1,0:T(8,128)(2,1)S(1)}, u32[]{:S(2)}, u32[]{:S(2)}) collective-permute-start(bf16[4,17,32,128]{3,2,1,0:T(8,128)(2,1)} %pad_maximum_fusion.1), channel_id=1, source_target_pairs={{0,12},{4,32},{8,20},{12,40},{16,28},{20,48},{24,4},{28,56},{32,44... | collective-permute-start | bytes 1671176 | tf_op jit(solution)/shard_map/ppermute | solution.py:44
  17.7 10.5 %collective-permute-start.10 = (bf16[4,17,32,128]{3,2,1,0:T(8,128)(2,1)}, bf16[4,17,32,128]{3,2,1,0:T(8,128)(2,1)S(1)}, u32[]{:S(2)}, u32[]{:S(2)}) collective-permute-start(bf16[4,17,32,128]{3,2,1,0:T(8,128)(2,1)} %pad_maximum_fusion.1), channel_id=1, source_target_pairs={{0,28},{4,96},{8,4},{12,104},{16,12},{20,112},{24,20},{28,120},{32... | collective-permute-start | bytes 1671176 | tf_op jit(solution)/shard_map/ppermute | solution.py:45
  20.3 12.7 %collective-permute-start.4 = (bf16[4,17,32,128]{3,2,1,0:T(8,128)(2,1)S(1)}, bf16[4,17,32,128]{3,2,1,0:T(8,128)(2,1)S(1)}, u32[]{:S(2)}, u32[]{:S(2)}) collective-permute-start(bf16[4,17,32,128]{3,2,1,0:T(8,128)(2,1)S(1)} %pad_maximum_fusion.refs_0_), channel_id=1, source_target_pairs={{0,8},{4,36},{8,16},{12,44},{16,24},{20,52},{24,0},{28,60},{32,40}... | collective-permute-start | bytes 1671176 | tf_op jit(solution)/shard_map/ppermute | solution.py:44
  20.4 17.0 %collective-permute-start.5 = (bf16[4,17,32,128]{3,2,1,0:T(8,128)(2,1)S(1)}, bf16[4,17,32,128]{3,2,1,0:T(8,128)(2,1)S(1)}, u32[]{:S(2)}, u32[]{:S(2)}) collective-permute-start(bf16[4,17,32,128]{3,2,1,0:T(8,128)(2,1)S(1)} %pad_maximum_fusion.refs_0_), channel_id=1, source_target_pairs={{0,24},{4,100},{8,0},{12,108},{16,8},{20,116},{24,16},{28,124},{32... | collective-permute-start | bytes 1671176 | tf_op jit(solution)/shard_map/ppermute | solution.py:45
  27.1 11.1 %collective-permute-start.8 = (bf16[4,17,32,128]{3,2,1,0:T(8,128)(2,1)}, bf16[4,17,32,128]{3,2,1,0:T(8,128)(2,1)}, u32[]{:S(2)}, u32[]{:S(2)}) collective-permute-start(bf16[4,17,32,128]{3,2,1,0:T(8,128)(2,1)} %pad_maximum_fusion.1), channel_id=1, source_target_pairs={{0,4},{4,0},{1,5},{5,1},{2,6},{6,2},{3,7},{7,3},{8,12},{12,8},{9,1... | collective-permute-start | bytes 1671176 | tf_op jit(solution)/shard_map/ppermute | solution.py:23
  29.4 11.5 %collective-permute-start.11 = (bf16[2,17,32,128]{3,2,1,0:T(8,128)(2,1)S(1)}, bf16[2,17,32,128]{3,2,1,0:T(8,128)(2,1)}, u32[]{:S(2)}, u32[]{:S(2)}) collective-permute-start(bf16[2,17,32,128]{3,2,1,0:T(8,128)(2,1)S(1)} %slice.120), channel_id=1, source_target_pairs={{0,32},{4,12},{8,40},{12,20},{16,48},{20,28},{24,56},{28,4},{32,64... | collective-permute-start | bytes 835592 | tf_op jit(solution)/shard_map/ppermute | solution.py:46
  33.0 9.2 %collective-permute-start.12 = (bf16[2,17,32,128]{3,2,1,0:T(8,128)(2,1)}, bf16[2,17,32,128]{3,2,1,0:T(8,128)(2,1)}, u32[]{:S(2)}, u32[]{:S(2)}) collective-permute-start(bf16[2,17,32,128]{3,2,1,0:T(8,128)(2,1)} %slice.121), channel_id=1, source_target_pairs={{0,96},{4,28},{8,104},{12,4},{16,112},{20,12},{24,120},{28,20},{32... | collective-permute-start | bytes 835592 | tf_op jit(solution)/shard_map/ppermute | solution.py:47
  37.4 7.2 %collective-permute-start.6 = (bf16[2,17,32,128]{3,2,1,0:T(8,128)(2,1)}, bf16[2,17,32,128]{3,2,1,0:T(8,128)(2,1)}, u32[]{:S(2)}, u32[]{:S(2)}) collective-permute-start(bf16[2,17,32,128]{3,2,1,0:T(8,128)(2,1)} %slice.115), channel_id=1, source_target_pairs={{0,8},{4,36},{8,16},{12,44},{16,24},{20,52},{24,0},{28,60},{32,40}... | collective-permute-start | bytes 835592 | tf_op jit(solution)/shard_map/ppermute | solution.py:46
  38.2 6.4 %collective-permute-start.7 = (bf16[2,17,32,128]{3,2,1,0:T(8,128)(2,1)}, bf16[2,17,32,128]{3,2,1,0:T(8,128)(2,1)}, u32[]{:S(2)}, u32[]{:S(2)}) collective-permute-start(bf16[2,17,32,128]{3,2,1,0:T(8,128)(2,1)} %slice.116), channel_id=1, source_target_pairs={{0,24},{4,100},{8,0},{12,108},{16,8},{20,116},{24,16},{28,124},{32... | collective-permute-start | bytes 835592 | tf_op jit(solution)/shard_map/ppermute | solution.py:47
  40.9 14.2 %collective-permute-start.18 = (bf16[8,1,128,128]{3,2,1,0:T(8,128)(2,1)S(1)}, bf16[8,1,128,128]{3,2,1,0:T(8,128)(2,1)S(1)}, u32[]{:S(2)}, u32[]{:S(2)}) collective-permute-start(bf16[8,1,128,128]{3,2,1,0:T(8,128)(2,1)S(1)} %copy-done), channel_id=1, source_target_pairs={{0,4},{4,0},{1,5},{5,1},{2,6},{6,2},{3,7},{7,3},{8,12},{12,8},{9,1... | collective-permute-start | bytes 786440 | tf_op jit(solution)/shard_map/ppermute | solution.py:23
  42.2 12.9 %collective-permute-start.17 = (bf16[8,1,32,128]{3,2,1,0:T(8,128)(2,1)S(1)}, bf16[8,1,32,128]{3,2,1,0:T(8,128)(2,1)S(1)}, u32[]{:S(2)}, u32[]{:S(2)}) collective-permute-start(bf16[8,1,32,128]{3,2,1,0:T(8,128)(2,1)S(1)} %get-tuple-element.108), channel_id=1, source_target_pairs={{0,4},{4,0},{1,5},{5,1},{2,6},{6,2},{3,7},{7,3},{8,12},{12,8},{9,1... | collective-permute-start | bytes 196616 | tf_op jit(solution)/shard_map/ppermute | solution.py:23
  61.0 12.3 %all-to-all-start = ((bf16[16,2,32,128]{3,2,1,0:T(8,128)(2,1)}), bf16[16,2,32,128]{3,2,1,0:T(8,128)(2,1)S(1)}, u32[]{:S(2)}, u32[]{:S(2)}) async-start(bf16[16,2,32,128]{3,2,1,0:T(8,128)(2,1)} %get-tuple-element.60), calls=%async_computation | async-start | bytes 524288 | tf_op jit(solution)/shard_map/all_to_all | solution.py:334
  80.7 12.1 %all-to-all-start.1 = ((bf16[16,2,32,128]{3,2,1,0:T(8,128)(2,1)}), bf16[16,2,32,128]{3,2,1,0:T(8,128)(2,1)S(1)}, u32[]{:S(2)}, u32[]{:S(2)}) async-start(bf16[16,2,32,128]{3,2,1,0:T(8,128)(2,1)} %get-tuple-element.67), calls=%async_computation.1 | async-start | bytes 524288 | tf_op jit(solution)/shard_map/all_to_all | solution.py:334
  94.5 5.2 %collective-permute-start.23 = (f32[2,32,128]{2,1,0:T(8,128)S(1)}, f32[2,32,128]{2,1,0:T(8,128)S(1)}, u32[]{:S(2)}, u32[]{:S(2)}) collective-permute-start(f32[2,32,128]{2,1,0:T(8,128)S(1)} %fresh_sum.7.p0), channel_id=1, source_target_pairs={{0,2},{1,3},{2,0},{3,1},{4,6},{5,7},{6,4},{7,5},{8,10},{9,11},{10,... | collective-permute-start | bytes 98312 | tf_op jit(solution)/shard_map/ppermute | solution.py:327
  102.9 12.3 %all-to-all-start.2 = ((bf16[16,2,32,128]{3,2,1,0:T(8,128)(2,1)}), bf16[16,2,32,128]{3,2,1,0:T(8,128)(2,1)S(1)}, u32[]{:S(2)}, u32[]{:S(2)}) async-start(bf16[16,2,32,128]{3,2,1,0:T(8,128)(2,1)} %get-tuple-element.74), calls=%async_computation.2 | async-start | bytes 524288 | tf_op jit(solution)/shard_map/all_to_all | solution.py:334
  122.6 12.7 %all-to-all-start.3 = ((bf16[16,2,32,128]{3,2,1,0:T(8,128)(2,1)}), bf16[16,2,32,128]{3,2,1,0:T(8,128)(2,1)S(1)}, u32[]{:S(2)}, u32[]{:S(2)}) async-start(bf16[16,2,32,128]{3,2,1,0:T(8,128)(2,1)} %get-tuple-element.81), calls=%async_computation.3 | async-start | bytes 524288 | tf_op jit(solution)/shard_map/all_to_all | solution.py:334
  143.9 12.5 %all-to-all-start.4 = ((bf16[16,2,32,128]{3,2,1,0:T(8,128)(2,1)}), bf16[16,2,32,128]{3,2,1,0:T(8,128)(2,1)S(1)}, u32[]{:S(2)}, u32[]{:S(2)}) async-start(bf16[16,2,32,128]{3,2,1,0:T(8,128)(2,1)} %get-tuple-element.88), calls=%async_computation.4 | async-start | bytes 524288 | tf_op jit(solution)/shard_map/all_to_all | solution.py:334
  164.9 11.9 %all-to-all-start.5 = ((bf16[16,2,32,128]{3,2,1,0:T(8,128)(2,1)}), bf16[16,2,32,128]{3,2,1,0:T(8,128)(2,1)S(1)}, u32[]{:S(2)}, u32[]{:S(2)}) async-start(bf16[16,2,32,128]{3,2,1,0:T(8,128)(2,1)} %get-tuple-element.95), calls=%async_computation.5 | async-start | bytes 524288 | tf_op jit(solution)/shard_map/all_to_all | solution.py:334
  177.8 4.8 %collective-permute-start.35 = (f32[2,32,128]{2,1,0:T(8,128)S(1)}, f32[2,32,128]{2,1,0:T(8,128)S(1)}, u32[]{:S(2)}, u32[]{:S(2)}) collective-permute-start(f32[2,32,128]{2,1,0:T(8,128)S(1)} %fresh_sum.11.p0), channel_id=1, source_target_pairs={{0,2},{1,3},{2,0},{3,1},{4,6},{5,7},{6,4},{7,5},{8,10},{9,11},{10,... | collective-permute-start | bytes 98312 | tf_op jit(solution)/shard_map/ppermute | solution.py:327
  185.1 18.5 %collective-permute-start.37 = (bf16[7,32,128]{2,1,0:T(8,128)(2,1)S(1)}, bf16[7,32,128]{2,1,0:T(8,128)(2,1)S(1)}, u32[]{:S(2)}, u32[]{:S(2)}) collective-permute-start(bf16[7,32,128]{2,1,0:T(8,128)(2,1)S(1)} %get-tuple-element.112), channel_id=1, source_target_pairs={{0,4},{4,0},{1,5},{5,1},{2,6},{6,2},{3,7},{7,3},{8,12},{12,8},{9,1... | collective-permute-start | bytes 172040 | tf_op jit(solution)/shard_map/ppermute | solution.py:23
  (28 other events, 220.2 us)

commit v12 on v11

--- a/solution.py
+++ b/solution.py
@@ -34,9 +34,12 @@
     return result
 
 
-def gather_parts(v):
+def gather_near(v):
+    return [v] + [lax.ppermute(v, ROWS, pairs(1, lambda i, k=k: i ^ k)) for k in (1, 2, 3)]
+
+
+def gather_parts(near):
     after_one, before_one = lambda i: (i + 1) % 4, lambda i: (i + 3) % 4
-    near = [v] + [lax.ppermute(v, ROWS, pairs(1, lambda i, k=k: i ^ k)) for k in (1, 2, 3)]
     mine, theirs = jnp.stack([one[0] for one in near]), jnp.stack([one[1] for one in near])
 
     def spread(part, cross):
@@ -88,25 +91,26 @@
 
 def first_kernel(code_ref, *refs):
     sources, refs = refs[:-9], refs[-9:]
-    own_ref, other_ref, out_ref, store_ref, blocks, block_sems, pack_sems, packed, store_sem = refs
-    packs, start = [], 0
+    own_ref, other_ref, out_ref, store_ref, blocks, block_sems, pack_sems, packed, store_sems = refs
+    packs, keeps, start = [], [], 0
     for i, source in enumerate(sources):
         target = packed.at[pl.ds(start, source.shape[0])]
         packs.append(pltpu.make_async_copy(source, target, pack_sems.at[i]))
+        keeps.append(pltpu.make_async_copy(target, store_ref.at[pl.ds(start, source.shape[0])], store_sems.at[i]))
         start += source.shape[0]
-    keep = pltpu.make_async_copy(packed, store_ref.at[pl.ds(0, start)], store_sem)
 
     def between():
         for pack in packs:
             pack.start()
-        for pack in packs:
+        for pack, keep in zip(packs, keeps):
             pack.wait()
-        keep.start()
+            keep.start()
 
     each = packed.shape[1]
     picks = lambda k, code: packed[code // each, code % each]
     gather_sum(1, code_ref, picks, start * each, None, own_ref, other_ref, out_ref, blocks, block_sems, between)
-    keep.wait()
+    for keep in keeps:
+        keep.wait()
 
 
 def old_kernel(level, known, code_ref, fresh_ref, store_ref, *refs):
@@ -170,10 +174,10 @@
     extra = [
         pltpu.SemaphoreType.DMA((len(sources),)),
         pltpu.VMEM((parts, each) + one, jnp.bfloat16),
-        pltpu.SemaphoreType.DMA,
+        pltpu.SemaphoreType.DMA((len(sources),)),
     ]
     spaces = [pl.ANY] * len(sources)
-    return sum_call(first_kernel, [code], sources, spaces, own, other, [store], [pltpu.HBM], extra, "first_sum", 60 * 1024 * 1024)
+    return sum_call(first_kernel, [code], sources, spaces, own, other, [store], [pltpu.HBM], extra, "first_sum", 54 * 1024 * 1024)
 
 
 def old_sum(level, known, code, fresh, store, solved, own, other):
@@ -299,7 +303,7 @@
     off_sent, known = lax.optimization_barrier((off_blocks, known))
     off_other = swap_cores(off_sent)
 
-    pieces = gather_parts(known)
+    near_known = gather_near(known)
 
     keep, index = code_both >= 1024, code_both % 1024
     in_outer = index < outer
@@ -320,6 +324,8 @@
     fresh_code = jnp.where(keep & is_fresh, place_level, -1).reshape(levels - 1, -1)
 
     own_rows, other_rows = [], []
+    near_known, rhs_both, old_code, fresh_code = lax.optimization_barrier((near_known, rhs_both, old_code, fresh_code))
+    pieces = gather_parts(near_known)
     value, store = first_sum(old_code, pieces, off_blocks, off_other)
     store = store.reshape((-1,) + store.shape[2:])
     solved_levels = []

time: 205 us -> 207 us (level)
  waiting for transfers between devices: 47.8 us -> 54 us
  starting transfers between devices: 95.5 us -> 92.6 us
    ppermute x3, waiting for transfers between devices: 6.8 us -> 1.29 us  [gather_near(): lax.ppermute(v, ROWS, pairs(1, lambda i, k=k: i ^ k))]
    ppermute x6, waiting for transfers between devices: 1.1 us -> 4.99 us  [swap_cores(): return lax.ppermute(v, 'core', xor_pairs(2, 1))]
    ppermute x2, waiting for transfers between devices: 6.37 us -> 10.1 us  [spread(): before = lax.ppermute(part, ROWS, pairs(2, after_one, cross))]
  transfers between devices with their start and end apart: 44 -> 44, of which waited for: 28 -> 29; matrix products, arithmetic and copies ran while one was open for 3% -> 1% of each run, Pallas kernels for 20% -> 20%
where the time goes in v12:
time: 207 us; the launch traced here: 206 us
  starting transfers between devices  92.6 us (45%)
  waiting for transfers between devices  54 us (26%)
  Pallas kernels  51.7 us (25%)
  other arithmetic  3.25 us (2%)
  local copies, waits for them, and re-layouts  2.61 us (1%)
    pallas_call x7, Pallas kernels, sum_call(): pl.pallas_call(kernel, out_shape=[jax.ShapeDtypeStruct((2, rhs_cols, bloc...  40.3 us
    ppermute x21, starting transfers between devices, on_device(): lax.ppermute(value, 'x', xor_pairs(4, k))  27.5 us
    all_to_all x6, starting transfers between devices, on_device(): solved = lax.all_to_all(sent, ('z', 'y'), 0, 0).reshape(32, half, block)  26.6 us
    ppermute x21, waiting for transfers between devices, on_device(): lax.ppermute(value, 'x', xor_pairs(4, k))  21.1 us
    ppermute x6, starting transfers between devices, swap_cores(): return lax.ppermute(v, 'core', xor_pairs(2, 1))  20.4 us
    all_to_all x6, waiting for transfers between devices, on_device(): solved = lax.all_to_all(sent, ('z', 'y'), 0, 0).reshape(32, half, block)  12.1 us
    ppermute x2, waiting for transfers between devices, spread(): before = lax.ppermute(part, ROWS, pairs(2, after_one, cross))  10.1 us
    ppermute x2, starting transfers between devices, spread(): after = lax.ppermute(part, ROWS, pairs(2, before_one, cross))  6.09 us
  transfers between devices with their start and end apart: 44, of which 29 were waited for; matrix products, arithmetic and copies ran while one was open for 1% of the time, Pallas kernels for 20%

profile of v12, /device:TPU:1, one launch (start us, length us, event | category | flops | bytes accessed | tf_op | source)
XLA Modules:
  0.0 205.6 jit_solution(10758645291583225374)
XLA Ops:
  10.9 3.9 %collective-permute-done.4 = s32[7,32]{1,0:T(8,128)S(1)} collective-permute-done((s32[7,32]{1,0:T(8,128)S(1)}, s32[7,32]{1,0:T(8,128)S(1)}, u32[]{:S(2)}, u32[]{:S(2)}) %collective-permute-start.4) | collective-permute-done | bytes 928 | tf_op jit(solution)/shard_map/ppermute | solution.py:23
  18.4 3.4 %collective-permute-start.11 = (bf16[4,17,32,128]{3,2,1,0:T(8,128)(2,1)S(1)}, bf16[4,17,32,128]{3,2,1,0:T(8,128)(2,1)S(1)}, u32[]{:S(2)}, u32[]{:S(2)}) collective-permute-start(bf16[4,17,32,128]{3,2,1,0:T(8,128)(2,1)S(1)} %pad_maximum_fusion.1), channel_id=1, source_target_pairs={{0,28},{4,96},{8,4},{12,104},{16,12},{20,112},{24,20},{28,120},{32... | collective-permute-start | bytes 1671176 | tf_op jit(solution)/shard_map/ppermute | solution.py:48
  24.6 5.1 %collective-permute-done.10.refs_6_ = bf16[4,17,32,128]{3,2,1,0:T(8,128)(2,1)S(1)} collective-permute-done((bf16[4,17,32,128]{3,2,1,0:T(8,128)(2,1)S(1)}, bf16[4,17,32,128]{3,2,1,0:T(8,128)(2,1)S(1)}, u32[]{:S(2)}, u32[]{:S(2)}) %collective-permute-start.10) | collective-permute-done | bytes 557088 | tf_op jit(solution)/shard_map/ppermute | solution.py:47
  31.5 5.0 %collective-permute-done.5.refs_1_ = bf16[4,17,32,128]{3,2,1,0:T(8,128)(2,1)S(1)} collective-permute-done((bf16[4,17,32,128]{3,2,1,0:T(8,128)(2,1)S(1)}, bf16[4,17,32,128]{3,2,1,0:T(8,128)(2,1)S(1)}, u32[]{:S(2)}, u32[]{:S(2)}) %collective-permute-start.5) | collective-permute-done | bytes 557088 | tf_op jit(solution)/shard_map/ppermute | solution.py:47
  36.5 2.9 %collective-permute-start.13 = (bf16[2,17,32,128]{3,2,1,0:T(8,128)(2,1)S(1)}, bf16[2,17,32,128]{3,2,1,0:T(8,128)(2,1)S(1)}, u32[]{:S(2)}, u32[]{:S(2)}) collective-permute-start(bf16[2,17,32,128]{3,2,1,0:T(8,128)(2,1)S(1)} %slice.115), channel_id=1, source_target_pairs={{0,96},{4,28},{8,104},{12,4},{16,112},{20,12},{24,120},{28,20},{32... | collective-permute-start | bytes 835592 | tf_op jit(solution)/shard_map/ppermute | solution.py:50
  39.6 2.7 %collective-permute-start.8 = (bf16[2,17,32,128]{3,2,1,0:T(8,128)(2,1)S(1)}, bf16[2,17,32,128]{3,2,1,0:T(8,128)(2,1)S(1)}, u32[]{:S(2)}, u32[]{:S(2)}) collective-permute-start(bf16[2,17,32,128]{3,2,1,0:T(8,128)(2,1)S(1)} %slice.113), channel_id=1, source_target_pairs={{0,24},{4,100},{8,0},{12,108},{16,8},{20,116},{24,16},{28,124},{32... | collective-permute-start | bytes 835592 | tf_op jit(solution)/shard_map/ppermute | solution.py:50
  42.9 3.5 %collective-permute-done.7.refs_3_ = bf16[2,17,32,128]{3,2,1,0:T(8,128)(2,1)S(1)} collective-permute-done((bf16[2,17,32,128]{3,2,1,0:T(8,128)(2,1)S(1)}, bf16[2,17,32,128]{3,2,1,0:T(8,128)(2,1)S(1)}, u32[]{:S(2)}, u32[]{:S(2)}) %collective-permute-start.7) | collective-permute-done | bytes 278560 | tf_op jit(solution)/shard_map/ppermute | solution.py:49
  47.7 7.1 %first_sum.1 = (f32[2,32,128]{2,1,0:T(8,128)}, bf16[120,17,32,128]{3,2,1,0:T(8,128)(2,1)}) custom-call(s32[7,64]{1,0:T(8,128)} %get-tuple-element.59.code_ref, bf16[4,17,32,128]{3,2,1,0:T(8,128)(2,1)} %copy-done.3, bf16[4,17,32,128]{3,2,1,0:T(8,128)(2,1)} %copy-done.6, bf16[4,17,32,128]{3,2,1,0:T(8,128)(2,1)} %copy-done.7, ...), custom_call_target="tpu_custom_call" | custom-call | flops 67108864 | bytes 6291456 | tf_op jit(solution)/shard_map/first_sum/pallas_call | solution.py:151
  64.4 3.8 %all-to-all-start = ((bf16[16,2,32,128]{3,2,1,0:T(8,128)(2,1)}), bf16[16,2,32,128]{3,2,1,0:T(8,128)(2,1)S(1)}, u32[]{:S(2)}, u32[]{:S(2)}) async-start(bf16[16,2,32,128]{3,2,1,0:T(8,128)(2,1)} %get-tuple-element.74), calls=%async_computation | async-start | bytes 524288 | tf_op jit(solution)/shard_map/all_to_all | solution.py:340
  68.3 5.5 %old_sum.6 = (f32[2,32,128]{2,1,0:T(8,128)S(1)}, s32[65]{0:T(128)S(1)}, bf16[16,128,128]{2,1,0:T(8,128)(2,1)S(1)}) custom-call(s32[7,64]{1,0:T(8,128)S(1)} %copy-done.1, s32[7,64]{1,0:T(8,128)S(1)} %get-tuple-element.106.fresh_ref, bf16[2040,32,128]{2,1,0:T(8,128)(2,1)} %bitcast.47, bf16[7,1,32,128,128]{4,3,2,1,0:T(8,128)(2,1)} %own_ref.11, ...), custom_call_target="tpu_custom_call" | custom-call | flops 67108864 | bytes 6291456 | tf_op jit(solution)/shard_map/old_sum/pallas_call | solution.py:151
  83.5 5.0 %all-to-all-start.1 = ((bf16[16,2,32,128]{3,2,1,0:T(8,128)(2,1)}), bf16[16,2,32,128]{3,2,1,0:T(8,128)(2,1)S(1)}, u32[]{:S(2)}, u32[]{:S(2)}) async-start(bf16[16,2,32,128]{3,2,1,0:T(8,128)(2,1)} %get-tuple-element.81), calls=%async_computation.1 | async-start | bytes 524288 | tf_op jit(solution)/shard_map/all_to_all | solution.py:340
  88.5 5.7 %old_sum.7 = (f32[2,32,128]{2,1,0:T(8,128)S(1)}, s32[65]{0:T(128)S(1)}, bf16[16,128,128]{2,1,0:T(8,128)(2,1)S(1)}) custom-call(s32[7,64]{1,0:T(8,128)S(1)} %copy-done.1, s32[7,64]{1,0:T(8,128)S(1)} %get-tuple-element.106.fresh_ref, bf16[2040,32,128]{2,1,0:T(8,128)(2,1)} %bitcast.48, bf16[32,32,128]{2,1,0:T(8,128)(2,1)S(1)} %bitcast.27, ...), custom_call_target="tpu_custom_call" | custom-call | flops 67108864 | bytes 6291456 | tf_op jit(solution)/shard_map/old_sum/pallas_call | solution.py:151
  97.0 3.1 %collective-permute-start.23 = (f32[2,32,128]{2,1,0:T(8,128)S(1)}, f32[2,32,128]{2,1,0:T(8,128)S(1)}, u32[]{:S(2)}, u32[]{:S(2)}) collective-permute-start(f32[2,32,128]{2,1,0:T(8,128)S(1)} %fresh_sum.7.p0), channel_id=1, source_target_pairs={{0,2},{1,3},{2,0},{3,1},{4,6},{5,7},{6,4},{7,5},{8,10},{9,11},{10,... | collective-permute-start | bytes 98312 | tf_op jit(solution)/shard_map/ppermute | solution.py:333
  105.0 4.9 %all-to-all-start.2 = ((bf16[16,2,32,128]{3,2,1,0:T(8,128)(2,1)}), bf16[16,2,32,128]{3,2,1,0:T(8,128)(2,1)S(1)}, u32[]{:S(2)}, u32[]{:S(2)}) async-start(bf16[16,2,32,128]{3,2,1,0:T(8,128)(2,1)} %get-tuple-element.88), calls=%async_computation.2 | async-start | bytes 524288 | tf_op jit(solution)/shard_map/all_to_all | solution.py:340
  109.9 5.5 %old_sum.8 = (f32[2,32,128]{2,1,0:T(8,128)S(1)}, s32[65]{0:T(128)S(1)}, bf16[16,128,128]{2,1,0:T(8,128)(2,1)S(1)}) custom-call(s32[7,64]{1,0:T(8,128)S(1)} %copy-done.1, s32[7,64]{1,0:T(8,128)S(1)} %get-tuple-element.106.fresh_ref, bf16[2040,32,128]{2,1,0:T(8,128)(2,1)} %bitcast.49, bf16[32,32,128]{2,1,0:T(8,128)(2,1)S(1)} %bitcast.28, ...), custom_call_target="tpu_custom_call" | custom-call | flops 67108864 | bytes 6291456 | tf_op jit(solution)/shard_map/old_sum/pallas_call | solution.py:151
  118.4 2.9 %collective-permute-start.26 = (f32[2,32,128]{2,1,0:T(8,128)S(1)}, f32[2,32,128]{2,1,0:T(8,128)S(1)}, u32[]{:S(2)}, u32[]{:S(2)}) collective-permute-start(f32[2,32,128]{2,1,0:T(8,128)S(1)} %fresh_sum.8.p0), channel_id=1, source_target_pairs={{0,2},{1,3},{2,0},{3,1},{4,6},{5,7},{6,4},{7,5},{8,10},{9,11},{10,... | collective-permute-start | bytes 98312 | tf_op jit(solution)/shard_map/ppermute | solution.py:333
  126.4 4.4 %all-to-all-start.3 = ((bf16[16,2,32,128]{3,2,1,0:T(8,128)(2,1)}), bf16[16,2,32,128]{3,2,1,0:T(8,128)(2,1)S(1)}, u32[]{:S(2)}, u32[]{:S(2)}) async-start(bf16[16,2,32,128]{3,2,1,0:T(8,128)(2,1)} %get-tuple-element.95), calls=%async_computation.3 | async-start | bytes 524288 | tf_op jit(solution)/shard_map/all_to_all | solution.py:340
  130.8 5.7 %old_sum.9 = (f32[2,32,128]{2,1,0:T(8,128)S(1)}, s32[65]{0:T(128)S(1)}, bf16[16,128,128]{2,1,0:T(8,128)(2,1)S(1)}) custom-call(s32[7,64]{1,0:T(8,128)S(1)} %copy-done.1, s32[7,64]{1,0:T(8,128)S(1)} %get-tuple-element.106.fresh_ref, bf16[2040,32,128]{2,1,0:T(8,128)(2,1)} %bitcast.50, bf16[32,32,128]{2,1,0:T(8,128)(2,1)S(1)} %bitcast.29, ...), custom_call_target="tpu_custom_call" | custom-call | flops 67108864 | bytes 6291456 | tf_op jit(solution)/shard_map/old_sum/pallas_call | solution.py:151
  147.2 4.6 %all-to-all-start.4 = ((bf16[16,2,32,128]{3,2,1,0:T(8,128)(2,1)}), bf16[16,2,32,128]{3,2,1,0:T(8,128)(2,1)S(1)}, u32[]{:S(2)}, u32[]{:S(2)}) async-start(bf16[16,2,32,128]{3,2,1,0:T(8,128)(2,1)} %get-tuple-element.102), calls=%async_computation.4 | async-start | bytes 524288 | tf_op jit(solution)/shard_map/all_to_all | solution.py:340
  151.8 5.4 %old_sum.10 = (f32[2,32,128]{2,1,0:T(8,128)S(1)}, s32[65]{0:T(128)S(1)}, bf16[16,128,128]{2,1,0:T(8,128)(2,1)S(1)}) custom-call(s32[7,64]{1,0:T(8,128)S(1)} %copy-done.1, s32[7,64]{1,0:T(8,128)S(1)} %get-tuple-element.106.fresh_ref, bf16[2040,32,128]{2,1,0:T(8,128)(2,1)} %bitcast.51, bf16[32,32,128]{2,1,0:T(8,128)(2,1)S(1)} %bitcast.30, ...), custom_call_target="tpu_custom_call" | custom-call | flops 67108864 | bytes 6291456 | tf_op jit(solution)/shard_map/old_sum/pallas_call | solution.py:151
  160.1 3.7 %collective-permute-start.32 = (f32[2,32,128]{2,1,0:T(8,128)S(1)}, f32[2,32,128]{2,1,0:T(8,128)S(1)}, u32[]{:S(2)}, u32[]{:S(2)}) collective-permute-start(f32[2,32,128]{2,1,0:T(8,128)S(1)} %fresh_sum.10.p0), channel_id=1, source_target_pairs={{0,2},{1,3},{2,0},{3,1},{4,6},{5,7},{6,4},{7,5},{8,10},{9,11},{10,... | collective-permute-start | bytes 98312 | tf_op jit(solution)/shard_map/ppermute | solution.py:333
  169.0 3.9 %all-to-all-start.5 = ((bf16[16,2,32,128]{3,2,1,0:T(8,128)(2,1)}), bf16[16,2,32,128]{3,2,1,0:T(8,128)(2,1)S(1)}, u32[]{:S(2)}, u32[]{:S(2)}) async-start(bf16[16,2,32,128]{3,2,1,0:T(8,128)(2,1)} %get-tuple-element.109), calls=%async_computation.5 | async-start | bytes 524288 | tf_op jit(solution)/shard_map/all_to_all | solution.py:340
  172.9 5.4 %old_sum.11 = (f32[2,32,128]{2,1,0:T(8,128)S(1)}, s32[65]{0:T(128)S(1)}, bf16[16,128,128]{2,1,0:T(8,128)(2,1)S(1)}) custom-call(s32[7,64]{1,0:T(8,128)S(1)} %copy-done.1, s32[7,64]{1,0:T(8,128)S(1)} %get-tuple-element.106.fresh_ref, bf16[2040,32,128]{2,1,0:T(8,128)(2,1)} %bitcast.52, bf16[32,32,128]{2,1,0:T(8,128)(2,1)S(1)} %bitcast.31, ...), custom_call_target="tpu_custom_call" | custom-call | flops 67108864 | bytes 6291456 | tf_op jit(solution)/shard_map/old_sum/pallas_call | solution.py:151
  187.9 16.2 %collective-permute-start.37 = (bf16[7,32,128]{2,1,0:T(8,128)(2,1)S(1)}, bf16[7,32,128]{2,1,0:T(8,128)(2,1)S(1)}, u32[]{:S(2)}, u32[]{:S(2)}) collective-permute-start(bf16[7,32,128]{2,1,0:T(8,128)(2,1)S(1)} %get-tuple-element.126), channel_id=1, source_target_pairs={{0,4},{4,0},{1,5},{5,1},{2,6},{6,2},{3,7},{7,3},{8,12},{12,8},{9,1... | collective-permute-start | bytes 172040 | tf_op jit(solution)/shard_map/ppermute | solution.py:23
  (138 shorter events, 85.8 us)
Async XLA Ops:
  2.0 45.0 %collective-permute-start.14 = (bf16[7,1,32,128,128]{4,3,2,1,0:T(8,128)(2,1)}, bf16[7,1,32,128,128]{4,3,2,1,0:T(8,128)(2,1)}, u32[]{:S(2)}, u32[]{:S(2)}) collective-permute-start(bf16[7,1,32,128,128]{4,3,2,1,0:T(8,128)(2,1)} %own_ref.11), channel_id=1, source_target_pairs={{0,4},{4,0},{1,5},{5,1},{2,6},{6,2},{3,7},{7,3},{8,12},{12,8},{9,1... | collective-permute-start | bytes 22020104 | tf_op jit(solution)/shard_map/ppermute | solution.py:23
  3.5 12.6 %collective-permute-start = (bf16[2,17,32,128]{3,2,1,0:T(8,128)(2,1)S(1)}, bf16[2,17,32,128]{3,2,1,0:T(8,128)(2,1)S(1)}, u32[]{:S(2)}, u32[]{:S(2)}) collective-permute-start(bf16[2,17,32,128]{3,2,1,0:T(8,128)(2,1)S(1)} %pad_maximum_fusion.2), channel_id=1, source_target_pairs={{0,32},{4,12},{8,40},{12,4},{16,48},{20,28},{24,56},{28,20},{32,0}... | collective-permute-start | bytes 835592 | tf_op jit(solution)/shard_map/ppermute | solution.py:38
  4.9 11.2 %collective-permute-start.1 = (bf16[2,17,32,128]{3,2,1,0:T(8,128)(2,1)S(1)}, bf16[2,17,32,128]{3,2,1,0:T(8,128)(2,1)S(1)}, u32[]{:S(2)}, u32[]{:S(2)}) collective-permute-start(bf16[2,17,32,128]{3,2,1,0:T(8,128)(2,1)S(1)} %pad_maximum_fusion.2), channel_id=1, source_target_pairs={{0,64},{4,20},{8,72},{12,28},{16,80},{20,4},{24,88},{28,12},{32,96... | collective-permute-start | bytes 835592 | tf_op jit(solution)/shard_map/ppermute | solution.py:38
  7.5 9.9 %collective-permute-start.2 = (bf16[2,17,32,128]{3,2,1,0:T(8,128)(2,1)S(1)}, bf16[2,17,32,128]{3,2,1,0:T(8,128)(2,1)S(1)}, u32[]{:S(2)}, u32[]{:S(2)}) collective-permute-start(bf16[2,17,32,128]{3,2,1,0:T(8,128)(2,1)S(1)} %pad_maximum_fusion.2), channel_id=1, source_target_pairs={{0,96},{4,28},{8,104},{12,20},{16,112},{20,12},{24,120},{28,4},{32... | collective-permute-start | bytes 835592 | tf_op jit(solution)/shard_map/ppermute | solution.py:38
  8.2 6.6 %collective-permute-start.4 = (s32[7,32]{1,0:T(8,128)S(1)}, s32[7,32]{1,0:T(8,128)S(1)}, u32[]{:S(2)}, u32[]{:S(2)}) collective-permute-start(s32[7,32]{1,0:T(8,128)S(1)} %bitcast.53), channel_id=1, source_target_pairs={{0,4},{4,0},{1,5},{5,1},{2,6},{6,2},{3,7},{7,3},{8,12},{12,8},{9,1... | collective-permute-start | bytes 2696 | tf_op jit(solution)/shard_map/ppermute | solution.py:23
  17.6 12.2 %collective-permute-start.10 = (bf16[4,17,32,128]{3,2,1,0:T(8,128)(2,1)S(1)}, bf16[4,17,32,128]{3,2,1,0:T(8,128)(2,1)S(1)}, u32[]{:S(2)}, u32[]{:S(2)}) collective-permute-start(bf16[4,17,32,128]{3,2,1,0:T(8,128)(2,1)S(1)} %pad_maximum_fusion.1), channel_id=1, source_target_pairs={{0,12},{4,32},{8,20},{12,40},{16,28},{20,48},{24,4},{28,56},{32,44... | collective-permute-start | bytes 1671176 | tf_op jit(solution)/shard_map/ppermute | solution.py:47
  18.4 11.8 %collective-permute-start.11 = (bf16[4,17,32,128]{3,2,1,0:T(8,128)(2,1)S(1)}, bf16[4,17,32,128]{3,2,1,0:T(8,128)(2,1)S(1)}, u32[]{:S(2)}, u32[]{:S(2)}) collective-permute-start(bf16[4,17,32,128]{3,2,1,0:T(8,128)(2,1)S(1)} %pad_maximum_fusion.1), channel_id=1, source_target_pairs={{0,28},{4,96},{8,4},{12,104},{16,12},{20,112},{24,20},{28,120},{32... | collective-permute-start | bytes 1671176 | tf_op jit(solution)/shard_map/ppermute | solution.py:48
  21.9 14.6 %collective-permute-start.5 = (bf16[4,17,32,128]{3,2,1,0:T(8,128)(2,1)S(1)}, bf16[4,17,32,128]{3,2,1,0:T(8,128)(2,1)S(1)}, u32[]{:S(2)}, u32[]{:S(2)}) collective-permute-start(bf16[4,17,32,128]{3,2,1,0:T(8,128)(2,1)S(1)} %pad_maximum_fusion.refs_0_), channel_id=1, source_target_pairs={{0,8},{4,36},{8,16},{12,44},{16,24},{20,52},{24,0},{28,60},{32,40}... | collective-permute-start | bytes 1671176 | tf_op jit(solution)/shard_map/ppermute | solution.py:47
  22.0 17.5 %collective-permute-start.6 = (bf16[4,17,32,128]{3,2,1,0:T(8,128)(2,1)S(1)}, bf16[4,17,32,128]{3,2,1,0:T(8,128)(2,1)S(1)}, u32[]{:S(2)}, u32[]{:S(2)}) collective-permute-start(bf16[4,17,32,128]{3,2,1,0:T(8,128)(2,1)S(1)} %pad_maximum_fusion.refs_0_), channel_id=1, source_target_pairs={{0,24},{4,100},{8,0},{12,108},{16,8},{20,116},{24,16},{28,124},{32... | collective-permute-start | bytes 1671176 | tf_op jit(solution)/shard_map/ppermute | solution.py:48
  29.8 9.8 %collective-permute-start.9 = (bf16[4,17,32,128]{3,2,1,0:T(8,128)(2,1)S(1)}, bf16[4,17,32,128]{3,2,1,0:T(8,128)(2,1)S(1)}, u32[]{:S(2)}, u32[]{:S(2)}) collective-permute-start(bf16[4,17,32,128]{3,2,1,0:T(8,128)(2,1)S(1)} %pad_maximum_fusion.1), channel_id=1, source_target_pairs={{0,4},{4,0},{1,5},{5,1},{2,6},{6,2},{3,7},{7,3},{8,12},{12,8},{9,1... | collective-permute-start | bytes 1671176 | tf_op jit(solution)/shard_map/ppermute | solution.py:23
  30.1 12.2 %collective-permute-start.12 = (bf16[2,17,32,128]{3,2,1,0:T(8,128)(2,1)S(1)}, bf16[2,17,32,128]{3,2,1,0:T(8,128)(2,1)S(1)}, u32[]{:S(2)}, u32[]{:S(2)}) collective-permute-start(bf16[2,17,32,128]{3,2,1,0:T(8,128)(2,1)S(1)} %slice.114), channel_id=1, source_target_pairs={{0,32},{4,12},{8,40},{12,20},{16,48},{20,28},{24,56},{28,4},{32,64... | collective-permute-start | bytes 835592 | tf_op jit(solution)/shard_map/ppermute | solution.py:49
  36.5 6.4 %collective-permute-start.13 = (bf16[2,17,32,128]{3,2,1,0:T(8,128)(2,1)S(1)}, bf16[2,17,32,128]{3,2,1,0:T(8,128)(2,1)S(1)}, u32[]{:S(2)}, u32[]{:S(2)}) collective-permute-start(bf16[2,17,32,128]{3,2,1,0:T(8,128)(2,1)S(1)} %slice.115), channel_id=1, source_target_pairs={{0,96},{4,28},{8,104},{12,4},{16,112},{20,12},{24,120},{28,20},{32... | collective-permute-start | bytes 835592 | tf_op jit(solution)/shard_map/ppermute | solution.py:50
  39.5 7.0 %collective-permute-start.7 = (bf16[2,17,32,128]{3,2,1,0:T(8,128)(2,1)S(1)}, bf16[2,17,32,128]{3,2,1,0:T(8,128)(2,1)S(1)}, u32[]{:S(2)}, u32[]{:S(2)}) collective-permute-start(bf16[2,17,32,128]{3,2,1,0:T(8,128)(2,1)S(1)} %slice.112), channel_id=1, source_target_pairs={{0,8},{4,36},{8,16},{12,44},{16,24},{20,52},{24,0},{28,60},{32,40}... | collective-permute-start | bytes 835592 | tf_op jit(solution)/shard_map/ppermute | solution.py:49
  39.6 7.4 %collective-permute-start.8 = (bf16[2,17,32,128]{3,2,1,0:T(8,128)(2,1)S(1)}, bf16[2,17,32,128]{3,2,1,0:T(8,128)(2,1)S(1)}, u32[]{:S(2)}, u32[]{:S(2)}) collective-permute-start(bf16[2,17,32,128]{3,2,1,0:T(8,128)(2,1)S(1)} %slice.113), channel_id=1, source_target_pairs={{0,24},{4,100},{8,0},{12,108},{16,8},{20,116},{24,16},{28,124},{32... | collective-permute-start | bytes 835592 | tf_op jit(solution)/shard_map/ppermute | solution.py:50
  42.3 16.5 %collective-permute-start.18 = (bf16[8,1,128,128]{3,2,1,0:T(8,128)(2,1)S(1)}, bf16[8,1,128,128]{3,2,1,0:T(8,128)(2,1)S(1)}, u32[]{:S(2)}, u32[]{:S(2)}) collective-permute-start(bf16[8,1,128,128]{3,2,1,0:T(8,128)(2,1)S(1)} %copy-done), channel_id=1, source_target_pairs={{0,4},{4,0},{1,5},{5,1},{2,6},{6,2},{3,7},{7,3},{8,12},{12,8},{9,1... | collective-permute-start | bytes 786440 | tf_op jit(solution)/shard_map/ppermute | solution.py:23
  64.4 11.5 %all-to-all-start = ((bf16[16,2,32,128]{3,2,1,0:T(8,128)(2,1)}), bf16[16,2,32,128]{3,2,1,0:T(8,128)(2,1)S(1)}, u32[]{:S(2)}, u32[]{:S(2)}) async-start(bf16[16,2,32,128]{3,2,1,0:T(8,128)(2,1)} %get-tuple-element.74), calls=%async_computation | async-start | bytes 524288 | tf_op jit(solution)/shard_map/all_to_all | solution.py:340
  83.5 12.5 %all-to-all-start.1 = ((bf16[16,2,32,128]{3,2,1,0:T(8,128)(2,1)}), bf16[16,2,32,128]{3,2,1,0:T(8,128)(2,1)S(1)}, u32[]{:S(2)}, u32[]{:S(2)}) async-start(bf16[16,2,32,128]{3,2,1,0:T(8,128)(2,1)} %get-tuple-element.81), calls=%async_computation.1 | async-start | bytes 524288 | tf_op jit(solution)/shard_map/all_to_all | solution.py:340
  97.0 5.0 %collective-permute-start.23 = (f32[2,32,128]{2,1,0:T(8,128)S(1)}, f32[2,32,128]{2,1,0:T(8,128)S(1)}, u32[]{:S(2)}, u32[]{:S(2)}) collective-permute-start(f32[2,32,128]{2,1,0:T(8,128)S(1)} %fresh_sum.7.p0), channel_id=1, source_target_pairs={{0,2},{1,3},{2,0},{3,1},{4,6},{5,7},{6,4},{7,5},{8,10},{9,11},{10,... | collective-permute-start | bytes 98312 | tf_op jit(solution)/shard_map/ppermute | solution.py:333
  105.0 12.5 %all-to-all-start.2 = ((bf16[16,2,32,128]{3,2,1,0:T(8,128)(2,1)}), bf16[16,2,32,128]{3,2,1,0:T(8,128)(2,1)S(1)}, u32[]{:S(2)}, u32[]{:S(2)}) async-start(bf16[16,2,32,128]{3,2,1,0:T(8,128)(2,1)} %get-tuple-element.88), calls=%async_computation.2 | async-start | bytes 524288 | tf_op jit(solution)/shard_map/all_to_all | solution.py:340
  126.4 11.9 %all-to-all-start.3 = ((bf16[16,2,32,128]{3,2,1,0:T(8,128)(2,1)}), bf16[16,2,32,128]{3,2,1,0:T(8,128)(2,1)S(1)}, u32[]{:S(2)}, u32[]{:S(2)}) async-start(bf16[16,2,32,128]{3,2,1,0:T(8,128)(2,1)} %get-tuple-element.95), calls=%async_computation.3 | async-start | bytes 524288 | tf_op jit(solution)/shard_map/all_to_all | solution.py:340
  147.2 12.1 %all-to-all-start.4 = ((bf16[16,2,32,128]{3,2,1,0:T(8,128)(2,1)}), bf16[16,2,32,128]{3,2,1,0:T(8,128)(2,1)S(1)}, u32[]{:S(2)}, u32[]{:S(2)}) async-start(bf16[16,2,32,128]{3,2,1,0:T(8,128)(2,1)} %get-tuple-element.102), calls=%async_computation.4 | async-start | bytes 524288 | tf_op jit(solution)/shard_map/all_to_all | solution.py:340
  160.1 5.3 %collective-permute-start.32 = (f32[2,32,128]{2,1,0:T(8,128)S(1)}, f32[2,32,128]{2,1,0:T(8,128)S(1)}, u32[]{:S(2)}, u32[]{:S(2)}) collective-permute-start(f32[2,32,128]{2,1,0:T(8,128)S(1)} %fresh_sum.10.p0), channel_id=1, source_target_pairs={{0,2},{1,3},{2,0},{3,1},{4,6},{5,7},{6,4},{7,5},{8,10},{9,11},{10,... | collective-permute-start | bytes 98312 | tf_op jit(solution)/shard_map/ppermute | solution.py:333
  169.0 11.5 %all-to-all-start.5 = ((bf16[16,2,32,128]{3,2,1,0:T(8,128)(2,1)}), bf16[16,2,32,128]{3,2,1,0:T(8,128)(2,1)S(1)}, u32[]{:S(2)}, u32[]{:S(2)}) async-start(bf16[16,2,32,128]{3,2,1,0:T(8,128)(2,1)} %get-tuple-element.109), calls=%async_computation.5 | async-start | bytes 524288 | tf_op jit(solution)/shard_map/all_to_all | solution.py:340
  187.9 17.1 %collective-permute-start.37 = (bf16[7,32,128]{2,1,0:T(8,128)(2,1)S(1)}, bf16[7,32,128]{2,1,0:T(8,128)(2,1)S(1)}, u32[]{:S(2)}, u32[]{:S(2)}) collective-permute-start(bf16[7,32,128]{2,1,0:T(8,128)(2,1)S(1)} %get-tuple-element.126), channel_id=1, source_target_pairs={{0,4},{4,0},{1,5},{5,1},{2,6},{6,2},{3,7},{7,3},{8,12},{12,8},{9,1... | collective-permute-start | bytes 172040 | tf_op jit(solution)/shard_map/ppermute | solution.py:23
  (33 other events, 247.7 us)

commit v13 on v11

--- a/solution.py
+++ b/solution.py
@@ -87,26 +87,29 @@
 
 
 def first_kernel(code_ref, *refs):
-    sources, refs = refs[:-9], refs[-9:]
-    own_ref, other_ref, out_ref, store_ref, blocks, block_sems, pack_sems, packed, store_sem = refs
-    packs, start = [], 0
+    sources, refs = refs[:-7], refs[-7:]
+    own_ref, other_ref, out_ref, store_ref, blocks, block_sems, store_sems = refs
+    keeps, starts, known = [], [], 0
     for i, source in enumerate(sources):
-        target = packed.at[pl.ds(start, source.shape[0])]
-        packs.append(pltpu.make_async_copy(source, target, pack_sems.at[i]))
-        start += source.shape[0]
-    keep = pltpu.make_async_copy(packed, store_ref.at[pl.ds(0, start)], store_sem)
+        target = store_ref.at[pl.ds(known, source.shape[0])]
+        keeps.append(pltpu.make_async_copy(source, target, store_sems.at[i]))
+        starts.append(known)
+        known += source.shape[0]
 
     def between():
-        for pack in packs:
-            pack.start()
-        for pack in packs:
-            pack.wait()
-        keep.start()
-
-    each = packed.shape[1]
-    picks = lambda k, code: packed[code // each, code % each]
-    gather_sum(1, code_ref, picks, start * each, None, own_ref, other_ref, out_ref, blocks, block_sems, between)
-    keep.wait()
+        for keep in keeps:
+            keep.start()
+
+    def picks(k, code):
+        value = None
+        for start, source in zip(starts, sources):
+            one = source[jnp.clip(code - start, 0, source.shape[0] - 1)]
+            value = one if value is None else jnp.where(code >= start, one, value)
+        return value
+
+    gather_sum(1, code_ref, picks, known, None, own_ref, other_ref, out_ref, blocks, block_sems, between)
+    for keep in keeps:
+        keep.wait()
 
 
 def old_kernel(level, known, code_ref, fresh_ref, store_ref, *refs):
@@ -163,17 +166,10 @@
 
 
 def first_sum(code, sources, own, other):
-    one = sources[0].shape[2:]
-    parts = sum(v.shape[0] for v in sources)
-    each = sources[0].shape[1]
-    store = jax.ShapeDtypeStruct((2048 // each, each) + one, jnp.bfloat16)
-    extra = [
-        pltpu.SemaphoreType.DMA((len(sources),)),
-        pltpu.VMEM((parts, each) + one, jnp.bfloat16),
-        pltpu.SemaphoreType.DMA,
-    ]
-    spaces = [pl.ANY] * len(sources)
-    return sum_call(first_kernel, [code], sources, spaces, own, other, [store], [pltpu.HBM], extra, "first_sum", 60 * 1024 * 1024)
+    store = jax.ShapeDtypeStruct((2048,) + sources[0].shape[1:], jnp.bfloat16)
+    extra = [pltpu.SemaphoreType.DMA((len(sources),))]
+    spaces = [pltpu.VMEM] * len(sources)
+    return sum_call(first_kernel, [code], sources, spaces, own, other, [store], [pltpu.HBM], extra, "first_sum", VMEM_LIMIT)
 
 
 def old_sum(level, known, code, fresh, store, solved, own, other):
@@ -299,7 +295,7 @@
     off_sent, known = lax.optimization_barrier((off_blocks, known))
     off_other = swap_cores(off_sent)
 
-    pieces = gather_parts(known)
+    pieces = [piece.reshape((-1,) + piece.shape[2:]) for piece in gather_parts(known)]
 
     keep, index = code_both >= 1024, code_both % 1024
     in_outer = index < outer
@@ -321,7 +317,6 @@
 
     own_rows, other_rows = [], []
     value, store = first_sum(old_code, pieces, off_blocks, off_other)
-    store = store.reshape((-1,) + store.shape[2:])
     solved_levels = []
     for level in range(1, levels):
         partials = [value] + [lax.ppermute(value, "x", xor_pairs(4, k)) for k in (1, 2, 3)]

time: 205 us -> 204 us (level)
  waiting for transfers between devices: 47.8 us -> 50.7 us
  Pallas kernels: 51.4 us -> 49.3 us
  transfers between devices with their start and end apart: 44 -> 44, of which waited for: 28 -> 29; matrix products, arithmetic and copies ran while one was open for 3% -> 3% of each run, Pallas kernels for 20% -> 19%
where the time goes in v13:
time: 204 us; the launch traced here: 203 us
  starting transfers between devices  94.9 us (47%)
  waiting for transfers between devices  50.7 us (25%)
  Pallas kernels  49.3 us (24%)
  local copies, waits for them, and re-layouts  3.58 us (2%)
  other arithmetic  3.49 us (2%)
    pallas_call x7, Pallas kernels, sum_call(): pl.pallas_call(kernel, out_shape=[jax.ShapeDtypeStruct((2, rhs_cols, bloc...  38.8 us
    all_to_all x6, starting transfers between devices, on_device(): solved = lax.all_to_all(sent, ('z', 'y'), 0, 0).reshape(32, half, block)  28.1 us
    ppermute x21, starting transfers between devices, on_device(): lax.ppermute(value, 'x', xor_pairs(4, k))  27.6 us
    ppermute x21, waiting for transfers between devices, on_device(): lax.ppermute(value, 'x', xor_pairs(4, k))  21.2 us
    ppermute x6, starting transfers between devices, swap_cores(): return lax.ppermute(v, 'core', xor_pairs(2, 1))  20.8 us
    all_to_all x6, waiting for transfers between devices, on_device(): solved = lax.all_to_all(sent, ('z', 'y'), 0, 0).reshape(32, half, block)  12.1 us
    ppermute x3, waiting for transfers between devices, gather_parts(): lax.ppermute(v, ROWS, pairs(1, lambda i, k=k: i ^ k))  6.8 us
    ppermute x2, waiting for transfers between devices, spread(): before = lax.ppermute(part, ROWS, pairs(2, after_one, cross))  6.39 us
  transfers between devices with their start and end apart: 44, of which 29 were waited for; matrix products, arithmetic and copies ran while one was open for 3% of the time, Pallas kernels for 19%

profile of v13, /device:TPU:1, one launch (start us, length us, event | category | flops | bytes accessed | tf_op | source)
XLA Modules:
  0.0 203.3 jit_solution(2038375060328297271)
XLA Ops:
  3.5 3.0 %collective-permute-start.2 = (bf16[2,17,32,128]{3,2,1,0:T(8,128)(2,1)S(1)}, bf16[2,17,32,128]{3,2,1,0:T(8,128)(2,1)S(1)}, u32[]{:S(2)}, u32[]{:S(2)}) collective-permute-start(bf16[2,17,32,128]{3,2,1,0:T(8,128)(2,1)S(1)} %pad_maximum_fusion.2), channel_id=1, source_target_pairs={{0,64},{4,20},{8,72},{12,28},{16,80},{20,4},{24,88},{28,12},{32,96... | collective-permute-start | bytes 835592 | tf_op jit(solution)/shard_map/ppermute | solution.py:39
  7.3 3.4 %collective-permute-done.2 = bf16[2,17,32,128]{3,2,1,0:T(8,128)(2,1)S(1)} collective-permute-done((bf16[2,17,32,128]{3,2,1,0:T(8,128)(2,1)S(1)}, bf16[2,17,32,128]{3,2,1,0:T(8,128)(2,1)S(1)}, u32[]{:S(2)}, u32[]{:S(2)}) %collective-permute-start.2) | collective-permute-done | bytes 278560 | tf_op jit(solution)/shard_map/ppermute | solution.py:39
  10.8 3.0 %collective-permute-done.3 = bf16[2,17,32,128]{3,2,1,0:T(8,128)(2,1)S(1)} collective-permute-done((bf16[2,17,32,128]{3,2,1,0:T(8,128)(2,1)S(1)}, bf16[2,17,32,128]{3,2,1,0:T(8,128)(2,1)S(1)}, u32[]{:S(2)}, u32[]{:S(2)}) %collective-permute-start.3) | collective-permute-done | bytes 278560 | tf_op jit(solution)/shard_map/ppermute | solution.py:39
  23.0 4.1 %collective-permute-done.9 = bf16[4,17,32,128]{3,2,1,0:T(8,128)(2,1)S(1)} collective-permute-done((bf16[4,17,32,128]{3,2,1,0:T(8,128)(2,1)}, bf16[4,17,32,128]{3,2,1,0:T(8,128)(2,1)S(1)}, u32[]{:S(2)}, u32[]{:S(2)}) %collective-permute-start.9) | collective-permute-done | bytes 557088 | tf_op jit(solution)/shard_map/ppermute | solution.py:44
  33.0 2.8 %collective-permute-start.12 = (bf16[2,17,32,128]{3,2,1,0:T(8,128)(2,1)S(1)}, bf16[2,17,32,128]{3,2,1,0:T(8,128)(2,1)}, u32[]{:S(2)}, u32[]{:S(2)}) collective-permute-start(bf16[2,17,32,128]{3,2,1,0:T(8,128)(2,1)S(1)} %slice.121), channel_id=1, source_target_pairs={{0,96},{4,28},{8,104},{12,4},{16,112},{20,12},{24,120},{28,20},{32... | collective-permute-start | bytes 835592 | tf_op jit(solution)/shard_map/ppermute | solution.py:47
  39.2 2.7 %collective-permute-start.7 = (bf16[2,17,32,128]{3,2,1,0:T(8,128)(2,1)}, bf16[2,17,32,128]{3,2,1,0:T(8,128)(2,1)}, u32[]{:S(2)}, u32[]{:S(2)}) collective-permute-start(bf16[2,17,32,128]{3,2,1,0:T(8,128)(2,1)} %slice.116), channel_id=1, source_target_pairs={{0,24},{4,100},{8,0},{12,108},{16,8},{20,116},{24,16},{28,124},{32... | collective-permute-start | bytes 835592 | tf_op jit(solution)/shard_map/ppermute | solution.py:47
  45.7 5.8 %first_sum.1 = (f32[2,32,128]{2,1,0:T(8,128)S(1)}, bf16[2048,32,128]{2,1,0:T(8,128)(2,1)}) custom-call(s32[7,64]{1,0:T(8,128)S(1)} %get-tuple-element.126.code_ref, bf16[68,32,128]{2,1,0:T(8,128)(2,1)S(1)} %bitcast.55, bf16[68,32,128]{2,1,0:T(8,128)(2,1)S(1)} %bitcast.58, bf16[68,32,128]{2,1,0:T(8,128)(2,1)} %bitcast.7.refs_2_, ...), custom_call_target="tpu_custom_call" | custom-call | flops 67108864 | bytes 6291456 | tf_op jit(solution)/shard_map/first_sum/pallas_call | solution.py:150
  60.4 4.6 %all-to-all-start = ((bf16[16,2,32,128]{3,2,1,0:T(8,128)(2,1)}), bf16[16,2,32,128]{3,2,1,0:T(8,128)(2,1)S(1)}, u32[]{:S(2)}, u32[]{:S(2)}) async-start(bf16[16,2,32,128]{3,2,1,0:T(8,128)(2,1)} %get-tuple-element.60), calls=%async_computation | async-start | bytes 524288 | tf_op jit(solution)/shard_map/all_to_all | solution.py:329
  65.0 5.6 %old_sum.6 = (f32[2,32,128]{2,1,0:T(8,128)S(1)}, s32[65]{0:T(128)S(1)}, bf16[16,128,128]{2,1,0:T(8,128)(2,1)S(1)}) custom-call(s32[7,64]{1,0:T(8,128)S(1)} %get-tuple-element.126.code_ref, s32[7,64]{1,0:T(8,128)S(1)} %get-tuple-element.92.fresh_ref, bf16[2048,32,128]{2,1,0:T(8,128)(2,1)} %get-tuple-element.57.store_ref, ...), custom_call_target="tpu_custom_call" | custom-call | flops 67108864 | bytes 6291456 | tf_op jit(solution)/shard_map/old_sum/pallas_call | solution.py:150
  79.9 4.1 %all-to-all-start.1 = ((bf16[16,2,32,128]{3,2,1,0:T(8,128)(2,1)}), bf16[16,2,32,128]{3,2,1,0:T(8,128)(2,1)S(1)}, u32[]{:S(2)}, u32[]{:S(2)}) async-start(bf16[16,2,32,128]{3,2,1,0:T(8,128)(2,1)} %get-tuple-element.67), calls=%async_computation.1 | async-start | bytes 524288 | tf_op jit(solution)/shard_map/all_to_all | solution.py:329
  84.0 5.3 %old_sum.7 = (f32[2,32,128]{2,1,0:T(8,128)S(1)}, s32[65]{0:T(128)S(1)}, bf16[16,128,128]{2,1,0:T(8,128)(2,1)S(1)}) custom-call(s32[7,64]{1,0:T(8,128)S(1)} %get-tuple-element.126.code_ref, s32[7,64]{1,0:T(8,128)S(1)} %get-tuple-element.92.fresh_ref, bf16[2048,32,128]{2,1,0:T(8,128)(2,1)} %get-tuple-element.57.store_ref, bf16[32,32,128]{2,1,0:T(8,128)(2,1)S(1)} %bitcast.36, ...), custom_call_target="tpu_custom_call" | custom-call | flops 67108864 | bytes 6291456 | tf_op jit(solution)/shard_map/old_sum/pallas_call | solution.py:150
  92.9 3.7 %collective-permute-start.23 = (f32[2,32,128]{2,1,0:T(8,128)S(1)}, f32[2,32,128]{2,1,0:T(8,128)S(1)}, u32[]{:S(2)}, u32[]{:S(2)}) collective-permute-start(f32[2,32,128]{2,1,0:T(8,128)S(1)} %fresh_sum.7.p0), channel_id=1, source_target_pairs={{0,2},{1,3},{2,0},{3,1},{4,6},{5,7},{6,4},{7,5},{8,10},{9,11},{10,... | collective-permute-start | bytes 98312 | tf_op jit(solution)/shard_map/ppermute | solution.py:322
  101.5 4.8 %all-to-all-start.2 = ((bf16[16,2,32,128]{3,2,1,0:T(8,128)(2,1)}), bf16[16,2,32,128]{3,2,1,0:T(8,128)(2,1)S(1)}, u32[]{:S(2)}, u32[]{:S(2)}) async-start(bf16[16,2,32,128]{3,2,1,0:T(8,128)(2,1)} %get-tuple-element.74), calls=%async_computation.2 | async-start | bytes 524288 | tf_op jit(solution)/shard_map/all_to_all | solution.py:329
  106.4 5.8 %old_sum.8 = (f32[2,32,128]{2,1,0:T(8,128)S(1)}, s32[65]{0:T(128)S(1)}, bf16[16,128,128]{2,1,0:T(8,128)(2,1)S(1)}) custom-call(s32[7,64]{1,0:T(8,128)S(1)} %get-tuple-element.126.code_ref, s32[7,64]{1,0:T(8,128)S(1)} %get-tuple-element.92.fresh_ref, bf16[2048,32,128]{2,1,0:T(8,128)(2,1)} %get-tuple-element.57.store_ref, bf16[32,32,128]{2,1,0:T(8,128)(2,1)S(1)} %bitcast.37, ...), custom_call_target="tpu_custom_call" | custom-call | flops 67108864 | bytes 6291456 | tf_op jit(solution)/shard_map/old_sum/pallas_call | solution.py:150
  116.4 2.7 %collective-permute-start.27 = (f32[2,32,128]{2,1,0:T(8,128)S(1)}, f32[2,32,128]{2,1,0:T(8,128)S(1)}, u32[]{:S(2)}, u32[]{:S(2)}) collective-permute-start(f32[2,32,128]{2,1,0:T(8,128)S(1)} %fresh_sum.8.p0), channel_id=1, source_target_pairs={{0,3},{1,2},{2,1},{3,0},{4,7},{5,6},{6,5},{7,4},{8,11},{9,10},{10,... | collective-permute-start | bytes 98312 | tf_op jit(solution)/shard_map/ppermute | solution.py:322
  121.6 4.5 %all-to-all-start.3 = ((bf16[16,2,32,128]{3,2,1,0:T(8,128)(2,1)}), bf16[16,2,32,128]{3,2,1,0:T(8,128)(2,1)S(1)}, u32[]{:S(2)}, u32[]{:S(2)}) async-start(bf16[16,2,32,128]{3,2,1,0:T(8,128)(2,1)} %get-tuple-element.81), calls=%async_computation.3 | async-start | bytes 524288 | tf_op jit(solution)/shard_map/all_to_all | solution.py:329
  126.0 5.5 %old_sum.9 = (f32[2,32,128]{2,1,0:T(8,128)S(1)}, s32[65]{0:T(128)S(1)}, bf16[16,128,128]{2,1,0:T(8,128)(2,1)S(1)}) custom-call(s32[7,64]{1,0:T(8,128)S(1)} %get-tuple-element.126.code_ref, s32[7,64]{1,0:T(8,128)S(1)} %get-tuple-element.92.fresh_ref, bf16[2048,32,128]{2,1,0:T(8,128)(2,1)} %get-tuple-element.57.store_ref, bf16[32,32,128]{2,1,0:T(8,128)(2,1)S(1)} %bitcast.38, ...), custom_call_target="tpu_custom_call" | custom-call | flops 67108864 | bytes 6291456 | tf_op jit(solution)/shard_map/old_sum/pallas_call | solution.py:150
  134.9 3.1 %collective-permute-start.29 = (f32[2,32,128]{2,1,0:T(8,128)S(1)}, f32[2,32,128]{2,1,0:T(8,128)S(1)}, u32[]{:S(2)}, u32[]{:S(2)}) collective-permute-start(f32[2,32,128]{2,1,0:T(8,128)S(1)} %fresh_sum.9.p0), channel_id=1, source_target_pairs={{0,2},{1,3},{2,0},{3,1},{4,6},{5,7},{6,4},{7,5},{8,10},{9,11},{10,... | collective-permute-start | bytes 98312 | tf_op jit(solution)/shard_map/ppermute | solution.py:322
  143.2 4.9 %all-to-all-start.4 = ((bf16[16,2,32,128]{3,2,1,0:T(8,128)(2,1)}), bf16[16,2,32,128]{3,2,1,0:T(8,128)(2,1)S(1)}, u32[]{:S(2)}, u32[]{:S(2)}) async-start(bf16[16,2,32,128]{3,2,1,0:T(8,128)(2,1)} %get-tuple-element.88), calls=%async_computation.4 | async-start | bytes 524288 | tf_op jit(solution)/shard_map/all_to_all | solution.py:329
  148.1 5.4 %old_sum.10 = (f32[2,32,128]{2,1,0:T(8,128)S(1)}, s32[65]{0:T(128)S(1)}, bf16[16,128,128]{2,1,0:T(8,128)(2,1)S(1)}) custom-call(s32[7,64]{1,0:T(8,128)S(1)} %get-tuple-element.126.code_ref, s32[7,64]{1,0:T(8,128)S(1)} %get-tuple-element.92.fresh_ref, bf16[2048,32,128]{2,1,0:T(8,128)(2,1)} %get-tuple-element.57.store_ref, bf16[32,32,128]{2,1,0:T(8,128)(2,1)S(1)} %bitcast.39, ...), custom_call_target="tpu_custom_call" | custom-call | flops 67108864 | bytes 6291456 | tf_op jit(solution)/shard_map/old_sum/pallas_call | solution.py:150
  162.6 5.2 %all-to-all-start.5 = ((bf16[16,2,32,128]{3,2,1,0:T(8,128)(2,1)}), bf16[16,2,32,128]{3,2,1,0:T(8,128)(2,1)S(1)}, u32[]{:S(2)}, u32[]{:S(2)}) async-start(bf16[16,2,32,128]{3,2,1,0:T(8,128)(2,1)} %get-tuple-element.95), calls=%async_computation.5 | async-start | bytes 524288 | tf_op jit(solution)/shard_map/all_to_all | solution.py:329
  167.9 5.4 %old_sum.11 = (f32[2,32,128]{2,1,0:T(8,128)S(1)}, s32[65]{0:T(128)S(1)}, bf16[16,128,128]{2,1,0:T(8,128)(2,1)S(1)}) custom-call(s32[7,64]{1,0:T(8,128)S(1)} %get-tuple-element.126.code_ref, s32[7,64]{1,0:T(8,128)S(1)} %get-tuple-element.92.fresh_ref, bf16[2048,32,128]{2,1,0:T(8,128)(2,1)} %get-tuple-element.57.store_ref, bf16[32,32,128]{2,1,0:T(8,128)(2,1)S(1)} %bitcast.40, ...), custom_call_target="tpu_custom_call" | custom-call | flops 67108864 | bytes 6291456 | tf_op jit(solution)/shard_map/old_sum/pallas_call | solution.py:150
  176.8 3.4 %collective-permute-start.35 = (f32[2,32,128]{2,1,0:T(8,128)S(1)}, f32[2,32,128]{2,1,0:T(8,128)S(1)}, u32[]{:S(2)}, u32[]{:S(2)}) collective-permute-start(f32[2,32,128]{2,1,0:T(8,128)S(1)} %fresh_sum.11.p0), channel_id=1, source_target_pairs={{0,2},{1,3},{2,0},{3,1},{4,6},{5,7},{6,4},{7,5},{8,10},{9,11},{10,... | collective-permute-start | bytes 98312 | tf_op jit(solution)/shard_map/ppermute | solution.py:322
  184.4 17.4 %collective-permute-start.37 = (bf16[7,32,128]{2,1,0:T(8,128)(2,1)S(1)}, bf16[7,32,128]{2,1,0:T(8,128)(2,1)S(1)}, u32[]{:S(2)}, u32[]{:S(2)}) collective-permute-start(bf16[7,32,128]{2,1,0:T(8,128)(2,1)S(1)} %get-tuple-element.112), channel_id=1, source_target_pairs={{0,4},{4,0},{1,5},{5,1},{2,6},{6,2},{3,7},{7,3},{8,12},{12,8},{9,1... | collective-permute-start | bytes 172040 | tf_op jit(solution)/shard_map/ppermute | solution.py:23
  (116 shorter events, 86.8 us)
Async XLA Ops:
  2.0 43.7 %collective-permute-start.13 = (bf16[7,1,32,128,128]{4,3,2,1,0:T(8,128)(2,1)}, bf16[7,1,32,128,128]{4,3,2,1,0:T(8,128)(2,1)}, u32[]{:S(2)}, u32[]{:S(2)}) collective-permute-start(bf16[7,1,32,128,128]{4,3,2,1,0:T(8,128)(2,1)} %own_ref.11), channel_id=1, source_target_pairs={{0,4},{4,0},{1,5},{5,1},{2,6},{6,2},{3,7},{7,3},{8,12},{12,8},{9,1... | collective-permute-start | bytes 22020104 | tf_op jit(solution)/shard_map/ppermute | solution.py:23
  3.5 7.2 %collective-permute-start.2 = (bf16[2,17,32,128]{3,2,1,0:T(8,128)(2,1)S(1)}, bf16[2,17,32,128]{3,2,1,0:T(8,128)(2,1)S(1)}, u32[]{:S(2)}, u32[]{:S(2)}) collective-permute-start(bf16[2,17,32,128]{3,2,1,0:T(8,128)(2,1)S(1)} %pad_maximum_fusion.2), channel_id=1, source_target_pairs={{0,64},{4,20},{8,72},{12,28},{16,80},{20,4},{24,88},{28,12},{32,96... | collective-permute-start | bytes 835592 | tf_op jit(solution)/shard_map/ppermute | solution.py:39
  6.5 7.2 %collective-permute-start.3 = (bf16[2,17,32,128]{3,2,1,0:T(8,128)(2,1)S(1)}, bf16[2,17,32,128]{3,2,1,0:T(8,128)(2,1)S(1)}, u32[]{:S(2)}, u32[]{:S(2)}) collective-permute-start(bf16[2,17,32,128]{3,2,1,0:T(8,128)(2,1)S(1)} %pad_maximum_fusion.2), channel_id=1, source_target_pairs={{0,96},{4,28},{8,104},{12,20},{16,112},{20,12},{24,120},{28,4},{32... | collective-permute-start | bytes 835592 | tf_op jit(solution)/shard_map/ppermute | solution.py:39
  7.3 6.9 %collective-permute-start.1 = (bf16[2,17,32,128]{3,2,1,0:T(8,128)(2,1)S(1)}, bf16[2,17,32,128]{3,2,1,0:T(8,128)(2,1)S(1)}, u32[]{:S(2)}, u32[]{:S(2)}) collective-permute-start(bf16[2,17,32,128]{3,2,1,0:T(8,128)(2,1)S(1)} %pad_maximum_fusion.2), channel_id=1, source_target_pairs={{0,32},{4,12},{8,40},{12,4},{16,48},{20,28},{24,56},{28,20},{32,0}... | collective-permute-start | bytes 835592 | tf_op jit(solution)/shard_map/ppermute | solution.py:39
  15.1 12.0 %collective-permute-start.9 = (bf16[4,17,32,128]{3,2,1,0:T(8,128)(2,1)}, bf16[4,17,32,128]{3,2,1,0:T(8,128)(2,1)S(1)}, u32[]{:S(2)}, u32[]{:S(2)}) collective-permute-start(bf16[4,17,32,128]{3,2,1,0:T(8,128)(2,1)} %pad_maximum_fusion.1), channel_id=1, source_target_pairs={{0,12},{4,32},{8,20},{12,40},{16,28},{20,48},{24,4},{28,56},{32,44... | collective-permute-start | bytes 1671176 | tf_op jit(solution)/shard_map/ppermute | solution.py:44
  17.7 10.5 %collective-permute-start.10 = (bf16[4,17,32,128]{3,2,1,0:T(8,128)(2,1)}, bf16[4,17,32,128]{3,2,1,0:T(8,128)(2,1)S(1)}, u32[]{:S(2)}, u32[]{:S(2)}) collective-permute-start(bf16[4,17,32,128]{3,2,1,0:T(8,128)(2,1)} %pad_maximum_fusion.1), channel_id=1, source_target_pairs={{0,28},{4,96},{8,4},{12,104},{16,12},{20,112},{24,20},{28,120},{32... | collective-permute-start | bytes 1671176 | tf_op jit(solution)/shard_map/ppermute | solution.py:45
  20.3 12.7 %collective-permute-start.4 = (bf16[4,17,32,128]{3,2,1,0:T(8,128)(2,1)S(1)}, bf16[4,17,32,128]{3,2,1,0:T(8,128)(2,1)S(1)}, u32[]{:S(2)}, u32[]{:S(2)}) collective-permute-start(bf16[4,17,32,128]{3,2,1,0:T(8,128)(2,1)S(1)} %pad_maximum_fusion), channel_id=1, source_target_pairs={{0,8},{4,36},{8,16},{12,44},{16,24},{20,52},{24,0},{28,60},{32,40}... | collective-permute-start | bytes 1671176 | tf_op jit(solution)/shard_map/ppermute | solution.py:44
  20.4 17.1 %collective-permute-start.5 = (bf16[4,17,32,128]{3,2,1,0:T(8,128)(2,1)S(1)}, bf16[4,17,32,128]{3,2,1,0:T(8,128)(2,1)}, u32[]{:S(2)}, u32[]{:S(2)}) collective-permute-start(bf16[4,17,32,128]{3,2,1,0:T(8,128)(2,1)S(1)} %pad_maximum_fusion), channel_id=1, source_target_pairs={{0,24},{4,100},{8,0},{12,108},{16,8},{20,116},{24,16},{28,124},{32... | collective-permute-start | bytes 1671176 | tf_op jit(solution)/shard_map/ppermute | solution.py:45
  27.1 12.1 %collective-permute-start.8 = (bf16[4,17,32,128]{3,2,1,0:T(8,128)(2,1)}, bf16[4,17,32,128]{3,2,1,0:T(8,128)(2,1)}, u32[]{:S(2)}, u32[]{:S(2)}) collective-permute-start(bf16[4,17,32,128]{3,2,1,0:T(8,128)(2,1)} %pad_maximum_fusion.1), channel_id=1, source_target_pairs={{0,4},{4,0},{1,5},{5,1},{2,6},{6,2},{3,7},{7,3},{8,12},{12,8},{9,1... | collective-permute-start | bytes 1671176 | tf_op jit(solution)/shard_map/ppermute | solution.py:23
  29.4 12.6 %collective-permute-start.11 = (bf16[2,17,32,128]{3,2,1,0:T(8,128)(2,1)S(1)}, bf16[2,17,32,128]{3,2,1,0:T(8,128)(2,1)S(1)}, u32[]{:S(2)}, u32[]{:S(2)}) collective-permute-start(bf16[2,17,32,128]{3,2,1,0:T(8,128)(2,1)S(1)} %slice.120), channel_id=1, source_target_pairs={{0,32},{4,12},{8,40},{12,20},{16,48},{20,28},{24,56},{28,4},{32,64... | collective-permute-start | bytes 835592 | tf_op jit(solution)/shard_map/ppermute | solution.py:46
  33.0 10.1 %collective-permute-start.12 = (bf16[2,17,32,128]{3,2,1,0:T(8,128)(2,1)S(1)}, bf16[2,17,32,128]{3,2,1,0:T(8,128)(2,1)}, u32[]{:S(2)}, u32[]{:S(2)}) collective-permute-start(bf16[2,17,32,128]{3,2,1,0:T(8,128)(2,1)S(1)} %slice.121), channel_id=1, source_target_pairs={{0,96},{4,28},{8,104},{12,4},{16,112},{20,12},{24,120},{28,20},{32... | collective-permute-start | bytes 835592 | tf_op jit(solution)/shard_map/ppermute | solution.py:47
  37.5 7.2 %collective-permute-start.6 = (bf16[2,17,32,128]{3,2,1,0:T(8,128)(2,1)}, bf16[2,17,32,128]{3,2,1,0:T(8,128)(2,1)}, u32[]{:S(2)}, u32[]{:S(2)}) collective-permute-start(bf16[2,17,32,128]{3,2,1,0:T(8,128)(2,1)} %slice.115), channel_id=1, source_target_pairs={{0,8},{4,36},{8,16},{12,44},{16,24},{20,52},{24,0},{28,60},{32,40}... | collective-permute-start | bytes 835592 | tf_op jit(solution)/shard_map/ppermute | solution.py:46
  39.2 6.5 %collective-permute-start.7 = (bf16[2,17,32,128]{3,2,1,0:T(8,128)(2,1)}, bf16[2,17,32,128]{3,2,1,0:T(8,128)(2,1)}, u32[]{:S(2)}, u32[]{:S(2)}) collective-permute-start(bf16[2,17,32,128]{3,2,1,0:T(8,128)(2,1)} %slice.116), channel_id=1, source_target_pairs={{0,24},{4,100},{8,0},{12,108},{16,8},{20,116},{24,16},{28,124},{32... | collective-permute-start | bytes 835592 | tf_op jit(solution)/shard_map/ppermute | solution.py:47
  42.0 13.5 %collective-permute-start.18 = (bf16[8,1,128,128]{3,2,1,0:T(8,128)(2,1)S(1)}, bf16[8,1,128,128]{3,2,1,0:T(8,128)(2,1)S(1)}, u32[]{:S(2)}, u32[]{:S(2)}) collective-permute-start(bf16[8,1,128,128]{3,2,1,0:T(8,128)(2,1)S(1)} %copy-done), channel_id=1, source_target_pairs={{0,4},{4,0},{1,5},{5,1},{2,6},{6,2},{3,7},{7,3},{8,12},{12,8},{9,1... | collective-permute-start | bytes 786440 | tf_op jit(solution)/shard_map/ppermute | solution.py:23
  43.2 12.3 %collective-permute-start.17 = (bf16[8,1,32,128]{3,2,1,0:T(8,128)(2,1)S(1)}, bf16[8,1,32,128]{3,2,1,0:T(8,128)(2,1)S(1)}, u32[]{:S(2)}, u32[]{:S(2)}) collective-permute-start(bf16[8,1,32,128]{3,2,1,0:T(8,128)(2,1)S(1)} %get-tuple-element.108), channel_id=1, source_target_pairs={{0,4},{4,0},{1,5},{5,1},{2,6},{6,2},{3,7},{7,3},{8,12},{12,8},{9,1... | collective-permute-start | bytes 196616 | tf_op jit(solution)/shard_map/ppermute | solution.py:23
  60.4 12.1 %all-to-all-start = ((bf16[16,2,32,128]{3,2,1,0:T(8,128)(2,1)}), bf16[16,2,32,128]{3,2,1,0:T(8,128)(2,1)S(1)}, u32[]{:S(2)}, u32[]{:S(2)}) async-start(bf16[16,2,32,128]{3,2,1,0:T(8,128)(2,1)} %get-tuple-element.60), calls=%async_computation | async-start | bytes 524288 | tf_op jit(solution)/shard_map/all_to_all | solution.py:329
  79.9 11.7 %all-to-all-start.1 = ((bf16[16,2,32,128]{3,2,1,0:T(8,128)(2,1)}), bf16[16,2,32,128]{3,2,1,0:T(8,128)(2,1)S(1)}, u32[]{:S(2)}, u32[]{:S(2)}) async-start(bf16[16,2,32,128]{3,2,1,0:T(8,128)(2,1)} %get-tuple-element.67), calls=%async_computation.1 | async-start | bytes 524288 | tf_op jit(solution)/shard_map/all_to_all | solution.py:329
  92.9 5.6 %collective-permute-start.23 = (f32[2,32,128]{2,1,0:T(8,128)S(1)}, f32[2,32,128]{2,1,0:T(8,128)S(1)}, u32[]{:S(2)}, u32[]{:S(2)}) collective-permute-start(f32[2,32,128]{2,1,0:T(8,128)S(1)} %fresh_sum.7.p0), channel_id=1, source_target_pairs={{0,2},{1,3},{2,0},{3,1},{4,6},{5,7},{6,4},{7,5},{8,10},{9,11},{10,... | collective-permute-start | bytes 98312 | tf_op jit(solution)/shard_map/ppermute | solution.py:322
  101.5 12.4 %all-to-all-start.2 = ((bf16[16,2,32,128]{3,2,1,0:T(8,128)(2,1)}), bf16[16,2,32,128]{3,2,1,0:T(8,128)(2,1)S(1)}, u32[]{:S(2)}, u32[]{:S(2)}) async-start(bf16[16,2,32,128]{3,2,1,0:T(8,128)(2,1)} %get-tuple-element.74), calls=%async_computation.2 | async-start | bytes 524288 | tf_op jit(solution)/shard_map/all_to_all | solution.py:329
  121.6 12.0 %all-to-all-start.3 = ((bf16[16,2,32,128]{3,2,1,0:T(8,128)(2,1)}), bf16[16,2,32,128]{3,2,1,0:T(8,128)(2,1)S(1)}, u32[]{:S(2)}, u32[]{:S(2)}) async-start(bf16[16,2,32,128]{3,2,1,0:T(8,128)(2,1)} %get-tuple-element.81), calls=%async_computation.3 | async-start | bytes 524288 | tf_op jit(solution)/shard_map/all_to_all | solution.py:329
  143.2 12.4 %all-to-all-start.4 = ((bf16[16,2,32,128]{3,2,1,0:T(8,128)(2,1)}), bf16[16,2,32,128]{3,2,1,0:T(8,128)(2,1)S(1)}, u32[]{:S(2)}, u32[]{:S(2)}) async-start(bf16[16,2,32,128]{3,2,1,0:T(8,128)(2,1)} %get-tuple-element.88), calls=%async_computation.4 | async-start | bytes 524288 | tf_op jit(solution)/shard_map/all_to_all | solution.py:329
  162.6 12.8 %all-to-all-start.5 = ((bf16[16,2,32,128]{3,2,1,0:T(8,128)(2,1)}), bf16[16,2,32,128]{3,2,1,0:T(8,128)(2,1)S(1)}, u32[]{:S(2)}, u32[]{:S(2)}) async-start(bf16[16,2,32,128]{3,2,1,0:T(8,128)(2,1)} %get-tuple-element.95), calls=%async_computation.5 | async-start | bytes 524288 | tf_op jit(solution)/shard_map/all_to_all | solution.py:329
  176.8 5.1 %collective-permute-start.35 = (f32[2,32,128]{2,1,0:T(8,128)S(1)}, f32[2,32,128]{2,1,0:T(8,128)S(1)}, u32[]{:S(2)}, u32[]{:S(2)}) collective-permute-start(f32[2,32,128]{2,1,0:T(8,128)S(1)} %fresh_sum.11.p0), channel_id=1, source_target_pairs={{0,2},{1,3},{2,0},{3,1},{4,6},{5,7},{6,4},{7,5},{8,10},{9,11},{10,... | collective-permute-start | bytes 98312 | tf_op jit(solution)/shard_map/ppermute | solution.py:322
  184.4 18.3 %collective-permute-start.37 = (bf16[7,32,128]{2,1,0:T(8,128)(2,1)S(1)}, bf16[7,32,128]{2,1,0:T(8,128)(2,1)S(1)}, u32[]{:S(2)}, u32[]{:S(2)}) collective-permute-start(bf16[7,32,128]{2,1,0:T(8,128)(2,1)S(1)} %get-tuple-element.112), channel_id=1, source_target_pairs={{0,4},{4,0},{1,5},{5,1},{2,6},{6,2},{3,7},{7,3},{8,12},{12,8},{9,1... | collective-permute-start | bytes 172040 | tf_op jit(solution)/shard_map/ppermute | solution.py:23
  (21 other events, 122.0 us)

commit v14 on v13

--- a/solution.py
+++ b/solution.py
@@ -290,7 +290,6 @@
     known = jnp.stack([my_half(known, 1), their_half(known, 1)])
     code_own = (coupling + 1024 * present)[:, 0]
     code_both = jnp.stack([code_own, swap_cores(code_own)], axis=1)
-    rhs_both = jnp.concatenate([my_half(rhs, 2), swap_cores(their_half(rhs, 2))], axis=1)
     diag_other = swap_cores(diag_inv)
     off_sent, known = lax.optimization_barrier((off_blocks, known))
     off_other = swap_cores(off_sent)
@@ -318,6 +317,8 @@
     own_rows, other_rows = [], []
     value, store = first_sum(old_code, pieces, off_blocks, off_other)
     solved_levels = []
+    rhs_late, value = lax.optimization_barrier((rhs, value))
+    rhs_both = jnp.concatenate([my_half(rhs_late, 2), swap_cores(their_half(rhs_late, 2))], axis=1)
     for level in range(1, levels):
         partials = [value] + [lax.ppermute(value, "x", xor_pairs(4, k)) for k in (1, 2, 3)]
         last = level == levels - 1

time: 204 us -> 209 us (1.025)
  waiting for transfers between devices: 50.7 us -> 54 us
    ppermute x3, waiting for transfers between devices: 6.8 us -> 9.82 us  [gather_parts(): lax.ppermute(v, ROWS, pairs(1, lambda i, k=k: i ^ k))]
  transfers between devices with their start and end apart: 44 -> 44, of which waited for: 29 -> 29; matrix products, arithmetic and copies ran while one was open for 3% -> 2% of each run, Pallas kernels for 19% -> 19%
where the time goes in v14:
time: 209 us; the launch traced here: 208 us
  starting transfers between devices  95.1 us (46%)
  waiting for transfers between devices  54 us (26%)
  Pallas kernels  50.5 us (24%)
  other arithmetic  3.48 us (2%)
  local copies, waits for them, and re-layouts  3.42 us (2%)
    pallas_call x7, Pallas kernels, sum_call(): pl.pallas_call(kernel, out_shape=[jax.ShapeDtypeStruct((2, rhs_cols, bloc...  39.6 us
    all_to_all x6, starting transfers between devices, on_device(): solved = lax.all_to_all(sent, ('z', 'y'), 0, 0).reshape(32, half, block)  29.5 us
    ppermute x21, starting transfers between devices, on_device(): lax.ppermute(value, 'x', xor_pairs(4, k))  27.7 us
    ppermute x21, waiting for transfers between devices, on_device(): lax.ppermute(value, 'x', xor_pairs(4, k))  21.1 us
    ppermute x6, starting transfers between devices, swap_cores(): return lax.ppermute(v, 'core', xor_pairs(2, 1))  20.7 us
    all_to_all x6, waiting for transfers between devices, on_device(): solved = lax.all_to_all(sent, ('z', 'y'), 0, 0).reshape(32, half, block)  11.4 us
    ppermute x3, waiting for transfers between devices, gather_parts(): lax.ppermute(v, ROWS, pairs(1, lambda i, k=k: i ^ k))  9.82 us
    ppermute x2, waiting for transfers between devices, spread(): before = lax.ppermute(part, ROWS, pairs(2, after_one, cross))  7.07 us
  transfers between devices with their start and end apart: 44, of which 29 were waited for; matrix products, arithmetic and copies ran while one was open for 2% of the time, Pallas kernels for 19%

profile of v14, /device:TPU:1, one launch (start us, length us, event | category | flops | bytes accessed | tf_op | source)
XLA Modules:
  0.0 207.8 jit_solution(1049419848783680658)
XLA Ops:
  9.2 5.5 %collective-permute-done.2 = bf16[2,17,32,128]{3,2,1,0:T(8,128)(2,1)S(1)} collective-permute-done((bf16[2,17,32,128]{3,2,1,0:T(8,128)(2,1)S(1)}, bf16[2,17,32,128]{3,2,1,0:T(8,128)(2,1)S(1)}, u32[]{:S(2)}, u32[]{:S(2)}) %collective-permute-start.2) | collective-permute-done | bytes 278560 | tf_op jit(solution)/shard_map/ppermute | solution.py:39
  21.4 3.0 %collective-permute-start.10 = (bf16[4,17,32,128]{3,2,1,0:T(8,128)(2,1)}, bf16[4,17,32,128]{3,2,1,0:T(8,128)(2,1)S(1)}, u32[]{:S(2)}, u32[]{:S(2)}) collective-permute-start(bf16[4,17,32,128]{3,2,1,0:T(8,128)(2,1)} %pad_maximum_fusion.1), channel_id=1, source_target_pairs={{0,28},{4,96},{8,4},{12,104},{16,12},{20,112},{24,20},{28,120},{32... | collective-permute-start | bytes 1671176 | tf_op jit(solution)/shard_map/ppermute | solution.py:45
  27.2 3.5 %collective-permute-done.9 = bf16[4,17,32,128]{3,2,1,0:T(8,128)(2,1)S(1)} collective-permute-done((bf16[4,17,32,128]{3,2,1,0:T(8,128)(2,1)}, bf16[4,17,32,128]{3,2,1,0:T(8,128)(2,1)S(1)}, u32[]{:S(2)}, u32[]{:S(2)}) %collective-permute-start.9) | collective-permute-done | bytes 557088 | tf_op jit(solution)/shard_map/ppermute | solution.py:44
  33.2 3.6 %collective-permute-done.4 = bf16[4,17,32,128]{3,2,1,0:T(8,128)(2,1)S(1)} collective-permute-done((bf16[4,17,32,128]{3,2,1,0:T(8,128)(2,1)S(1)}, bf16[4,17,32,128]{3,2,1,0:T(8,128)(2,1)S(1)}, u32[]{:S(2)}, u32[]{:S(2)}) %collective-permute-start.4) | collective-permute-done | bytes 557088 | tf_op jit(solution)/shard_map/ppermute | solution.py:44
  36.8 2.8 %collective-permute-start.12 = (bf16[2,17,32,128]{3,2,1,0:T(8,128)(2,1)}, bf16[2,17,32,128]{3,2,1,0:T(8,128)(2,1)}, u32[]{:S(2)}, u32[]{:S(2)}) collective-permute-start(bf16[2,17,32,128]{3,2,1,0:T(8,128)(2,1)} %slice.121), channel_id=1, source_target_pairs={{0,96},{4,28},{8,104},{12,4},{16,112},{20,12},{24,120},{28,20},{32... | collective-permute-start | bytes 835592 | tf_op jit(solution)/shard_map/ppermute | solution.py:47
  48.5 5.8 %first_sum.1 = (f32[2,32,128]{2,1,0:T(8,128)S(1)}, bf16[2048,32,128]{2,1,0:T(8,128)(2,1)}) custom-call(s32[7,64]{1,0:T(8,128)S(1)} %get-tuple-element.130.code_ref, bf16[68,32,128]{2,1,0:T(8,128)(2,1)S(1)} %bitcast.55, bf16[68,32,128]{2,1,0:T(8,128)(2,1)S(1)} %bitcast.58, bf16[68,32,128]{2,1,0:T(8,128)(2,1)} %bitcast.7.refs_2_, ...), custom_call_target="tpu_custom_call" | custom-call | flops 67108864 | bytes 6291456 | tf_op jit(solution)/shard_map/first_sum/pallas_call | solution.py:150
  63.7 6.3 %all-to-all-start = ((bf16[16,2,32,128]{3,2,1,0:T(8,128)(2,1)}), bf16[16,2,32,128]{3,2,1,0:T(8,128)(2,1)S(1)}, u32[]{:S(2)}, u32[]{:S(2)}) async-start(bf16[16,2,32,128]{3,2,1,0:T(8,128)(2,1)} %get-tuple-element.64), calls=%async_computation | async-start | bytes 524288 | tf_op jit(solution)/shard_map/all_to_all | solution.py:330
  70.0 5.6 %old_sum.6 = (f32[2,32,128]{2,1,0:T(8,128)S(1)}, s32[65]{0:T(128)S(1)}, bf16[16,128,128]{2,1,0:T(8,128)(2,1)S(1)}) custom-call(s32[7,64]{1,0:T(8,128)S(1)} %get-tuple-element.130.code_ref, s32[7,64]{1,0:T(8,128)S(1)} %get-tuple-element.96.fresh_ref, bf16[2048,32,128]{2,1,0:T(8,128)(2,1)} %get-tuple-element.61.store_ref, ...), custom_call_target="tpu_custom_call" | custom-call | flops 67108864 | bytes 6291456 | tf_op jit(solution)/shard_map/old_sum/pallas_call | solution.py:150
  85.8 4.1 %all-to-all-start.1 = ((bf16[16,2,32,128]{3,2,1,0:T(8,128)(2,1)}), bf16[16,2,32,128]{3,2,1,0:T(8,128)(2,1)S(1)}, u32[]{:S(2)}, u32[]{:S(2)}) async-start(bf16[16,2,32,128]{3,2,1,0:T(8,128)(2,1)} %get-tuple-element.71), calls=%async_computation.1 | async-start | bytes 524288 | tf_op jit(solution)/shard_map/all_to_all | solution.py:330
  89.9 5.3 %old_sum.7 = (f32[2,32,128]{2,1,0:T(8,128)S(1)}, s32[65]{0:T(128)S(1)}, bf16[16,128,128]{2,1,0:T(8,128)(2,1)S(1)}) custom-call(s32[7,64]{1,0:T(8,128)S(1)} %get-tuple-element.130.code_ref, s32[7,64]{1,0:T(8,128)S(1)} %get-tuple-element.96.fresh_ref, bf16[2048,32,128]{2,1,0:T(8,128)(2,1)} %get-tuple-element.61.store_ref, bf16[32,32,128]{2,1,0:T(8,128)(2,1)S(1)} %bitcast.36, ...), custom_call_target="tpu_custom_call" | custom-call | flops 67108864 | bytes 6291456 | tf_op jit(solution)/shard_map/old_sum/pallas_call | solution.py:150
  99.1 3.3 %collective-permute-start.23 = (f32[2,32,128]{2,1,0:T(8,128)S(1)}, f32[2,32,128]{2,1,0:T(8,128)S(1)}, u32[]{:S(2)}, u32[]{:S(2)}) collective-permute-start(f32[2,32,128]{2,1,0:T(8,128)S(1)} %fresh_sum.7.p0), channel_id=1, source_target_pairs={{0,2},{1,3},{2,0},{3,1},{4,6},{5,7},{6,4},{7,5},{8,10},{9,11},{10,... | collective-permute-start | bytes 98312 | tf_op jit(solution)/shard_map/ppermute | solution.py:323
  107.2 5.0 %all-to-all-start.2 = ((bf16[16,2,32,128]{3,2,1,0:T(8,128)(2,1)}), bf16[16,2,32,128]{3,2,1,0:T(8,128)(2,1)S(1)}, u32[]{:S(2)}, u32[]{:S(2)}) async-start(bf16[16,2,32,128]{3,2,1,0:T(8,128)(2,1)} %get-tuple-element.78), calls=%async_computation.2 | async-start | bytes 524288 | tf_op jit(solution)/shard_map/all_to_all | solution.py:330
  112.3 5.6 %old_sum.8 = (f32[2,32,128]{2,1,0:T(8,128)S(1)}, s32[65]{0:T(128)S(1)}, bf16[16,128,128]{2,1,0:T(8,128)(2,1)S(1)}) custom-call(s32[7,64]{1,0:T(8,128)S(1)} %get-tuple-element.130.code_ref, s32[7,64]{1,0:T(8,128)S(1)} %get-tuple-element.96.fresh_ref, bf16[2048,32,128]{2,1,0:T(8,128)(2,1)} %get-tuple-element.61.store_ref, bf16[32,32,128]{2,1,0:T(8,128)(2,1)S(1)} %bitcast.37, ...), custom_call_target="tpu_custom_call" | custom-call | flops 67108864 | bytes 6291456 | tf_op jit(solution)/shard_map/old_sum/pallas_call | solution.py:150
  121.6 2.8 %collective-permute-start.27 = (f32[2,32,128]{2,1,0:T(8,128)S(1)}, f32[2,32,128]{2,1,0:T(8,128)S(1)}, u32[]{:S(2)}, u32[]{:S(2)}) collective-permute-start(f32[2,32,128]{2,1,0:T(8,128)S(1)} %fresh_sum.8.p0), channel_id=1, source_target_pairs={{0,3},{1,2},{2,1},{3,0},{4,7},{5,6},{6,5},{7,4},{8,11},{9,10},{10,... | collective-permute-start | bytes 98312 | tf_op jit(solution)/shard_map/ppermute | solution.py:323
  126.9 5.0 %all-to-all-start.3 = ((bf16[16,2,32,128]{3,2,1,0:T(8,128)(2,1)}), bf16[16,2,32,128]{3,2,1,0:T(8,128)(2,1)S(1)}, u32[]{:S(2)}, u32[]{:S(2)}) async-start(bf16[16,2,32,128]{3,2,1,0:T(8,128)(2,1)} %get-tuple-element.85), calls=%async_computation.3 | async-start | bytes 524288 | tf_op jit(solution)/shard_map/all_to_all | solution.py:330
  132.0 5.7 %old_sum.9 = (f32[2,32,128]{2,1,0:T(8,128)S(1)}, s32[65]{0:T(128)S(1)}, bf16[16,128,128]{2,1,0:T(8,128)(2,1)S(1)}) custom-call(s32[7,64]{1,0:T(8,128)S(1)} %get-tuple-element.130.code_ref, s32[7,64]{1,0:T(8,128)S(1)} %get-tuple-element.96.fresh_ref, bf16[2048,32,128]{2,1,0:T(8,128)(2,1)} %get-tuple-element.61.store_ref, bf16[32,32,128]{2,1,0:T(8,128)(2,1)S(1)} %bitcast.38, ...), custom_call_target="tpu_custom_call" | custom-call | flops 67108864 | bytes 6291456 | tf_op jit(solution)/shard_map/old_sum/pallas_call | solution.py:150
  140.7 3.6 %collective-permute-start.29 = (f32[2,32,128]{2,1,0:T(8,128)S(1)}, f32[2,32,128]{2,1,0:T(8,128)S(1)}, u32[]{:S(2)}, u32[]{:S(2)}) collective-permute-start(f32[2,32,128]{2,1,0:T(8,128)S(1)} %fresh_sum.9.p0), channel_id=1, source_target_pairs={{0,2},{1,3},{2,0},{3,1},{4,6},{5,7},{6,4},{7,5},{8,10},{9,11},{10,... | collective-permute-start | bytes 98312 | tf_op jit(solution)/shard_map/ppermute | solution.py:323
  149.4 4.5 %all-to-all-start.4 = ((bf16[16,2,32,128]{3,2,1,0:T(8,128)(2,1)}), bf16[16,2,32,128]{3,2,1,0:T(8,128)(2,1)S(1)}, u32[]{:S(2)}, u32[]{:S(2)}) async-start(bf16[16,2,32,128]{3,2,1,0:T(8,128)(2,1)} %get-tuple-element.92), calls=%async_computation.4 | async-start | bytes 524288 | tf_op jit(solution)/shard_map/all_to_all | solution.py:330
  154.0 5.8 %old_sum.10 = (f32[2,32,128]{2,1,0:T(8,128)S(1)}, s32[65]{0:T(128)S(1)}, bf16[16,128,128]{2,1,0:T(8,128)(2,1)S(1)}) custom-call(s32[7,64]{1,0:T(8,128)S(1)} %get-tuple-element.130.code_ref, s32[7,64]{1,0:T(8,128)S(1)} %get-tuple-element.96.fresh_ref, bf16[2048,32,128]{2,1,0:T(8,128)(2,1)} %get-tuple-element.61.store_ref, bf16[32,32,128]{2,1,0:T(8,128)(2,1)S(1)} %bitcast.39, ...), custom_call_target="tpu_custom_call" | custom-call | flops 67108864 | bytes 6291456 | tf_op jit(solution)/shard_map/old_sum/pallas_call | solution.py:150
  163.8 2.7 %collective-permute-start.33 = (f32[2,32,128]{2,1,0:T(8,128)S(1)}, f32[2,32,128]{2,1,0:T(8,128)S(1)}, u32[]{:S(2)}, u32[]{:S(2)}) collective-permute-start(f32[2,32,128]{2,1,0:T(8,128)S(1)} %fresh_sum.10.p0), channel_id=1, source_target_pairs={{0,3},{1,2},{2,1},{3,0},{4,7},{5,6},{6,5},{7,4},{8,11},{9,10},{10,... | collective-permute-start | bytes 98312 | tf_op jit(solution)/shard_map/ppermute | solution.py:323
  168.6 4.5 %all-to-all-start.5 = ((bf16[16,2,32,128]{3,2,1,0:T(8,128)(2,1)}), bf16[16,2,32,128]{3,2,1,0:T(8,128)(2,1)S(1)}, u32[]{:S(2)}, u32[]{:S(2)}) async-start(bf16[16,2,32,128]{3,2,1,0:T(8,128)(2,1)} %get-tuple-element.99), calls=%async_computation.5 | async-start | bytes 524288 | tf_op jit(solution)/shard_map/all_to_all | solution.py:330
  173.2 5.8 %old_sum.11 = (f32[2,32,128]{2,1,0:T(8,128)S(1)}, s32[65]{0:T(128)S(1)}, bf16[16,128,128]{2,1,0:T(8,128)(2,1)S(1)}) custom-call(s32[7,64]{1,0:T(8,128)S(1)} %get-tuple-element.130.code_ref, s32[7,64]{1,0:T(8,128)S(1)} %get-tuple-element.96.fresh_ref, bf16[2048,32,128]{2,1,0:T(8,128)(2,1)} %get-tuple-element.61.store_ref, bf16[32,32,128]{2,1,0:T(8,128)(2,1)S(1)} %bitcast.40, ...), custom_call_target="tpu_custom_call" | custom-call | flops 67108864 | bytes 6291456 | tf_op jit(solution)/shard_map/old_sum/pallas_call | solution.py:150
  182.3 3.4 %collective-permute-start.35 = (f32[2,32,128]{2,1,0:T(8,128)S(1)}, f32[2,32,128]{2,1,0:T(8,128)S(1)}, u32[]{:S(2)}, u32[]{:S(2)}) collective-permute-start(f32[2,32,128]{2,1,0:T(8,128)S(1)} %fresh_sum.11.p0), channel_id=1, source_target_pairs={{0,2},{1,3},{2,0},{3,1},{4,6},{5,7},{6,4},{7,5},{8,10},{9,11},{10,... | collective-permute-start | bytes 98312 | tf_op jit(solution)/shard_map/ppermute | solution.py:323
  189.9 16.4 %collective-permute-start.37 = (bf16[7,32,128]{2,1,0:T(8,128)(2,1)S(1)}, bf16[7,32,128]{2,1,0:T(8,128)(2,1)S(1)}, u32[]{:S(2)}, u32[]{:S(2)}) collective-permute-start(bf16[7,32,128]{2,1,0:T(8,128)(2,1)S(1)} %get-tuple-element.116), channel_id=1, source_target_pairs={{0,4},{4,0},{1,5},{5,1},{2,6},{6,2},{3,7},{7,3},{8,12},{12,8},{9,1... | collective-permute-start | bytes 172040 | tf_op jit(solution)/shard_map/ppermute | solution.py:23
  (118 shorter events, 87.8 us)
Async XLA Ops:
  2.0 46.5 %collective-permute-start.13 = (bf16[7,1,32,128,128]{4,3,2,1,0:T(8,128)(2,1)}, bf16[7,1,32,128,128]{4,3,2,1,0:T(8,128)(2,1)}, u32[]{:S(2)}, u32[]{:S(2)}) collective-permute-start(bf16[7,1,32,128,128]{4,3,2,1,0:T(8,128)(2,1)} %own_ref.11), channel_id=1, source_target_pairs={{0,4},{4,0},{1,5},{5,1},{2,6},{6,2},{3,7},{7,3},{8,12},{12,8},{9,1... | collective-permute-start | bytes 22020104 | tf_op jit(solution)/shard_map/ppermute | solution.py:23
  3.5 5.7 %collective-permute-start.1 = (bf16[2,17,32,128]{3,2,1,0:T(8,128)(2,1)S(1)}, bf16[2,17,32,128]{3,2,1,0:T(8,128)(2,1)S(1)}, u32[]{:S(2)}, u32[]{:S(2)}) collective-permute-start(bf16[2,17,32,128]{3,2,1,0:T(8,128)(2,1)S(1)} %pad_maximum_fusion.2), channel_id=1, source_target_pairs={{0,32},{4,12},{8,40},{12,4},{16,48},{20,28},{24,56},{28,20},{32,0}... | collective-permute-start | bytes 835592 | tf_op jit(solution)/shard_map/ppermute | solution.py:39
  4.9 9.9 %collective-permute-start.2 = (bf16[2,17,32,128]{3,2,1,0:T(8,128)(2,1)S(1)}, bf16[2,17,32,128]{3,2,1,0:T(8,128)(2,1)S(1)}, u32[]{:S(2)}, u32[]{:S(2)}) collective-permute-start(bf16[2,17,32,128]{3,2,1,0:T(8,128)(2,1)S(1)} %pad_maximum_fusion.2), channel_id=1, source_target_pairs={{0,64},{4,20},{8,72},{12,28},{16,80},{20,4},{24,88},{28,12},{32,96... | collective-permute-start | bytes 835592 | tf_op jit(solution)/shard_map/ppermute | solution.py:39
  7.5 9.9 %collective-permute-start.3 = (bf16[2,17,32,128]{3,2,1,0:T(8,128)(2,1)S(1)}, bf16[2,17,32,128]{3,2,1,0:T(8,128)(2,1)S(1)}, u32[]{:S(2)}, u32[]{:S(2)}) collective-permute-start(bf16[2,17,32,128]{3,2,1,0:T(8,128)(2,1)S(1)} %pad_maximum_fusion.2), channel_id=1, source_target_pairs={{0,96},{4,28},{8,104},{12,20},{16,112},{20,12},{24,120},{28,4},{32... | collective-permute-start | bytes 835592 | tf_op jit(solution)/shard_map/ppermute | solution.py:39
  18.3 12.3 %collective-permute-start.9 = (bf16[4,17,32,128]{3,2,1,0:T(8,128)(2,1)}, bf16[4,17,32,128]{3,2,1,0:T(8,128)(2,1)S(1)}, u32[]{:S(2)}, u32[]{:S(2)}) collective-permute-start(bf16[4,17,32,128]{3,2,1,0:T(8,128)(2,1)} %pad_maximum_fusion.1), channel_id=1, source_target_pairs={{0,12},{4,32},{8,20},{12,40},{16,28},{20,48},{24,4},{28,56},{32,44... | collective-permute-start | bytes 1671176 | tf_op jit(solution)/shard_map/ppermute | solution.py:44
  21.4 9.7 %collective-permute-start.10 = (bf16[4,17,32,128]{3,2,1,0:T(8,128)(2,1)}, bf16[4,17,32,128]{3,2,1,0:T(8,128)(2,1)S(1)}, u32[]{:S(2)}, u32[]{:S(2)}) collective-permute-start(bf16[4,17,32,128]{3,2,1,0:T(8,128)(2,1)} %pad_maximum_fusion.1), channel_id=1, source_target_pairs={{0,28},{4,96},{8,4},{12,104},{16,12},{20,112},{24,20},{28,120},{32... | collective-permute-start | bytes 1671176 | tf_op jit(solution)/shard_map/ppermute | solution.py:45
  24.4 12.3 %collective-permute-start.4 = (bf16[4,17,32,128]{3,2,1,0:T(8,128)(2,1)S(1)}, bf16[4,17,32,128]{3,2,1,0:T(8,128)(2,1)S(1)}, u32[]{:S(2)}, u32[]{:S(2)}) collective-permute-start(bf16[4,17,32,128]{3,2,1,0:T(8,128)(2,1)S(1)} %pad_maximum_fusion), channel_id=1, source_target_pairs={{0,8},{4,36},{8,16},{12,44},{16,24},{20,52},{24,0},{28,60},{32,40}... | collective-permute-start | bytes 1671176 | tf_op jit(solution)/shard_map/ppermute | solution.py:44
  24.5 15.8 %collective-permute-start.5 = (bf16[4,17,32,128]{3,2,1,0:T(8,128)(2,1)S(1)}, bf16[4,17,32,128]{3,2,1,0:T(8,128)(2,1)}, u32[]{:S(2)}, u32[]{:S(2)}) collective-permute-start(bf16[4,17,32,128]{3,2,1,0:T(8,128)(2,1)S(1)} %pad_maximum_fusion), channel_id=1, source_target_pairs={{0,24},{4,100},{8,0},{12,108},{16,8},{20,116},{24,16},{28,124},{32... | collective-permute-start | bytes 1671176 | tf_op jit(solution)/shard_map/ppermute | solution.py:45
  30.7 11.4 %collective-permute-start.8 = (bf16[4,17,32,128]{3,2,1,0:T(8,128)(2,1)}, bf16[4,17,32,128]{3,2,1,0:T(8,128)(2,1)}, u32[]{:S(2)}, u32[]{:S(2)}) collective-permute-start(bf16[4,17,32,128]{3,2,1,0:T(8,128)(2,1)} %pad_maximum_fusion.1), channel_id=1, source_target_pairs={{0,4},{4,0},{1,5},{5,1},{2,6},{6,2},{3,7},{7,3},{8,12},{12,8},{9,1... | collective-permute-start | bytes 1671176 | tf_op jit(solution)/shard_map/ppermute | solution.py:23
  31.2 13.7 %collective-permute-start.11 = (bf16[2,17,32,128]{3,2,1,0:T(8,128)(2,1)S(1)}, bf16[2,17,32,128]{3,2,1,0:T(8,128)(2,1)S(1)}, u32[]{:S(2)}, u32[]{:S(2)}) collective-permute-start(bf16[2,17,32,128]{3,2,1,0:T(8,128)(2,1)S(1)} %slice.120), channel_id=1, source_target_pairs={{0,32},{4,12},{8,40},{12,20},{16,48},{20,28},{24,56},{28,4},{32,64... | collective-permute-start | bytes 835592 | tf_op jit(solution)/shard_map/ppermute | solution.py:46
  36.8 8.3 %collective-permute-start.12 = (bf16[2,17,32,128]{3,2,1,0:T(8,128)(2,1)}, bf16[2,17,32,128]{3,2,1,0:T(8,128)(2,1)}, u32[]{:S(2)}, u32[]{:S(2)}) collective-permute-start(bf16[2,17,32,128]{3,2,1,0:T(8,128)(2,1)} %slice.121), channel_id=1, source_target_pairs={{0,96},{4,28},{8,104},{12,4},{16,112},{20,12},{24,120},{28,20},{32... | collective-permute-start | bytes 835592 | tf_op jit(solution)/shard_map/ppermute | solution.py:47
  40.4 7.2 %collective-permute-start.6 = (bf16[2,17,32,128]{3,2,1,0:T(8,128)(2,1)}, bf16[2,17,32,128]{3,2,1,0:T(8,128)(2,1)}, u32[]{:S(2)}, u32[]{:S(2)}) collective-permute-start(bf16[2,17,32,128]{3,2,1,0:T(8,128)(2,1)} %slice.115), channel_id=1, source_target_pairs={{0,8},{4,36},{8,16},{12,44},{16,24},{20,52},{24,0},{28,60},{32,40}... | collective-permute-start | bytes 835592 | tf_op jit(solution)/shard_map/ppermute | solution.py:46
  42.1 6.5 %collective-permute-start.7 = (bf16[2,17,32,128]{3,2,1,0:T(8,128)(2,1)}, bf16[2,17,32,128]{3,2,1,0:T(8,128)(2,1)}, u32[]{:S(2)}, u32[]{:S(2)}) collective-permute-start(bf16[2,17,32,128]{3,2,1,0:T(8,128)(2,1)} %slice.116), channel_id=1, source_target_pairs={{0,24},{4,100},{8,0},{12,108},{16,8},{20,116},{24,16},{28,124},{32... | collective-permute-start | bytes 835592 | tf_op jit(solution)/shard_map/ppermute | solution.py:47
  44.9 14.1 %collective-permute-start.18 = (bf16[8,1,128,128]{3,2,1,0:T(8,128)(2,1)S(1)}, bf16[8,1,128,128]{3,2,1,0:T(8,128)(2,1)S(1)}, u32[]{:S(2)}, u32[]{:S(2)}) collective-permute-start(bf16[8,1,128,128]{3,2,1,0:T(8,128)(2,1)S(1)} %copy-done), channel_id=1, source_target_pairs={{0,4},{4,0},{1,5},{5,1},{2,6},{6,2},{3,7},{7,3},{8,12},{12,8},{9,1... | collective-permute-start | bytes 786440 | tf_op jit(solution)/shard_map/ppermute | solution.py:23
  63.7 13.9 %all-to-all-start = ((bf16[16,2,32,128]{3,2,1,0:T(8,128)(2,1)}), bf16[16,2,32,128]{3,2,1,0:T(8,128)(2,1)S(1)}, u32[]{:S(2)}, u32[]{:S(2)}) async-start(bf16[16,2,32,128]{3,2,1,0:T(8,128)(2,1)} %get-tuple-element.64), calls=%async_computation | async-start | bytes 524288 | tf_op jit(solution)/shard_map/all_to_all | solution.py:330
  85.8 11.6 %all-to-all-start.1 = ((bf16[16,2,32,128]{3,2,1,0:T(8,128)(2,1)}), bf16[16,2,32,128]{3,2,1,0:T(8,128)(2,1)S(1)}, u32[]{:S(2)}, u32[]{:S(2)}) async-start(bf16[16,2,32,128]{3,2,1,0:T(8,128)(2,1)} %get-tuple-element.71), calls=%async_computation.1 | async-start | bytes 524288 | tf_op jit(solution)/shard_map/all_to_all | solution.py:330
  99.1 4.9 %collective-permute-start.23 = (f32[2,32,128]{2,1,0:T(8,128)S(1)}, f32[2,32,128]{2,1,0:T(8,128)S(1)}, u32[]{:S(2)}, u32[]{:S(2)}) collective-permute-start(f32[2,32,128]{2,1,0:T(8,128)S(1)} %fresh_sum.7.p0), channel_id=1, source_target_pairs={{0,2},{1,3},{2,0},{3,1},{4,6},{5,7},{6,4},{7,5},{8,10},{9,11},{10,... | collective-permute-start | bytes 98312 | tf_op jit(solution)/shard_map/ppermute | solution.py:323
  107.2 12.6 %all-to-all-start.2 = ((bf16[16,2,32,128]{3,2,1,0:T(8,128)(2,1)}), bf16[16,2,32,128]{3,2,1,0:T(8,128)(2,1)S(1)}, u32[]{:S(2)}, u32[]{:S(2)}) async-start(bf16[16,2,32,128]{3,2,1,0:T(8,128)(2,1)} %get-tuple-element.78), calls=%async_computation.2 | async-start | bytes 524288 | tf_op jit(solution)/shard_map/all_to_all | solution.py:330
  126.9 12.6 %all-to-all-start.3 = ((bf16[16,2,32,128]{3,2,1,0:T(8,128)(2,1)}), bf16[16,2,32,128]{3,2,1,0:T(8,128)(2,1)S(1)}, u32[]{:S(2)}, u32[]{:S(2)}) async-start(bf16[16,2,32,128]{3,2,1,0:T(8,128)(2,1)} %get-tuple-element.85), calls=%async_computation.3 | async-start | bytes 524288 | tf_op jit(solution)/shard_map/all_to_all | solution.py:330
  140.7 5.4 %collective-permute-start.29 = (f32[2,32,128]{2,1,0:T(8,128)S(1)}, f32[2,32,128]{2,1,0:T(8,128)S(1)}, u32[]{:S(2)}, u32[]{:S(2)}) collective-permute-start(f32[2,32,128]{2,1,0:T(8,128)S(1)} %fresh_sum.9.p0), channel_id=1, source_target_pairs={{0,2},{1,3},{2,0},{3,1},{4,6},{5,7},{6,4},{7,5},{8,10},{9,11},{10,... | collective-permute-start | bytes 98312 | tf_op jit(solution)/shard_map/ppermute | solution.py:323
  149.4 12.1 %all-to-all-start.4 = ((bf16[16,2,32,128]{3,2,1,0:T(8,128)(2,1)}), bf16[16,2,32,128]{3,2,1,0:T(8,128)(2,1)S(1)}, u32[]{:S(2)}, u32[]{:S(2)}) async-start(bf16[16,2,32,128]{3,2,1,0:T(8,128)(2,1)} %get-tuple-element.92), calls=%async_computation.4 | async-start | bytes 524288 | tf_op jit(solution)/shard_map/all_to_all | solution.py:330
  168.6 12.0 %all-to-all-start.5 = ((bf16[16,2,32,128]{3,2,1,0:T(8,128)(2,1)}), bf16[16,2,32,128]{3,2,1,0:T(8,128)(2,1)S(1)}, u32[]{:S(2)}, u32[]{:S(2)}) async-start(bf16[16,2,32,128]{3,2,1,0:T(8,128)(2,1)} %get-tuple-element.99), calls=%async_computation.5 | async-start | bytes 524288 | tf_op jit(solution)/shard_map/all_to_all | solution.py:330
  182.3 5.1 %collective-permute-start.35 = (f32[2,32,128]{2,1,0:T(8,128)S(1)}, f32[2,32,128]{2,1,0:T(8,128)S(1)}, u32[]{:S(2)}, u32[]{:S(2)}) collective-permute-start(f32[2,32,128]{2,1,0:T(8,128)S(1)} %fresh_sum.11.p0), channel_id=1, source_target_pairs={{0,2},{1,3},{2,0},{3,1},{4,6},{5,7},{6,4},{7,5},{8,10},{9,11},{10,... | collective-permute-start | bytes 98312 | tf_op jit(solution)/shard_map/ppermute | solution.py:323
  189.9 17.3 %collective-permute-start.37 = (bf16[7,32,128]{2,1,0:T(8,128)(2,1)S(1)}, bf16[7,32,128]{2,1,0:T(8,128)(2,1)S(1)}, u32[]{:S(2)}, u32[]{:S(2)}) collective-permute-start(bf16[7,32,128]{2,1,0:T(8,128)(2,1)S(1)} %get-tuple-element.116), channel_id=1, source_target_pairs={{0,4},{4,0},{1,5},{5,1},{2,6},{6,2},{3,7},{7,3},{8,12},{12,8},{9,1... | collective-permute-start | bytes 172040 | tf_op jit(solution)/shard_map/ppermute | solution.py:23
  (22 other events, 134.4 us)

commit v15 on v14

--- a/solution.py
+++ b/solution.py
@@ -36,7 +36,7 @@
 
 def gather_parts(v):
     after_one, before_one = lambda i: (i + 1) % 4, lambda i: (i + 3) % 4
-    near = [v] + [lax.ppermute(v, ROWS, pairs(1, lambda i, k=k: i ^ k)) for k in (1, 2, 3)]
+    near = [v] + [lax.ppermute(v, ROWS, pairs(1, lambda i, k=k: i ^ k)) for k in (2, 3, 1)]
     mine, theirs = jnp.stack([one[0] for one in near]), jnp.stack([one[1] for one in near])
 
     def spread(part, cross):
@@ -304,7 +304,8 @@
     each = outer_each + 1
     away = jnp.where(src_core == 0, src_y - y, src_z - z) % 4
     part = jnp.where(away == 3, 1, jnp.where(away == 1, 2, jnp.where(away == 2, 3, 0))) * 4
-    part = part + jnp.where(src_core == 0, src_z ^ z, src_y ^ y) + jnp.where(src_core == core, 0, 16)
+    apart = jnp.where(src_core == 0, src_z ^ z, src_y ^ y)
+    part = part + jnp.where(apart == 0, 0, jnp.where(apart == 1, 3, apart - 1)) + jnp.where(src_core == core, 0, 16)
     known_place = part * each + member
     level_of = jnp.maximum(index - outer, 0) // 32
     this = jnp.arange(levels - 1)[:, None, None]

time: 209 us -> 205 us (0.981)
  waiting for transfers between devices: 54 us -> 48.6 us
    ppermute x3, waiting for transfers between devices: 9.82 us -> 6.8 us  [gather_parts(): lax.ppermute(v, ROWS, pairs(1, lambda i, k=k: i ^ k))]
  transfers between devices with their start and end apart: 44 -> 44, of which waited for: 29 -> 29; matrix products, arithmetic and copies ran while one was open for 2% -> 3% of each run, Pallas kernels for 19% -> 19%
where the time goes in v15:
time: 205 us; the launch traced here: 203 us
  starting transfers between devices  96.6 us (47%)
  Pallas kernels  49.9 us (24%)
  waiting for transfers between devices  48.6 us (24%)
  other arithmetic  3.48 us (2%)
  local copies, waits for them, and re-layouts  3.42 us (2%)
    pallas_call x7, Pallas kernels, sum_call(): pl.pallas_call(kernel, out_shape=[jax.ShapeDtypeStruct((2, rhs_cols, bloc...  38.6 us
    all_to_all x6, starting transfers between devices, on_device(): solved = lax.all_to_all(sent, ('z', 'y'), 0, 0).reshape(32, half, block)  29.4 us
    ppermute x21, starting transfers between devices, on_device(): lax.ppermute(value, 'x', xor_pairs(4, k))  27.5 us
    ppermute x6, starting transfers between devices, swap_cores(): return lax.ppermute(v, 'core', xor_pairs(2, 1))  21 us
    ppermute x21, waiting for transfers between devices, on_device(): lax.ppermute(value, 'x', xor_pairs(4, k))  20 us
    all_to_all x6, waiting for transfers between devices, on_device(): solved = lax.all_to_all(sent, ('z', 'y'), 0, 0).reshape(32, half, block)  12.4 us
    ppermute x3, waiting for transfers between devices, gather_parts(): lax.ppermute(v, ROWS, pairs(1, lambda i, k=k: i ^ k))  6.8 us
    ppermute x2, waiting for transfers between devices, spread(): before = lax.ppermute(part, ROWS, pairs(2, after_one, cross))  6.19 us
  transfers between devices with their start and end apart: 44, of which 29 were waited for; matrix products, arithmetic and copies ran while one was open for 3% of the time, Pallas kernels for 19%

profile of v15, /device:TPU:1, one launch (start us, length us, event | category | flops | bytes accessed | tf_op | source)
XLA Modules:
  0.0 203.4 jit_solution(1485676995605748861)
XLA Ops:
  3.5 3.0 %collective-permute-start.1 = (bf16[2,17,32,128]{3,2,1,0:T(8,128)(2,1)S(1)}, bf16[2,17,32,128]{3,2,1,0:T(8,128)(2,1)S(1)}, u32[]{:S(2)}, u32[]{:S(2)}) collective-permute-start(bf16[2,17,32,128]{3,2,1,0:T(8,128)(2,1)S(1)} %pad_maximum_fusion.2), channel_id=1, source_target_pairs={{0,64},{4,20},{8,72},{12,28},{16,80},{20,4},{24,88},{28,12},{32,96... | collective-permute-start | bytes 835592 | tf_op jit(solution)/shard_map/ppermute | solution.py:39
  7.3 3.4 %collective-permute-done.1 = bf16[2,17,32,128]{3,2,1,0:T(8,128)(2,1)S(1)} collective-permute-done((bf16[2,17,32,128]{3,2,1,0:T(8,128)(2,1)S(1)}, bf16[2,17,32,128]{3,2,1,0:T(8,128)(2,1)S(1)}, u32[]{:S(2)}, u32[]{:S(2)}) %collective-permute-start.1) | collective-permute-done | bytes 278560 | tf_op jit(solution)/shard_map/ppermute | solution.py:39
  10.8 3.0 %collective-permute-done.2 = bf16[2,17,32,128]{3,2,1,0:T(8,128)(2,1)S(1)} collective-permute-done((bf16[2,17,32,128]{3,2,1,0:T(8,128)(2,1)S(1)}, bf16[2,17,32,128]{3,2,1,0:T(8,128)(2,1)S(1)}, u32[]{:S(2)}, u32[]{:S(2)}) %collective-permute-start.2) | collective-permute-done | bytes 278560 | tf_op jit(solution)/shard_map/ppermute | solution.py:39
  23.9 3.2 %collective-permute-done.9 = bf16[4,17,32,128]{3,2,1,0:T(8,128)(2,1)S(1)} collective-permute-done((bf16[4,17,32,128]{3,2,1,0:T(8,128)(2,1)}, bf16[4,17,32,128]{3,2,1,0:T(8,128)(2,1)S(1)}, u32[]{:S(2)}, u32[]{:S(2)}) %collective-permute-start.9) | collective-permute-done | bytes 557088 | tf_op jit(solution)/shard_map/ppermute | solution.py:44
  30.0 3.0 %collective-permute-done.4 = bf16[4,17,32,128]{3,2,1,0:T(8,128)(2,1)S(1)} collective-permute-done((bf16[4,17,32,128]{3,2,1,0:T(8,128)(2,1)S(1)}, bf16[4,17,32,128]{3,2,1,0:T(8,128)(2,1)S(1)}, u32[]{:S(2)}, u32[]{:S(2)}) %collective-permute-start.4) | collective-permute-done | bytes 557088 | tf_op jit(solution)/shard_map/ppermute | solution.py:44
  33.0 3.1 %collective-permute-start.12 = (bf16[2,17,32,128]{3,2,1,0:T(8,128)(2,1)}, bf16[2,17,32,128]{3,2,1,0:T(8,128)(2,1)}, u32[]{:S(2)}, u32[]{:S(2)}) collective-permute-start(bf16[2,17,32,128]{3,2,1,0:T(8,128)(2,1)} %slice.121), channel_id=1, source_target_pairs={{0,96},{4,28},{8,104},{12,4},{16,112},{20,12},{24,120},{28,20},{32... | collective-permute-start | bytes 835592 | tf_op jit(solution)/shard_map/ppermute | solution.py:47
  45.0 5.8 %first_sum.1 = (f32[2,32,128]{2,1,0:T(8,128)S(1)}, bf16[2048,32,128]{2,1,0:T(8,128)(2,1)}) custom-call(s32[7,64]{1,0:T(8,128)S(1)} %get-tuple-element.130.code_ref, bf16[68,32,128]{2,1,0:T(8,128)(2,1)S(1)} %bitcast.55, bf16[68,32,128]{2,1,0:T(8,128)(2,1)S(1)} %bitcast.58, bf16[68,32,128]{2,1,0:T(8,128)(2,1)} %bitcast.7.refs_2_, ...), custom_call_target="tpu_custom_call" | custom-call | flops 67108864 | bytes 6291456 | tf_op jit(solution)/shard_map/first_sum/pallas_call | solution.py:150
  61.8 5.2 %all-to-all-start = ((bf16[16,2,32,128]{3,2,1,0:T(8,128)(2,1)}), bf16[16,2,32,128]{3,2,1,0:T(8,128)(2,1)S(1)}, u32[]{:S(2)}, u32[]{:S(2)}) async-start(bf16[16,2,32,128]{3,2,1,0:T(8,128)(2,1)} %get-tuple-element.64), calls=%async_computation | async-start | bytes 524288 | tf_op jit(solution)/shard_map/all_to_all | solution.py:331
  67.0 5.3 %old_sum.6 = (f32[2,32,128]{2,1,0:T(8,128)S(1)}, s32[65]{0:T(128)S(1)}, bf16[16,128,128]{2,1,0:T(8,128)(2,1)S(1)}) custom-call(s32[7,64]{1,0:T(8,128)S(1)} %get-tuple-element.130.code_ref, s32[7,64]{1,0:T(8,128)S(1)} %get-tuple-element.96.fresh_ref, bf16[2048,32,128]{2,1,0:T(8,128)(2,1)} %get-tuple-element.61.store_ref, ...), custom_call_target="tpu_custom_call" | custom-call | flops 67108864 | bytes 6291456 | tf_op jit(solution)/shard_map/old_sum/pallas_call | solution.py:150
  82.4 5.2 %all-to-all-start.1 = ((bf16[16,2,32,128]{3,2,1,0:T(8,128)(2,1)}), bf16[16,2,32,128]{3,2,1,0:T(8,128)(2,1)S(1)}, u32[]{:S(2)}, u32[]{:S(2)}) async-start(bf16[16,2,32,128]{3,2,1,0:T(8,128)(2,1)} %get-tuple-element.71), calls=%async_computation.1 | async-start | bytes 524288 | tf_op jit(solution)/shard_map/all_to_all | solution.py:331
  87.5 5.4 %old_sum.7 = (f32[2,32,128]{2,1,0:T(8,128)S(1)}, s32[65]{0:T(128)S(1)}, bf16[16,128,128]{2,1,0:T(8,128)(2,1)S(1)}) custom-call(s32[7,64]{1,0:T(8,128)S(1)} %get-tuple-element.130.code_ref, s32[7,64]{1,0:T(8,128)S(1)} %get-tuple-element.96.fresh_ref, bf16[2048,32,128]{2,1,0:T(8,128)(2,1)} %get-tuple-element.61.store_ref, bf16[32,32,128]{2,1,0:T(8,128)(2,1)S(1)} %bitcast.36, ...), custom_call_target="tpu_custom_call" | custom-call | flops 67108864 | bytes 6291456 | tf_op jit(solution)/shard_map/old_sum/pallas_call | solution.py:150
  96.0 3.5 %collective-permute-start.23 = (f32[2,32,128]{2,1,0:T(8,128)S(1)}, f32[2,32,128]{2,1,0:T(8,128)S(1)}, u32[]{:S(2)}, u32[]{:S(2)}) collective-permute-start(f32[2,32,128]{2,1,0:T(8,128)S(1)} %fresh_sum.7.p0), channel_id=1, source_target_pairs={{0,2},{1,3},{2,0},{3,1},{4,6},{5,7},{6,4},{7,5},{8,10},{9,11},{10,... | collective-permute-start | bytes 98312 | tf_op jit(solution)/shard_map/ppermute | solution.py:324
  104.4 5.3 %all-to-all-start.2 = ((bf16[16,2,32,128]{3,2,1,0:T(8,128)(2,1)}), bf16[16,2,32,128]{3,2,1,0:T(8,128)(2,1)S(1)}, u32[]{:S(2)}, u32[]{:S(2)}) async-start(bf16[16,2,32,128]{3,2,1,0:T(8,128)(2,1)} %get-tuple-element.78), calls=%async_computation.2 | async-start | bytes 524288 | tf_op jit(solution)/shard_map/all_to_all | solution.py:331
  109.8 5.4 %old_sum.8 = (f32[2,32,128]{2,1,0:T(8,128)S(1)}, s32[65]{0:T(128)S(1)}, bf16[16,128,128]{2,1,0:T(8,128)(2,1)S(1)}) custom-call(s32[7,64]{1,0:T(8,128)S(1)} %get-tuple-element.130.code_ref, s32[7,64]{1,0:T(8,128)S(1)} %get-tuple-element.96.fresh_ref, bf16[2048,32,128]{2,1,0:T(8,128)(2,1)} %get-tuple-element.61.store_ref, bf16[32,32,128]{2,1,0:T(8,128)(2,1)S(1)} %bitcast.37, ...), custom_call_target="tpu_custom_call" | custom-call | flops 67108864 | bytes 6291456 | tf_op jit(solution)/shard_map/old_sum/pallas_call | solution.py:150
  119.2 2.8 %collective-permute-start.27 = (f32[2,32,128]{2,1,0:T(8,128)S(1)}, f32[2,32,128]{2,1,0:T(8,128)S(1)}, u32[]{:S(2)}, u32[]{:S(2)}) collective-permute-start(f32[2,32,128]{2,1,0:T(8,128)S(1)} %fresh_sum.8.p0), channel_id=1, source_target_pairs={{0,3},{1,2},{2,1},{3,0},{4,7},{5,6},{6,5},{7,4},{8,11},{9,10},{10,... | collective-permute-start | bytes 98312 | tf_op jit(solution)/shard_map/ppermute | solution.py:324
  124.5 4.5 %all-to-all-start.3 = ((bf16[16,2,32,128]{3,2,1,0:T(8,128)(2,1)}), bf16[16,2,32,128]{3,2,1,0:T(8,128)(2,1)S(1)}, u32[]{:S(2)}, u32[]{:S(2)}) async-start(bf16[16,2,32,128]{3,2,1,0:T(8,128)(2,1)} %get-tuple-element.85), calls=%async_computation.3 | async-start | bytes 524288 | tf_op jit(solution)/shard_map/all_to_all | solution.py:331
  129.0 5.5 %old_sum.9 = (f32[2,32,128]{2,1,0:T(8,128)S(1)}, s32[65]{0:T(128)S(1)}, bf16[16,128,128]{2,1,0:T(8,128)(2,1)S(1)}) custom-call(s32[7,64]{1,0:T(8,128)S(1)} %get-tuple-element.130.code_ref, s32[7,64]{1,0:T(8,128)S(1)} %get-tuple-element.96.fresh_ref, bf16[2048,32,128]{2,1,0:T(8,128)(2,1)} %get-tuple-element.61.store_ref, bf16[32,32,128]{2,1,0:T(8,128)(2,1)S(1)} %bitcast.38, ...), custom_call_target="tpu_custom_call" | custom-call | flops 67108864 | bytes 6291456 | tf_op jit(solution)/shard_map/old_sum/pallas_call | solution.py:150
  137.8 3.5 %collective-permute-start.29 = (f32[2,32,128]{2,1,0:T(8,128)S(1)}, f32[2,32,128]{2,1,0:T(8,128)S(1)}, u32[]{:S(2)}, u32[]{:S(2)}) collective-permute-start(f32[2,32,128]{2,1,0:T(8,128)S(1)} %fresh_sum.9.p0), channel_id=1, source_target_pairs={{0,2},{1,3},{2,0},{3,1},{4,6},{5,7},{6,4},{7,5},{8,10},{9,11},{10,... | collective-permute-start | bytes 98312 | tf_op jit(solution)/shard_map/ppermute | solution.py:324
  146.3 4.9 %all-to-all-start.4 = ((bf16[16,2,32,128]{3,2,1,0:T(8,128)(2,1)}), bf16[16,2,32,128]{3,2,1,0:T(8,128)(2,1)S(1)}, u32[]{:S(2)}, u32[]{:S(2)}) async-start(bf16[16,2,32,128]{3,2,1,0:T(8,128)(2,1)} %get-tuple-element.92), calls=%async_computation.4 | async-start | bytes 524288 | tf_op jit(solution)/shard_map/all_to_all | solution.py:331
  151.2 5.3 %old_sum.10 = (f32[2,32,128]{2,1,0:T(8,128)S(1)}, s32[65]{0:T(128)S(1)}, bf16[16,128,128]{2,1,0:T(8,128)(2,1)S(1)}) custom-call(s32[7,64]{1,0:T(8,128)S(1)} %get-tuple-element.130.code_ref, s32[7,64]{1,0:T(8,128)S(1)} %get-tuple-element.96.fresh_ref, bf16[2048,32,128]{2,1,0:T(8,128)(2,1)} %get-tuple-element.61.store_ref, bf16[32,32,128]{2,1,0:T(8,128)(2,1)S(1)} %bitcast.39, ...), custom_call_target="tpu_custom_call" | custom-call | flops 67108864 | bytes 6291456 | tf_op jit(solution)/shard_map/old_sum/pallas_call | solution.py:150
  166.6 4.3 %all-to-all-start.5 = ((bf16[16,2,32,128]{3,2,1,0:T(8,128)(2,1)}), bf16[16,2,32,128]{3,2,1,0:T(8,128)(2,1)S(1)}, u32[]{:S(2)}, u32[]{:S(2)}) async-start(bf16[16,2,32,128]{3,2,1,0:T(8,128)(2,1)} %get-tuple-element.99), calls=%async_computation.5 | async-start | bytes 524288 | tf_op jit(solution)/shard_map/all_to_all | solution.py:331
  171.0 5.9 %old_sum.11 = (f32[2,32,128]{2,1,0:T(8,128)S(1)}, s32[65]{0:T(128)S(1)}, bf16[16,128,128]{2,1,0:T(8,128)(2,1)S(1)}) custom-call(s32[7,64]{1,0:T(8,128)S(1)} %get-tuple-element.130.code_ref, s32[7,64]{1,0:T(8,128)S(1)} %get-tuple-element.96.fresh_ref, bf16[2048,32,128]{2,1,0:T(8,128)(2,1)} %get-tuple-element.61.store_ref, bf16[32,32,128]{2,1,0:T(8,128)(2,1)S(1)} %bitcast.40, ...), custom_call_target="tpu_custom_call" | custom-call | flops 67108864 | bytes 6291456 | tf_op jit(solution)/shard_map/old_sum/pallas_call | solution.py:150
  179.9 3.0 %collective-permute-start.35 = (f32[2,32,128]{2,1,0:T(8,128)S(1)}, f32[2,32,128]{2,1,0:T(8,128)S(1)}, u32[]{:S(2)}, u32[]{:S(2)}) collective-permute-start(f32[2,32,128]{2,1,0:T(8,128)S(1)} %fresh_sum.11.p0), channel_id=1, source_target_pairs={{0,2},{1,3},{2,0},{3,1},{4,6},{5,7},{6,4},{7,5},{8,10},{9,11},{10,... | collective-permute-start | bytes 98312 | tf_op jit(solution)/shard_map/ppermute | solution.py:324
  187.0 14.9 %collective-permute-start.37 = (bf16[7,32,128]{2,1,0:T(8,128)(2,1)S(1)}, bf16[7,32,128]{2,1,0:T(8,128)(2,1)S(1)}, u32[]{:S(2)}, u32[]{:S(2)}) collective-permute-start(bf16[7,32,128]{2,1,0:T(8,128)(2,1)S(1)} %get-tuple-element.116), channel_id=1, source_target_pairs={{0,4},{4,0},{1,5},{5,1},{2,6},{6,2},{3,7},{7,3},{8,12},{12,8},{9,1... | collective-permute-start | bytes 172040 | tf_op jit(solution)/shard_map/ppermute | solution.py:23
  (118 shorter events, 88.6 us)
Async XLA Ops:
  2.0 43.0 %collective-permute-start.13 = (bf16[7,1,32,128,128]{4,3,2,1,0:T(8,128)(2,1)}, bf16[7,1,32,128,128]{4,3,2,1,0:T(8,128)(2,1)}, u32[]{:S(2)}, u32[]{:S(2)}) collective-permute-start(bf16[7,1,32,128,128]{4,3,2,1,0:T(8,128)(2,1)} %own_ref.11), channel_id=1, source_target_pairs={{0,4},{4,0},{1,5},{5,1},{2,6},{6,2},{3,7},{7,3},{8,12},{12,8},{9,1... | collective-permute-start | bytes 22020104 | tf_op jit(solution)/shard_map/ppermute | solution.py:23
  3.5 7.2 %collective-permute-start.1 = (bf16[2,17,32,128]{3,2,1,0:T(8,128)(2,1)S(1)}, bf16[2,17,32,128]{3,2,1,0:T(8,128)(2,1)S(1)}, u32[]{:S(2)}, u32[]{:S(2)}) collective-permute-start(bf16[2,17,32,128]{3,2,1,0:T(8,128)(2,1)S(1)} %pad_maximum_fusion.2), channel_id=1, source_target_pairs={{0,64},{4,20},{8,72},{12,28},{16,80},{20,4},{24,88},{28,12},{32,96... | collective-permute-start | bytes 835592 | tf_op jit(solution)/shard_map/ppermute | solution.py:39
  6.5 7.2 %collective-permute-start.2 = (bf16[2,17,32,128]{3,2,1,0:T(8,128)(2,1)S(1)}, bf16[2,17,32,128]{3,2,1,0:T(8,128)(2,1)S(1)}, u32[]{:S(2)}, u32[]{:S(2)}) collective-permute-start(bf16[2,17,32,128]{3,2,1,0:T(8,128)(2,1)S(1)} %pad_maximum_fusion.2), channel_id=1, source_target_pairs={{0,96},{4,28},{8,104},{12,20},{16,112},{20,12},{24,120},{28,4},{32... | collective-permute-start | bytes 835592 | tf_op jit(solution)/shard_map/ppermute | solution.py:39
  7.3 6.9 %collective-permute-start.3 = (bf16[2,17,32,128]{3,2,1,0:T(8,128)(2,1)S(1)}, bf16[2,17,32,128]{3,2,1,0:T(8,128)(2,1)S(1)}, u32[]{:S(2)}, u32[]{:S(2)}) collective-permute-start(bf16[2,17,32,128]{3,2,1,0:T(8,128)(2,1)S(1)} %pad_maximum_fusion.2), channel_id=1, source_target_pairs={{0,32},{4,12},{8,40},{12,4},{16,48},{20,28},{24,56},{28,20},{32,0}... | collective-permute-start | bytes 835592 | tf_op jit(solution)/shard_map/ppermute | solution.py:39
  15.1 12.0 %collective-permute-start.9 = (bf16[4,17,32,128]{3,2,1,0:T(8,128)(2,1)}, bf16[4,17,32,128]{3,2,1,0:T(8,128)(2,1)S(1)}, u32[]{:S(2)}, u32[]{:S(2)}) collective-permute-start(bf16[4,17,32,128]{3,2,1,0:T(8,128)(2,1)} %pad_maximum_fusion.1), channel_id=1, source_target_pairs={{0,12},{4,32},{8,20},{12,40},{16,28},{20,48},{24,4},{28,56},{32,44... | collective-permute-start | bytes 1671176 | tf_op jit(solution)/shard_map/ppermute | solution.py:44
  18.5 9.5 %collective-permute-start.10 = (bf16[4,17,32,128]{3,2,1,0:T(8,128)(2,1)}, bf16[4,17,32,128]{3,2,1,0:T(8,128)(2,1)S(1)}, u32[]{:S(2)}, u32[]{:S(2)}) collective-permute-start(bf16[4,17,32,128]{3,2,1,0:T(8,128)(2,1)} %pad_maximum_fusion.1), channel_id=1, source_target_pairs={{0,28},{4,96},{8,4},{12,104},{16,12},{20,112},{24,20},{28,120},{32... | collective-permute-start | bytes 1671176 | tf_op jit(solution)/shard_map/ppermute | solution.py:45
  21.1 11.9 %collective-permute-start.4 = (bf16[4,17,32,128]{3,2,1,0:T(8,128)(2,1)S(1)}, bf16[4,17,32,128]{3,2,1,0:T(8,128)(2,1)S(1)}, u32[]{:S(2)}, u32[]{:S(2)}) collective-permute-start(bf16[4,17,32,128]{3,2,1,0:T(8,128)(2,1)S(1)} %pad_maximum_fusion), channel_id=1, source_target_pairs={{0,8},{4,36},{8,16},{12,44},{16,24},{20,52},{24,0},{28,60},{32,40}... | collective-permute-start | bytes 1671176 | tf_op jit(solution)/shard_map/ppermute | solution.py:44
  21.2 15.6 %collective-permute-start.5 = (bf16[4,17,32,128]{3,2,1,0:T(8,128)(2,1)S(1)}, bf16[4,17,32,128]{3,2,1,0:T(8,128)(2,1)}, u32[]{:S(2)}, u32[]{:S(2)}) collective-permute-start(bf16[4,17,32,128]{3,2,1,0:T(8,128)(2,1)S(1)} %pad_maximum_fusion), channel_id=1, source_target_pairs={{0,24},{4,100},{8,0},{12,108},{16,8},{20,116},{24,16},{28,124},{32... | collective-permute-start | bytes 1671176 | tf_op jit(solution)/shard_map/ppermute | solution.py:45
  27.1 11.4 %collective-permute-start.8 = (bf16[4,17,32,128]{3,2,1,0:T(8,128)(2,1)}, bf16[4,17,32,128]{3,2,1,0:T(8,128)(2,1)}, u32[]{:S(2)}, u32[]{:S(2)}) collective-permute-start(bf16[4,17,32,128]{3,2,1,0:T(8,128)(2,1)} %pad_maximum_fusion.1), channel_id=1, source_target_pairs={{0,4},{4,0},{1,5},{5,1},{2,6},{6,2},{3,7},{7,3},{8,12},{12,8},{9,1... | collective-permute-start | bytes 1671176 | tf_op jit(solution)/shard_map/ppermute | solution.py:23
  28.0 13.3 %collective-permute-start.11 = (bf16[2,17,32,128]{3,2,1,0:T(8,128)(2,1)S(1)}, bf16[2,17,32,128]{3,2,1,0:T(8,128)(2,1)S(1)}, u32[]{:S(2)}, u32[]{:S(2)}) collective-permute-start(bf16[2,17,32,128]{3,2,1,0:T(8,128)(2,1)S(1)} %slice.120), channel_id=1, source_target_pairs={{0,32},{4,12},{8,40},{12,20},{16,48},{20,28},{24,56},{28,4},{32,64... | collective-permute-start | bytes 835592 | tf_op jit(solution)/shard_map/ppermute | solution.py:46
  33.0 10.1 %collective-permute-start.12 = (bf16[2,17,32,128]{3,2,1,0:T(8,128)(2,1)}, bf16[2,17,32,128]{3,2,1,0:T(8,128)(2,1)}, u32[]{:S(2)}, u32[]{:S(2)}) collective-permute-start(bf16[2,17,32,128]{3,2,1,0:T(8,128)(2,1)} %slice.121), channel_id=1, source_target_pairs={{0,96},{4,28},{8,104},{12,4},{16,112},{20,12},{24,120},{28,20},{32... | collective-permute-start | bytes 835592 | tf_op jit(solution)/shard_map/ppermute | solution.py:47
  36.8 7.2 %collective-permute-start.6 = (bf16[2,17,32,128]{3,2,1,0:T(8,128)(2,1)}, bf16[2,17,32,128]{3,2,1,0:T(8,128)(2,1)}, u32[]{:S(2)}, u32[]{:S(2)}) collective-permute-start(bf16[2,17,32,128]{3,2,1,0:T(8,128)(2,1)} %slice.115), channel_id=1, source_target_pairs={{0,8},{4,36},{8,16},{12,44},{16,24},{20,52},{24,0},{28,60},{32,40}... | collective-permute-start | bytes 835592 | tf_op jit(solution)/shard_map/ppermute | solution.py:46
  38.5 6.5 %collective-permute-start.7 = (bf16[2,17,32,128]{3,2,1,0:T(8,128)(2,1)}, bf16[2,17,32,128]{3,2,1,0:T(8,128)(2,1)}, u32[]{:S(2)}, u32[]{:S(2)}) collective-permute-start(bf16[2,17,32,128]{3,2,1,0:T(8,128)(2,1)} %slice.116), channel_id=1, source_target_pairs={{0,24},{4,100},{8,0},{12,108},{16,8},{20,116},{24,16},{28,124},{32... | collective-permute-start | bytes 835592 | tf_op jit(solution)/shard_map/ppermute | solution.py:47
  41.4 15.8 %collective-permute-start.18 = (bf16[8,1,128,128]{3,2,1,0:T(8,128)(2,1)S(1)}, bf16[8,1,128,128]{3,2,1,0:T(8,128)(2,1)S(1)}, u32[]{:S(2)}, u32[]{:S(2)}) collective-permute-start(bf16[8,1,128,128]{3,2,1,0:T(8,128)(2,1)S(1)} %copy-done), channel_id=1, source_target_pairs={{0,4},{4,0},{1,5},{5,1},{2,6},{6,2},{3,7},{7,3},{8,12},{12,8},{9,1... | collective-permute-start | bytes 786440 | tf_op jit(solution)/shard_map/ppermute | solution.py:23
  50.9 6.3 %collective-permute-start.17 = (bf16[8,1,32,128]{3,2,1,0:T(8,128)(2,1)S(1)}, bf16[8,1,32,128]{3,2,1,0:T(8,128)(2,1)S(1)}, u32[]{:S(2)}, u32[]{:S(2)}) collective-permute-start(bf16[8,1,32,128]{3,2,1,0:T(8,128)(2,1)S(1)} %get-tuple-element.112), channel_id=1, source_target_pairs={{0,4},{4,0},{1,5},{5,1},{2,6},{6,2},{3,7},{7,3},{8,12},{12,8},{9,1... | collective-permute-start | bytes 196616 | tf_op jit(solution)/shard_map/ppermute | solution.py:23
  61.8 12.8 %all-to-all-start = ((bf16[16,2,32,128]{3,2,1,0:T(8,128)(2,1)}), bf16[16,2,32,128]{3,2,1,0:T(8,128)(2,1)S(1)}, u32[]{:S(2)}, u32[]{:S(2)}) async-start(bf16[16,2,32,128]{3,2,1,0:T(8,128)(2,1)} %get-tuple-element.64), calls=%async_computation | async-start | bytes 524288 | tf_op jit(solution)/shard_map/all_to_all | solution.py:331
  82.4 12.7 %all-to-all-start.1 = ((bf16[16,2,32,128]{3,2,1,0:T(8,128)(2,1)}), bf16[16,2,32,128]{3,2,1,0:T(8,128)(2,1)S(1)}, u32[]{:S(2)}, u32[]{:S(2)}) async-start(bf16[16,2,32,128]{3,2,1,0:T(8,128)(2,1)} %get-tuple-element.71), calls=%async_computation.1 | async-start | bytes 524288 | tf_op jit(solution)/shard_map/all_to_all | solution.py:331
  96.0 5.2 %collective-permute-start.23 = (f32[2,32,128]{2,1,0:T(8,128)S(1)}, f32[2,32,128]{2,1,0:T(8,128)S(1)}, u32[]{:S(2)}, u32[]{:S(2)}) collective-permute-start(f32[2,32,128]{2,1,0:T(8,128)S(1)} %fresh_sum.7.p0), channel_id=1, source_target_pairs={{0,2},{1,3},{2,0},{3,1},{4,6},{5,7},{6,4},{7,5},{8,10},{9,11},{10,... | collective-permute-start | bytes 98312 | tf_op jit(solution)/shard_map/ppermute | solution.py:324
  104.4 12.9 %all-to-all-start.2 = ((bf16[16,2,32,128]{3,2,1,0:T(8,128)(2,1)}), bf16[16,2,32,128]{3,2,1,0:T(8,128)(2,1)S(1)}, u32[]{:S(2)}, u32[]{:S(2)}) async-start(bf16[16,2,32,128]{3,2,1,0:T(8,128)(2,1)} %get-tuple-element.78), calls=%async_computation.2 | async-start | bytes 524288 | tf_op jit(solution)/shard_map/all_to_all | solution.py:331
  124.5 12.1 %all-to-all-start.3 = ((bf16[16,2,32,128]{3,2,1,0:T(8,128)(2,1)}), bf16[16,2,32,128]{3,2,1,0:T(8,128)(2,1)S(1)}, u32[]{:S(2)}, u32[]{:S(2)}) async-start(bf16[16,2,32,128]{3,2,1,0:T(8,128)(2,1)} %get-tuple-element.85), calls=%async_computation.3 | async-start | bytes 524288 | tf_op jit(solution)/shard_map/all_to_all | solution.py:331
  137.8 5.5 %collective-permute-start.29 = (f32[2,32,128]{2,1,0:T(8,128)S(1)}, f32[2,32,128]{2,1,0:T(8,128)S(1)}, u32[]{:S(2)}, u32[]{:S(2)}) collective-permute-start(f32[2,32,128]{2,1,0:T(8,128)S(1)} %fresh_sum.9.p0), channel_id=1, source_target_pairs={{0,2},{1,3},{2,0},{3,1},{4,6},{5,7},{6,4},{7,5},{8,10},{9,11},{10,... | collective-permute-start | bytes 98312 | tf_op jit(solution)/shard_map/ppermute | solution.py:324
  146.3 12.4 %all-to-all-start.4 = ((bf16[16,2,32,128]{3,2,1,0:T(8,128)(2,1)}), bf16[16,2,32,128]{3,2,1,0:T(8,128)(2,1)S(1)}, u32[]{:S(2)}, u32[]{:S(2)}) async-start(bf16[16,2,32,128]{3,2,1,0:T(8,128)(2,1)} %get-tuple-element.92), calls=%async_computation.4 | async-start | bytes 524288 | tf_op jit(solution)/shard_map/all_to_all | solution.py:331
  166.6 11.9 %all-to-all-start.5 = ((bf16[16,2,32,128]{3,2,1,0:T(8,128)(2,1)}), bf16[16,2,32,128]{3,2,1,0:T(8,128)(2,1)S(1)}, u32[]{:S(2)}, u32[]{:S(2)}) async-start(bf16[16,2,32,128]{3,2,1,0:T(8,128)(2,1)} %get-tuple-element.99), calls=%async_computation.5 | async-start | bytes 524288 | tf_op jit(solution)/shard_map/all_to_all | solution.py:331
  187.0 15.8 %collective-permute-start.37 = (bf16[7,32,128]{2,1,0:T(8,128)(2,1)S(1)}, bf16[7,32,128]{2,1,0:T(8,128)(2,1)S(1)}, u32[]{:S(2)}, u32[]{:S(2)}) collective-permute-start(bf16[7,32,128]{2,1,0:T(8,128)(2,1)S(1)} %get-tuple-element.116), channel_id=1, source_target_pairs={{0,4},{4,0},{1,5},{5,1},{2,6},{6,2},{3,7},{7,3},{8,12},{12,8},{9,1... | collective-permute-start | bytes 172040 | tf_op jit(solution)/shard_map/ppermute | solution.py:23
  (22 other events, 128.8 us)

commit v16 on v15

--- a/solution.py
+++ b/solution.py
@@ -169,7 +169,7 @@
     store = jax.ShapeDtypeStruct((2048,) + sources[0].shape[1:], jnp.bfloat16)
     extra = [pltpu.SemaphoreType.DMA((len(sources),))]
     spaces = [pltpu.VMEM] * len(sources)
-    return sum_call(first_kernel, [code], sources, spaces, own, other, [store], [pltpu.HBM], extra, "first_sum", VMEM_LIMIT)
+    return sum_call(first_kernel, [code], sources, spaces, own, other, [store], [pltpu.HBM], extra, "first_sum", 54 * 1024 * 1024)
 
 
 def old_sum(level, known, code, fresh, store, solved, own, other):

time: 205 us -> 208 us (1.015)
  waiting for transfers between devices: 48.6 us -> 44 us
  Pallas kernels: 49.9 us -> 54.4 us
  starting transfers between devices: 96.6 us -> 98.8 us
    pallas_call x7, Pallas kernels: 38.6 us -> 42.1 us  [sum_call(): pl.pallas_call(kernel, out_shape=[jax.ShapeDtypeStruct((2, rhs_cols, bloc...]
    all_to_all x6, waiting for transfers between devices: 12.4 us -> 10.2 us  [on_device(): solved = lax.all_to_all(sent, ('z', 'y'), 0, 0).reshape(32, half, block)]
  transfers between devices with their start and end apart: 44 -> 44, of which waited for: 29 -> 28; matrix products, arithmetic and copies ran while one was open for 3% -> 3% of each run, Pallas kernels for 19% -> 20%
where the time goes in v16:
time: 208 us; the launch traced here: 207 us
  starting transfers between devices  98.8 us (48%)
  Pallas kernels  54.4 us (26%)
  waiting for transfers between devices  44 us (21%)
  other arithmetic  4.04 us (2%)
  local copies, waits for them, and re-layouts  4.01 us (2%)
    pallas_call x7, Pallas kernels, sum_call(): pl.pallas_call(kernel, out_shape=[jax.ShapeDtypeStruct((2, rhs_cols, bloc...  42.1 us
    all_to_all x6, starting transfers between devices, on_device(): solved = lax.all_to_all(sent, ('z', 'y'), 0, 0).reshape(32, half, block)  31 us
    ppermute x21, starting transfers between devices, on_device(): lax.ppermute(value, 'x', xor_pairs(4, k))  27.5 us
    ppermute x6, starting transfers between devices, swap_cores(): return lax.ppermute(v, 'core', xor_pairs(2, 1))  22 us
    ppermute x21, waiting for transfers between devices, on_device(): lax.ppermute(value, 'x', xor_pairs(4, k))  18.6 us
    all_to_all x6, waiting for transfers between devices, on_device(): solved = lax.all_to_all(sent, ('z', 'y'), 0, 0).reshape(32, half, block)  10.2 us
    ppermute x3, waiting for transfers between devices, gather_parts(): lax.ppermute(v, ROWS, pairs(1, lambda i, k=k: i ^ k))  6.8 us
    pallas_call x6, Pallas kernels, fresh_sum(): pl.pallas_call(functools.partial(fresh_kernel, level), out_shape=jax.Shap...  6.8 us
  transfers between devices with their start and end apart: 44, of which 28 were waited for; matrix products, arithmetic and copies ran while one was open for 3% of the time, Pallas kernels for 20%

profile of v16, /device:TPU:1, one launch (start us, length us, event | category | flops | bytes accessed | tf_op | source)
XLA Modules:
  0.0 206.7 jit_solution(7164204063073346137)
XLA Ops:
  3.5 3.0 %collective-permute-start.1 = (bf16[2,17,32,128]{3,2,1,0:T(8,128)(2,1)S(1)}, bf16[2,17,32,128]{3,2,1,0:T(8,128)(2,1)S(1)}, u32[]{:S(2)}, u32[]{:S(2)}) collective-permute-start(bf16[2,17,32,128]{3,2,1,0:T(8,128)(2,1)S(1)} %pad_maximum_fusion.2), channel_id=1, source_target_pairs={{0,64},{4,20},{8,72},{12,28},{16,80},{20,4},{24,88},{28,12},{32,96... | collective-permute-start | bytes 835592 | tf_op jit(solution)/shard_map/ppermute | solution.py:39
  7.3 3.4 %collective-permute-done.1 = bf16[2,17,32,128]{3,2,1,0:T(8,128)(2,1)S(1)} collective-permute-done((bf16[2,17,32,128]{3,2,1,0:T(8,128)(2,1)S(1)}, bf16[2,17,32,128]{3,2,1,0:T(8,128)(2,1)S(1)}, u32[]{:S(2)}, u32[]{:S(2)}) %collective-permute-start.1) | collective-permute-done | bytes 278560 | tf_op jit(solution)/shard_map/ppermute | solution.py:39
  10.8 3.0 %collective-permute-done.2 = bf16[2,17,32,128]{3,2,1,0:T(8,128)(2,1)S(1)} collective-permute-done((bf16[2,17,32,128]{3,2,1,0:T(8,128)(2,1)S(1)}, bf16[2,17,32,128]{3,2,1,0:T(8,128)(2,1)S(1)}, u32[]{:S(2)}, u32[]{:S(2)}) %collective-permute-start.2) | collective-permute-done | bytes 278560 | tf_op jit(solution)/shard_map/ppermute | solution.py:39
  21.2 2.7 %collective-permute-start.5 = (bf16[4,17,32,128]{3,2,1,0:T(8,128)(2,1)S(1)}, bf16[4,17,32,128]{3,2,1,0:T(8,128)(2,1)S(1)}, u32[]{:S(2)}, u32[]{:S(2)}) collective-permute-start(bf16[4,17,32,128]{3,2,1,0:T(8,128)(2,1)S(1)} %pad_maximum_fusion), channel_id=1, source_target_pairs={{0,24},{4,100},{8,0},{12,108},{16,8},{20,116},{24,16},{28,124},{32... | collective-permute-start | bytes 1671176 | tf_op jit(solution)/shard_map/ppermute | solution.py:45
  23.9 3.2 %collective-permute-done.9 = bf16[4,17,32,128]{3,2,1,0:T(8,128)(2,1)S(1)} collective-permute-done((bf16[4,17,32,128]{3,2,1,0:T(8,128)(2,1)}, bf16[4,17,32,128]{3,2,1,0:T(8,128)(2,1)S(1)}, u32[]{:S(2)}, u32[]{:S(2)}) %collective-permute-start.9) | collective-permute-done | bytes 557088 | tf_op jit(solution)/shard_map/ppermute | solution.py:44
  30.2 2.8 %collective-permute-done.4 = bf16[4,17,32,128]{3,2,1,0:T(8,128)(2,1)S(1)} collective-permute-done((bf16[4,17,32,128]{3,2,1,0:T(8,128)(2,1)S(1)}, bf16[4,17,32,128]{3,2,1,0:T(8,128)(2,1)S(1)}, u32[]{:S(2)}, u32[]{:S(2)}) %collective-permute-start.4) | collective-permute-done | bytes 557088 | tf_op jit(solution)/shard_map/ppermute | solution.py:44
  33.0 2.7 %collective-permute-start.12 = (bf16[2,17,32,128]{3,2,1,0:T(8,128)(2,1)}, bf16[2,17,32,128]{3,2,1,0:T(8,128)(2,1)}, u32[]{:S(2)}, u32[]{:S(2)}) collective-permute-start(bf16[2,17,32,128]{3,2,1,0:T(8,128)(2,1)} %slice.121), channel_id=1, source_target_pairs={{0,96},{4,28},{8,104},{12,4},{16,112},{20,12},{24,120},{28,20},{32... | collective-permute-start | bytes 835592 | tf_op jit(solution)/shard_map/ppermute | solution.py:47
  44.0 7.2 %first_sum.1 = (f32[2,32,128]{2,1,0:T(8,128)}, bf16[2048,32,128]{2,1,0:T(8,128)(2,1)}) custom-call(s32[7,64]{1,0:T(8,128)} %get-tuple-element.130.code_ref, bf16[68,32,128]{2,1,0:T(8,128)(2,1)} %bitcast.56, bf16[68,32,128]{2,1,0:T(8,128)(2,1)} %bitcast.59, bf16[68,32,128]{2,1,0:T(8,128)(2,1)} %bitcast.60, bf16[34,32,128]{2,1,0:T(8,128)(2,1)} %bitcast.8.refs_3_, ...), custom_call_target="tpu_custom_call" | custom-call | flops 67108864 | bytes 6291456 | tf_op jit(solution)/shard_map/first_sum/pallas_call | solution.py:150
  63.0 5.5 %all-to-all-start = ((bf16[16,2,32,128]{3,2,1,0:T(8,128)(2,1)}), bf16[16,2,32,128]{3,2,1,0:T(8,128)(2,1)S(1)}, u32[]{:S(2)}, u32[]{:S(2)}) async-start(bf16[16,2,32,128]{3,2,1,0:T(8,128)(2,1)} %get-tuple-element.64), calls=%async_computation | async-start | bytes 524288 | tf_op jit(solution)/shard_map/all_to_all | solution.py:331
  68.5 5.5 %old_sum.6 = (f32[2,32,128]{2,1,0:T(8,128)S(1)}, s32[65]{0:T(128)S(1)}, bf16[16,128,128]{2,1,0:T(8,128)(2,1)S(1)}) custom-call(s32[7,64]{1,0:T(8,128)S(1)} %copy-done.1, s32[7,64]{1,0:T(8,128)S(1)} %get-tuple-element.96.fresh_ref, bf16[2048,32,128]{2,1,0:T(8,128)(2,1)} %get-tuple-element.61.store_ref, bf16[7,1,32,128,128]{4,3,2,1,0:T(8,128)(2,1)} %own_ref.11, ...), custom_call_target="tpu_custom_call" | custom-call | flops 67108864 | bytes 6291456 | tf_op jit(solution)/shard_map/old_sum/pallas_call | solution.py:150
  83.7 4.6 %all-to-all-start.1 = ((bf16[16,2,32,128]{3,2,1,0:T(8,128)(2,1)}), bf16[16,2,32,128]{3,2,1,0:T(8,128)(2,1)S(1)}, u32[]{:S(2)}, u32[]{:S(2)}) async-start(bf16[16,2,32,128]{3,2,1,0:T(8,128)(2,1)} %get-tuple-element.71), calls=%async_computation.1 | async-start | bytes 524288 | tf_op jit(solution)/shard_map/all_to_all | solution.py:331
  88.3 6.1 %old_sum.7 = (f32[2,32,128]{2,1,0:T(8,128)S(1)}, s32[65]{0:T(128)S(1)}, bf16[16,128,128]{2,1,0:T(8,128)(2,1)S(1)}) custom-call(s32[7,64]{1,0:T(8,128)S(1)} %copy-done.1, s32[7,64]{1,0:T(8,128)S(1)} %get-tuple-element.96.fresh_ref, bf16[2048,32,128]{2,1,0:T(8,128)(2,1)} %get-tuple-element.61.store_ref, bf16[32,32,128]{2,1,0:T(8,128)(2,1)S(1)} %bitcast.36, ...), custom_call_target="tpu_custom_call" | custom-call | flops 67108864 | bytes 6291456 | tf_op jit(solution)/shard_map/old_sum/pallas_call | solution.py:150
  97.4 3.0 %collective-permute-start.23 = (f32[2,32,128]{2,1,0:T(8,128)S(1)}, f32[2,32,128]{2,1,0:T(8,128)S(1)}, u32[]{:S(2)}, u32[]{:S(2)}) collective-permute-start(f32[2,32,128]{2,1,0:T(8,128)S(1)} %fresh_sum.7.p0), channel_id=1, source_target_pairs={{0,2},{1,3},{2,0},{3,1},{4,6},{5,7},{6,4},{7,5},{8,10},{9,11},{10,... | collective-permute-start | bytes 98312 | tf_op jit(solution)/shard_map/ppermute | solution.py:324
  105.2 5.9 %all-to-all-start.2 = ((bf16[16,2,32,128]{3,2,1,0:T(8,128)(2,1)}), bf16[16,2,32,128]{3,2,1,0:T(8,128)(2,1)S(1)}, u32[]{:S(2)}, u32[]{:S(2)}) async-start(bf16[16,2,32,128]{3,2,1,0:T(8,128)(2,1)} %get-tuple-element.78), calls=%async_computation.2 | async-start | bytes 524288 | tf_op jit(solution)/shard_map/all_to_all | solution.py:331
  111.2 5.8 %old_sum.8 = (f32[2,32,128]{2,1,0:T(8,128)S(1)}, s32[65]{0:T(128)S(1)}, bf16[16,128,128]{2,1,0:T(8,128)(2,1)S(1)}) custom-call(s32[7,64]{1,0:T(8,128)S(1)} %copy-done.1, s32[7,64]{1,0:T(8,128)S(1)} %get-tuple-element.96.fresh_ref, bf16[2048,32,128]{2,1,0:T(8,128)(2,1)} %get-tuple-element.61.store_ref, bf16[32,32,128]{2,1,0:T(8,128)(2,1)S(1)} %bitcast.37, ...), custom_call_target="tpu_custom_call" | custom-call | flops 67108864 | bytes 6291456 | tf_op jit(solution)/shard_map/old_sum/pallas_call | solution.py:150
  120.7 3.1 %collective-permute-start.27 = (f32[2,32,128]{2,1,0:T(8,128)S(1)}, f32[2,32,128]{2,1,0:T(8,128)S(1)}, u32[]{:S(2)}, u32[]{:S(2)}) collective-permute-start(f32[2,32,128]{2,1,0:T(8,128)S(1)} %fresh_sum.8.p0), channel_id=1, source_target_pairs={{0,3},{1,2},{2,1},{3,0},{4,7},{5,6},{6,5},{7,4},{8,11},{9,10},{10,... | collective-permute-start | bytes 98312 | tf_op jit(solution)/shard_map/ppermute | solution.py:324
  126.3 4.5 %all-to-all-start.3 = ((bf16[16,2,32,128]{3,2,1,0:T(8,128)(2,1)}), bf16[16,2,32,128]{3,2,1,0:T(8,128)(2,1)S(1)}, u32[]{:S(2)}, u32[]{:S(2)}) async-start(bf16[16,2,32,128]{3,2,1,0:T(8,128)(2,1)} %get-tuple-element.85), calls=%async_computation.3 | async-start | bytes 524288 | tf_op jit(solution)/shard_map/all_to_all | solution.py:331
  130.9 5.8 %old_sum.9 = (f32[2,32,128]{2,1,0:T(8,128)S(1)}, s32[65]{0:T(128)S(1)}, bf16[16,128,128]{2,1,0:T(8,128)(2,1)S(1)}) custom-call(s32[7,64]{1,0:T(8,128)S(1)} %copy-done.1, s32[7,64]{1,0:T(8,128)S(1)} %get-tuple-element.96.fresh_ref, bf16[2048,32,128]{2,1,0:T(8,128)(2,1)} %get-tuple-element.61.store_ref, bf16[32,32,128]{2,1,0:T(8,128)(2,1)S(1)} %bitcast.38, ...), custom_call_target="tpu_custom_call" | custom-call | flops 67108864 | bytes 6291456 | tf_op jit(solution)/shard_map/old_sum/pallas_call | solution.py:150
  147.9 4.7 %all-to-all-start.4 = ((bf16[16,2,32,128]{3,2,1,0:T(8,128)(2,1)}), bf16[16,2,32,128]{3,2,1,0:T(8,128)(2,1)S(1)}, u32[]{:S(2)}, u32[]{:S(2)}) async-start(bf16[16,2,32,128]{3,2,1,0:T(8,128)(2,1)} %get-tuple-element.92), calls=%async_computation.4 | async-start | bytes 524288 | tf_op jit(solution)/shard_map/all_to_all | solution.py:331
  152.6 5.8 %old_sum.10 = (f32[2,32,128]{2,1,0:T(8,128)S(1)}, s32[65]{0:T(128)S(1)}, bf16[16,128,128]{2,1,0:T(8,128)(2,1)S(1)}) custom-call(s32[7,64]{1,0:T(8,128)S(1)} %copy-done.1, s32[7,64]{1,0:T(8,128)S(1)} %get-tuple-element.96.fresh_ref, bf16[2048,32,128]{2,1,0:T(8,128)(2,1)} %get-tuple-element.61.store_ref, bf16[32,32,128]{2,1,0:T(8,128)(2,1)S(1)} %bitcast.39, ...), custom_call_target="tpu_custom_call" | custom-call | flops 67108864 | bytes 6291456 | tf_op jit(solution)/shard_map/old_sum/pallas_call | solution.py:150
  167.7 5.7 %all-to-all-start.5 = ((bf16[16,2,32,128]{3,2,1,0:T(8,128)(2,1)}), bf16[16,2,32,128]{3,2,1,0:T(8,128)(2,1)S(1)}, u32[]{:S(2)}, u32[]{:S(2)}) async-start(bf16[16,2,32,128]{3,2,1,0:T(8,128)(2,1)} %get-tuple-element.99), calls=%async_computation.5 | async-start | bytes 524288 | tf_op jit(solution)/shard_map/all_to_all | solution.py:331
  173.4 5.9 %old_sum.11 = (f32[2,32,128]{2,1,0:T(8,128)S(1)}, s32[65]{0:T(128)S(1)}, bf16[16,128,128]{2,1,0:T(8,128)(2,1)S(1)}) custom-call(s32[7,64]{1,0:T(8,128)S(1)} %copy-done.1, s32[7,64]{1,0:T(8,128)S(1)} %get-tuple-element.96.fresh_ref, bf16[2048,32,128]{2,1,0:T(8,128)(2,1)} %get-tuple-element.61.store_ref, bf16[32,32,128]{2,1,0:T(8,128)(2,1)S(1)} %bitcast.40, ...), custom_call_target="tpu_custom_call" | custom-call | flops 67108864 | bytes 6291456 | tf_op jit(solution)/shard_map/old_sum/pallas_call | solution.py:150
  182.0 2.9 %collective-permute-start.35 = (f32[2,32,128]{2,1,0:T(8,128)S(1)}, f32[2,32,128]{2,1,0:T(8,128)S(1)}, u32[]{:S(2)}, u32[]{:S(2)}) collective-permute-start(f32[2,32,128]{2,1,0:T(8,128)S(1)} %fresh_sum.11.p0), channel_id=1, source_target_pairs={{0,2},{1,3},{2,0},{3,1},{4,6},{5,7},{6,4},{7,5},{8,10},{9,11},{10,... | collective-permute-start | bytes 98312 | tf_op jit(solution)/shard_map/ppermute | solution.py:324
  189.0 16.1 %collective-permute-start.37 = (bf16[7,32,128]{2,1,0:T(8,128)(2,1)S(1)}, bf16[7,32,128]{2,1,0:T(8,128)(2,1)S(1)}, u32[]{:S(2)}, u32[]{:S(2)}) collective-permute-start(bf16[7,32,128]{2,1,0:T(8,128)(2,1)S(1)} %get-tuple-element.116), channel_id=1, source_target_pairs={{0,4},{4,0},{1,5},{5,1},{2,6},{6,2},{3,7},{7,3},{8,12},{12,8},{9,1... | collective-permute-start | bytes 172040 | tf_op jit(solution)/shard_map/ppermute | solution.py:23
  (132 shorter events, 87.3 us)
Async XLA Ops:
  2.0 42.0 %collective-permute-start.13 = (bf16[7,1,32,128,128]{4,3,2,1,0:T(8,128)(2,1)}, bf16[7,1,32,128,128]{4,3,2,1,0:T(8,128)(2,1)}, u32[]{:S(2)}, u32[]{:S(2)}) collective-permute-start(bf16[7,1,32,128,128]{4,3,2,1,0:T(8,128)(2,1)} %own_ref.11), channel_id=1, source_target_pairs={{0,4},{4,0},{1,5},{5,1},{2,6},{6,2},{3,7},{7,3},{8,12},{12,8},{9,1... | collective-permute-start | bytes 22020104 | tf_op jit(solution)/shard_map/ppermute | solution.py:23
  3.5 7.2 %collective-permute-start.1 = (bf16[2,17,32,128]{3,2,1,0:T(8,128)(2,1)S(1)}, bf16[2,17,32,128]{3,2,1,0:T(8,128)(2,1)S(1)}, u32[]{:S(2)}, u32[]{:S(2)}) collective-permute-start(bf16[2,17,32,128]{3,2,1,0:T(8,128)(2,1)S(1)} %pad_maximum_fusion.2), channel_id=1, source_target_pairs={{0,64},{4,20},{8,72},{12,28},{16,80},{20,4},{24,88},{28,12},{32,96... | collective-permute-start | bytes 835592 | tf_op jit(solution)/shard_map/ppermute | solution.py:39
  6.5 7.2 %collective-permute-start.2 = (bf16[2,17,32,128]{3,2,1,0:T(8,128)(2,1)S(1)}, bf16[2,17,32,128]{3,2,1,0:T(8,128)(2,1)S(1)}, u32[]{:S(2)}, u32[]{:S(2)}) collective-permute-start(bf16[2,17,32,128]{3,2,1,0:T(8,128)(2,1)S(1)} %pad_maximum_fusion.2), channel_id=1, source_target_pairs={{0,96},{4,28},{8,104},{12,20},{16,112},{20,12},{24,120},{28,4},{32... | collective-permute-start | bytes 835592 | tf_op jit(solution)/shard_map/ppermute | solution.py:39
  7.3 6.9 %collective-permute-start.3 = (bf16[2,17,32,128]{3,2,1,0:T(8,128)(2,1)S(1)}, bf16[2,17,32,128]{3,2,1,0:T(8,128)(2,1)S(1)}, u32[]{:S(2)}, u32[]{:S(2)}) collective-permute-start(bf16[2,17,32,128]{3,2,1,0:T(8,128)(2,1)S(1)} %pad_maximum_fusion.2), channel_id=1, source_target_pairs={{0,32},{4,12},{8,40},{12,4},{16,48},{20,28},{24,56},{28,20},{32,0}... | collective-permute-start | bytes 835592 | tf_op jit(solution)/shard_map/ppermute | solution.py:39
  15.1 12.0 %collective-permute-start.9 = (bf16[4,17,32,128]{3,2,1,0:T(8,128)(2,1)}, bf16[4,17,32,128]{3,2,1,0:T(8,128)(2,1)S(1)}, u32[]{:S(2)}, u32[]{:S(2)}) collective-permute-start(bf16[4,17,32,128]{3,2,1,0:T(8,128)(2,1)} %pad_maximum_fusion.1), channel_id=1, source_target_pairs={{0,12},{4,32},{8,20},{12,40},{16,28},{20,48},{24,4},{28,56},{32,44... | collective-permute-start | bytes 1671176 | tf_op jit(solution)/shard_map/ppermute | solution.py:44
  18.5 9.7 %collective-permute-start.10 = (bf16[4,17,32,128]{3,2,1,0:T(8,128)(2,1)}, bf16[4,17,32,128]{3,2,1,0:T(8,128)(2,1)S(1)}, u32[]{:S(2)}, u32[]{:S(2)}) collective-permute-start(bf16[4,17,32,128]{3,2,1,0:T(8,128)(2,1)} %pad_maximum_fusion.1), channel_id=1, source_target_pairs={{0,28},{4,96},{8,4},{12,104},{16,12},{20,112},{24,20},{28,120},{32... | collective-permute-start | bytes 1671176 | tf_op jit(solution)/shard_map/ppermute | solution.py:45
  21.1 11.9 %collective-permute-start.4 = (bf16[4,17,32,128]{3,2,1,0:T(8,128)(2,1)S(1)}, bf16[4,17,32,128]{3,2,1,0:T(8,128)(2,1)S(1)}, u32[]{:S(2)}, u32[]{:S(2)}) collective-permute-start(bf16[4,17,32,128]{3,2,1,0:T(8,128)(2,1)S(1)} %pad_maximum_fusion), channel_id=1, source_target_pairs={{0,8},{4,36},{8,16},{12,44},{16,24},{20,52},{24,0},{28,60},{32,40}... | collective-permute-start | bytes 1671176 | tf_op jit(solution)/shard_map/ppermute | solution.py:44
  21.2 15.2 %collective-permute-start.5 = (bf16[4,17,32,128]{3,2,1,0:T(8,128)(2,1)S(1)}, bf16[4,17,32,128]{3,2,1,0:T(8,128)(2,1)S(1)}, u32[]{:S(2)}, u32[]{:S(2)}) collective-permute-start(bf16[4,17,32,128]{3,2,1,0:T(8,128)(2,1)S(1)} %pad_maximum_fusion), channel_id=1, source_target_pairs={{0,24},{4,100},{8,0},{12,108},{16,8},{20,116},{24,16},{28,124},{32... | collective-permute-start | bytes 1671176 | tf_op jit(solution)/shard_map/ppermute | solution.py:45
  27.1 10.2 %collective-permute-start.8 = (bf16[4,17,32,128]{3,2,1,0:T(8,128)(2,1)}, bf16[4,17,32,128]{3,2,1,0:T(8,128)(2,1)}, u32[]{:S(2)}, u32[]{:S(2)}) collective-permute-start(bf16[4,17,32,128]{3,2,1,0:T(8,128)(2,1)} %pad_maximum_fusion.1), channel_id=1, source_target_pairs={{0,4},{4,0},{1,5},{5,1},{2,6},{6,2},{3,7},{7,3},{8,12},{12,8},{9,1... | collective-permute-start | bytes 1671176 | tf_op jit(solution)/shard_map/ppermute | solution.py:23
  28.2 12.5 %collective-permute-start.11 = (bf16[2,17,32,128]{3,2,1,0:T(8,128)(2,1)}, bf16[2,17,32,128]{3,2,1,0:T(8,128)(2,1)}, u32[]{:S(2)}, u32[]{:S(2)}) collective-permute-start(bf16[2,17,32,128]{3,2,1,0:T(8,128)(2,1)} %slice.120), channel_id=1, source_target_pairs={{0,32},{4,12},{8,40},{12,20},{16,48},{20,28},{24,56},{28,4},{32,64... | collective-permute-start | bytes 835592 | tf_op jit(solution)/shard_map/ppermute | solution.py:46
  33.0 9.5 %collective-permute-start.12 = (bf16[2,17,32,128]{3,2,1,0:T(8,128)(2,1)}, bf16[2,17,32,128]{3,2,1,0:T(8,128)(2,1)}, u32[]{:S(2)}, u32[]{:S(2)}) collective-permute-start(bf16[2,17,32,128]{3,2,1,0:T(8,128)(2,1)} %slice.121), channel_id=1, source_target_pairs={{0,96},{4,28},{8,104},{12,4},{16,112},{20,12},{24,120},{28,20},{32... | collective-permute-start | bytes 835592 | tf_op jit(solution)/shard_map/ppermute | solution.py:47
  36.5 7.2 %collective-permute-start.6 = (bf16[2,17,32,128]{3,2,1,0:T(8,128)(2,1)}, bf16[2,17,32,128]{3,2,1,0:T(8,128)(2,1)}, u32[]{:S(2)}, u32[]{:S(2)}) collective-permute-start(bf16[2,17,32,128]{3,2,1,0:T(8,128)(2,1)} %slice.115), channel_id=1, source_target_pairs={{0,8},{4,36},{8,16},{12,44},{16,24},{20,52},{24,0},{28,60},{32,40}... | collective-permute-start | bytes 835592 | tf_op jit(solution)/shard_map/ppermute | solution.py:46
  37.3 6.7 %collective-permute-start.7 = (bf16[2,17,32,128]{3,2,1,0:T(8,128)(2,1)}, bf16[2,17,32,128]{3,2,1,0:T(8,128)(2,1)}, u32[]{:S(2)}, u32[]{:S(2)}) collective-permute-start(bf16[2,17,32,128]{3,2,1,0:T(8,128)(2,1)} %slice.116), channel_id=1, source_target_pairs={{0,24},{4,100},{8,0},{12,108},{16,8},{20,116},{24,16},{28,124},{32... | collective-permute-start | bytes 835592 | tf_op jit(solution)/shard_map/ppermute | solution.py:47
  40.6 16.7 %collective-permute-start.18 = (bf16[8,1,128,128]{3,2,1,0:T(8,128)(2,1)S(1)}, bf16[8,1,128,128]{3,2,1,0:T(8,128)(2,1)S(1)}, u32[]{:S(2)}, u32[]{:S(2)}) collective-permute-start(bf16[8,1,128,128]{3,2,1,0:T(8,128)(2,1)S(1)} %copy-done), channel_id=1, source_target_pairs={{0,4},{4,0},{1,5},{5,1},{2,6},{6,2},{3,7},{7,3},{8,12},{12,8},{9,1... | collective-permute-start | bytes 786440 | tf_op jit(solution)/shard_map/ppermute | solution.py:23
  51.2 6.1 %collective-permute-start.17 = (bf16[8,1,32,128]{3,2,1,0:T(8,128)(2,1)S(1)}, bf16[8,1,32,128]{3,2,1,0:T(8,128)(2,1)S(1)}, u32[]{:S(2)}, u32[]{:S(2)}) collective-permute-start(bf16[8,1,32,128]{3,2,1,0:T(8,128)(2,1)S(1)} %get-tuple-element.112), channel_id=1, source_target_pairs={{0,4},{4,0},{1,5},{5,1},{2,6},{6,2},{3,7},{7,3},{8,12},{12,8},{9,1... | collective-permute-start | bytes 196616 | tf_op jit(solution)/shard_map/ppermute | solution.py:23
  54.7 4.8 %collective-permute-start.15 = (f32[2,32,128]{2,1,0:T(8,128)}, f32[2,32,128]{2,1,0:T(8,128)S(1)}, u32[]{:S(2)}, u32[]{:S(2)}) collective-permute-start(f32[2,32,128]{2,1,0:T(8,128)} %get-tuple-element.56.p0), channel_id=1, source_target_pairs={{0,2},{1,3},{2,0},{3,1},{4,6},{5,7},{6,4},{7,5},{8,10},{9,11},{10,... | collective-permute-start | bytes 98312 | tf_op jit(solution)/shard_map/ppermute | solution.py:324
  63.0 13.0 %all-to-all-start = ((bf16[16,2,32,128]{3,2,1,0:T(8,128)(2,1)}), bf16[16,2,32,128]{3,2,1,0:T(8,128)(2,1)S(1)}, u32[]{:S(2)}, u32[]{:S(2)}) async-start(bf16[16,2,32,128]{3,2,1,0:T(8,128)(2,1)} %get-tuple-element.64), calls=%async_computation | async-start | bytes 524288 | tf_op jit(solution)/shard_map/all_to_all | solution.py:331
  83.7 12.2 %all-to-all-start.1 = ((bf16[16,2,32,128]{3,2,1,0:T(8,128)(2,1)}), bf16[16,2,32,128]{3,2,1,0:T(8,128)(2,1)S(1)}, u32[]{:S(2)}, u32[]{:S(2)}) async-start(bf16[16,2,32,128]{3,2,1,0:T(8,128)(2,1)} %get-tuple-element.71), calls=%async_computation.1 | async-start | bytes 524288 | tf_op jit(solution)/shard_map/all_to_all | solution.py:331
  105.2 13.5 %all-to-all-start.2 = ((bf16[16,2,32,128]{3,2,1,0:T(8,128)(2,1)}), bf16[16,2,32,128]{3,2,1,0:T(8,128)(2,1)S(1)}, u32[]{:S(2)}, u32[]{:S(2)}) async-start(bf16[16,2,32,128]{3,2,1,0:T(8,128)(2,1)} %get-tuple-element.78), calls=%async_computation.2 | async-start | bytes 524288 | tf_op jit(solution)/shard_map/all_to_all | solution.py:331
  120.7 4.7 %collective-permute-start.27 = (f32[2,32,128]{2,1,0:T(8,128)S(1)}, f32[2,32,128]{2,1,0:T(8,128)S(1)}, u32[]{:S(2)}, u32[]{:S(2)}) collective-permute-start(f32[2,32,128]{2,1,0:T(8,128)S(1)} %fresh_sum.8.p0), channel_id=1, source_target_pairs={{0,3},{1,2},{2,1},{3,0},{4,7},{5,6},{6,5},{7,4},{8,11},{9,10},{10,... | collective-permute-start | bytes 98312 | tf_op jit(solution)/shard_map/ppermute | solution.py:324
  126.3 12.1 %all-to-all-start.3 = ((bf16[16,2,32,128]{3,2,1,0:T(8,128)(2,1)}), bf16[16,2,32,128]{3,2,1,0:T(8,128)(2,1)S(1)}, u32[]{:S(2)}, u32[]{:S(2)}) async-start(bf16[16,2,32,128]{3,2,1,0:T(8,128)(2,1)} %get-tuple-element.85), calls=%async_computation.3 | async-start | bytes 524288 | tf_op jit(solution)/shard_map/all_to_all | solution.py:331
  147.9 12.3 %all-to-all-start.4 = ((bf16[16,2,32,128]{3,2,1,0:T(8,128)(2,1)}), bf16[16,2,32,128]{3,2,1,0:T(8,128)(2,1)S(1)}, u32[]{:S(2)}, u32[]{:S(2)}) async-start(bf16[16,2,32,128]{3,2,1,0:T(8,128)(2,1)} %get-tuple-element.92), calls=%async_computation.4 | async-start | bytes 524288 | tf_op jit(solution)/shard_map/all_to_all | solution.py:331
  167.7 13.2 %all-to-all-start.5 = ((bf16[16,2,32,128]{3,2,1,0:T(8,128)(2,1)}), bf16[16,2,32,128]{3,2,1,0:T(8,128)(2,1)S(1)}, u32[]{:S(2)}, u32[]{:S(2)}) async-start(bf16[16,2,32,128]{3,2,1,0:T(8,128)(2,1)} %get-tuple-element.99), calls=%async_computation.5 | async-start | bytes 524288 | tf_op jit(solution)/shard_map/all_to_all | solution.py:331
  189.0 17.0 %collective-permute-start.37 = (bf16[7,32,128]{2,1,0:T(8,128)(2,1)S(1)}, bf16[7,32,128]{2,1,0:T(8,128)(2,1)S(1)}, u32[]{:S(2)}, u32[]{:S(2)}) collective-permute-start(bf16[7,32,128]{2,1,0:T(8,128)(2,1)S(1)} %get-tuple-element.116), channel_id=1, source_target_pairs={{0,4},{4,0},{1,5},{5,1},{2,6},{6,2},{3,7},{7,3},{8,12},{12,8},{9,1... | collective-permute-start | bytes 172040 | tf_op jit(solution)/shard_map/ppermute | solution.py:23
  (29 other events, 228.9 us)
